TPU v7x, 32 devices: a whole 2x2x4 slice. The times are simulated.
32 devices in a mesh: group: 4 (over y, core), vocab: 8 (over z, x).
Axes of the slice: x: 2, y: 2, z: 4, core: 2. Of those that a mesh axis runs over, the one named last changes fastest.
Arguments:
- hidden: bfloat16 [2, 2048, 2304], P(None, ('group', 'vocab')), may hold values from -120 to 120
- head: bfloat16 [32768, 2304], P('vocab'), may hold values from -0.125 to 0.125
- factor_u: bfloat16 [32768, 64], P(('group', 'vocab')), may hold values from -0.29882812 to 0.29882812
- factor_v: bfloat16 [2304, 64], P('vocab'), may hold values from -0.125 to 0.125
- sampled: int32 [2, 2048], P(None, 'group'), may hold values from 0 to 32767
Outputs:
- logprob: float32 [2, 2048], P(None, 'group')
- log_total: float32 [2, 2048], P(None, 'group')
All inputs are finite; a program needn't handle non-finite values.
Results may differ from a plain program's by a relative error of at most 0.00044.
Values may be sent and summed in bfloat16 or wider, within the bound.
No kernel may reach another device: no remote copies, remote signals or barrier semaphores. Data moves between devices by JAX's collectives and lax.ppermute only.
A program may use at most 128 MiB of HBM per device.

v0:
```python
import jax
import jax.numpy as jnp
from jax import lax
from jax.sharding import PartitionSpec as P


def body(hidden, head, factor_u, factor_v, sampled):
    voc_dev = head.shape[0]
    vocab_index = lax.axis_index("vocab")
    total_dev = lax.axis_size("group") * lax.axis_size("vocab")
    rows_each, rank_cols = factor_u.shape
    fragments = factor_u.reshape(total_dev, rows_each * rank_cols // total_dev)
    spread = lax.all_to_all(fragments, ("group", "vocab"), split_axis=0, concat_axis=0, tiled=True)
    ordered = (
        spread.reshape(lax.axis_size("vocab"), lax.axis_size("group"), -1)
        .transpose(1, 0, 2)
        .reshape(total_dev, -1)
    )
    assembled = lax.all_to_all(
        ordered, ("group", "vocab"), split_axis=0, concat_axis=0, tiled=True
    ).reshape(rows_each, rank_cols)
    owned = lax.all_gather(assembled, "group", axis=0, tiled=True)
    full_v = lax.all_gather(factor_v, "vocab", axis=0, tiled=True)
    first_entry = vocab_index * voc_dev
    logprobs = []
    totals = []
    for step in range(hidden.shape[0]):
        rows = lax.all_gather(hidden[step], "vocab", axis=0, tiled=True)
        base = jnp.dot(rows, head.T, preferred_element_type=jnp.float32)
        projected = jnp.dot(rows, full_v, preferred_element_type=jnp.float32).astype(jnp.bfloat16)
        logits = base + jnp.dot(projected, owned.T, preferred_element_type=jnp.float32)
        offset = sampled[step] - first_entry
        inside = (offset >= 0) & (offset < voc_dev)
        column = jnp.clip(offset, 0, voc_dev - 1)
        local_pick = jnp.take_along_axis(logits, column[:, None], axis=1)[:, 0]
        local_pick = jnp.where(inside, local_pick, jnp.zeros_like(local_pick))
        local_top = jnp.max(logits, axis=1)
        top = lax.pmax(local_top, "vocab")
        local_sum = jnp.sum(jnp.exp(logits - top[:, None]), axis=1)
        total, picked = lax.psum((local_sum, local_pick), "vocab")
        log_total = top + jnp.log(total)
        logprobs.append(picked - log_total)
        totals.append(log_total)
    return (jnp.stack(logprobs), jnp.stack(totals))


def solution(mesh):
    in_specs = (
        P(None, ("group", "vocab"), None),
        P("vocab", None),
        P(("group", "vocab"), None),
        P("vocab", None),
        P(None, "group"),
    )
    out_specs = (P(None, "group"), P(None, "group"))
    return jax.shard_map(body, mesh=mesh, in_specs=in_specs, out_specs=out_specs, check_vma=False)
```

profile of v0, /device:TPU:0, one launch (start us, length us, event | category | flops | bytes accessed | tf_op | source)
XLA Modules:
  0.0 209.6 jit_solution(8426570040792395231)
XLA Ops:
  7.2 0.0 all-gather.6.cloned.1.call-start
  7.2 1.9 fusion.28
  9.1 0.0 all-gather.6.cloned.1.call-update
  9.1 1.1 copy.11
  10.2 0.2 all_to_all.16
  10.4 0.5 broadcast.138
  10.9 1.4 reduce.6
  12.3 0.7 reshape.127
  13.0 7.3 %all-to-all-start = ((bf16[32,2,1024]{2,1,0:T(2,128)(2,1)}), bf16[32,2,1024]{2,1,0:T(2,128)(2,1)S(1)}, u32[]{:S(2)}, u32[]{:S(2)}) async-start(bf16[32,2,1024]{2,1,0:T(2,128)(2,1)} %reshape.127), calls=%async_computation | async-start | bytes 262144 | tf_op jit(solution)/shard_map/all_to_all | solution.py:13
  20.3 0.0 all-gather.8.cloned.1.call-start
  20.4 0.7 all-gather.8.cloned.1.call-update
  21.1 0.8 compare_select_fusion.1
  21.9 33.7 %all-gather.2 = bf16[8,288,64]{1,2,0:T(8,128)(2,1)S(1)} all-gather(bf16[1,288,64]{1,2,0:T(8,128)(2,1)} %bitcast.59), channel_id=1, replica_groups=mesh['group'=4,'vocab'=8] {'vocab'}, dimensions={0}, use_global_device_ids=true | all-gather | bytes 331776 | tf_op jit(solution)/shard_map/all_gather | solution.py:23
  55.6 0.0 all-to-all-done
  55.6 0.1 reshape.128
  55.7 0.8 reduce.1
  56.5 0.1 reshape.88
  56.5 0.1 copy.17
  56.6 0.7 reduce.7
  57.3 0.7 reshape.129
  58.0 4.5 %all-to-all-start.1 = ((bf16[32,2,1024]{2,1,0:T(2,128)(2,1)}), bf16[32,2,1024]{2,1,0:T(2,128)(2,1)S(1)}, u32[]{:S(2)}, u32[]{:S(2)}) async-start(bf16[32,2,1024]{2,1,0:T(2,128)(2,1)} %reshape.129), calls=%async_computation.1 | async-start | bytes 262144 | tf_op jit(solution)/shard_map/all_to_all | solution.py:19
  62.5 0.8 and_reduce_fusion.1
  63.3 0.2 copy.10
  63.6 0.3 reshape.110
  63.9 7.5 %all-to-all-done.1 = bf16[32,2,1024]{2,1,0:T(2,128)(2,1)S(1)} async-done(((bf16[32,2,1024]{2,1,0:T(2,128)(2,1)}), bf16[32,2,1024]{2,1,0:T(2,128)(2,1)S(1)}, u32[]{:S(2)}, u32[]{:S(2)}) %all-to-all-start.1) | async-done | bytes 131104 | tf_op jit(solution)/shard_map/all_to_all | solution.py:19
  71.4 0.1 reshape.130
  71.5 0.8 reduce.2
  72.3 0.2 reshape.89
  72.5 10.2 %all_gather.14 = bf16[4096,64]{1,0:T(8,128)(2,1)S(1)} all-gather(bf16[1024,64]{1,0:T(8,128)(2,1)S(1)} %reshape.89), channel_id=1, replica_groups=mesh['group'=4,'vocab'=8] {'group'}, dimensions={0}, use_global_device_ids=true | all-gather | bytes 655360 | tf_op jit(solution)/shard_map/all_gather | solution.py:22
  82.7 0.0 all-gather.6.cloned.1.call-done
  82.7 7.0 %fusion.16 = f32[512,4096]{1,0:T(8,128)} fusion(bf16[4096,64]{1,0:T(8,128)(2,1)S(1)} %all_gather.14, bf16[2304,64]{0,1:T(8,128)(2,1)S(1)} %reshape.110, bf16[1,512,2304]{2,1,0:T(8,128)(2,1)} %all-gather.6.cloned.1.call-done), kind=kOutput, calls=%fused_computation.15 | convolution fusion | flops 419463168 | bytes 11567104 | tf_op jit(solution)/shard_map/dot_general | solution.py:31
  89.7 17.8 %fusion.30 = (f32[512]{0:T(512)S(1)}, f32[512,4096]{1,0:T(8,128)}) fusion(f32[512,4096]{1,0:T(8,128)} %fusion.16, bf16[4096,2304]{1,0:T(8,128)(2,1)} %param.8, bf16[1,512,2304]{2,1,0:T(8,128)(2,1)} %all-gather.6.cloned.1.call-done), kind=kOutput, calls=%fused_computation.49 | convolution fusion | flops 9667870720 | bytes 38012928 | tf_op jit(solution)/shard_map/dot_general | solution.py:29
  107.5 8.1 %gather_fusion = f32[512]{0:T(512)S(1)} fusion(f32[512,4096]{1,0:T(8,128)} %get-tuple-element.24, s32[512]{0:T(512)S(1)} %bitcast.55), kind=kCustom, calls=%fused_computation.clone | custom fusion | bytes 8192 | tf_op jit(solution)/shard_map/jit(take_along_axis)/gather | solution.py:35
  115.7 8.8 %all-gather.8.cloned.1.call-done = bf16[1,512,2304]{2,1,0:T(8,128)(2,1)} async-done(((bf16[1,64,2304]{2,1,0:T(8,128)(2,1)}), bf16[1,512,2304]{2,1,0:T(8,128)(2,1)}) %all-gather.8.cloned.1.call-update) | async-done | bytes 2359312 | tf_op jit(solution)/shard_map/all_gather | solution.py:28
  124.4 7.0 %fusion.13 = f32[512,4096]{1,0:T(8,128)} fusion(bf16[4096,64]{1,0:T(8,128)(2,1)S(1)} %all_gather.14, bf16[2304,64]{0,1:T(8,128)(2,1)S(1)} %reshape.110, bf16[1,512,2304]{2,1,0:T(8,128)(2,1)} %all-gather.8.cloned.1.call-done), kind=kOutput, calls=%fused_computation.14 | convolution fusion | flops 419463168 | bytes 11567104 | tf_op jit(solution)/shard_map/dot_general | solution.py:31
  131.5 17.9 %fusion.29 = (f32[512]{0:T(512)S(1)}, f32[512,4096]{1,0:T(8,128)}) fusion(f32[512,4096]{1,0:T(8,128)} %fusion.13, bf16[4096,2304]{1,0:T(8,128)(2,1)} %param.8, bf16[1,512,2304]{2,1,0:T(8,128)(2,1)} %all-gather.8.cloned.1.call-done), kind=kOutput, calls=%fused_computation.48 | convolution fusion | flops 9667870720 | bytes 38012928 | tf_op jit(solution)/shard_map/dot_general | solution.py:29
  149.3 8.2 %gather_fusion.1 = f32[512]{0:T(512)S(1)} fusion(f32[512,4096]{1,0:T(8,128)} %get-tuple-element.22, s32[512]{0:T(512)S(1)} %bitcast.56), kind=kCustom, calls=%fused_computation.1.clone | custom fusion | bytes 8192 | tf_op jit(solution)/shard_map/jit(take_along_axis)/gather | solution.py:35
  157.5 19.5 %all-reduce.1 = (f32[512]{0:T(512)S(1)}, f32[512]{0:T(512)S(1)}) all-reduce(f32[512]{0:T(512)S(1)} %get-tuple-element.21, f32[512]{0:T(512)S(1)} %get-tuple-element.23), channel_id=1, replica_groups=mesh['group'=4,'vocab'=8] {'vocab'}, use_global_device_ids=true, to_apply=%region_7.9 | all-reduce | flops 1024 | bytes 8192 | tf_op jit(solution)/shard_map/pmax | solution.py:38
  177.1 7.1 %exponential_reduce_fusion = (f32[512]{0:T(512)S(1)}, f32[512]{0:T(512)S(1)}) fusion(f32[512,4096]{1,0:T(8,128)} %get-tuple-element.22, f32[512]{0:T(512)S(1)} %get-tuple-element.9, f32[512,4096]{1,0:T(8,128)} %get-tuple-element.24, f32[512]{0:T(512)S(1)} %get-tuple-element.10), kind=kLoop, calls=%fused_computation.2 | loop fusion | flops 8387584 | bytes 16785408 | tf_op jit(solution)/shard_map/reduce_sum | solution.py:39
  184.2 17.4 %all-reduce = (f32[512]{0:T(512)S(1)}, f32[512]{0:T(512)S(1)}, f32[512]{0:T(512)S(1)}, f32[512]{0:T(512)S(1)}) all-reduce(f32[512]{0:T(512)S(1)} %get-tuple-element.25, f32[512]{0:T(512)S(1)} %get-tuple-element.27, f32[512]{0:T(512)S(1)} %get-tuple-element.26, ...), channel_id=1, replica_groups=mesh['group'=4,'vocab'=8] {'vocab'}, use_global_device_ids=true, to_apply=%region_5.7 | all-reduce | flops 2048 | bytes 16384 | tf_op jit(solution)/shard_map/psum | solution.py:40
  201.6 0.6 pad_maximum_fusion.1
  202.2 0.6 pad_maximum_fusion
  (9 shorter events, 0.1 us)
Async XLA Ops:
  7.2 75.6 %all-gather.6.cloned.1.call-start = ((), (), s32[]{:S(2)}) async-start(), calls=%async_computation.2 | async-start | bytes 2654208 | tf_op jit(solution)/shard_map/all_gather | solution.py:28
  13.0 42.6 %all-to-all-start = ((bf16[32,2,1024]{2,1,0:T(2,128)(2,1)}), bf16[32,2,1024]{2,1,0:T(2,128)(2,1)S(1)}, u32[]{:S(2)}, u32[]{:S(2)}) async-start(bf16[32,2,1024]{2,1,0:T(2,128)(2,1)} %reshape.127), calls=%async_computation | async-start | bytes 262144 | tf_op jit(solution)/shard_map/all_to_all | solution.py:13
  20.3 104.1 %all-gather.8.cloned.1.call-start = ((), (), s32[]{:S(2)}) async-start(), calls=%async_computation.3 | async-start | bytes 2654208 | tf_op jit(solution)/shard_map/all_gather | solution.py:28
  58.0 13.4 %all-to-all-start.1 = ((bf16[32,2,1024]{2,1,0:T(2,128)(2,1)}), bf16[32,2,1024]{2,1,0:T(2,128)(2,1)S(1)}, u32[]{:S(2)}, u32[]{:S(2)}) async-start(bf16[32,2,1024]{2,1,0:T(2,128)(2,1)} %reshape.129), calls=%async_computation.1 | async-start | bytes 262144 | tf_op jit(solution)/shard_map/all_to_all | solution.py:19
Sparse Core Ops, SparseCore 0:
  10.2 60.8 all-gather.5
  73.3 51.1 all-gather.7
where the time goes:
time: 211 us; the launch traced here: 210 us
  blocking collectives  80.8 us (38%)
  matrix products  49.7 us (24%)
  local copies, waits for them, and re-layouts  22.6 us (11%)
  waiting for transfers between devices  17 us (8%)
  between operations  14.2 us (7%)
  other arithmetic  13.6 us (6%)
  starting transfers between devices  11.9 us (6%)
    dot_general x2, matrix products, body(): base = jnp.dot(rows, head.T, preferred_element_type=jnp.float32)  35.6 us
    all_gather x1, blocking collectives, body(): full_v = lax.all_gather(factor_v, 'vocab', axis=0, tiled=True)  33.7 us
    pmax x1, blocking collectives, body(): top = lax.pmax(local_top, 'vocab')  19.5 us
    psum x1, blocking collectives, body(): total, picked = lax.psum((local_sum, local_pick), 'vocab')  17.4 us
    gather x2, local copies, waits for them, and re-layouts, body(): local_pick = jnp.take_along_axis(logits, column[:, None], axis=1)[:, 0]  16.3 us
    dot_general x2, matrix products, body(): jnp.dot(projected, owned.T, preferred_element_type=jnp.float32)  14 us
    all_gather x1, blocking collectives, body(): owned = lax.all_gather(assembled, 'group', axis=0, tiled=True)  10.2 us
    all_gather x2, waiting for transfers between devices, body(): rows = lax.all_gather(hidden[step], 'vocab', axis=0, tiled=True)  8.76 us
  transfers between devices with their start and end apart: 4, of which 2 were waited for; matrix products, arithmetic and copies ran while one was open for 20% of the time, Pallas kernels for 0%

commit v1 on v0

v1 whole, which is shorter than its diff:
```python
import jax
import jax.numpy as jnp
from jax import lax
from jax.experimental import pallas as pl
from jax.experimental.pallas import tpu as pltpu
from jax.sharding import PartitionSpec as P

VMEM_LIMIT = 40 * 1024 * 1024
NT = (((1,), (1,)), ((), ()))


def ring_order(n):
    if n % 2:
        return list(range(n))
    return [2 * i for i in range(n // 2)] + [2 * i + 1 for i in reversed(range(n // 2))]


def tile_rows(entries):
    for rows in (512, 256, 128, 64, 32, 16):
        if entries % rows == 0:
            return rows
    return entries


def make_assemble(n_u, n_v, u_rows, v_rows, rank):
    def kernel(place_ref, *refs):
        u_in = refs[:n_u]
        v_in = refs[n_u : n_u + n_v]
        u_out, v_out, v_wide = refs[n_u + n_v :]
        for k in range(n_u):
            start = pl.multiple_of(place_ref[k] * u_rows, u_rows)
            u_out[pl.ds(start, u_rows), :] = u_in[k][...]
        for k in range(n_v):
            v_wide[place_ref[n_u + k]] = v_in[k][...].astype(jnp.float32)
        v_out[...] = v_wide[...].reshape(n_v * v_rows, rank).astype(jnp.bfloat16)

    return pl.pallas_call(
        kernel,
        out_shape=(
            jax.ShapeDtypeStruct((n_u * u_rows, rank), jnp.bfloat16),
            jax.ShapeDtypeStruct((n_v * v_rows, rank), jnp.bfloat16),
        ),
        in_specs=[pl.BlockSpec(memory_space=pltpu.SMEM)]
        + [pl.BlockSpec(memory_space=pltpu.VMEM)] * (n_u + n_v),
        out_specs=(pl.BlockSpec(memory_space=pltpu.VMEM),) * 2,
        scratch_shapes=[pltpu.VMEM((n_v, v_rows, rank), jnp.float32)],
        compiler_params=pltpu.CompilerParams(vmem_limit_bytes=VMEM_LIMIT),
        name="assemble",
    )


def make_chunk(pieces, r, depth, entries, rank, n_voc):
    tile = tile_rows(entries)
    sub = min(tile, 256)
    steps = entries // tile
    n = pieces * r

    def kernel(src_ref, *refs):
        piece = refs[:pieces]
        head_ref, u_ref, v_ref, want_ref, out_ref, rows, proj, top, total, pick = refs[pieces:]
        i = pl.program_id(0)

        @pl.when(i == 0)
        def _():
            for k in range(pieces):
                rows[k * r : (k + 1) * r, :] = piece[k][...]
            proj[...] = jnp.dot(
                rows[...], v_ref[...], preferred_element_type=jnp.float32
            ).astype(jnp.bfloat16)
            top[...] = jnp.full(top.shape, -jnp.inf, jnp.float32)
            total[...] = jnp.zeros(total.shape, jnp.float32)
            pick[...] = jnp.zeros(pick.shape, jnp.float32)

        want = jnp.concatenate([want_ref[src_ref[0]], want_ref[src_ref[1]]], axis=1) - i * tile
        for j in range(tile // sub):
            span = slice(j * sub, (j + 1) * sub)
            x = lax.dot_general(head_ref[span, :], rows[...], NT, preferred_element_type=jnp.float32)
            x = x + lax.dot_general(u_ref[span, :], proj[...], NT, preferred_element_type=jnp.float32)
            entry = lax.broadcasted_iota(jnp.int32, (sub, n), 0) + j * sub
            hit = jnp.where(entry == want, x, 0.0)
            x3 = x.reshape(sub // 8, 8, n)
            new = jnp.maximum(top[...], jnp.max(x3, axis=0))
            total[...] = total[...] * jnp.exp(top[...] - new) + jnp.sum(jnp.exp(x3 - new[None]), axis=0)
            pick[...] = pick[...] + jnp.sum(hit.reshape(sub // 8, 8, n), axis=0)
            top[...] = new

        @pl.when(i == steps - 1)
        def _():
            best = jnp.max(top[...], axis=0, keepdims=True)
            out_ref[0:1, :] = best
            out_ref[1:2, :] = jnp.sum(total[...] * jnp.exp(top[...] - best), axis=0, keepdims=True)
            out_ref[2:3, :] = jnp.sum(pick[...], axis=0, keepdims=True)

    whole = pl.BlockSpec(memory_space=pltpu.VMEM)
    return pl.pallas_call(
        kernel,
        grid=(steps,),
        out_shape=jax.ShapeDtypeStruct((3, n), jnp.float32),
        in_specs=[pl.BlockSpec(memory_space=pltpu.SMEM)]
        + [whole] * pieces
        + [
            pl.BlockSpec((tile, depth), lambda i: (i, 0)),
            pl.BlockSpec((tile, rank), lambda i: (i, 0)),
            whole,
            whole,
        ],
        out_specs=whole,
        scratch_shapes=[
            pltpu.VMEM((n, depth), jnp.bfloat16),
            pltpu.VMEM((n, rank), jnp.bfloat16),
            pltpu.VMEM((8, n), jnp.float32),
            pltpu.VMEM((8, n), jnp.float32),
            pltpu.VMEM((8, n), jnp.float32),
        ],
        compiler_params=pltpu.CompilerParams(vmem_limit_bytes=VMEM_LIMIT),
        cost_estimate=pl.CostEstimate(
            flops=2 * n * entries * (depth + 256),
            bytes_accessed=2 * entries * (depth + 128),
            transcendentals=n * entries,
        ),
        name="chunk",
    )


def make_place(n_chunks, r, n_voc):
    def kernel(src_ref, *refs):
        out_ref = refs[-1]
        for c in range(n_chunks):
            for half in range(2):
                value = refs[c][:, half * 2 * r : (half + 1) * 2 * r]
                for q in range(3):
                    out_ref[q, pl.ds(src_ref[2 * c + half], 1), :] = value[q : q + 1]

    return pl.pallas_call(
        kernel,
        out_shape=jax.ShapeDtypeStruct((3, n_voc, 2 * r), jnp.float32),
        in_specs=[pl.BlockSpec(memory_space=pltpu.SMEM)]
        + [pl.BlockSpec(memory_space=pltpu.VMEM)] * n_chunks,
        out_specs=pl.BlockSpec(memory_space=pltpu.VMEM),
        name="place",
    )


def make_finish(r, n_voc):
    def kernel(src_ref, *refs):
        stats = refs[:n_voc]
        prob_ref, log_ref, held = refs[n_voc:]
        for k in range(n_voc):
            held[src_ref[k]] = stats[k][...]
        top = held[0, 0]
        for k in range(1, n_voc):
            top = jnp.maximum(top, held[k, 0])
        total = jnp.zeros_like(top)
        pick = jnp.zeros_like(top)
        for k in range(n_voc):
            total = total + held[k, 1] * jnp.exp(held[k, 0] - top)
            pick = pick + held[k, 2]
        log_total = top + jnp.log(total)
        prob = pick - log_total
        for k in range(n_voc):
            for s in range(2):
                log_ref[s : s + 1, k * r : (k + 1) * r] = log_total[k : k + 1, s * r : (s + 1) * r]
                prob_ref[s : s + 1, k * r : (k + 1) * r] = prob[k : k + 1, s * r : (s + 1) * r]

    shape = jax.ShapeDtypeStruct((2, n_voc * r), jnp.float32)
    return pl.pallas_call(
        kernel,
        out_shape=(shape, shape),
        in_specs=[pl.BlockSpec(memory_space=pltpu.SMEM)]
        + [pl.BlockSpec(memory_space=pltpu.VMEM)] * n_voc,
        out_specs=(pl.BlockSpec(memory_space=pltpu.VMEM),) * 2,
        scratch_shapes=[pltpu.VMEM((n_voc, 3, n_voc, 2 * r), jnp.float32)],
        name="finish",
    )


def body(hidden, head, factor_u, factor_v, sampled):
    n_group = lax.axis_size("group")
    n_voc = lax.axis_size("vocab")
    group = lax.axis_index("group")
    voc = lax.axis_index("vocab")
    _, r, depth = hidden.shape
    entries = head.shape[0]
    rank = factor_u.shape[1]

    order = ring_order(n_voc)
    ahead = [(order[i], order[(i + 1) % n_voc]) for i in range(n_voc)]
    behind = [(b, a) for a, b in ahead]
    ring = jnp.array(order, jnp.int32)
    position = jnp.array([order.index(v) for v in range(n_voc)], jnp.int32)[voc]

    half = n_voc // 2
    own = [hidden[0], hidden[1]]
    up = {0: own}
    down = {0: own}
    for hop in range(1, half):
        up[hop] = [lax.ppermute(x, "vocab", ahead) for x in up[hop - 1]]
        down[hop] = [lax.ppermute(x, "vocab", behind) for x in down[hop - 1]]
    last = [
        lax.ppermute(up[half - 1][0], "vocab", ahead),
        lax.ppermute(down[half - 1][1], "vocab", behind),
    ]

    moves = [
        (v * n_group + g, g * n_voc + v) for v in range(n_voc) for g in range(n_group)
    ]
    mine = lax.ppermute(factor_u, ("group", "vocab"), moves)
    u_parts = [mine]
    for k in range(1, n_group):
        u_parts.append(
            lax.ppermute(mine, "group", [((g + k) % n_group, g) for g in range(n_group)])
        )
    v_parts = [factor_v]
    for k in range(1, n_voc):
        v_parts.append(
            lax.ppermute(factor_v, "vocab", [((v + k) % n_voc, v) for v in range(n_voc)])
        )
    place = jnp.concatenate(
        [
            (group + jnp.arange(n_group, dtype=jnp.int32)) % n_group,
            (voc + jnp.arange(n_voc, dtype=jnp.int32)) % n_voc,
        ]
    )
    full_u, full_v = make_assemble(n_group, n_voc, mine.shape[0], factor_v.shape[0], rank)(
        place, *u_parts, *v_parts
    )

    want = sampled - voc * entries
    want = want.reshape(2, n_voc, r).transpose(1, 0, 2).reshape(n_voc, 1, 2 * r)
    chunk = make_chunk(4, r, depth, entries, rank, n_voc)
    stats = []
    sources = []
    for hop in range(1, half + 1):
        if hop < half:
            rows = up[hop] + down[hop]
            src = ring[jnp.stack([(position - hop) % n_voc, (position + hop) % n_voc])]
        else:
            rows = own + last
            src = ring[jnp.stack([position, (position + half) % n_voc])]
        stats.append(chunk(src, *rows, head, full_u, full_v, want))
        sources.append(src)
    part = make_place(half, r, n_voc)(jnp.concatenate(sources), *stats)
    parts = [part]
    for k in range(1, n_voc):
        parts.append(
            lax.ppermute(part, "vocab", [((v + k) % n_voc, v) for v in range(n_voc)])
        )
    from_whom = (voc + jnp.arange(n_voc, dtype=jnp.int32)) % n_voc
    return make_finish(r, n_voc)(from_whom, *parts)


def solution(mesh):
    in_specs = (
        P(None, ("group", "vocab"), None),
        P("vocab", None),
        P(("group", "vocab"), None),
        P("vocab", None),
        P(None, "group"),
    )
    out_specs = (P(None, "group"), P(None, "group"))
    return jax.shard_map(body, mesh=mesh, in_specs=in_specs, out_specs=out_specs, check_vma=False)
```

time: 211 us -> 132 us (0.63)
  blocking collectives: 80.8 us -> 0 us
  Pallas kernels: 0 us -> 53.8 us
  matrix products: 49.7 us -> 0 us
  starting transfers between devices: 11.9 us -> 47.5 us
  other arithmetic: 13.6 us -> 2.32 us
  local copies, waits for them, and re-layouts: 22.6 us -> 11.5 us
  between operations: 14.2 us -> 5.53 us
  waiting for transfers between devices: 17 us -> 8.93 us
    pallas_call x0 -> x7, Pallas kernels: none -> 53.8 us  [the longest x4 49.8 us: body(): stats.append(chunk(src, *rows, head, full_u, full_v, want))]
    dot_general x4 -> x0, matrix products: 49.7 us -> none  [the longest x2 35.6 us: body(): base = jnp.dot(rows, head.T, preferred_element_type=jnp.float32)]
    ppermute x0 -> x32, starting transfers between devices: none -> 47.5 us  [the longest x7 17.1 us: body(): lax.ppermute(factor_v, 'vocab', [((v + k) % n_voc, v) for v in range(n_vo...]
    all_gather x2 -> x0, blocking collectives: 43.9 us -> none  [the longest x1 33.7 us: body(): full_v = lax.all_gather(factor_v, 'vocab', axis=0, tiled=True)]
    pmax x1 -> x0, blocking collectives: 19.5 us -> none  [body(): top = lax.pmax(local_top, 'vocab')]
    psum x1 -> x0, blocking collectives: 17.4 us -> none  [body(): total, picked = lax.psum((local_sum, local_pick), 'vocab')]
    all_to_all x2 -> x0, starting transfers between devices: 11.8 us -> none  [the longest x1 7.3 us: body(): lax.all_to_all(fragments, ('group', 'vocab'), split_axis=0, concat_axis=0...]
    gather x2 -> x4, local copies, waits for them, and re-layouts: 16.3 us -> 5.17 us  [the longest x3 3.88 us: body(): src = ring[jnp.stack([(position - hop) % n_voc, (position + hop) % n_voc])]]
  transfers between devices with their start and end apart: 4 -> 32, of which waited for: 2 -> 6; matrix products, arithmetic and copies ran while one was open for 20% -> 9% of each run, Pallas kernels for 0% -> 30%
where the time goes in v1:
time: 132 us; the launch traced here: 129 us
  Pallas kernels  53.8 us (41%)
  starting transfers between devices  47.5 us (36%)
  local copies, waits for them, and re-layouts  11.5 us (9%)
  waiting for transfers between devices  8.93 us (7%)
  between operations  5.53 us (4%)
  other arithmetic  2.32 us (2%)
    pallas_call x4, Pallas kernels, body(): stats.append(chunk(src, *rows, head, full_u, full_v, want))  49.8 us
    ppermute x7, starting transfers between devices, body(): lax.ppermute(factor_v, 'vocab', [((v + k) % n_voc, v) for v in range(n_vo...  17.1 us
    ppermute x7, starting transfers between devices, body(): lax.ppermute(part, 'vocab', [((v + k) % n_voc, v) for v in range(n_voc)])  8.62 us
    ppermute x6, starting transfers between devices, body(): down[hop] = [lax.ppermute(x, 'vocab', behind) for x in down[hop - 1]]  7.54 us
    ppermute x3, starting transfers between devices, body(): lax.ppermute(mine, 'group', [((g + k) % n_group, g) for g in range(n_grou...  7.01 us
    ppermute x7, waiting for transfers between devices, body(): lax.ppermute(part, 'vocab', [((v + k) % n_voc, v) for v in range(n_voc)])  5.37 us
    ppermute x6, starting transfers between devices, body(): up[hop] = [lax.ppermute(x, 'vocab', ahead) for x in up[hop - 1]]  4.47 us
    gather x3, local copies, waits for them, and re-layouts, body(): src = ring[jnp.stack([(position - hop) % n_voc, (position + hop) % n_voc])]  3.88 us
  transfers between devices with their start and end apart: 32, of which 6 were waited for; matrix products, arithmetic and copies ran while one was open for 9% of the time, Pallas kernels for 30%

profile of v1, /device:TPU:0, one launch (start us, length us, event | category | flops | bytes accessed | tf_op | source)
XLA Modules:
  0.0 129.5 jit_solution(13295531929770455549)
XLA Ops:
  0.6 0.9 copy.27.refs_4_
  1.5 6.0 %collective-permute-start.8 = (bf16[288,64]{1,0:T(8,128)(2,1)S(1)}, bf16[288,64]{1,0:T(8,128)(2,1)S(1)}, u32[]{:S(2)}, u32[]{:S(2)}) collective-permute-start(bf16[288,64]{1,0:T(8,128)(2,1)S(1)} %copy.27.refs_4_), channel_id=1, source_target_pairs={{1,0},{2,1},{3,2},{4,3},{5,4},{6,5},{7,6},{0,7},{9,8},{10,9},{11,1... | collective-permute-start | bytes 110600 | tf_op jit(solution)/shard_map/ppermute | solution.py:216
  8.0 3.0 %collective-permute-start.11 = (bf16[288,64]{1,0:T(8,128)(2,1)S(1)}, bf16[288,64]{1,0:T(8,128)(2,1)S(1)}, u32[]{:S(2)}, u32[]{:S(2)}) collective-permute-start(bf16[288,64]{1,0:T(8,128)(2,1)S(1)} %copy.27.refs_4_), channel_id=1, source_target_pairs={{4,0},{5,1},{6,2},{7,3},{0,4},{1,5},{2,6},{3,7},{12,8},{13,9},{14,... | collective-permute-start | bytes 110600 | tf_op jit(solution)/shard_map/ppermute | solution.py:216
  11.0 1.1 copy.19
  12.1 0.7 collective-permute-start.4
  12.8 1.2 dynamic_slice.3
  18.7 0.7 fusion.5
  19.5 1.1 slice_bitcast_fusion
  20.7 0.7 broadcast_subtract_fusion
  21.4 3.7 %collective-permute-start.5 = (bf16[1024,64]{1,0:T(8,128)(2,1)S(1)}, bf16[1024,64]{1,0:T(8,128)(2,1)S(1)}, u32[]{:S(2)}, u32[]{:S(2)}) collective-permute-start(bf16[1024,64]{1,0:T(8,128)(2,1)S(1)} %collective-permute-done.4.refs_0_), channel_id=1, source_target_pairs={{8,0},{16,8},{24,16},{0,24},{9,1},{17,9},{25,17},{1,25},{10,2},{18... | collective-permute-start | bytes 393224 | tf_op jit(solution)/shard_map/ppermute | solution.py:211
  25.1 3.6 %collective-permute-start.12 = (bf16[288,64]{1,0:T(8,128)(2,1)S(1)}, bf16[288,64]{1,0:T(8,128)(2,1)S(1)}, u32[]{:S(2)}, u32[]{:S(2)}) collective-permute-start(bf16[288,64]{1,0:T(8,128)(2,1)S(1)} %copy.27.refs_4_), channel_id=1, source_target_pairs={{5,0},{6,1},{7,2},{0,3},{1,4},{2,5},{3,6},{4,7},{13,8},{14,9},{15,... | collective-permute-start | bytes 110600 | tf_op jit(solution)/shard_map/ppermute | solution.py:216
  28.8 2.2 %collective-permute-start.13 = (bf16[288,64]{1,0:T(8,128)(2,1)S(1)}, bf16[288,64]{1,0:T(8,128)(2,1)S(1)}, u32[]{:S(2)}, u32[]{:S(2)}) collective-permute-start(bf16[288,64]{1,0:T(8,128)(2,1)S(1)} %copy.27.refs_4_), channel_id=1, source_target_pairs={{6,0},{7,1},{0,2},{1,3},{2,4},{3,5},{4,6},{5,7},{14,8},{15,9},{8,1... | collective-permute-start | bytes 110600 | tf_op jit(solution)/shard_map/ppermute | solution.py:216
  31.0 1.7 %collective-permute-start.14 = (bf16[288,64]{1,0:T(8,128)(2,1)S(1)}, bf16[288,64]{1,0:T(8,128)(2,1)S(1)}, u32[]{:S(2)}, u32[]{:S(2)}) collective-permute-start(bf16[288,64]{1,0:T(8,128)(2,1)S(1)} %copy.27.refs_4_), channel_id=1, source_target_pairs={{7,0},{0,1},{1,2},{2,3},{3,4},{4,5},{5,6},{6,7},{15,8},{8,9},{9,10... | collective-permute-start | bytes 110600 | tf_op jit(solution)/shard_map/ppermute | solution.py:216
  32.7 3.3 %collective-permute-start.6 = (bf16[1024,64]{1,0:T(8,128)(2,1)S(1)}, bf16[1024,64]{1,0:T(8,128)(2,1)S(1)}, u32[]{:S(2)}, u32[]{:S(2)}) collective-permute-start(bf16[1024,64]{1,0:T(8,128)(2,1)S(1)} %collective-permute-done.4.refs_0_), channel_id=1, source_target_pairs={{16,0},{24,8},{0,16},{8,24},{17,1},{25,9},{1,17},{9,25},{18,2},{26... | collective-permute-start | bytes 393224 | tf_op jit(solution)/shard_map/ppermute | solution.py:211
  36.1 1.9 %collective-permute-start = (bf16[64,2304]{1,0:T(8,128)(2,1)S(1)}, bf16[64,2304]{1,0:T(8,128)(2,1)S(1)}, u32[]{:S(2)}, u32[]{:S(2)}) collective-permute-start(bf16[64,2304]{1,0:T(8,128)(2,1)S(1)} %get-tuple-element.7.refs_0_), channel_id=1, source_target_pairs={{0,2},{2,4},{4,6},{6,7},{7,5},{5,3},{3,1},{1,0},{8,10},{10,12},{12... | collective-permute-start | bytes 884744 | tf_op jit(solution)/shard_map/ppermute | solution.py:197
  38.6 1.4 %collective-permute-start.1 = (bf16[64,2304]{1,0:T(8,128)(2,1)S(1)}, bf16[64,2304]{1,0:T(8,128)(2,1)S(1)}, u32[]{:S(2)}, u32[]{:S(2)}) collective-permute-start(bf16[64,2304]{1,0:T(8,128)(2,1)S(1)} %get-tuple-element.6.refs_1_), channel_id=1, source_target_pairs={{0,2},{2,4},{4,6},{6,7},{7,5},{5,3},{3,1},{1,0},{8,10},{10,12},{12... | collective-permute-start | bytes 884744 | tf_op jit(solution)/shard_map/ppermute | solution.py:197
  40.0 0.6 collective-permute-start.3
  40.6 1.6 %collective-permute-done.6.refs_2_ = bf16[1024,64]{1,0:T(8,128)(2,1)S(1)} collective-permute-done((bf16[1024,64]{1,0:T(8,128)(2,1)S(1)}, bf16[1024,64]{1,0:T(8,128)(2,1)S(1)}, u32[]{:S(2)}, u32[]{:S(2)}) %collective-permute-start.6) | collective-permute-done | bytes 131104 | tf_op jit(solution)/shard_map/ppermute | solution.py:211
  42.3 1.3 gather_fusion.3
  43.5 1.3 gather_fusion.2
  44.8 1.3 gather_fusion.1
  46.1 1.3 gather_fusion
  48.2 0.9 assemble.1
  49.5 1.6 %collective-permute-done.1.refs_1_ = bf16[64,2304]{1,0:T(8,128)(2,1)S(1)} collective-permute-done((bf16[64,2304]{1,0:T(8,128)(2,1)S(1)}, bf16[64,2304]{1,0:T(8,128)(2,1)S(1)}, u32[]{:S(2)}, u32[]{:S(2)}) %collective-permute-start.1) | collective-permute-done | bytes 294944 | tf_op jit(solution)/shard_map/ppermute | solution.py:197
  51.2 2.0 %collective-permute-start.17 = (bf16[64,2304]{1,0:T(8,128)(2,1)S(1)}, bf16[64,2304]{1,0:T(8,128)(2,1)S(1)}, u32[]{:S(2)}, u32[]{:S(2)}) collective-permute-start(bf16[64,2304]{1,0:T(8,128)(2,1)S(1)} %collective-permute-done.2.refs_2_), channel_id=1, source_target_pairs={{2,0},{4,2},{6,4},{7,6},{5,7},{3,5},{1,3},{0,1},{10,8},{12,10},{14... | collective-permute-start | bytes 884744 | tf_op jit(solution)/shard_map/ppermute | solution.py:198
  53.2 1.3 %collective-permute-start.18 = (bf16[64,2304]{1,0:T(8,128)(2,1)S(1)}, bf16[64,2304]{1,0:T(8,128)(2,1)S(1)}, u32[]{:S(2)}, u32[]{:S(2)}) collective-permute-start(bf16[64,2304]{1,0:T(8,128)(2,1)S(1)} %collective-permute-done.3.refs_3_), channel_id=1, source_target_pairs={{2,0},{4,2},{6,4},{7,6},{5,7},{3,5},{1,3},{0,1},{10,8},{12,10},{14... | collective-permute-start | bytes 884744 | tf_op jit(solution)/shard_map/ppermute | solution.py:198
  54.5 12.5 %chunk.4.refs_0_ = f32[3,256]{1,0:T(4,128)S(1)} custom-call(s32[2]{0:T(128)S(1)} %gather_fusion, bf16[64,2304]{1,0:T(8,128)(2,1)S(1)} %collective-permute-done.refs_0_, bf16[64,2304]{1,0:T(8,128)(2,1)S(1)} %collective-permute-done.1.refs_1_, bf16[64,2304]{1,0:T(8,128)(2,1)S(1)} %collective-permute-done.2.refs_2_, ...), custom_call_target="tpu_custom_call" | custom-call | flops 5368709120 | bytes 19922944 | tf_op jit(solution)/shard_map/chunk/pallas_call | solution.py:240
  67.0 0.6 copy-done
  67.6 0.7 collective-permute-start.19
  68.3 2.0 %collective-permute-start.21 = (bf16[64,2304]{1,0:T(8,128)(2,1)S(1)}, bf16[64,2304]{1,0:T(8,128)(2,1)S(1)}, u32[]{:S(2)}, u32[]{:S(2)}) collective-permute-start(bf16[64,2304]{1,0:T(8,128)(2,1)S(1)} %collective-permute-done.17.refs_2_), channel_id=1, source_target_pairs={{2,0},{4,2},{6,4},{7,6},{5,7},{3,5},{1,3},{0,1},{10,8},{12,10},{14... | collective-permute-start | bytes 884744 | tf_op jit(solution)/shard_map/ppermute | solution.py:198
  70.3 1.3 %collective-permute-start.22 = (bf16[64,2304]{1,0:T(8,128)(2,1)S(1)}, bf16[64,2304]{1,0:T(8,128)(2,1)S(1)}, u32[]{:S(2)}, u32[]{:S(2)}) collective-permute-start(bf16[64,2304]{1,0:T(8,128)(2,1)S(1)} %collective-permute-done.18.refs_3_), channel_id=1, source_target_pairs={{2,0},{4,2},{6,4},{7,6},{5,7},{3,5},{1,3},{0,1},{10,8},{12,10},{14... | collective-permute-start | bytes 884744 | tf_op jit(solution)/shard_map/ppermute | solution.py:198
  71.6 12.5 %chunk.5.refs_1_ = f32[3,256]{1,0:T(4,128)S(1)} custom-call(s32[2]{0:T(128)S(1)} %gather_fusion.1, bf16[64,2304]{1,0:T(8,128)(2,1)S(1)} %collective-permute-done.15.refs_0_, bf16[64,2304]{1,0:T(8,128)(2,1)S(1)} %collective-permute-done.16.refs_1_, bf16[64,2304]{1,0:T(8,128)(2,1)S(1)} %collective-permute-done.17.refs_2_, ...), custom_call_target="tpu_custom_call" | custom-call | flops 5368709120 | bytes 19922944 | tf_op jit(solution)/shard_map/chunk/pallas_call | solution.py:240
  84.1 0.8 collective-permute-start.23
  84.9 1.3 %collective-permute-start.24 = (bf16[64,2304]{1,0:T(8,128)(2,1)S(1)}, bf16[64,2304]{1,0:T(8,128)(2,1)S(1)}, u32[]{:S(2)}, u32[]{:S(2)}) collective-permute-start(bf16[64,2304]{1,0:T(8,128)(2,1)S(1)} %collective-permute-done.22.refs_3_), channel_id=1, source_target_pairs={{2,0},{4,2},{6,4},{7,6},{5,7},{3,5},{1,3},{0,1},{10,8},{12,10},{14... | collective-permute-start | bytes 884744 | tf_op jit(solution)/shard_map/ppermute | solution.py:201
  86.2 12.5 %chunk.6.refs_2_ = f32[3,256]{1,0:T(4,128)S(1)} custom-call(s32[2]{0:T(128)S(1)} %gather_fusion.2, bf16[64,2304]{1,0:T(8,128)(2,1)S(1)} %collective-permute-done.19.refs_0_, bf16[64,2304]{1,0:T(8,128)(2,1)S(1)} %collective-permute-done.20.refs_1_, bf16[64,2304]{1,0:T(8,128)(2,1)S(1)} %collective-permute-done.21.refs_2_, ...), custom_call_target="tpu_custom_call" | custom-call | flops 5368709120 | bytes 19922944 | tf_op jit(solution)/shard_map/chunk/pallas_call | solution.py:240
  98.7 12.5 %chunk.7.refs_3_ = f32[3,256]{1,0:T(4,128)S(1)} custom-call(s32[2]{0:T(128)S(1)} %gather_fusion.3, bf16[64,2304]{1,0:T(8,128)(2,1)S(1)} %get-tuple-element.7.refs_0_, bf16[64,2304]{1,0:T(8,128)(2,1)S(1)} %get-tuple-element.6.refs_1_, bf16[64,2304]{1,0:T(8,128)(2,1)S(1)} %collective-permute-done.23.refs_2_, ...), custom_call_target="tpu_custom_call" | custom-call | flops 5368709120 | bytes 19922944 | tf_op jit(solution)/shard_map/chunk/pallas_call | solution.py:240
  111.8 1.4 %place.1.refs_0_ = f32[3,8,128]{2,1,0:T(8,128)} custom-call(s32[8]{0:T(128)} %pad_add_fusion.src_ref, f32[3,256]{1,0:T(4,128)} %copy-done, f32[3,256]{1,0:T(4,128)} %copy-done.1, f32[3,256]{1,0:T(4,128)} %copy-done.2, f32[3,256]{1,0:T(4,128)} %copy-done.3), custom_call_target="tpu_custom_call" | custom-call | tf_op jit(solution)/shard_map/place/pallas_call | solution.py:242
  113.2 2.2 %collective-permute-start.25 = (f32[3,8,128]{2,1,0:T(8,128)}, f32[3,8,128]{2,1,0:T(8,128)S(1)}, u32[]{:S(2)}, u32[]{:S(2)}) collective-permute-start(f32[3,8,128]{2,1,0:T(8,128)} %place.1.refs_0_), channel_id=1, source_target_pairs={{1,0},{2,1},{3,2},{4,3},{5,4},{6,5},{7,6},{0,7},{9,8},{10,9},{11,1... | collective-permute-start | bytes 36872 | tf_op jit(solution)/shard_map/ppermute | solution.py:246
  115.8 1.1 collective-permute-start.27
  116.9 1.9 %collective-permute-start.28 = (f32[3,8,128]{2,1,0:T(8,128)}, f32[3,8,128]{2,1,0:T(8,128)S(1)}, u32[]{:S(2)}, u32[]{:S(2)}) collective-permute-start(f32[3,8,128]{2,1,0:T(8,128)} %place.1.refs_0_), channel_id=1, source_target_pairs={{4,0},{5,1},{6,2},{7,3},{0,4},{1,5},{2,6},{3,7},{12,8},{13,9},{14,... | collective-permute-start | bytes 36872 | tf_op jit(solution)/shard_map/ppermute | solution.py:246
  118.8 0.6 collective-permute-start.29
  119.4 1.2 collective-permute-start.30
  120.6 1.2 collective-permute-start.31
  121.9 2.6 %collective-permute-done.29.refs_5_ = f32[3,8,128]{2,1,0:T(8,128)S(1)} collective-permute-done((f32[3,8,128]{2,1,0:T(8,128)}, f32[3,8,128]{2,1,0:T(8,128)S(1)}, u32[]{:S(2)}, u32[]{:S(2)}) %collective-permute-start.29) | collective-permute-done | bytes 12320 | tf_op jit(solution)/shard_map/ppermute | solution.py:246
  124.5 1.1 collective-permute-done.30.refs_6_
  125.7 1.6 %collective-permute-done.31.refs_7_ = f32[3,8,128]{2,1,0:T(8,128)S(1)} collective-permute-done((f32[3,8,128]{2,1,0:T(8,128)}, f32[3,8,128]{2,1,0:T(8,128)S(1)}, u32[]{:S(2)}, u32[]{:S(2)}) %collective-permute-start.31) | collective-permute-done | bytes 12320 | tf_op jit(solution)/shard_map/ppermute | solution.py:246
  127.3 0.6 copy-done.10
  127.9 1.6 %finish.1 = (f32[2,512]{1,0:T(2,128)}, f32[2,512]{1,0:T(2,128)}) custom-call(s32[8]{0:T(128)} %copy-done.11, f32[3,8,128]{2,1,0:T(8,128)} %place.1.refs_0_, f32[3,8,128]{2,1,0:T(8,128)} %copy-done.4, f32[3,8,128]{2,1,0:T(8,128)} %copy-done.5, f32[3,8,128]{2,1,0:T(8,128)} %copy-done.6, f32[3,8,128]{2,1,0:T(8,128)} %copy-done.7, f32[3,8,128]{2,1,0:T(8,128)} %copy-done.8, ...), custom_call_target="tpu_custom_call" | custom-call | tf_op jit(solution)/shard_map/finish/pallas_call | solution.py:249
  (71 shorter events, 3.6 us)
Async XLA Ops:
  1.5 23.6 %collective-permute-start.8 = (bf16[288,64]{1,0:T(8,128)(2,1)S(1)}, bf16[288,64]{1,0:T(8,128)(2,1)S(1)}, u32[]{:S(2)}, u32[]{:S(2)}) collective-permute-start(bf16[288,64]{1,0:T(8,128)(2,1)S(1)} %copy.27.refs_4_), channel_id=1, source_target_pairs={{1,0},{2,1},{3,2},{4,3},{5,4},{6,5},{7,6},{0,7},{9,8},{10,9},{11,1... | collective-permute-start | bytes 110600 | tf_op jit(solution)/shard_map/ppermute | solution.py:216
  7.6 21.2 %collective-permute-start.9 = (bf16[288,64]{1,0:T(8,128)(2,1)S(1)}, bf16[288,64]{1,0:T(8,128)(2,1)S(1)}, u32[]{:S(2)}, u32[]{:S(2)}) collective-permute-start(bf16[288,64]{1,0:T(8,128)(2,1)S(1)} %copy.27.refs_4_), channel_id=1, source_target_pairs={{2,0},{3,1},{4,2},{5,3},{6,4},{7,5},{0,6},{1,7},{10,8},{11,9},{12,... | collective-permute-start | bytes 110600 | tf_op jit(solution)/shard_map/ppermute | solution.py:216
  8.0 23.0 %collective-permute-start.10 = (bf16[288,64]{1,0:T(8,128)(2,1)S(1)}, bf16[288,64]{1,0:T(8,128)(2,1)S(1)}, u32[]{:S(2)}, u32[]{:S(2)}) collective-permute-start(bf16[288,64]{1,0:T(8,128)(2,1)S(1)} %copy.27.refs_4_), channel_id=1, source_target_pairs={{3,0},{4,1},{5,2},{6,3},{7,4},{0,5},{1,6},{2,7},{11,8},{12,9},{13,... | collective-permute-start | bytes 110600 | tf_op jit(solution)/shard_map/ppermute | solution.py:216
  8.0 24.7 %collective-permute-start.11 = (bf16[288,64]{1,0:T(8,128)(2,1)S(1)}, bf16[288,64]{1,0:T(8,128)(2,1)S(1)}, u32[]{:S(2)}, u32[]{:S(2)}) collective-permute-start(bf16[288,64]{1,0:T(8,128)(2,1)S(1)} %copy.27.refs_4_), channel_id=1, source_target_pairs={{4,0},{5,1},{6,2},{7,3},{0,4},{1,5},{2,6},{3,7},{12,8},{13,9},{14,... | collective-permute-start | bytes 110600 | tf_op jit(solution)/shard_map/ppermute | solution.py:216
  12.1 9.3 %collective-permute-start.4 = (bf16[1024,64]{1,0:T(8,128)(2,1)S(1)}, bf16[1024,64]{1,0:T(8,128)(2,1)S(1)}, u32[]{:S(2)}, u32[]{:S(2)}) collective-permute-start(bf16[1024,64]{1,0:T(8,128)(2,1)S(1)} %copy.19), channel_id=1, source_target_pairs={{0,0},{1,8},{2,16},{3,24},{4,1},{5,9},{6,17},{7,25},{8,2},{9,10},{... | collective-permute-start | bytes 393224 | tf_op jit(solution)/shard_map/ppermute | solution.py:207
  21.4 18.6 %collective-permute-start.5 = (bf16[1024,64]{1,0:T(8,128)(2,1)S(1)}, bf16[1024,64]{1,0:T(8,128)(2,1)S(1)}, u32[]{:S(2)}, u32[]{:S(2)}) collective-permute-start(bf16[1024,64]{1,0:T(8,128)(2,1)S(1)} %collective-permute-done.4.refs_0_), channel_id=1, source_target_pairs={{8,0},{16,8},{24,16},{0,24},{9,1},{17,9},{25,17},{1,25},{10,2},{18... | collective-permute-start | bytes 393224 | tf_op jit(solution)/shard_map/ppermute | solution.py:211
  25.1 10.9 %collective-permute-start.12 = (bf16[288,64]{1,0:T(8,128)(2,1)S(1)}, bf16[288,64]{1,0:T(8,128)(2,1)S(1)}, u32[]{:S(2)}, u32[]{:S(2)}) collective-permute-start(bf16[288,64]{1,0:T(8,128)(2,1)S(1)} %copy.27.refs_4_), channel_id=1, source_target_pairs={{5,0},{6,1},{7,2},{0,3},{1,4},{2,5},{3,6},{4,7},{13,8},{14,9},{15,... | collective-permute-start | bytes 110600 | tf_op jit(solution)/shard_map/ppermute | solution.py:216
  28.8 9.2 %collective-permute-start.13 = (bf16[288,64]{1,0:T(8,128)(2,1)S(1)}, bf16[288,64]{1,0:T(8,128)(2,1)S(1)}, u32[]{:S(2)}, u32[]{:S(2)}) collective-permute-start(bf16[288,64]{1,0:T(8,128)(2,1)S(1)} %copy.27.refs_4_), channel_id=1, source_target_pairs={{6,0},{7,1},{0,2},{1,3},{2,4},{3,5},{4,6},{5,7},{14,8},{15,9},{8,1... | collective-permute-start | bytes 110600 | tf_op jit(solution)/shard_map/ppermute | solution.py:216
  31.0 7.6 %collective-permute-start.14 = (bf16[288,64]{1,0:T(8,128)(2,1)S(1)}, bf16[288,64]{1,0:T(8,128)(2,1)S(1)}, u32[]{:S(2)}, u32[]{:S(2)}) collective-permute-start(bf16[288,64]{1,0:T(8,128)(2,1)S(1)} %copy.27.refs_4_), channel_id=1, source_target_pairs={{7,0},{0,1},{1,2},{2,3},{3,4},{4,5},{5,6},{6,7},{15,8},{8,9},{9,10... | collective-permute-start | bytes 110600 | tf_op jit(solution)/shard_map/ppermute | solution.py:216
  32.7 9.4 %collective-permute-start.6 = (bf16[1024,64]{1,0:T(8,128)(2,1)S(1)}, bf16[1024,64]{1,0:T(8,128)(2,1)S(1)}, u32[]{:S(2)}, u32[]{:S(2)}) collective-permute-start(bf16[1024,64]{1,0:T(8,128)(2,1)S(1)} %collective-permute-done.4.refs_0_), channel_id=1, source_target_pairs={{16,0},{24,8},{0,16},{8,24},{17,1},{25,9},{1,17},{9,25},{18,2},{26... | collective-permute-start | bytes 393224 | tf_op jit(solution)/shard_map/ppermute | solution.py:211
  36.1 48.0 %copy-start.11 = (s32[8]{0:T(128)}, s32[8]{0:T(128)S(1)}, u32[]{:S(2)}) copy-start(s32[8]{0:T(128)S(1)} %and_select_fusion.1.src_ref) | copy-start | bytes 100
  36.1 13.0 %collective-permute-start = (bf16[64,2304]{1,0:T(8,128)(2,1)S(1)}, bf16[64,2304]{1,0:T(8,128)(2,1)S(1)}, u32[]{:S(2)}, u32[]{:S(2)}) collective-permute-start(bf16[64,2304]{1,0:T(8,128)(2,1)S(1)} %get-tuple-element.7.refs_0_), channel_id=1, source_target_pairs={{0,2},{2,4},{4,6},{6,7},{7,5},{5,3},{3,1},{1,0},{8,10},{10,12},{12... | collective-permute-start | bytes 884744 | tf_op jit(solution)/shard_map/ppermute | solution.py:197
  38.0 13.2 %collective-permute-start.2 = (bf16[64,2304]{1,0:T(8,128)(2,1)S(1)}, bf16[64,2304]{1,0:T(8,128)(2,1)S(1)}, u32[]{:S(2)}, u32[]{:S(2)}) collective-permute-start(bf16[64,2304]{1,0:T(8,128)(2,1)S(1)} %get-tuple-element.7.refs_0_), channel_id=1, source_target_pairs={{2,0},{4,2},{6,4},{7,6},{5,7},{3,5},{1,3},{0,1},{10,8},{12,10},{14... | collective-permute-start | bytes 884744 | tf_op jit(solution)/shard_map/ppermute | solution.py:198
  38.6 12.6 %collective-permute-start.1 = (bf16[64,2304]{1,0:T(8,128)(2,1)S(1)}, bf16[64,2304]{1,0:T(8,128)(2,1)S(1)}, u32[]{:S(2)}, u32[]{:S(2)}) collective-permute-start(bf16[64,2304]{1,0:T(8,128)(2,1)S(1)} %get-tuple-element.6.refs_1_), channel_id=1, source_target_pairs={{0,2},{2,4},{4,6},{6,7},{7,5},{5,3},{3,1},{1,0},{8,10},{10,12},{12... | collective-permute-start | bytes 884744 | tf_op jit(solution)/shard_map/ppermute | solution.py:197
  40.0 13.2 %collective-permute-start.3 = (bf16[64,2304]{1,0:T(8,128)(2,1)S(1)}, bf16[64,2304]{1,0:T(8,128)(2,1)S(1)}, u32[]{:S(2)}, u32[]{:S(2)}) collective-permute-start(bf16[64,2304]{1,0:T(8,128)(2,1)S(1)} %get-tuple-element.6.refs_1_), channel_id=1, source_target_pairs={{2,0},{4,2},{6,4},{7,6},{5,7},{3,5},{1,3},{0,1},{10,8},{12,10},{14... | collective-permute-start | bytes 884744 | tf_op jit(solution)/shard_map/ppermute | solution.py:198
  42.2 6.0 %collective-permute-start.7 = (bf16[1024,64]{1,0:T(8,128)(2,1)S(1)}, bf16[1024,64]{1,0:T(8,128)(2,1)S(1)}, u32[]{:S(2)}, u32[]{:S(2)}) collective-permute-start(bf16[1024,64]{1,0:T(8,128)(2,1)S(1)} %collective-permute-done.4.refs_0_), channel_id=1, source_target_pairs={{24,0},{0,8},{8,16},{16,24},{25,1},{1,9},{9,17},{17,25},{26,2},{2,... | collective-permute-start | bytes 393224 | tf_op jit(solution)/shard_map/ppermute | solution.py:211
  49.1 18.4 %collective-permute-start.15 = (bf16[64,2304]{1,0:T(8,128)(2,1)S(1)}, bf16[64,2304]{1,0:T(8,128)(2,1)S(1)}, u32[]{:S(2)}, u32[]{:S(2)}) collective-permute-start(bf16[64,2304]{1,0:T(8,128)(2,1)S(1)} %collective-permute-done.refs_0_), channel_id=1, source_target_pairs={{0,2},{2,4},{4,6},{6,7},{7,5},{5,3},{3,1},{1,0},{8,10},{10,12},{12... | collective-permute-start | bytes 884744 | tf_op jit(solution)/shard_map/ppermute | solution.py:197
  51.2 17.1 %collective-permute-start.16 = (bf16[64,2304]{1,0:T(8,128)(2,1)S(1)}, bf16[64,2304]{1,0:T(8,128)(2,1)S(1)}, u32[]{:S(2)}, u32[]{:S(2)}) collective-permute-start(bf16[64,2304]{1,0:T(8,128)(2,1)S(1)} %collective-permute-done.1.refs_1_), channel_id=1, source_target_pairs={{0,2},{2,4},{4,6},{6,7},{7,5},{5,3},{3,1},{1,0},{8,10},{10,12},{12... | collective-permute-start | bytes 884744 | tf_op jit(solution)/shard_map/ppermute | solution.py:197
  51.2 17.2 %collective-permute-start.17 = (bf16[64,2304]{1,0:T(8,128)(2,1)S(1)}, bf16[64,2304]{1,0:T(8,128)(2,1)S(1)}, u32[]{:S(2)}, u32[]{:S(2)}) collective-permute-start(bf16[64,2304]{1,0:T(8,128)(2,1)S(1)} %collective-permute-done.2.refs_2_), channel_id=1, source_target_pairs={{2,0},{4,2},{6,4},{7,6},{5,7},{3,5},{1,3},{0,1},{10,8},{12,10},{14... | collective-permute-start | bytes 884744 | tf_op jit(solution)/shard_map/ppermute | solution.py:198
  53.2 17.1 %collective-permute-start.18 = (bf16[64,2304]{1,0:T(8,128)(2,1)S(1)}, bf16[64,2304]{1,0:T(8,128)(2,1)S(1)}, u32[]{:S(2)}, u32[]{:S(2)}) collective-permute-start(bf16[64,2304]{1,0:T(8,128)(2,1)S(1)} %collective-permute-done.3.refs_3_), channel_id=1, source_target_pairs={{2,0},{4,2},{6,4},{7,6},{5,7},{3,5},{1,3},{0,1},{10,8},{12,10},{14... | collective-permute-start | bytes 884744 | tf_op jit(solution)/shard_map/ppermute | solution.py:198
  67.0 0.6 copy-start
  67.6 16.6 %collective-permute-start.19 = (bf16[64,2304]{1,0:T(8,128)(2,1)S(1)}, bf16[64,2304]{1,0:T(8,128)(2,1)S(1)}, u32[]{:S(2)}, u32[]{:S(2)}) collective-permute-start(bf16[64,2304]{1,0:T(8,128)(2,1)S(1)} %collective-permute-done.15.refs_0_), channel_id=1, source_target_pairs={{0,2},{2,4},{4,6},{6,7},{7,5},{5,3},{3,1},{1,0},{8,10},{10,12},{12... | collective-permute-start | bytes 884744 | tf_op jit(solution)/shard_map/ppermute | solution.py:197
  68.3 17.9 %collective-permute-start.20 = (bf16[64,2304]{1,0:T(8,128)(2,1)S(1)}, bf16[64,2304]{1,0:T(8,128)(2,1)S(1)}, u32[]{:S(2)}, u32[]{:S(2)}) collective-permute-start(bf16[64,2304]{1,0:T(8,128)(2,1)S(1)} %collective-permute-done.16.refs_1_), channel_id=1, source_target_pairs={{0,2},{2,4},{4,6},{6,7},{7,5},{5,3},{3,1},{1,0},{8,10},{10,12},{12... | collective-permute-start | bytes 884744 | tf_op jit(solution)/shard_map/ppermute | solution.py:197
  68.3 17.9 %collective-permute-start.21 = (bf16[64,2304]{1,0:T(8,128)(2,1)S(1)}, bf16[64,2304]{1,0:T(8,128)(2,1)S(1)}, u32[]{:S(2)}, u32[]{:S(2)}) collective-permute-start(bf16[64,2304]{1,0:T(8,128)(2,1)S(1)} %collective-permute-done.17.refs_2_), channel_id=1, source_target_pairs={{2,0},{4,2},{6,4},{7,6},{5,7},{3,5},{1,3},{0,1},{10,8},{12,10},{14... | collective-permute-start | bytes 884744 | tf_op jit(solution)/shard_map/ppermute | solution.py:198
  70.3 14.6 %collective-permute-start.22 = (bf16[64,2304]{1,0:T(8,128)(2,1)S(1)}, bf16[64,2304]{1,0:T(8,128)(2,1)S(1)}, u32[]{:S(2)}, u32[]{:S(2)}) collective-permute-start(bf16[64,2304]{1,0:T(8,128)(2,1)S(1)} %collective-permute-done.18.refs_3_), channel_id=1, source_target_pairs={{2,0},{4,2},{6,4},{7,6},{5,7},{3,5},{1,3},{0,1},{10,8},{12,10},{14... | collective-permute-start | bytes 884744 | tf_op jit(solution)/shard_map/ppermute | solution.py:198
  84.1 14.6 %copy-start.1 = (f32[3,256]{1,0:T(4,128)}, f32[3,256]{1,0:T(4,128)S(1)}, u32[]{:S(2)}) copy-start(f32[3,256]{1,0:T(4,128)S(1)} %chunk.5.refs_1_) | copy-start | bytes 9220
  84.1 14.6 %collective-permute-start.23 = (bf16[64,2304]{1,0:T(8,128)(2,1)S(1)}, bf16[64,2304]{1,0:T(8,128)(2,1)S(1)}, u32[]{:S(2)}, u32[]{:S(2)}) collective-permute-start(bf16[64,2304]{1,0:T(8,128)(2,1)S(1)} %collective-permute-done.19.refs_0_), channel_id=1, source_target_pairs={{0,2},{2,4},{4,6},{6,7},{7,5},{5,3},{3,1},{1,0},{8,10},{10,12},{12... | collective-permute-start | bytes 884744 | tf_op jit(solution)/shard_map/ppermute | solution.py:200
  84.9 13.8 %collective-permute-start.24 = (bf16[64,2304]{1,0:T(8,128)(2,1)S(1)}, bf16[64,2304]{1,0:T(8,128)(2,1)S(1)}, u32[]{:S(2)}, u32[]{:S(2)}) collective-permute-start(bf16[64,2304]{1,0:T(8,128)(2,1)S(1)} %collective-permute-done.22.refs_3_), channel_id=1, source_target_pairs={{2,0},{4,2},{6,4},{7,6},{5,7},{3,5},{1,3},{0,1},{10,8},{12,10},{14... | collective-permute-start | bytes 884744 | tf_op jit(solution)/shard_map/ppermute | solution.py:201
  98.7 12.5 %copy-start.2 = (f32[3,256]{1,0:T(4,128)}, f32[3,256]{1,0:T(4,128)S(1)}, u32[]{:S(2)}) copy-start(f32[3,256]{1,0:T(4,128)S(1)} %chunk.6.refs_2_) | copy-start | bytes 9220
  111.2 0.6 copy-start.3
  113.2 6.2 %collective-permute-start.25 = (f32[3,8,128]{2,1,0:T(8,128)}, f32[3,8,128]{2,1,0:T(8,128)S(1)}, u32[]{:S(2)}, u32[]{:S(2)}) collective-permute-start(f32[3,8,128]{2,1,0:T(8,128)} %place.1.refs_0_), channel_id=1, source_target_pairs={{1,0},{2,1},{3,2},{4,3},{5,4},{6,5},{7,6},{0,7},{9,8},{10,9},{11,1... | collective-permute-start | bytes 36872 | tf_op jit(solution)/shard_map/ppermute | solution.py:246
  115.4 5.2 %collective-permute-start.26 = (f32[3,8,128]{2,1,0:T(8,128)}, f32[3,8,128]{2,1,0:T(8,128)S(1)}, u32[]{:S(2)}, u32[]{:S(2)}) collective-permute-start(f32[3,8,128]{2,1,0:T(8,128)} %place.1.refs_0_), channel_id=1, source_target_pairs={{2,0},{3,1},{4,2},{5,3},{6,4},{7,5},{0,6},{1,7},{10,8},{11,9},{12,... | collective-permute-start | bytes 36872 | tf_op jit(solution)/shard_map/ppermute | solution.py:246
  115.8 6.1 %collective-permute-start.27 = (f32[3,8,128]{2,1,0:T(8,128)}, f32[3,8,128]{2,1,0:T(8,128)S(1)}, u32[]{:S(2)}, u32[]{:S(2)}) collective-permute-start(f32[3,8,128]{2,1,0:T(8,128)} %place.1.refs_0_), channel_id=1, source_target_pairs={{3,0},{4,1},{5,2},{6,3},{7,4},{0,5},{1,6},{2,7},{11,8},{12,9},{13,... | collective-permute-start | bytes 36872 | tf_op jit(solution)/shard_map/ppermute | solution.py:246
  116.9 5.0 %collective-permute-start.28 = (f32[3,8,128]{2,1,0:T(8,128)}, f32[3,8,128]{2,1,0:T(8,128)S(1)}, u32[]{:S(2)}, u32[]{:S(2)}) collective-permute-start(f32[3,8,128]{2,1,0:T(8,128)} %place.1.refs_0_), channel_id=1, source_target_pairs={{4,0},{5,1},{6,2},{7,3},{0,4},{1,5},{2,6},{3,7},{12,8},{13,9},{14,... | collective-permute-start | bytes 36872 | tf_op jit(solution)/shard_map/ppermute | solution.py:246
  118.8 5.7 %collective-permute-start.29 = (f32[3,8,128]{2,1,0:T(8,128)}, f32[3,8,128]{2,1,0:T(8,128)S(1)}, u32[]{:S(2)}, u32[]{:S(2)}) collective-permute-start(f32[3,8,128]{2,1,0:T(8,128)} %place.1.refs_0_), channel_id=1, source_target_pairs={{5,0},{6,1},{7,2},{0,3},{1,4},{2,5},{3,6},{4,7},{13,8},{14,9},{15,... | collective-permute-start | bytes 36872 | tf_op jit(solution)/shard_map/ppermute | solution.py:246
  119.4 7.9 %copy-start.4 = (f32[3,8,128]{2,1,0:T(8,128)}, f32[3,8,128]{2,1,0:T(8,128)S(1)}, u32[]{:S(2)}) copy-start(f32[3,8,128]{2,1,0:T(8,128)S(1)} %collective-permute-done.25.refs_1_) | copy-start | bytes 36868
  119.4 6.3 %collective-permute-start.30 = (f32[3,8,128]{2,1,0:T(8,128)}, f32[3,8,128]{2,1,0:T(8,128)S(1)}, u32[]{:S(2)}, u32[]{:S(2)}) collective-permute-start(f32[3,8,128]{2,1,0:T(8,128)} %place.1.refs_0_), channel_id=1, source_target_pairs={{6,0},{7,1},{0,2},{1,3},{2,4},{3,5},{4,6},{5,7},{14,8},{15,9},{8,1... | collective-permute-start | bytes 36872 | tf_op jit(solution)/shard_map/ppermute | solution.py:246
  120.6 6.6 %copy-start.5 = (f32[3,8,128]{2,1,0:T(8,128)}, f32[3,8,128]{2,1,0:T(8,128)S(1)}, u32[]{:S(2)}) copy-start(f32[3,8,128]{2,1,0:T(8,128)S(1)} %collective-permute-done.26.refs_2_) | copy-start | bytes 36868
  120.6 6.6 %collective-permute-start.31 = (f32[3,8,128]{2,1,0:T(8,128)}, f32[3,8,128]{2,1,0:T(8,128)S(1)}, u32[]{:S(2)}, u32[]{:S(2)}) collective-permute-start(f32[3,8,128]{2,1,0:T(8,128)} %place.1.refs_0_), channel_id=1, source_target_pairs={{7,0},{0,1},{1,2},{2,3},{3,4},{4,5},{5,6},{6,7},{15,8},{8,9},{9,10... | collective-permute-start | bytes 36872 | tf_op jit(solution)/shard_map/ppermute | solution.py:246
  121.9 5.4 %copy-start.6 = (f32[3,8,128]{2,1,0:T(8,128)}, f32[3,8,128]{2,1,0:T(8,128)S(1)}, u32[]{:S(2)}) copy-start(f32[3,8,128]{2,1,0:T(8,128)S(1)} %collective-permute-done.27.refs_3_) | copy-start | bytes 36868
  121.9 5.4 %copy-start.7 = (f32[3,8,128]{2,1,0:T(8,128)}, f32[3,8,128]{2,1,0:T(8,128)S(1)}, u32[]{:S(2)}) copy-start(f32[3,8,128]{2,1,0:T(8,128)S(1)} %collective-permute-done.28.refs_4_) | copy-start | bytes 36868
  124.5 2.8 %copy-start.8 = (f32[3,8,128]{2,1,0:T(8,128)}, f32[3,8,128]{2,1,0:T(8,128)S(1)}, u32[]{:S(2)}) copy-start(f32[3,8,128]{2,1,0:T(8,128)S(1)} %collective-permute-done.29.refs_5_) | copy-start | bytes 36868
  125.7 1.6 %copy-start.9 = (f32[3,8,128]{2,1,0:T(8,128)}, f32[3,8,128]{2,1,0:T(8,128)S(1)}, u32[]{:S(2)}) copy-start(f32[3,8,128]{2,1,0:T(8,128)S(1)} %collective-permute-done.30.refs_6_) | copy-start | bytes 36868
  127.3 0.6 copy-start.10

commit v2 on v0

v2 whole, which is shorter than its diff:
```python
import jax
import jax.numpy as jnp
from jax import lax
from jax.experimental import pallas as pl
from jax.experimental.pallas import tpu as pltpu
from jax.sharding import PartitionSpec as P

VMEM_LIMIT = 48 * 1024 * 1024
LANES = 128
WHOLE = pl.BlockSpec(memory_space=pltpu.VMEM)


def ring_order(n):
    return [2 * i for i in range(n // 2)] + [2 * i + 1 for i in reversed(range(n // 2))]


def ring_position(device, n):
    return jnp.where(device % 2 == 0, device // 2, n - 1 - device // 2)


def ring_device(position, n):
    position = lax.rem(position + n, n)
    return jnp.where(position < n // 2, 2 * position, 2 * (n - 1 - position) + 1)


def tile_rows(entries):
    for rows in (512, 256, 128, 64, 32, 16):
        if entries % (2 * rows) == 0:
            return rows
    raise ValueError(entries)


def padded(size):
    return -(-size // LANES) * LANES


def make_assemble(n_group, n_voc, u_rows, v_rows, rank, r, entries):
    per = n_voc // n_group
    wide = padded(v_rows)

    def kernel(sampled_ref, *refs):
        packs = refs[:n_group]
        u_out, v_out, want_out, v_wide = refs[n_group:]
        group = lax.axis_index("group")
        voc = lax.axis_index("vocab")
        for k in range(n_group):
            member = group ^ k
            start = pl.multiple_of(member * u_rows, u_rows)
            u_out[pl.ds(start, u_rows), :] = packs[k][:, :u_rows].T
            for t in range(per):
                shard = member * per + lax.rem(t + voc // n_group, per)
                at = u_rows + t * wide
                block = packs[k][:, at : at + wide].astype(jnp.float32).T
                v_wide[pl.ds(pl.multiple_of(shard * v_rows, 8), v_rows), :] = block[:v_rows]
        v_out[...] = v_wide[...].T.astype(jnp.bfloat16)
        for k in range(n_voc):
            for s in range(2):
                want_out[k, :, s * r : (s + 1) * r] = (
                    sampled_ref[s : s + 1, k * r : (k + 1) * r] - voc * entries
                )

    return pl.pallas_call(
        kernel,
        out_shape=(
            jax.ShapeDtypeStruct((n_group * u_rows, rank), jnp.bfloat16),
            jax.ShapeDtypeStruct((rank, n_voc * v_rows), jnp.bfloat16),
            jax.ShapeDtypeStruct((n_voc, 1, 2 * r), jnp.int32),
        ),
        in_specs=[WHOLE] * (1 + n_group),
        out_specs=(WHOLE,) * 3,
        scratch_shapes=[pltpu.VMEM((n_voc * v_rows, rank), jnp.float32)],
        compiler_params=pltpu.CompilerParams(vmem_limit_bytes=VMEM_LIMIT),
        name="assemble",
    )


def sources_of(hop, n_voc):
    position = ring_position(lax.axis_index("vocab"), n_voc)
    if hop < n_voc // 2:
        return ring_device(position - hop, n_voc), ring_device(position + hop, n_voc)
    return ring_device(position, n_voc), ring_device(position + hop, n_voc)


def make_chunk(hop, pieces, r, depth, entries, rank, n_voc):
    tile = tile_rows(entries)
    tiles = entries // tile
    n = 4 * r
    last = hop == n_voc // 2
    earlier = hop - 1 if last else 0

    def kernel(*refs):
        piece = refs[:pieces]
        head_ref, u_ref, v_ref, want_ref = refs[pieces : pieces + 4]
        before = refs[pieces + 4 : pieces + 4 + earlier]
        out_ref, held, rows, proj, first, second, top, total, pick, sems = refs[
            pieces + 4 + earlier :
        ]

        def fetch(t, slot):
            return pltpu.make_async_copy(
                head_ref.at[pl.ds(pl.multiple_of(t * tile, tile), tile), :],
                held.at[slot],
                sems.at[slot],
            )

        for t in range(min(4, tiles)):
            fetch(t, t).start()
        at = 0
        for ref in piece:
            block = ref[...].reshape(-1, depth)
            rows[:, at : at + block.shape[0]] = block.T
            at += block.shape[0]
        proj[...] = jnp.dot(v_ref[...], rows[...], preferred_element_type=jnp.float32).astype(
            jnp.bfloat16
        )
        top[...] = jnp.full(top.shape, -1e30, jnp.float32)
        second[...] = jnp.full(second.shape, -1e30, jnp.float32)
        total[...] = jnp.zeros(total.shape, jnp.float32)
        pick[...] = jnp.zeros(pick.shape, jnp.float32)
        left, right = sources_of(hop, n_voc)
        want = jnp.concatenate([want_ref[left], want_ref[right]], axis=1)

        def multiply(t, slot, into):
            u_tile = u_ref[pl.ds(pl.multiple_of(t * tile, tile), tile), :]
            into[...] = jnp.dot(
                held[slot], rows[...], preferred_element_type=jnp.float32
            ) + jnp.dot(u_tile, proj[...], preferred_element_type=jnp.float32)

        def reduce(start, values):
            x = values[...]
            entry = lax.broadcasted_iota(jnp.int32, (tile, n), 0)
            hit = jnp.where(entry == want - start, x, 0.0)
            x3 = x.reshape(tile // 8, 8, n)
            new = jnp.maximum(top[...], jnp.max(x3, axis=0))
            total[...] = total[...] * jnp.exp(top[...] - new) + jnp.sum(
                jnp.exp(x3 - new[None]), axis=0
            )
            pick[...] = pick[...] + jnp.sum(hit.reshape(tile // 8, 8, n), axis=0)
            top[...] = new

        @pl.loop(0, tiles // 2)
        def _(i):
            slot = 2 * lax.rem(i, 2)
            fetch(2 * i, slot).wait()
            multiply(2 * i, slot, first)
            reduce(jnp.where(i == 0, 1 << 29, (2 * i - 1) * tile), second)
            fetch(2 * i + 1, slot + 1).wait()
            multiply(2 * i + 1, slot + 1, second)
            reduce(2 * i * tile, first)

            @pl.when(2 * i + 4 < tiles)
            def _():
                fetch(2 * i + 4, slot).start()
                fetch(2 * i + 5, slot + 1).start()

        reduce(entries - tile, second)
        best = jnp.max(top[...], axis=0, keepdims=True)
        sums = jnp.sum(total[...] * jnp.exp(top[...] - best), axis=0, keepdims=True)
        picked = jnp.sum(pick[...], axis=0, keepdims=True)
        if not last:
            for q, value in enumerate((best, sums, picked)):
                out_ref[q : q + 1, :] = value
            return
        for q, value in enumerate((best, sums, picked)):
            out_ref[q, pl.ds(left, 1), :] = value[:, : 2 * r]
            out_ref[q, pl.ds(right, 1), :] = value[:, 2 * r :]
            for k in range(1, hop):
                a, b = sources_of(k, n_voc)
                out_ref[q, pl.ds(a, 1), :] = before[k - 1][q : q + 1, : 2 * r]
                out_ref[q, pl.ds(b, 1), :] = before[k - 1][q : q + 1, 2 * r :]

    return pl.pallas_call(
        kernel,
        out_shape=jax.ShapeDtypeStruct((3, n_voc, 2 * r) if last else (3, n), jnp.float32),
        in_specs=[WHOLE] * pieces
        + [pl.BlockSpec(memory_space=pl.ANY)]
        + [WHOLE] * (3 + earlier),
        out_specs=WHOLE,
        scratch_shapes=[
            pltpu.VMEM((4, tile, depth), jnp.bfloat16),
            pltpu.VMEM((depth, n), jnp.bfloat16),
            pltpu.VMEM((rank, n), jnp.bfloat16),
            pltpu.VMEM((tile, n), jnp.float32),
            pltpu.VMEM((tile, n), jnp.float32),
            pltpu.VMEM((8, n), jnp.float32),
            pltpu.VMEM((8, n), jnp.float32),
            pltpu.VMEM((8, n), jnp.float32),
            pltpu.SemaphoreType.DMA((4,)),
        ],
        compiler_params=pltpu.CompilerParams(vmem_limit_bytes=VMEM_LIMIT),
        cost_estimate=pl.CostEstimate(
            flops=2 * n * entries * (depth + 256),
            bytes_accessed=2 * entries * (depth + LANES),
            transcendentals=n * entries,
        ),
        name="chunk",
    )


def make_combine(bit, r, n_voc, finish):
    def kernel(mine_ref, other_ref, *outs):
        high = (lax.axis_index("vocab") & bit) != 0
        low = [jnp.where(high, other_ref[q], mine_ref[q]) for q in range(3)]
        up = [jnp.where(high, mine_ref[q], other_ref[q]) for q in range(3)]
        top = jnp.maximum(low[0], up[0])
        total = low[1] * jnp.exp(low[0] - top) + up[1] * jnp.exp(up[0] - top)
        pick = low[2] + up[2]
        if not finish:
            for q, value in enumerate((top, total, pick)):
                outs[0][q] = value
            return
        log_total = top + jnp.log(total)
        for ref, value in zip(outs, (pick - log_total, log_total)):
            for k in range(n_voc):
                for s in range(2):
                    ref[s : s + 1, k * r : (k + 1) * r] = value[k : k + 1, s * r : (s + 1) * r]

    if finish:
        shape = (jax.ShapeDtypeStruct((2, n_voc * r), jnp.float32),) * 2
        specs = (WHOLE, WHOLE)
    else:
        shape, specs = jax.ShapeDtypeStruct((3, n_voc, 2 * r), jnp.float32), WHOLE
    return pl.pallas_call(
        kernel, out_shape=shape, in_specs=[WHOLE, WHOLE], out_specs=specs, name="combine"
    )


def body(hidden, head, factor_u, factor_v, sampled):
    n_group = lax.axis_size("group")
    n_voc = lax.axis_size("vocab")
    _, r, depth = hidden.shape
    entries = head.shape[0]
    rank = factor_u.shape[1]
    per = n_voc // n_group
    half = n_voc // 2

    order = ring_order(n_voc)
    ahead = [(order[i], order[(i + 1) % n_voc]) for i in range(n_voc)]
    behind = [(b, a) for a, b in ahead]

    def trade(x, axis, size, bit):
        return lax.ppermute(x, axis, [(i, i ^ bit) for i in range(size)])

    up, down = [hidden], [hidden]
    for hop in range(1, half):
        up.append(lax.ppermute(up[-1], "vocab", ahead))
        down.append(lax.ppermute(down[-1], "vocab", behind))
    ends = [
        lax.ppermute(up[-1][0], "vocab", ahead),
        lax.ppermute(down[-1][1], "vocab", behind),
    ]

    moves = [(v * n_group + g, g * n_voc + v) for v in range(n_voc) for g in range(n_group)]
    pack = [lax.ppermute(factor_u.T, ("group", "vocab"), moves)]
    for t in range(per):
        moves = [
            (
                (v % n_group) * n_voc + g * per + (t + v // n_group) % per,
                g * n_voc + v,
            )
            for v in range(n_voc)
            for g in range(n_group)
        ]
        shard = lax.ppermute(factor_v.T, ("group", "vocab"), moves)
        pack.append(jnp.pad(shard, ((0, 0), (0, padded(shard.shape[1]) - shard.shape[1]))))
    packs = {0: jnp.concatenate(pack, axis=1)}
    bit = n_group // 2
    while bit:
        for k in list(packs):
            packs[k ^ bit] = trade(packs[k], "group", n_group, bit)
        bit //= 2
    full_u, full_v, want = make_assemble(
        n_group, n_voc, factor_u.shape[0], factor_v.shape[0], rank, r, entries
    )(sampled, *[packs[k] for k in range(n_group)])

    stats = []
    for hop in range(1, half + 1):
        pieces = [up[hop], down[hop]] if hop < half else [hidden] + ends
        chunk = make_chunk(hop, len(pieces), r, depth, entries, rank, n_voc)
        before = stats if hop == half else []
        stats.append(chunk(*pieces, head, full_u, full_v, want, *before))
    part = stats[-1]
    bit = 1
    while bit < n_voc:
        other = trade(part, "vocab", n_voc, bit)
        part = make_combine(bit, r, n_voc, 2 * bit == n_voc)(part, other)
        bit *= 2
    return part


def solution(mesh):
    in_specs = (
        P(None, ("group", "vocab"), None),
        P("vocab", None),
        P(("group", "vocab"), None),
        P("vocab", None),
        P(None, "group"),
    )
    out_specs = (P(None, "group"), P(None, "group"))
    return jax.shard_map(body, mesh=mesh, in_specs=in_specs, out_specs=out_specs, check_vma=False)
```

time: 211 us -> 117 us (0.55)
  blocking collectives: 80.8 us -> 0 us
  Pallas kernels: 0 us -> 62 us
  matrix products: 49.7 us -> 0 us
  starting transfers between devices: 11.9 us -> 35.1 us
  local copies, waits for them, and re-layouts: 22.6 us -> 2.54 us
  other arithmetic: 13.6 us -> 0.02 us
  between operations: 14.2 us -> 0.76 us
    pallas_call x0 -> x8, Pallas kernels: none -> 62 us  [the longest x4 57.1 us: body(): stats.append(chunk(*pieces, head, full_u, full_v, want, *before))]
    dot_general x4 -> x0, matrix products: 49.7 us -> none  [the longest x2 35.6 us: body(): base = jnp.dot(rows, head.T, preferred_element_type=jnp.float32)]
    all_gather x2 -> x0, blocking collectives: 43.9 us -> none  [the longest x1 33.7 us: body(): full_v = lax.all_gather(factor_v, 'vocab', axis=0, tiled=True)]
    ppermute x0 -> x17, starting transfers between devices: none -> 35.1 us  [the longest x6 14.6 us: trade(): return lax.ppermute(x, axis, [(i, i ^ bit) for i in range(size)])]
    pmax x1 -> x0, blocking collectives: 19.5 us -> none  [body(): top = lax.pmax(local_top, 'vocab')]
    psum x1 -> x0, blocking collectives: 17.4 us -> none  [body(): total, picked = lax.psum((local_sum, local_pick), 'vocab')]
    gather x2 -> x0, local copies, waits for them, and re-layouts: 16.3 us -> none  [body(): local_pick = jnp.take_along_axis(logits, column[:, None], axis=1)[:, 0]]
    ppermute x0 -> x17, waiting for transfers between devices: none -> 16.3 us  [the longest x6 11.8 us: trade(): return lax.ppermute(x, axis, [(i, i ^ bit) for i in range(size)])]
  transfers between devices with their start and end apart: 4 -> 17, of which waited for: 2 -> 7; matrix products, arithmetic and copies ran while one was open for 20% -> 0% of each run, Pallas kernels for 0% -> 37%
where the time goes in v2:
time: 117 us
  Pallas kernels  62 us (53%)
  starting transfers between devices  35.1 us (30%)
  waiting for transfers between devices  16.3 us (14%)
  local copies, waits for them, and re-layouts  2.54 us (2%)
    pallas_call x4, Pallas kernels, body(): stats.append(chunk(*pieces, head, full_u, full_v, want, *before))  57.1 us
    ppermute x6, starting transfers between devices, trade(): return lax.ppermute(x, axis, [(i, i ^ bit) for i in range(size)])  14.6 us
    ppermute x6, waiting for transfers between devices, trade(): return lax.ppermute(x, axis, [(i, i ^ bit) for i in range(size)])  11.8 us
    ppermute x3, starting transfers between devices, body(): down.append(lax.ppermute(down[-1], 'vocab', behind))  6.26 us
    ppermute x3, starting transfers between devices, body(): up.append(lax.ppermute(up[-1], 'vocab', ahead))  6.06 us
    ppermute x2, starting transfers between devices, body(): shard = lax.ppermute(factor_v.T, ('group', 'vocab'), moves)  4.46 us
    ppermute x3, waiting for transfers between devices, body(): up.append(lax.ppermute(up[-1], 'vocab', ahead))  4.26 us
    pallas_call x3, Pallas kernels, body(): part = make_combine(bit, r, n_voc, 2 * bit == n_voc)(part, other)  4.1 us
  transfers between devices with their start and end apart: 17, of which 7 were waited for; matrix products, arithmetic and copies ran while one was open for 0% of the time, Pallas kernels for 37%

profile of v2, /device:TPU:0, one launch (start us, length us, event | category | flops | bytes accessed | tf_op | source)
XLA Modules:
  0.0 116.8 jit_solution(16197695092357184872)
XLA Ops:
  0.6 3.1 %collective-permute-start = (bf16[2,64,2304]{2,1,0:T(8,128)(2,1)}, bf16[2,64,2304]{2,1,0:T(8,128)(2,1)S(1)}, u32[]{:S(2)}, u32[]{:S(2)}) collective-permute-start(bf16[2,64,2304]{2,1,0:T(8,128)(2,1)} %refs_0_.1), channel_id=1, source_target_pairs={{0,2},{2,4},{4,6},{6,7},{7,5},{5,3},{3,1},{1,0},{8,10},{10,12},{12... | collective-permute-start | bytes 1769480 | tf_op jit(solution)/shard_map/ppermute | solution.py:246
  3.7 1.6 %collective-permute-start.8 = (bf16[64,1024]{1,0:T(8,128)(2,1)}, bf16[64,1024]{1,0:T(8,128)(2,1)S(1)}, u32[]{:S(2)}, u32[]{:S(2)}) collective-permute-start(bf16[64,1024]{1,0:T(8,128)(2,1)} %bitcast.6), channel_id=1, source_target_pairs={{0,0},{1,8},{2,16},{3,24},{4,1},{5,9},{6,17},{7,25},{8,2},{9,10},{... | collective-permute-start | bytes 393224 | tf_op jit(solution)/shard_map/ppermute | solution.py:254
  5.3 3.0 %collective-permute-start.10 = (bf16[64,288]{1,0:T(8,128)(2,1)}, bf16[64,288]{1,0:T(8,128)(2,1)S(1)}, u32[]{:S(2)}, u32[]{:S(2)}) collective-permute-start(bf16[64,288]{1,0:T(8,128)(2,1)} %bitcast.7), channel_id=1, source_target_pairs={{1,0},{3,8},{5,16},{7,24},{9,1},{11,9},{13,17},{15,25},{17,2},{19,... | collective-permute-start | bytes 110600 | tf_op jit(solution)/shard_map/ppermute | solution.py:264
  8.3 1.4 %collective-permute-start.9 = (bf16[64,288]{1,0:T(8,128)(2,1)}, bf16[64,288]{1,0:T(8,128)(2,1)S(1)}, u32[]{:S(2)}, u32[]{:S(2)}) collective-permute-start(bf16[64,288]{1,0:T(8,128)(2,1)} %bitcast.8), channel_id=1, source_target_pairs={{0,0},{2,8},{4,16},{6,24},{8,1},{10,9},{12,17},{14,25},{16,2},{18,... | collective-permute-start | bytes 110600 | tf_op jit(solution)/shard_map/ppermute | solution.py:264
  9.7 3.8 %collective-permute-start.4 = (bf16[2,64,2304]{2,1,0:T(8,128)(2,1)}, bf16[2,64,2304]{2,1,0:T(8,128)(2,1)S(1)}, u32[]{:S(2)}, u32[]{:S(2)}) collective-permute-start(bf16[2,64,2304]{2,1,0:T(8,128)(2,1)} %refs_0_.1), channel_id=1, source_target_pairs={{2,0},{4,2},{6,4},{7,6},{5,7},{3,5},{1,3},{0,1},{10,8},{12,10},{14... | collective-permute-start | bytes 1769480 | tf_op jit(solution)/shard_map/ppermute | solution.py:247
  13.5 4.3 %collective-permute-done.refs_0_ = bf16[2,64,2304]{2,1,0:T(8,128)(2,1)S(1)} collective-permute-done((bf16[2,64,2304]{2,1,0:T(8,128)(2,1)}, bf16[2,64,2304]{2,1,0:T(8,128)(2,1)S(1)}, u32[]{:S(2)}, u32[]{:S(2)}) %collective-permute-start) | collective-permute-done | bytes 589856 | tf_op jit(solution)/shard_map/ppermute | solution.py:246
  17.8 2.4 %collective-permute-start.1 = (bf16[2,64,2304]{2,1,0:T(8,128)(2,1)S(1)}, bf16[2,64,2304]{2,1,0:T(8,128)(2,1)S(1)}, u32[]{:S(2)}, u32[]{:S(2)}) collective-permute-start(bf16[2,64,2304]{2,1,0:T(8,128)(2,1)S(1)} %collective-permute-done.refs_0_), channel_id=1, source_target_pairs={{0,2},{2,4},{4,6},{6,7},{7,5},{5,3},{3,1},{1,0},{8,10},{10,12},{12... | collective-permute-start | bytes 1769480 | tf_op jit(solution)/shard_map/ppermute | solution.py:246
  20.1 0.3 collective-permute-done.10
  20.4 0.0 collective-permute-done.9
  20.4 0.0 collective-permute-done.8
  20.5 9.3 %collective-permute-start.12 = (bf16[64,1792]{1,0:T(8,128)(2,1)S(1)}, bf16[64,1792]{1,0:T(8,128)(2,1)S(1)}, u32[]{:S(2)}, u32[]{:S(2)}) collective-permute-start(bf16[64,1792]{1,0:T(8,128)(2,1)S(1)} %fusion.4.refs_0_), channel_id=1, source_target_pairs={{0,16},{8,24},{16,0},{24,8},{1,17},{9,25},{17,1},{25,9},{2,18},{10... | collective-permute-start | bytes 688136 | tf_op jit(solution)/shard_map/ppermute | solution.py:242
  29.8 0.0 collective-permute-start.11
  29.8 4.0 %collective-permute-done.12.refs_2_ = bf16[64,1792]{1,0:T(8,128)(2,1)S(1)} collective-permute-done((bf16[64,1792]{1,0:T(8,128)(2,1)S(1)}, bf16[64,1792]{1,0:T(8,128)(2,1)S(1)}, u32[]{:S(2)}, u32[]{:S(2)}) %collective-permute-start.12) | collective-permute-done | bytes 229408 | tf_op jit(solution)/shard_map/ppermute | solution.py:242
  33.8 0.0 collective-permute-start.13
  33.8 0.0 collective-permute-done.4.refs_1_
  33.8 0.9 collective-permute-start.5
  34.7 0.0 collective-permute-done.11.refs_1_
  34.7 0.6 collective-permute-done.13.refs_3_
  35.3 0.7 copy-done.2
  36.0 0.8 assemble.1
  36.8 0.0 collective-permute-done.1.refs_0_
  36.8 0.6 collective-permute-start.2
  37.4 14.3 %chunk.4.refs_7_ = f32[3,256]{1,0:T(4,128)S(1)} custom-call(bf16[2,64,2304]{2,1,0:T(8,128)(2,1)S(1)} %collective-permute-done.refs_0_, bf16[2,64,2304]{2,1,0:T(8,128)(2,1)S(1)} %collective-permute-done.4.refs_1_, bf16[4096,2304]{1,0:T(8,128)(2,1)} %refs_3_.1, bf16[4096,64]{1,0:T(8,128)(2,1)S(1)} %get-tuple-element.5.refs_3_.refs_4_, ...), custom_call_target="tpu_custom_call" | custom-call | flops 5368709120 | bytes 19922944 | tf_op jit(solution)/shard_map/chunk/pallas_call | solution.py:281
  51.7 0.0 copy-start
  51.7 0.0 collective-permute-done.5.refs_1_
  51.7 1.6 %collective-permute-start.6 = (bf16[2,64,2304]{2,1,0:T(8,128)(2,1)S(1)}, bf16[2,64,2304]{2,1,0:T(8,128)(2,1)S(1)}, u32[]{:S(2)}, u32[]{:S(2)}) collective-permute-start(bf16[2,64,2304]{2,1,0:T(8,128)(2,1)S(1)} %collective-permute-done.5.refs_1_), channel_id=1, source_target_pairs={{2,0},{4,2},{6,4},{7,6},{5,7},{3,5},{1,3},{0,1},{10,8},{12,10},{14... | collective-permute-start | bytes 1769480 | tf_op jit(solution)/shard_map/ppermute | solution.py:247
  53.3 14.3 %chunk.5.refs_8_ = f32[3,256]{1,0:T(4,128)S(1)} custom-call(bf16[2,64,2304]{2,1,0:T(8,128)(2,1)S(1)} %collective-permute-done.1.refs_0_, bf16[2,64,2304]{2,1,0:T(8,128)(2,1)S(1)} %collective-permute-done.5.refs_1_, bf16[4096,2304]{1,0:T(8,128)(2,1)} %refs_3_.1, bf16[4096,64]{1,0:T(8,128)(2,1)S(1)} %get-tuple-element.5.refs_3_.refs_4_, ...), custom_call_target="tpu_custom_call" | custom-call | flops 5368709120 | bytes 19922944 | tf_op jit(solution)/shard_map/chunk/pallas_call | solution.py:281
  67.6 0.0 collective-permute-done.2.refs_0_
  67.6 0.5 collective-permute-start.3
  68.2 0.0 collective-permute-done.6.refs_1_
  68.2 1.6 %collective-permute-start.7 = (bf16[64,2304]{1,0:T(8,128)(2,1)S(1)}, bf16[64,2304]{1,0:T(8,128)(2,1)S(1)}, u32[]{:S(2)}, u32[]{:S(2)}) collective-permute-start(bf16[64,2304]{1,0:T(8,128)(2,1)S(1)} %slice_bitcast_fusion), channel_id=1, source_target_pairs={{2,0},{4,2},{6,4},{7,6},{5,7},{3,5},{1,3},{0,1},{10,8},{12,10},{14... | collective-permute-start | bytes 884744 | tf_op jit(solution)/shard_map/ppermute | solution.py:250
  69.8 14.3 %chunk.6.refs_9_ = f32[3,256]{1,0:T(4,128)S(1)} custom-call(bf16[2,64,2304]{2,1,0:T(8,128)(2,1)S(1)} %collective-permute-done.2.refs_0_, bf16[2,64,2304]{2,1,0:T(8,128)(2,1)S(1)} %collective-permute-done.6.refs_1_, bf16[4096,2304]{1,0:T(8,128)(2,1)} %refs_3_.1, bf16[4096,64]{1,0:T(8,128)(2,1)S(1)} %get-tuple-element.5.refs_3_.refs_4_, ...), custom_call_target="tpu_custom_call" | custom-call | flops 5368709120 | bytes 19922944 | tf_op jit(solution)/shard_map/chunk/pallas_call | solution.py:281
  84.1 0.0 collective-permute-done.3.refs_1_
  84.1 0.0 collective-permute-done.7.refs_2_
  84.1 14.3 %chunk.7.mine_ref = f32[3,8,128]{2,1,0:T(8,128)S(1)} custom-call(bf16[2,64,2304]{2,1,0:T(8,128)(2,1)S(1)} %copy-done, bf16[64,2304]{1,0:T(8,128)(2,1)S(1)} %collective-permute-done.3.refs_1_, bf16[64,2304]{1,0:T(8,128)(2,1)S(1)} %collective-permute-done.7.refs_2_, bf16[4096,2304]{1,0:T(8,128)(2,1)} %refs_3_.1, ...), custom_call_target="tpu_custom_call" | custom-call | flops 5368709120 | bytes 19922944 | tf_op jit(solution)/shard_map/chunk/pallas_call | solution.py:281
  98.4 0.0 copy-start.1
  98.4 2.1 %collective-permute-start.14 = (f32[3,8,128]{2,1,0:T(8,128)S(1)}, f32[3,8,128]{2,1,0:T(8,128)S(1)}, u32[]{:S(2)}, u32[]{:S(2)}) collective-permute-start(f32[3,8,128]{2,1,0:T(8,128)S(1)} %chunk.7.mine_ref), channel_id=1, source_target_pairs={{0,1},{1,0},{2,3},{3,2},{4,5},{5,4},{6,7},{7,6},{8,9},{9,8},{10,11... | collective-permute-start | bytes 36872 | tf_op jit(solution)/shard_map/ppermute | solution.py:242
  100.5 1.7 %collective-permute-done.14.other_ref = f32[3,8,128]{2,1,0:T(8,128)S(1)} collective-permute-done((f32[3,8,128]{2,1,0:T(8,128)S(1)}, f32[3,8,128]{2,1,0:T(8,128)S(1)}, u32[]{:S(2)}, u32[]{:S(2)}) %collective-permute-start.14) | collective-permute-done | bytes 12320 | tf_op jit(solution)/shard_map/ppermute | solution.py:242
  102.2 0.6 copy-done.4
  102.8 1.3 %combine.3.mine_ref = f32[3,8,128]{2,1,0:T(8,128)} custom-call(f32[3,8,128]{2,1,0:T(8,128)} %copy-done.1, f32[3,8,128]{2,1,0:T(8,128)} %copy-done.4), custom_call_target="tpu_custom_call" | custom-call | tf_op jit(solution)/shard_map/combine/pallas_call | solution.py:286
  104.1 1.9 %collective-permute-start.15 = (f32[3,8,128]{2,1,0:T(8,128)}, f32[3,8,128]{2,1,0:T(8,128)S(1)}, u32[]{:S(2)}, u32[]{:S(2)}) collective-permute-start(f32[3,8,128]{2,1,0:T(8,128)} %combine.3.mine_ref), channel_id=1, source_target_pairs={{0,2},{1,3},{2,0},{3,1},{4,6},{5,7},{6,4},{7,5},{8,10},{9,11},{10,... | collective-permute-start | bytes 36872 | tf_op jit(solution)/shard_map/ppermute | solution.py:242
  106.0 2.0 %collective-permute-done.15.other_ref = f32[3,8,128]{2,1,0:T(8,128)S(1)} collective-permute-done((f32[3,8,128]{2,1,0:T(8,128)}, f32[3,8,128]{2,1,0:T(8,128)S(1)}, u32[]{:S(2)}, u32[]{:S(2)}) %collective-permute-start.15) | collective-permute-done | bytes 12320 | tf_op jit(solution)/shard_map/ppermute | solution.py:242
  108.0 0.6 copy-done.5
  108.6 1.3 %combine.4.mine_ref = f32[3,8,128]{2,1,0:T(8,128)} custom-call(f32[3,8,128]{2,1,0:T(8,128)} %combine.3.mine_ref, f32[3,8,128]{2,1,0:T(8,128)} %copy-done.5), custom_call_target="tpu_custom_call" | custom-call | tf_op jit(solution)/shard_map/combine/pallas_call | solution.py:286
  109.9 1.4 %collective-permute-start.16 = (f32[3,8,128]{2,1,0:T(8,128)}, f32[3,8,128]{2,1,0:T(8,128)S(1)}, u32[]{:S(2)}, u32[]{:S(2)}) collective-permute-start(f32[3,8,128]{2,1,0:T(8,128)} %combine.4.mine_ref), channel_id=1, source_target_pairs={{0,4},{1,5},{2,6},{3,7},{4,0},{5,1},{6,2},{7,3},{8,12},{9,13},{10,... | collective-permute-start | bytes 36872 | tf_op jit(solution)/shard_map/ppermute | solution.py:242
  111.3 3.4 %collective-permute-done.16.other_ref = f32[3,8,128]{2,1,0:T(8,128)S(1)} collective-permute-done((f32[3,8,128]{2,1,0:T(8,128)}, f32[3,8,128]{2,1,0:T(8,128)S(1)}, u32[]{:S(2)}, u32[]{:S(2)}) %collective-permute-start.16) | collective-permute-done | bytes 12320 | tf_op jit(solution)/shard_map/ppermute | solution.py:242
  114.7 0.6 copy-done.3
  115.3 1.4 %combine.5 = (f32[2,512]{1,0:T(2,128)}, f32[2,512]{1,0:T(2,128)}) custom-call(f32[3,8,128]{2,1,0:T(8,128)} %combine.4.mine_ref, f32[3,8,128]{2,1,0:T(8,128)} %copy-done.3), custom_call_target="tpu_custom_call" | custom-call | tf_op jit(solution)/shard_map/combine/pallas_call | solution.py:286
  (9 shorter events, 0.1 us)
Async XLA Ops:
  0.6 17.1 %collective-permute-start = (bf16[2,64,2304]{2,1,0:T(8,128)(2,1)}, bf16[2,64,2304]{2,1,0:T(8,128)(2,1)S(1)}, u32[]{:S(2)}, u32[]{:S(2)}) collective-permute-start(bf16[2,64,2304]{2,1,0:T(8,128)(2,1)} %refs_0_.1), channel_id=1, source_target_pairs={{0,2},{2,4},{4,6},{6,7},{7,5},{5,3},{3,1},{1,0},{8,10},{10,12},{12... | collective-permute-start | bytes 1769480 | tf_op jit(solution)/shard_map/ppermute | solution.py:246
  3.7 16.7 %collective-permute-start.8 = (bf16[64,1024]{1,0:T(8,128)(2,1)}, bf16[64,1024]{1,0:T(8,128)(2,1)S(1)}, u32[]{:S(2)}, u32[]{:S(2)}) collective-permute-start(bf16[64,1024]{1,0:T(8,128)(2,1)} %bitcast.6), channel_id=1, source_target_pairs={{0,0},{1,8},{2,16},{3,24},{4,1},{5,9},{6,17},{7,25},{8,2},{9,10},{... | collective-permute-start | bytes 393224 | tf_op jit(solution)/shard_map/ppermute | solution.py:254
  5.3 15.2 %collective-permute-start.10 = (bf16[64,288]{1,0:T(8,128)(2,1)}, bf16[64,288]{1,0:T(8,128)(2,1)S(1)}, u32[]{:S(2)}, u32[]{:S(2)}) collective-permute-start(bf16[64,288]{1,0:T(8,128)(2,1)} %bitcast.7), channel_id=1, source_target_pairs={{1,0},{3,8},{5,16},{7,24},{9,1},{11,9},{13,17},{15,25},{17,2},{19,... | collective-permute-start | bytes 110600 | tf_op jit(solution)/shard_map/ppermute | solution.py:264
  8.3 12.2 %collective-permute-start.9 = (bf16[64,288]{1,0:T(8,128)(2,1)}, bf16[64,288]{1,0:T(8,128)(2,1)S(1)}, u32[]{:S(2)}, u32[]{:S(2)}) collective-permute-start(bf16[64,288]{1,0:T(8,128)(2,1)} %bitcast.8), channel_id=1, source_target_pairs={{0,0},{2,8},{4,16},{6,24},{8,1},{10,9},{12,17},{14,25},{16,2},{18,... | collective-permute-start | bytes 110600 | tf_op jit(solution)/shard_map/ppermute | solution.py:264
  9.7 24.1 %collective-permute-start.4 = (bf16[2,64,2304]{2,1,0:T(8,128)(2,1)}, bf16[2,64,2304]{2,1,0:T(8,128)(2,1)S(1)}, u32[]{:S(2)}, u32[]{:S(2)}) collective-permute-start(bf16[2,64,2304]{2,1,0:T(8,128)(2,1)} %refs_0_.1), channel_id=1, source_target_pairs={{2,0},{4,2},{6,4},{7,6},{5,7},{3,5},{1,3},{0,1},{10,8},{12,10},{14... | collective-permute-start | bytes 1769480 | tf_op jit(solution)/shard_map/ppermute | solution.py:247
  17.8 19.1 %collective-permute-start.1 = (bf16[2,64,2304]{2,1,0:T(8,128)(2,1)S(1)}, bf16[2,64,2304]{2,1,0:T(8,128)(2,1)S(1)}, u32[]{:S(2)}, u32[]{:S(2)}) collective-permute-start(bf16[2,64,2304]{2,1,0:T(8,128)(2,1)S(1)} %collective-permute-done.refs_0_), channel_id=1, source_target_pairs={{0,2},{2,4},{4,6},{6,7},{7,5},{5,3},{3,1},{1,0},{8,10},{10,12},{12... | collective-permute-start | bytes 1769480 | tf_op jit(solution)/shard_map/ppermute | solution.py:246
  20.5 13.3 %collective-permute-start.12 = (bf16[64,1792]{1,0:T(8,128)(2,1)S(1)}, bf16[64,1792]{1,0:T(8,128)(2,1)S(1)}, u32[]{:S(2)}, u32[]{:S(2)}) collective-permute-start(bf16[64,1792]{1,0:T(8,128)(2,1)S(1)} %fusion.4.refs_0_), channel_id=1, source_target_pairs={{0,16},{8,24},{16,0},{24,8},{1,17},{9,25},{17,1},{25,9},{2,18},{10... | collective-permute-start | bytes 688136 | tf_op jit(solution)/shard_map/ppermute | solution.py:242
  29.8 4.9 %collective-permute-start.11 = (bf16[64,1792]{1,0:T(8,128)(2,1)S(1)}, bf16[64,1792]{1,0:T(8,128)(2,1)S(1)}, u32[]{:S(2)}, u32[]{:S(2)}) collective-permute-start(bf16[64,1792]{1,0:T(8,128)(2,1)S(1)} %fusion.4.refs_0_), channel_id=1, source_target_pairs={{0,8},{8,0},{16,24},{24,16},{1,9},{9,1},{17,25},{25,17},{2,10},{10... | collective-permute-start | bytes 688136 | tf_op jit(solution)/shard_map/ppermute | solution.py:242
  33.8 1.5 %collective-permute-start.13 = (bf16[64,1792]{1,0:T(8,128)(2,1)S(1)}, bf16[64,1792]{1,0:T(8,128)(2,1)S(1)}, u32[]{:S(2)}, u32[]{:S(2)}) collective-permute-start(bf16[64,1792]{1,0:T(8,128)(2,1)S(1)} %collective-permute-done.12.refs_2_), channel_id=1, source_target_pairs={{0,8},{8,0},{16,24},{24,16},{1,9},{9,1},{17,25},{25,17},{2,10},{10... | collective-permute-start | bytes 688136 | tf_op jit(solution)/shard_map/ppermute | solution.py:242
  33.8 17.9 %collective-permute-start.5 = (bf16[2,64,2304]{2,1,0:T(8,128)(2,1)S(1)}, bf16[2,64,2304]{2,1,0:T(8,128)(2,1)S(1)}, u32[]{:S(2)}, u32[]{:S(2)}) collective-permute-start(bf16[2,64,2304]{2,1,0:T(8,128)(2,1)S(1)} %collective-permute-done.4.refs_1_), channel_id=1, source_target_pairs={{2,0},{4,2},{6,4},{7,6},{5,7},{3,5},{1,3},{0,1},{10,8},{12,10},{14... | collective-permute-start | bytes 1769480 | tf_op jit(solution)/shard_map/ppermute | solution.py:247
  35.3 0.7 copy-start.2
  36.8 30.8 %collective-permute-start.2 = (bf16[2,64,2304]{2,1,0:T(8,128)(2,1)S(1)}, bf16[2,64,2304]{2,1,0:T(8,128)(2,1)S(1)}, u32[]{:S(2)}, u32[]{:S(2)}) collective-permute-start(bf16[2,64,2304]{2,1,0:T(8,128)(2,1)S(1)} %collective-permute-done.1.refs_0_), channel_id=1, source_target_pairs={{0,2},{2,4},{4,6},{6,7},{7,5},{5,3},{3,1},{1,0},{8,10},{10,12},{12... | collective-permute-start | bytes 1769480 | tf_op jit(solution)/shard_map/ppermute | solution.py:246
  51.7 32.4 %copy-start = (bf16[2,64,2304]{2,1,0:T(8,128)(2,1)S(1)}, bf16[2,64,2304]{2,1,0:T(8,128)(2,1)}, u32[]{:S(2)}) copy-start(bf16[2,64,2304]{2,1,0:T(8,128)(2,1)} %refs_0_.1) | copy-start | bytes 1769476
  51.7 16.4 %collective-permute-start.6 = (bf16[2,64,2304]{2,1,0:T(8,128)(2,1)S(1)}, bf16[2,64,2304]{2,1,0:T(8,128)(2,1)S(1)}, u32[]{:S(2)}, u32[]{:S(2)}) collective-permute-start(bf16[2,64,2304]{2,1,0:T(8,128)(2,1)S(1)} %collective-permute-done.5.refs_1_), channel_id=1, source_target_pairs={{2,0},{4,2},{6,4},{7,6},{5,7},{3,5},{1,3},{0,1},{10,8},{12,10},{14... | collective-permute-start | bytes 1769480 | tf_op jit(solution)/shard_map/ppermute | solution.py:247
  67.6 16.5 %collective-permute-start.3 = (bf16[64,2304]{1,0:T(8,128)(2,1)S(1)}, bf16[64,2304]{1,0:T(8,128)(2,1)S(1)}, u32[]{:S(2)}, u32[]{:S(2)}) collective-permute-start(bf16[64,2304]{1,0:T(8,128)(2,1)S(1)} %slice_bitcast_fusion.1), channel_id=1, source_target_pairs={{0,2},{2,4},{4,6},{6,7},{7,5},{5,3},{3,1},{1,0},{8,10},{10,12},{12... | collective-permute-start | bytes 884744 | tf_op jit(solution)/shard_map/ppermute | solution.py:249
  68.2 15.9 %collective-permute-start.7 = (bf16[64,2304]{1,0:T(8,128)(2,1)S(1)}, bf16[64,2304]{1,0:T(8,128)(2,1)S(1)}, u32[]{:S(2)}, u32[]{:S(2)}) collective-permute-start(bf16[64,2304]{1,0:T(8,128)(2,1)S(1)} %slice_bitcast_fusion), channel_id=1, source_target_pairs={{2,0},{4,2},{6,4},{7,6},{5,7},{3,5},{1,3},{0,1},{10,8},{12,10},{14... | collective-permute-start | bytes 884744 | tf_op jit(solution)/shard_map/ppermute | solution.py:250
  98.4 3.8 %copy-start.1 = (f32[3,8,128]{2,1,0:T(8,128)}, f32[3,8,128]{2,1,0:T(8,128)S(1)}, u32[]{:S(2)}) copy-start(f32[3,8,128]{2,1,0:T(8,128)S(1)} %chunk.7.mine_ref) | copy-start | bytes 36868
  98.4 3.8 %collective-permute-start.14 = (f32[3,8,128]{2,1,0:T(8,128)S(1)}, f32[3,8,128]{2,1,0:T(8,128)S(1)}, u32[]{:S(2)}, u32[]{:S(2)}) collective-permute-start(f32[3,8,128]{2,1,0:T(8,128)S(1)} %chunk.7.mine_ref), channel_id=1, source_target_pairs={{0,1},{1,0},{2,3},{3,2},{4,5},{5,4},{6,7},{7,6},{8,9},{9,8},{10,11... | collective-permute-start | bytes 36872 | tf_op jit(solution)/shard_map/ppermute | solution.py:242
  102.1 0.6 copy-start.4
  104.1 3.9 %collective-permute-start.15 = (f32[3,8,128]{2,1,0:T(8,128)}, f32[3,8,128]{2,1,0:T(8,128)S(1)}, u32[]{:S(2)}, u32[]{:S(2)}) collective-permute-start(f32[3,8,128]{2,1,0:T(8,128)} %combine.3.mine_ref), channel_id=1, source_target_pairs={{0,2},{1,3},{2,0},{3,1},{4,6},{5,7},{6,4},{7,5},{8,10},{9,11},{10,... | collective-permute-start | bytes 36872 | tf_op jit(solution)/shard_map/ppermute | solution.py:242
  108.0 0.6 copy-start.5
  109.9 4.8 %collective-permute-start.16 = (f32[3,8,128]{2,1,0:T(8,128)}, f32[3,8,128]{2,1,0:T(8,128)S(1)}, u32[]{:S(2)}, u32[]{:S(2)}) collective-permute-start(f32[3,8,128]{2,1,0:T(8,128)} %combine.4.mine_ref), channel_id=1, source_target_pairs={{0,4},{1,5},{2,6},{3,7},{4,0},{5,1},{6,2},{7,3},{8,12},{9,13},{10,... | collective-permute-start | bytes 36872 | tf_op jit(solution)/shard_map/ppermute | solution.py:242
  114.7 0.6 copy-start.3

commit v3 on v2

--- a/solution.py
+++ b/solution.py
@@ -5,7 +5,7 @@
 from jax.experimental.pallas import tpu as pltpu
 from jax.sharding import PartitionSpec as P
 
-VMEM_LIMIT = 48 * 1024 * 1024
+VMEM_LIMIT = 30 * 1024 * 1024
 LANES = 128
 WHOLE = pl.BlockSpec(memory_space=pltpu.VMEM)
 
@@ -92,19 +92,10 @@
         piece = refs[:pieces]
         head_ref, u_ref, v_ref, want_ref = refs[pieces : pieces + 4]
         before = refs[pieces + 4 : pieces + 4 + earlier]
-        out_ref, held, rows, proj, first, second, top, total, pick, sems = refs[
+        out_ref, rows, proj, first, second, top, total, pick = refs[
             pieces + 4 + earlier :
         ]
 
-        def fetch(t, slot):
-            return pltpu.make_async_copy(
-                head_ref.at[pl.ds(pl.multiple_of(t * tile, tile), tile), :],
-                held.at[slot],
-                sems.at[slot],
-            )
-
-        for t in range(min(4, tiles)):
-            fetch(t, t).start()
         at = 0
         for ref in piece:
             block = ref[...].reshape(-1, depth)
@@ -120,11 +111,11 @@
         left, right = sources_of(hop, n_voc)
         want = jnp.concatenate([want_ref[left], want_ref[right]], axis=1)
 
-        def multiply(t, slot, into):
-            u_tile = u_ref[pl.ds(pl.multiple_of(t * tile, tile), tile), :]
+        def multiply(t, into):
+            span = pl.ds(pl.multiple_of(t * tile, tile), tile)
             into[...] = jnp.dot(
-                held[slot], rows[...], preferred_element_type=jnp.float32
-            ) + jnp.dot(u_tile, proj[...], preferred_element_type=jnp.float32)
+                head_ref[span, :], rows[...], preferred_element_type=jnp.float32
+            ) + jnp.dot(u_ref[span, :], proj[...], preferred_element_type=jnp.float32)
 
         def reduce(start, values):
             x = values[...]
@@ -140,18 +131,10 @@
 
         @pl.loop(0, tiles // 2)
         def _(i):
-            slot = 2 * lax.rem(i, 2)
-            fetch(2 * i, slot).wait()
-            multiply(2 * i, slot, first)
+            multiply(2 * i, first)
             reduce(jnp.where(i == 0, 1 << 29, (2 * i - 1) * tile), second)
-            fetch(2 * i + 1, slot + 1).wait()
-            multiply(2 * i + 1, slot + 1, second)
+            multiply(2 * i + 1, second)
             reduce(2 * i * tile, first)
-
-            @pl.when(2 * i + 4 < tiles)
-            def _():
-                fetch(2 * i + 4, slot).start()
-                fetch(2 * i + 5, slot + 1).start()
 
         reduce(entries - tile, second)
         best = jnp.max(top[...], axis=0, keepdims=True)
@@ -172,12 +155,9 @@
     return pl.pallas_call(
         kernel,
         out_shape=jax.ShapeDtypeStruct((3, n_voc, 2 * r) if last else (3, n), jnp.float32),
-        in_specs=[WHOLE] * pieces
-        + [pl.BlockSpec(memory_space=pl.ANY)]
-        + [WHOLE] * (3 + earlier),
+        in_specs=[WHOLE] * (pieces + 4 + earlier),
         out_specs=WHOLE,
         scratch_shapes=[
-            pltpu.VMEM((4, tile, depth), jnp.bfloat16),
             pltpu.VMEM((depth, n), jnp.bfloat16),
             pltpu.VMEM((rank, n), jnp.bfloat16),
             pltpu.VMEM((tile, n), jnp.float32),
@@ -185,7 +165,6 @@
             pltpu.VMEM((8, n), jnp.float32),
             pltpu.VMEM((8, n), jnp.float32),
             pltpu.VMEM((8, n), jnp.float32),
-            pltpu.SemaphoreType.DMA((4,)),
         ],
         compiler_params=pltpu.CompilerParams(vmem_limit_bytes=VMEM_LIMIT),
         cost_estimate=pl.CostEstimate(

time: 117 us -> 103 us (0.88)
  Pallas kernels: 62 us -> 35.3 us
  local copies, waits for them, and re-layouts: 2.54 us -> 15.3 us
    pallas_call x4, Pallas kernels: 57.1 us -> 30.4 us  [body(): stats.append(chunk(*pieces, head, full_u, full_v, want, *before))]
    unnamed x12 -> x16, local copies, waits for them, and re-layouts: 2.5 us -> 15.2 us
  transfers between devices with their start and end apart: 17 -> 17, of which waited for: 7 -> 7; matrix products, arithmetic and copies ran while one was open for 0% -> 0% of each run, Pallas kernels for 37% -> 23%
where the time goes in v3:
time: 103 us
  Pallas kernels  35.3 us (34%)
  starting transfers between devices  35.1 us (34%)
  waiting for transfers between devices  16.4 us (16%)
  local copies, waits for them, and re-layouts  15.3 us (15%)
    pallas_call x4, Pallas kernels, body(): stats.append(chunk(*pieces, head, full_u, full_v, want, *before))  30.4 us
    unnamed x16, local copies, waits for them, and re-layouts  15.2 us
    ppermute x6, starting transfers between devices, trade(): return lax.ppermute(x, axis, [(i, i ^ bit) for i in range(size)])  14.6 us
    ppermute x6, waiting for transfers between devices, trade(): return lax.ppermute(x, axis, [(i, i ^ bit) for i in range(size)])  11.8 us
    ppermute x3, starting transfers between devices, body(): down.append(lax.ppermute(down[-1], 'vocab', behind))  6.26 us
    ppermute x3, starting transfers between devices, body(): up.append(lax.ppermute(up[-1], 'vocab', ahead))  6.06 us
    ppermute x2, starting transfers between devices, body(): shard = lax.ppermute(factor_v.T, ('group', 'vocab'), moves)  4.46 us
    ppermute x3, waiting for transfers between devices, body(): up.append(lax.ppermute(up[-1], 'vocab', ahead))  4.26 us
  transfers between devices with their start and end apart: 17, of which 7 were waited for; matrix products, arithmetic and copies ran while one was open for 0% of the time, Pallas kernels for 23%

profile of v3, /device:TPU:0, one launch (start us, length us, event | category | flops | bytes accessed | tf_op | source)
XLA Modules:
  0.0 102.8 jit_solution(8760208281559755739)
XLA Ops:
  0.6 3.1 %collective-permute-start = (bf16[2,64,2304]{2,1,0:T(8,128)(2,1)}, bf16[2,64,2304]{2,1,0:T(8,128)(2,1)S(1)}, u32[]{:S(2)}, u32[]{:S(2)}) collective-permute-start(bf16[2,64,2304]{2,1,0:T(8,128)(2,1)} %refs_0_.1), channel_id=1, source_target_pairs={{0,2},{2,4},{4,6},{6,7},{7,5},{5,3},{3,1},{1,0},{8,10},{10,12},{12... | collective-permute-start | bytes 1769480 | tf_op jit(solution)/shard_map/ppermute | solution.py:225
  3.7 1.6 %collective-permute-start.8 = (bf16[64,1024]{1,0:T(8,128)(2,1)}, bf16[64,1024]{1,0:T(8,128)(2,1)S(1)}, u32[]{:S(2)}, u32[]{:S(2)}) collective-permute-start(bf16[64,1024]{1,0:T(8,128)(2,1)} %bitcast.6), channel_id=1, source_target_pairs={{0,0},{1,8},{2,16},{3,24},{4,1},{5,9},{6,17},{7,25},{8,2},{9,10},{... | collective-permute-start | bytes 393224 | tf_op jit(solution)/shard_map/ppermute | solution.py:233
  5.3 3.0 %collective-permute-start.10 = (bf16[64,288]{1,0:T(8,128)(2,1)}, bf16[64,288]{1,0:T(8,128)(2,1)S(1)}, u32[]{:S(2)}, u32[]{:S(2)}) collective-permute-start(bf16[64,288]{1,0:T(8,128)(2,1)} %bitcast.7), channel_id=1, source_target_pairs={{1,0},{3,8},{5,16},{7,24},{9,1},{11,9},{13,17},{15,25},{17,2},{19,... | collective-permute-start | bytes 110600 | tf_op jit(solution)/shard_map/ppermute | solution.py:243
  8.3 1.4 %collective-permute-start.9 = (bf16[64,288]{1,0:T(8,128)(2,1)}, bf16[64,288]{1,0:T(8,128)(2,1)S(1)}, u32[]{:S(2)}, u32[]{:S(2)}) collective-permute-start(bf16[64,288]{1,0:T(8,128)(2,1)} %bitcast.8), channel_id=1, source_target_pairs={{0,0},{2,8},{4,16},{6,24},{8,1},{10,9},{12,17},{14,25},{16,2},{18,... | collective-permute-start | bytes 110600 | tf_op jit(solution)/shard_map/ppermute | solution.py:243
  9.7 3.8 %collective-permute-start.4 = (bf16[2,64,2304]{2,1,0:T(8,128)(2,1)}, bf16[2,64,2304]{2,1,0:T(8,128)(2,1)S(1)}, u32[]{:S(2)}, u32[]{:S(2)}) collective-permute-start(bf16[2,64,2304]{2,1,0:T(8,128)(2,1)} %refs_0_.1), channel_id=1, source_target_pairs={{2,0},{4,2},{6,4},{7,6},{5,7},{3,5},{1,3},{0,1},{10,8},{12,10},{14... | collective-permute-start | bytes 1769480 | tf_op jit(solution)/shard_map/ppermute | solution.py:226
  13.5 4.3 %collective-permute-done.refs_0_ = bf16[2,64,2304]{2,1,0:T(8,128)(2,1)S(1)} collective-permute-done((bf16[2,64,2304]{2,1,0:T(8,128)(2,1)}, bf16[2,64,2304]{2,1,0:T(8,128)(2,1)S(1)}, u32[]{:S(2)}, u32[]{:S(2)}) %collective-permute-start) | collective-permute-done | bytes 589856 | tf_op jit(solution)/shard_map/ppermute | solution.py:225
  17.8 2.4 %collective-permute-start.1 = (bf16[2,64,2304]{2,1,0:T(8,128)(2,1)S(1)}, bf16[2,64,2304]{2,1,0:T(8,128)(2,1)S(1)}, u32[]{:S(2)}, u32[]{:S(2)}) collective-permute-start(bf16[2,64,2304]{2,1,0:T(8,128)(2,1)S(1)} %collective-permute-done.refs_0_), channel_id=1, source_target_pairs={{0,2},{2,4},{4,6},{6,7},{7,5},{5,3},{3,1},{1,0},{8,10},{10,12},{12... | collective-permute-start | bytes 1769480 | tf_op jit(solution)/shard_map/ppermute | solution.py:225
  20.1 0.3 collective-permute-done.10
  20.4 0.0 collective-permute-done.9
  20.4 0.0 collective-permute-done.8
  20.5 9.3 %collective-permute-start.12 = (bf16[64,1792]{1,0:T(8,128)(2,1)S(1)}, bf16[64,1792]{1,0:T(8,128)(2,1)S(1)}, u32[]{:S(2)}, u32[]{:S(2)}) collective-permute-start(bf16[64,1792]{1,0:T(8,128)(2,1)S(1)} %fusion.4.refs_0_), channel_id=1, source_target_pairs={{0,16},{8,24},{16,0},{24,8},{1,17},{9,25},{17,1},{25,9},{2,18},{10... | collective-permute-start | bytes 688136 | tf_op jit(solution)/shard_map/ppermute | solution.py:221
  29.8 0.0 collective-permute-start.11
  29.8 4.0 %collective-permute-done.12.refs_2_ = bf16[64,1792]{1,0:T(8,128)(2,1)S(1)} collective-permute-done((bf16[64,1792]{1,0:T(8,128)(2,1)S(1)}, bf16[64,1792]{1,0:T(8,128)(2,1)S(1)}, u32[]{:S(2)}, u32[]{:S(2)}) %collective-permute-start.12) | collective-permute-done | bytes 229408 | tf_op jit(solution)/shard_map/ppermute | solution.py:221
  33.8 0.0 collective-permute-start.13
  33.8 0.0 collective-permute-done.4.refs_1_
  33.8 0.9 collective-permute-start.5
  34.7 0.0 collective-permute-done.11.refs_1_
  34.7 0.6 collective-permute-done.13.refs_3_
  35.3 0.7 copy-done.4
  36.0 0.8 assemble.1
  36.8 0.0 collective-permute-done.1.refs_0_
  36.8 0.6 collective-permute-start.2
  37.4 6.4 %copy-done = bf16[4096,2304]{1,0:T(8,128)(2,1)S(1)} copy-done((bf16[4096,2304]{1,0:T(8,128)(2,1)S(1)}, bf16[4096,2304]{1,0:T(8,128)(2,1)}, u32[]{:S(2)}) %copy-start) | copy-done | bytes 18874392
  43.8 7.5 %chunk.4.refs_7_ = f32[3,256]{1,0:T(4,128)S(1)} custom-call(bf16[2,64,2304]{2,1,0:T(8,128)(2,1)S(1)} %collective-permute-done.refs_0_, bf16[2,64,2304]{2,1,0:T(8,128)(2,1)S(1)} %collective-permute-done.4.refs_1_, bf16[4096,2304]{1,0:T(8,128)(2,1)S(1)} %copy-done, bf16[4096,64]{1,0:T(8,128)(2,1)S(1)} %get-tuple-element.5.refs_3_.refs_4_, ...), custom_call_target="tpu_custom_call" | custom-call | flops 5368709120 | bytes 19922944 | tf_op jit(solution)/shard_map/chunk/pallas_call | solution.py:260
  51.3 0.0 collective-permute-done.5.refs_1_
  51.3 1.6 %collective-permute-start.6 = (bf16[2,64,2304]{2,1,0:T(8,128)(2,1)S(1)}, bf16[2,64,2304]{2,1,0:T(8,128)(2,1)S(1)}, u32[]{:S(2)}, u32[]{:S(2)}) collective-permute-start(bf16[2,64,2304]{2,1,0:T(8,128)(2,1)S(1)} %collective-permute-done.5.refs_1_), channel_id=1, source_target_pairs={{2,0},{4,2},{6,4},{7,6},{5,7},{3,5},{1,3},{0,1},{10,8},{12,10},{14... | collective-permute-start | bytes 1769480 | tf_op jit(solution)/shard_map/ppermute | solution.py:226
  52.9 6.4 %copy-done.1 = bf16[4096,2304]{1,0:T(8,128)(2,1)S(1)} copy-done((bf16[4096,2304]{1,0:T(8,128)(2,1)S(1)}, bf16[4096,2304]{1,0:T(8,128)(2,1)}, u32[]{:S(2)}) %copy-start.1) | copy-done | bytes 18874392
  59.2 7.5 %chunk.5.refs_8_ = f32[3,256]{1,0:T(4,128)S(1)} custom-call(bf16[2,64,2304]{2,1,0:T(8,128)(2,1)S(1)} %collective-permute-done.1.refs_0_, bf16[2,64,2304]{2,1,0:T(8,128)(2,1)S(1)} %collective-permute-done.5.refs_1_, bf16[4096,2304]{1,0:T(8,128)(2,1)S(1)} %copy-done.1, bf16[4096,64]{1,0:T(8,128)(2,1)S(1)} %get-tuple-element.5.refs_3_.refs_4_, ...), custom_call_target="tpu_custom_call" | custom-call | flops 5368709120 | bytes 19922944 | tf_op jit(solution)/shard_map/chunk/pallas_call | solution.py:260
  66.7 0.0 collective-permute-done.2.refs_0_
  66.7 0.5 collective-permute-start.3
  67.3 0.0 collective-permute-done.6.refs_1_
  67.3 1.6 %collective-permute-start.7 = (bf16[64,2304]{1,0:T(8,128)(2,1)S(1)}, bf16[64,2304]{1,0:T(8,128)(2,1)S(1)}, u32[]{:S(2)}, u32[]{:S(2)}) collective-permute-start(bf16[64,2304]{1,0:T(8,128)(2,1)S(1)} %slice_bitcast_fusion), channel_id=1, source_target_pairs={{2,0},{4,2},{6,4},{7,6},{5,7},{3,5},{1,3},{0,1},{10,8},{12,10},{14... | collective-permute-start | bytes 884744 | tf_op jit(solution)/shard_map/ppermute | solution.py:229
  68.9 7.5 %chunk.6.refs_9_ = f32[3,256]{1,0:T(4,128)S(1)} custom-call(bf16[2,64,2304]{2,1,0:T(8,128)(2,1)S(1)} %collective-permute-done.2.refs_0_, bf16[2,64,2304]{2,1,0:T(8,128)(2,1)S(1)} %collective-permute-done.6.refs_1_, bf16[4096,2304]{1,0:T(8,128)(2,1)S(1)} %copy-done.1, bf16[4096,64]{1,0:T(8,128)(2,1)S(1)} %get-tuple-element.5.refs_3_.refs_4_, ...), custom_call_target="tpu_custom_call" | custom-call | flops 5368709120 | bytes 19922944 | tf_op jit(solution)/shard_map/chunk/pallas_call | solution.py:260
  76.4 0.0 collective-permute-done.3.refs_1_
  76.4 0.0 collective-permute-done.7.refs_2_
  76.4 8.0 %chunk.7.mine_ref = f32[3,8,128]{2,1,0:T(8,128)S(1)} custom-call(bf16[2,64,2304]{2,1,0:T(8,128)(2,1)S(1)} %copy-done.2, bf16[64,2304]{1,0:T(8,128)(2,1)S(1)} %collective-permute-done.3.refs_1_, bf16[64,2304]{1,0:T(8,128)(2,1)S(1)} %collective-permute-done.7.refs_2_, bf16[4096,2304]{1,0:T(8,128)(2,1)S(1)} %copy-done.1, ...), custom_call_target="tpu_custom_call" | custom-call | flops 5368709120 | bytes 19922944 | tf_op jit(solution)/shard_map/chunk/pallas_call | solution.py:260
  84.4 2.1 %collective-permute-start.14 = (f32[3,8,128]{2,1,0:T(8,128)S(1)}, f32[3,8,128]{2,1,0:T(8,128)S(1)}, u32[]{:S(2)}, u32[]{:S(2)}) collective-permute-start(f32[3,8,128]{2,1,0:T(8,128)S(1)} %chunk.7.mine_ref), channel_id=1, source_target_pairs={{0,1},{1,0},{2,3},{3,2},{4,5},{5,4},{6,7},{7,6},{8,9},{9,8},{10,11... | collective-permute-start | bytes 36872 | tf_op jit(solution)/shard_map/ppermute | solution.py:221
  86.5 1.7 %collective-permute-done.14.other_ref = f32[3,8,128]{2,1,0:T(8,128)S(1)} collective-permute-done((f32[3,8,128]{2,1,0:T(8,128)S(1)}, f32[3,8,128]{2,1,0:T(8,128)S(1)}, u32[]{:S(2)}, u32[]{:S(2)}) %collective-permute-start.14) | collective-permute-done | bytes 12320 | tf_op jit(solution)/shard_map/ppermute | solution.py:221
  88.2 0.6 copy-done.6
  88.8 1.3 %combine.3.mine_ref = f32[3,8,128]{2,1,0:T(8,128)} custom-call(f32[3,8,128]{2,1,0:T(8,128)} %copy-done.3, f32[3,8,128]{2,1,0:T(8,128)} %copy-done.6), custom_call_target="tpu_custom_call" | custom-call | tf_op jit(solution)/shard_map/combine/pallas_call | solution.py:265
  90.1 1.9 %collective-permute-start.15 = (f32[3,8,128]{2,1,0:T(8,128)}, f32[3,8,128]{2,1,0:T(8,128)S(1)}, u32[]{:S(2)}, u32[]{:S(2)}) collective-permute-start(f32[3,8,128]{2,1,0:T(8,128)} %combine.3.mine_ref), channel_id=1, source_target_pairs={{0,2},{1,3},{2,0},{3,1},{4,6},{5,7},{6,4},{7,5},{8,10},{9,11},{10,... | collective-permute-start | bytes 36872 | tf_op jit(solution)/shard_map/ppermute | solution.py:221
  92.0 2.0 %collective-permute-done.15.other_ref = f32[3,8,128]{2,1,0:T(8,128)S(1)} collective-permute-done((f32[3,8,128]{2,1,0:T(8,128)}, f32[3,8,128]{2,1,0:T(8,128)S(1)}, u32[]{:S(2)}, u32[]{:S(2)}) %collective-permute-start.15) | collective-permute-done | bytes 12320 | tf_op jit(solution)/shard_map/ppermute | solution.py:221
  94.0 0.6 copy-done.7
  94.6 1.3 %combine.4.mine_ref = f32[3,8,128]{2,1,0:T(8,128)} custom-call(f32[3,8,128]{2,1,0:T(8,128)} %combine.3.mine_ref, f32[3,8,128]{2,1,0:T(8,128)} %copy-done.7), custom_call_target="tpu_custom_call" | custom-call | tf_op jit(solution)/shard_map/combine/pallas_call | solution.py:265
  96.0 1.3 %collective-permute-start.16 = (f32[3,8,128]{2,1,0:T(8,128)}, f32[3,8,128]{2,1,0:T(8,128)S(1)}, u32[]{:S(2)}, u32[]{:S(2)}) collective-permute-start(f32[3,8,128]{2,1,0:T(8,128)} %combine.4.mine_ref), channel_id=1, source_target_pairs={{0,4},{1,5},{2,6},{3,7},{4,0},{5,1},{6,2},{7,3},{8,12},{9,13},{10,... | collective-permute-start | bytes 36872 | tf_op jit(solution)/shard_map/ppermute | solution.py:221
  97.3 3.5 %collective-permute-done.16.other_ref = f32[3,8,128]{2,1,0:T(8,128)S(1)} collective-permute-done((f32[3,8,128]{2,1,0:T(8,128)}, f32[3,8,128]{2,1,0:T(8,128)S(1)}, u32[]{:S(2)}, u32[]{:S(2)}) %collective-permute-start.16) | collective-permute-done | bytes 12320 | tf_op jit(solution)/shard_map/ppermute | solution.py:221
  100.8 0.6 copy-done.5
  101.4 1.4 %combine.5 = (f32[2,512]{1,0:T(2,128)}, f32[2,512]{1,0:T(2,128)}) custom-call(f32[3,8,128]{2,1,0:T(8,128)} %combine.4.mine_ref, f32[3,8,128]{2,1,0:T(8,128)} %copy-done.5), custom_call_target="tpu_custom_call" | custom-call | tf_op jit(solution)/shard_map/combine/pallas_call | solution.py:265
  (13 shorter events, 0.1 us)
Async XLA Ops:
  0.6 17.1 %collective-permute-start = (bf16[2,64,2304]{2,1,0:T(8,128)(2,1)}, bf16[2,64,2304]{2,1,0:T(8,128)(2,1)S(1)}, u32[]{:S(2)}, u32[]{:S(2)}) collective-permute-start(bf16[2,64,2304]{2,1,0:T(8,128)(2,1)} %refs_0_.1), channel_id=1, source_target_pairs={{0,2},{2,4},{4,6},{6,7},{7,5},{5,3},{3,1},{1,0},{8,10},{10,12},{12... | collective-permute-start | bytes 1769480 | tf_op jit(solution)/shard_map/ppermute | solution.py:225
  3.7 16.7 %collective-permute-start.8 = (bf16[64,1024]{1,0:T(8,128)(2,1)}, bf16[64,1024]{1,0:T(8,128)(2,1)S(1)}, u32[]{:S(2)}, u32[]{:S(2)}) collective-permute-start(bf16[64,1024]{1,0:T(8,128)(2,1)} %bitcast.6), channel_id=1, source_target_pairs={{0,0},{1,8},{2,16},{3,24},{4,1},{5,9},{6,17},{7,25},{8,2},{9,10},{... | collective-permute-start | bytes 393224 | tf_op jit(solution)/shard_map/ppermute | solution.py:233
  5.3 15.2 %collective-permute-start.10 = (bf16[64,288]{1,0:T(8,128)(2,1)}, bf16[64,288]{1,0:T(8,128)(2,1)S(1)}, u32[]{:S(2)}, u32[]{:S(2)}) collective-permute-start(bf16[64,288]{1,0:T(8,128)(2,1)} %bitcast.7), channel_id=1, source_target_pairs={{1,0},{3,8},{5,16},{7,24},{9,1},{11,9},{13,17},{15,25},{17,2},{19,... | collective-permute-start | bytes 110600 | tf_op jit(solution)/shard_map/ppermute | solution.py:243
  8.3 12.2 %collective-permute-start.9 = (bf16[64,288]{1,0:T(8,128)(2,1)}, bf16[64,288]{1,0:T(8,128)(2,1)S(1)}, u32[]{:S(2)}, u32[]{:S(2)}) collective-permute-start(bf16[64,288]{1,0:T(8,128)(2,1)} %bitcast.8), channel_id=1, source_target_pairs={{0,0},{2,8},{4,16},{6,24},{8,1},{10,9},{12,17},{14,25},{16,2},{18,... | collective-permute-start | bytes 110600 | tf_op jit(solution)/shard_map/ppermute | solution.py:243
  9.7 24.1 %collective-permute-start.4 = (bf16[2,64,2304]{2,1,0:T(8,128)(2,1)}, bf16[2,64,2304]{2,1,0:T(8,128)(2,1)S(1)}, u32[]{:S(2)}, u32[]{:S(2)}) collective-permute-start(bf16[2,64,2304]{2,1,0:T(8,128)(2,1)} %refs_0_.1), channel_id=1, source_target_pairs={{2,0},{4,2},{6,4},{7,6},{5,7},{3,5},{1,3},{0,1},{10,8},{12,10},{14... | collective-permute-start | bytes 1769480 | tf_op jit(solution)/shard_map/ppermute | solution.py:226
  17.8 19.1 %collective-permute-start.1 = (bf16[2,64,2304]{2,1,0:T(8,128)(2,1)S(1)}, bf16[2,64,2304]{2,1,0:T(8,128)(2,1)S(1)}, u32[]{:S(2)}, u32[]{:S(2)}) collective-permute-start(bf16[2,64,2304]{2,1,0:T(8,128)(2,1)S(1)} %collective-permute-done.refs_0_), channel_id=1, source_target_pairs={{0,2},{2,4},{4,6},{6,7},{7,5},{5,3},{3,1},{1,0},{8,10},{10,12},{12... | collective-permute-start | bytes 1769480 | tf_op jit(solution)/shard_map/ppermute | solution.py:225
  20.5 13.3 %collective-permute-start.12 = (bf16[64,1792]{1,0:T(8,128)(2,1)S(1)}, bf16[64,1792]{1,0:T(8,128)(2,1)S(1)}, u32[]{:S(2)}, u32[]{:S(2)}) collective-permute-start(bf16[64,1792]{1,0:T(8,128)(2,1)S(1)} %fusion.4.refs_0_), channel_id=1, source_target_pairs={{0,16},{8,24},{16,0},{24,8},{1,17},{9,25},{17,1},{25,9},{2,18},{10... | collective-permute-start | bytes 688136 | tf_op jit(solution)/shard_map/ppermute | solution.py:221
  29.8 4.9 %collective-permute-start.11 = (bf16[64,1792]{1,0:T(8,128)(2,1)S(1)}, bf16[64,1792]{1,0:T(8,128)(2,1)S(1)}, u32[]{:S(2)}, u32[]{:S(2)}) collective-permute-start(bf16[64,1792]{1,0:T(8,128)(2,1)S(1)} %fusion.4.refs_0_), channel_id=1, source_target_pairs={{0,8},{8,0},{16,24},{24,16},{1,9},{9,1},{17,25},{25,17},{2,10},{10... | collective-permute-start | bytes 688136 | tf_op jit(solution)/shard_map/ppermute | solution.py:221
  33.8 1.5 %collective-permute-start.13 = (bf16[64,1792]{1,0:T(8,128)(2,1)S(1)}, bf16[64,1792]{1,0:T(8,128)(2,1)S(1)}, u32[]{:S(2)}, u32[]{:S(2)}) collective-permute-start(bf16[64,1792]{1,0:T(8,128)(2,1)S(1)} %collective-permute-done.12.refs_2_), channel_id=1, source_target_pairs={{0,8},{8,0},{16,24},{24,16},{1,9},{9,1},{17,25},{25,17},{2,10},{10... | collective-permute-start | bytes 688136 | tf_op jit(solution)/shard_map/ppermute | solution.py:221
  33.8 17.5 %collective-permute-start.5 = (bf16[2,64,2304]{2,1,0:T(8,128)(2,1)S(1)}, bf16[2,64,2304]{2,1,0:T(8,128)(2,1)S(1)}, u32[]{:S(2)}, u32[]{:S(2)}) collective-permute-start(bf16[2,64,2304]{2,1,0:T(8,128)(2,1)S(1)} %collective-permute-done.4.refs_1_), channel_id=1, source_target_pairs={{2,0},{4,2},{6,4},{7,6},{5,7},{3,5},{1,3},{0,1},{10,8},{12,10},{14... | collective-permute-start | bytes 1769480 | tf_op jit(solution)/shard_map/ppermute | solution.py:226
  35.3 0.7 copy-start.4
  36.8 29.9 %collective-permute-start.2 = (bf16[2,64,2304]{2,1,0:T(8,128)(2,1)S(1)}, bf16[2,64,2304]{2,1,0:T(8,128)(2,1)S(1)}, u32[]{:S(2)}, u32[]{:S(2)}) collective-permute-start(bf16[2,64,2304]{2,1,0:T(8,128)(2,1)S(1)} %collective-permute-done.1.refs_0_), channel_id=1, source_target_pairs={{0,2},{2,4},{4,6},{6,7},{7,5},{5,3},{3,1},{1,0},{8,10},{10,12},{12... | collective-permute-start | bytes 1769480 | tf_op jit(solution)/shard_map/ppermute | solution.py:225
  37.4 6.4 %copy-start = (bf16[4096,2304]{1,0:T(8,128)(2,1)S(1)}, bf16[4096,2304]{1,0:T(8,128)(2,1)}, u32[]{:S(2)}) copy-start(bf16[4096,2304]{1,0:T(8,128)(2,1)} %refs_3_.1) | copy-start | bytes 56623108
  43.8 32.6 %copy-start.2 = (bf16[2,64,2304]{2,1,0:T(8,128)(2,1)S(1)}, bf16[2,64,2304]{2,1,0:T(8,128)(2,1)}, u32[]{:S(2)}) copy-start(bf16[2,64,2304]{2,1,0:T(8,128)(2,1)} %refs_0_.1) | copy-start | bytes 1769476
  51.3 16.0 %collective-permute-start.6 = (bf16[2,64,2304]{2,1,0:T(8,128)(2,1)S(1)}, bf16[2,64,2304]{2,1,0:T(8,128)(2,1)S(1)}, u32[]{:S(2)}, u32[]{:S(2)}) collective-permute-start(bf16[2,64,2304]{2,1,0:T(8,128)(2,1)S(1)} %collective-permute-done.5.refs_1_), channel_id=1, source_target_pairs={{2,0},{4,2},{6,4},{7,6},{5,7},{3,5},{1,3},{0,1},{10,8},{12,10},{14... | collective-permute-start | bytes 1769480 | tf_op jit(solution)/shard_map/ppermute | solution.py:226
  52.9 6.4 %copy-start.1 = (bf16[4096,2304]{1,0:T(8,128)(2,1)S(1)}, bf16[4096,2304]{1,0:T(8,128)(2,1)}, u32[]{:S(2)}) copy-start(bf16[4096,2304]{1,0:T(8,128)(2,1)} %refs_3_.1) | copy-start | bytes 56623108
  66.7 9.6 %collective-permute-start.3 = (bf16[64,2304]{1,0:T(8,128)(2,1)S(1)}, bf16[64,2304]{1,0:T(8,128)(2,1)S(1)}, u32[]{:S(2)}, u32[]{:S(2)}) collective-permute-start(bf16[64,2304]{1,0:T(8,128)(2,1)S(1)} %slice_bitcast_fusion.1), channel_id=1, source_target_pairs={{0,2},{2,4},{4,6},{6,7},{7,5},{5,3},{3,1},{1,0},{8,10},{10,12},{12... | collective-permute-start | bytes 884744 | tf_op jit(solution)/shard_map/ppermute | solution.py:228
  67.3 9.1 %collective-permute-start.7 = (bf16[64,2304]{1,0:T(8,128)(2,1)S(1)}, bf16[64,2304]{1,0:T(8,128)(2,1)S(1)}, u32[]{:S(2)}, u32[]{:S(2)}) collective-permute-start(bf16[64,2304]{1,0:T(8,128)(2,1)S(1)} %slice_bitcast_fusion), channel_id=1, source_target_pairs={{2,0},{4,2},{6,4},{7,6},{5,7},{3,5},{1,3},{0,1},{10,8},{12,10},{14... | collective-permute-start | bytes 884744 | tf_op jit(solution)/shard_map/ppermute | solution.py:229
  84.4 3.8 %copy-start.3 = (f32[3,8,128]{2,1,0:T(8,128)}, f32[3,8,128]{2,1,0:T(8,128)S(1)}, u32[]{:S(2)}) copy-start(f32[3,8,128]{2,1,0:T(8,128)S(1)} %chunk.7.mine_ref) | copy-start | bytes 36868
  84.4 3.8 %collective-permute-start.14 = (f32[3,8,128]{2,1,0:T(8,128)S(1)}, f32[3,8,128]{2,1,0:T(8,128)S(1)}, u32[]{:S(2)}, u32[]{:S(2)}) collective-permute-start(f32[3,8,128]{2,1,0:T(8,128)S(1)} %chunk.7.mine_ref), channel_id=1, source_target_pairs={{0,1},{1,0},{2,3},{3,2},{4,5},{5,4},{6,7},{7,6},{8,9},{9,8},{10,11... | collective-permute-start | bytes 36872 | tf_op jit(solution)/shard_map/ppermute | solution.py:221
  88.2 0.6 copy-start.6
  90.1 3.9 %collective-permute-start.15 = (f32[3,8,128]{2,1,0:T(8,128)}, f32[3,8,128]{2,1,0:T(8,128)S(1)}, u32[]{:S(2)}, u32[]{:S(2)}) collective-permute-start(f32[3,8,128]{2,1,0:T(8,128)} %combine.3.mine_ref), channel_id=1, source_target_pairs={{0,2},{1,3},{2,0},{3,1},{4,6},{5,7},{6,4},{7,5},{8,10},{9,11},{10,... | collective-permute-start | bytes 36872 | tf_op jit(solution)/shard_map/ppermute | solution.py:221
  94.0 0.6 copy-start.7
  96.0 4.8 %collective-permute-start.16 = (f32[3,8,128]{2,1,0:T(8,128)}, f32[3,8,128]{2,1,0:T(8,128)S(1)}, u32[]{:S(2)}, u32[]{:S(2)}) collective-permute-start(f32[3,8,128]{2,1,0:T(8,128)} %combine.4.mine_ref), channel_id=1, source_target_pairs={{0,4},{1,5},{2,6},{3,7},{4,0},{5,1},{6,2},{7,3},{8,12},{9,13},{10,... | collective-permute-start | bytes 36872 | tf_op jit(solution)/shard_map/ppermute | solution.py:221
  100.8 0.6 copy-start.5

commit v4 on v3

--- a/solution.py
+++ b/solution.py
@@ -5,7 +5,7 @@
 from jax.experimental.pallas import tpu as pltpu
 from jax.sharding import PartitionSpec as P
 
-VMEM_LIMIT = 30 * 1024 * 1024
+MIB = 1024 * 1024
 LANES = 128
 WHOLE = pl.BlockSpec(memory_space=pltpu.VMEM)
 
@@ -48,7 +48,7 @@
             start = pl.multiple_of(member * u_rows, u_rows)
             u_out[pl.ds(start, u_rows), :] = packs[k][:, :u_rows].T
             for t in range(per):
-                shard = member * per + lax.rem(t + voc // n_group, per)
+                shard = n_group * (lax.rem(voc, per) ^ t) + member
                 at = u_rows + t * wide
                 block = packs[k][:, at : at + wide].astype(jnp.float32).T
                 v_wide[pl.ds(pl.multiple_of(shard * v_rows, 8), v_rows), :] = block[:v_rows]
@@ -69,7 +69,7 @@
         in_specs=[WHOLE] * (1 + n_group),
         out_specs=(WHOLE,) * 3,
         scratch_shapes=[pltpu.VMEM((n_voc * v_rows, rank), jnp.float32)],
-        compiler_params=pltpu.CompilerParams(vmem_limit_bytes=VMEM_LIMIT),
+        compiler_params=pltpu.CompilerParams(vmem_limit_bytes=4 * MIB),
         name="assemble",
     )
 
@@ -85,16 +85,28 @@
     tile = tile_rows(entries)
     tiles = entries // tile
     n = 4 * r
-    last = hop == n_voc // 2
+    first, last = hop == 1, hop == n_voc // 2
     earlier = hop - 1 if last else 0
+    parts = 16 if entries % 4096 == 0 else tiles
+    part = entries // parts
 
     def kernel(*refs):
         piece = refs[:pieces]
         head_ref, u_ref, v_ref, want_ref = refs[pieces : pieces + 4]
         before = refs[pieces + 4 : pieces + 4 + earlier]
-        out_ref, rows, proj, first, second, top, total, pick = refs[
-            pieces + 4 + earlier :
-        ]
+        out_ref, *rest = refs[pieces + 4 + earlier :]
+        held = head_ref
+        if first:
+            held, *rest, sems = rest
+        rows, proj, even, odd, top, total, pick = rest
+
+        def fetch(t):
+            span = pl.ds(pl.multiple_of(t * part, part), part)
+            return pltpu.make_async_copy(head_ref.at[span, :], held.at[span, :], sems.at[t])
+
+        if first:
+            for t in range(parts):
+                fetch(t).start()
 
         at = 0
         for ref in piece:
@@ -105,16 +117,19 @@
             jnp.bfloat16
         )
         top[...] = jnp.full(top.shape, -1e30, jnp.float32)
-        second[...] = jnp.full(second.shape, -1e30, jnp.float32)
+        odd[...] = jnp.full(odd.shape, -1e30, jnp.float32)
         total[...] = jnp.zeros(total.shape, jnp.float32)
         pick[...] = jnp.zeros(pick.shape, jnp.float32)
         left, right = sources_of(hop, n_voc)
         want = jnp.concatenate([want_ref[left], want_ref[right]], axis=1)
 
         def multiply(t, into):
+            if first:
+                for k in range(parts // tiles):
+                    fetch(t * (parts // tiles) + k).wait()
             span = pl.ds(pl.multiple_of(t * tile, tile), tile)
             into[...] = jnp.dot(
-                head_ref[span, :], rows[...], preferred_element_type=jnp.float32
+                held[span, :], rows[...], preferred_element_type=jnp.float32
             ) + jnp.dot(u_ref[span, :], proj[...], preferred_element_type=jnp.float32)
 
         def reduce(start, values):
@@ -131,12 +146,12 @@
 
         @pl.loop(0, tiles // 2)
         def _(i):
-            multiply(2 * i, first)
-            reduce(jnp.where(i == 0, 1 << 29, (2 * i - 1) * tile), second)
-            multiply(2 * i + 1, second)
-            reduce(2 * i * tile, first)
-
-        reduce(entries - tile, second)
+            multiply(2 * i, even)
+            reduce(jnp.where(i == 0, 1 << 29, (2 * i - 1) * tile), odd)
+            multiply(2 * i + 1, odd)
+            reduce(2 * i * tile, even)
+
+        reduce(entries - tile, odd)
         best = jnp.max(top[...], axis=0, keepdims=True)
         sums = jnp.sum(total[...] * jnp.exp(top[...] - best), axis=0, keepdims=True)
         picked = jnp.sum(pick[...], axis=0, keepdims=True)
@@ -152,21 +167,30 @@
                 out_ref[q, pl.ds(a, 1), :] = before[k - 1][q : q + 1, : 2 * r]
                 out_ref[q, pl.ds(b, 1), :] = before[k - 1][q : q + 1, 2 * r :]
 
+    out_shape = jax.ShapeDtypeStruct((3, n_voc, 2 * r) if last else (3, n), jnp.float32)
+    out_specs = WHOLE
+    scratch = [
+        pltpu.VMEM((depth, n), jnp.bfloat16),
+        pltpu.VMEM((rank, n), jnp.bfloat16),
+        pltpu.VMEM((tile, n), jnp.float32),
+        pltpu.VMEM((tile, n), jnp.float32),
+        pltpu.VMEM((8, n), jnp.float32),
+        pltpu.VMEM((8, n), jnp.float32),
+        pltpu.VMEM((8, n), jnp.float32),
+    ]
+    if first:
+        out_shape = (out_shape, jax.ShapeDtypeStruct((entries, depth), jnp.bfloat16))
+        out_specs = (WHOLE, WHOLE)
+        scratch.append(pltpu.SemaphoreType.DMA((parts,)))
     return pl.pallas_call(
         kernel,
-        out_shape=jax.ShapeDtypeStruct((3, n_voc, 2 * r) if last else (3, n), jnp.float32),
-        in_specs=[WHOLE] * (pieces + 4 + earlier),
-        out_specs=WHOLE,
-        scratch_shapes=[
-            pltpu.VMEM((depth, n), jnp.bfloat16),
-            pltpu.VMEM((rank, n), jnp.bfloat16),
-            pltpu.VMEM((tile, n), jnp.float32),
-            pltpu.VMEM((tile, n), jnp.float32),
-            pltpu.VMEM((8, n), jnp.float32),
-            pltpu.VMEM((8, n), jnp.float32),
-            pltpu.VMEM((8, n), jnp.float32),
-        ],
-        compiler_params=pltpu.CompilerParams(vmem_limit_bytes=VMEM_LIMIT),
+        out_shape=out_shape,
+        in_specs=[WHOLE] * pieces
+        + [pl.BlockSpec(memory_space=pltpu.HBM) if first else WHOLE]
+        + [WHOLE] * (3 + earlier),
+        out_specs=out_specs,
+        scratch_shapes=scratch,
+        compiler_params=pltpu.CompilerParams(vmem_limit_bytes=8 * MIB),
         cost_estimate=pl.CostEstimate(
             flops=2 * n * entries * (depth + 256),
             bytes_accessed=2 * entries * (depth + LANES),
@@ -200,7 +224,12 @@
     else:
         shape, specs = jax.ShapeDtypeStruct((3, n_voc, 2 * r), jnp.float32), WHOLE
     return pl.pallas_call(
-        kernel, out_shape=shape, in_specs=[WHOLE, WHOLE], out_specs=specs, name="combine"
+        kernel,
+        out_shape=shape,
+        in_specs=[WHOLE, WHOLE],
+        out_specs=specs,
+        compiler_params=pltpu.CompilerParams(vmem_limit_bytes=MIB),
+        name="combine",
     )
 
 
@@ -229,27 +258,24 @@
         lax.ppermute(down[-1][1], "vocab", behind),
     ]
 
+    u_rows, v_rows = factor_u.shape[0], factor_v.shape[0]
     moves = [(v * n_group + g, g * n_voc + v) for v in range(n_voc) for g in range(n_group)]
-    pack = [lax.ppermute(factor_u.T, ("group", "vocab"), moves)]
-    for t in range(per):
-        moves = [
-            (
-                (v % n_group) * n_voc + g * per + (t + v // n_group) % per,
-                g * n_voc + v,
-            )
-            for v in range(n_voc)
-            for g in range(n_group)
-        ]
-        shard = lax.ppermute(factor_v.T, ("group", "vocab"), moves)
-        pack.append(jnp.pad(shard, ((0, 0), (0, padded(shard.shape[1]) - shard.shape[1]))))
-    packs = {0: jnp.concatenate(pack, axis=1)}
+    shard = jnp.pad(factor_v.T, ((0, 0), (0, padded(v_rows) - v_rows)))
+    pack = jnp.concatenate([factor_u.T, shard], axis=1)
+    pack = lax.ppermute(pack, ("group", "vocab"), moves)
+    bit = 1
+    while bit < per:
+        other = trade(pack[:, u_rows:], "vocab", n_voc, bit)
+        pack = jnp.concatenate([pack, other], axis=1)
+        bit *= 2
+    packs = {0: pack}
     bit = n_group // 2
     while bit:
         for k in list(packs):
             packs[k ^ bit] = trade(packs[k], "group", n_group, bit)
         bit //= 2
     full_u, full_v, want = make_assemble(
-        n_group, n_voc, factor_u.shape[0], factor_v.shape[0], rank, r, entries
+        n_group, n_voc, u_rows, v_rows, rank, r, entries
     )(sampled, *[packs[k] for k in range(n_group)])
 
     stats = []
@@ -257,7 +283,10 @@
         pieces = [up[hop], down[hop]] if hop < half else [hidden] + ends
         chunk = make_chunk(hop, len(pieces), r, depth, entries, rank, n_voc)
         before = stats if hop == half else []
-        stats.append(chunk(*pieces, head, full_u, full_v, want, *before))
+        out = chunk(*pieces, head, full_u, full_v, want, *before)
+        if hop == 1:
+            out, head = out
+        stats.append(out)
     part = stats[-1]
     bit = 1
     while bit < n_voc:

time: 103 us -> 108 us (1.049)
  local copies, waits for them, and re-layouts: 15.3 us -> 7.13 us
  Pallas kernels: 35.3 us -> 41.8 us
  waiting for transfers between devices: 16.4 us -> 19.9 us
  starting transfers between devices: 35.1 us -> 37.3 us
    pallas_call x5, Pallas kernels: 31.2 us -> 41 us  [the longest x4 40.2 us: body(): out = chunk(*pieces, head, full_u, full_v, want, *before)]
    ppermute x6 -> x7, starting transfers between devices: 14.6 us -> 23.8 us  [trade(): return lax.ppermute(x, axis, [(i, i ^ bit) for i in range(size)])]
    unnamed x16 -> x7, local copies, waits for them, and re-layouts: 15.2 us -> 7.07 us
    ppermute x3 -> x1, starting transfers between devices: 6.01 us -> 0.67 us  [body(): pack = lax.ppermute(pack, ('group', 'vocab'), moves)]
    ppermute x3, waiting for transfers between devices: 0.01 us -> 5.2 us  [body(): down.append(lax.ppermute(down[-1], 'vocab', behind))]
    ppermute x3, waiting for transfers between devices: 4.26 us -> 0.01 us  [body(): up.append(lax.ppermute(up[-1], 'vocab', ahead))]
    pallas_call x3, Pallas kernels: 4.1 us -> 0.73 us  [body(): part = make_combine(bit, r, n_voc, 2 * bit == n_voc)(part, other)]
    ppermute x6 -> x7, waiting for transfers between devices: 11.8 us -> 14.7 us  [trade(): return lax.ppermute(x, axis, [(i, i ^ bit) for i in range(size)])]
  transfers between devices with their start and end apart: 17 -> 16, of which waited for: 7 -> 6; matrix products, arithmetic and copies ran while one was open for 0% -> 1% of each run, Pallas kernels for 23% -> 31%
where the time goes in v4:
time: 108 us
  Pallas kernels  41.8 us (39%)
  starting transfers between devices  37.3 us (35%)
  waiting for transfers between devices  19.9 us (18%)
  local copies, waits for them, and re-layouts  7.13 us (7%)
    pallas_call x4, Pallas kernels, body(): out = chunk(*pieces, head, full_u, full_v, want, *before)  40.2 us
    ppermute x7, starting transfers between devices, trade(): return lax.ppermute(x, axis, [(i, i ^ bit) for i in range(size)])  23.8 us
    ppermute x7, waiting for transfers between devices, trade(): return lax.ppermute(x, axis, [(i, i ^ bit) for i in range(size)])  14.7 us
    unnamed x7, local copies, waits for them, and re-layouts  7.07 us
    ppermute x3, starting transfers between devices, body(): down.append(lax.ppermute(down[-1], 'vocab', behind))  6.54 us
    ppermute x3, waiting for transfers between devices, body(): down.append(lax.ppermute(down[-1], 'vocab', behind))  5.2 us
    ppermute x3, starting transfers between devices, body(): up.append(lax.ppermute(up[-1], 'vocab', ahead))  4.28 us
  transfers between devices with their start and end apart: 16, of which 6 were waited for; matrix products, arithmetic and copies ran while one was open for 1% of the time, Pallas kernels for 31%

profile of v4, /device:TPU:0, one launch (start us, length us, event | category | flops | bytes accessed | tf_op | source)
XLA Modules:
  0.0 107.8 jit_solution(2217188050484576182)
XLA Ops:
  0.6 3.1 %collective-permute-start = (bf16[2,64,2304]{2,1,0:T(8,128)(2,1)}, bf16[2,64,2304]{2,1,0:T(8,128)(2,1)S(1)}, u32[]{:S(2)}, u32[]{:S(2)}) collective-permute-start(bf16[2,64,2304]{2,1,0:T(8,128)(2,1)} %refs_0_.1), channel_id=1, source_target_pairs={{0,2},{2,4},{4,6},{6,7},{7,5},{5,3},{3,1},{1,0},{8,10},{10,12},{12... | collective-permute-start | bytes 1769480 | tf_op jit(solution)/shard_map/ppermute | solution.py:254
  3.7 0.9 fusion.1
  4.7 0.7 collective-permute-start.8
  5.3 2.5 %collective-permute-start.4 = (bf16[2,64,2304]{2,1,0:T(8,128)(2,1)}, bf16[2,64,2304]{2,1,0:T(8,128)(2,1)S(1)}, u32[]{:S(2)}, u32[]{:S(2)}) collective-permute-start(bf16[2,64,2304]{2,1,0:T(8,128)(2,1)} %refs_0_.1), channel_id=1, source_target_pairs={{2,0},{4,2},{6,4},{7,6},{5,7},{3,5},{1,3},{0,1},{10,8},{12,10},{14... | collective-permute-start | bytes 1769480 | tf_op jit(solution)/shard_map/ppermute | solution.py:255
  7.8 0.0 collective-permute-done.8
  7.8 12.7 %collective-permute-start.9 = (bf16[64,384]{1,0:T(8,128)(2,1)S(1)}, bf16[64,384]{1,0:T(8,128)(2,1)S(1)}, u32[]{:S(2)}, u32[]{:S(2)}) collective-permute-start(bf16[64,384]{1,0:T(8,128)(2,1)S(1)} %slice.14), channel_id=1, source_target_pairs={{0,1},{1,0},{2,3},{3,2},{4,5},{5,4},{6,7},{7,6},{8,9},{9,8},{10,11... | collective-permute-start | bytes 147464 | tf_op jit(solution)/shard_map/ppermute | solution.py:250
  20.6 0.0 collective-permute-done.refs_0_
  20.6 0.4 collective-permute-start.1
  21.0 5.1 %collective-permute-done.9 = bf16[64,384]{1,0:T(8,128)(2,1)S(1)} collective-permute-done((bf16[64,384]{1,0:T(8,128)(2,1)S(1)}, bf16[64,384]{1,0:T(8,128)(2,1)S(1)}, u32[]{:S(2)}, u32[]{:S(2)}) %collective-permute-start.9) | collective-permute-done | bytes 49184 | tf_op jit(solution)/shard_map/ppermute | solution.py:250
  26.1 1.9 %collective-permute-start.11 = (bf16[64,1792]{1,0:T(8,128)(2,1)S(1)}, bf16[64,1792]{1,0:T(8,128)(2,1)S(1)}, u32[]{:S(2)}, u32[]{:S(2)}) collective-permute-start(bf16[64,1792]{1,0:T(8,128)(2,1)S(1)} %constant_dynamic-update-slice_fusion.refs_0_), channel_id=1, source_target_pairs={{0,16},{8,24},{16,0},{24,8},{1,17},{9,25},{17,1},{25,9},{2,18},{10... | collective-permute-start | bytes 688136 | tf_op jit(solution)/shard_map/ppermute | solution.py:250
  28.0 1.8 %collective-permute-start.10 = (bf16[64,1792]{1,0:T(8,128)(2,1)S(1)}, bf16[64,1792]{1,0:T(8,128)(2,1)S(1)}, u32[]{:S(2)}, u32[]{:S(2)}) collective-permute-start(bf16[64,1792]{1,0:T(8,128)(2,1)S(1)} %constant_dynamic-update-slice_fusion.refs_0_), channel_id=1, source_target_pairs={{0,8},{8,0},{16,24},{24,16},{1,9},{9,1},{17,25},{25,17},{2,10},{10... | collective-permute-start | bytes 688136 | tf_op jit(solution)/shard_map/ppermute | solution.py:250
  29.8 3.2 %collective-permute-done.11.refs_2_ = bf16[64,1792]{1,0:T(8,128)(2,1)S(1)} collective-permute-done((bf16[64,1792]{1,0:T(8,128)(2,1)S(1)}, bf16[64,1792]{1,0:T(8,128)(2,1)S(1)}, u32[]{:S(2)}, u32[]{:S(2)}) %collective-permute-start.11) | collective-permute-done | bytes 229408 | tf_op jit(solution)/shard_map/ppermute | solution.py:250
  33.0 1.6 %collective-permute-start.12 = (bf16[64,1792]{1,0:T(8,128)(2,1)S(1)}, bf16[64,1792]{1,0:T(8,128)(2,1)S(1)}, u32[]{:S(2)}, u32[]{:S(2)}) collective-permute-start(bf16[64,1792]{1,0:T(8,128)(2,1)S(1)} %collective-permute-done.11.refs_2_), channel_id=1, source_target_pairs={{0,8},{8,0},{16,24},{24,16},{1,9},{9,1},{17,25},{25,17},{2,10},{10... | collective-permute-start | bytes 688136 | tf_op jit(solution)/shard_map/ppermute | solution.py:250
  34.6 0.0 collective-permute-done.4.refs_1_
  34.6 2.7 %collective-permute-start.5 = (bf16[2,64,2304]{2,1,0:T(8,128)(2,1)S(1)}, bf16[2,64,2304]{2,1,0:T(8,128)(2,1)S(1)}, u32[]{:S(2)}, u32[]{:S(2)}) collective-permute-start(bf16[2,64,2304]{2,1,0:T(8,128)(2,1)S(1)} %collective-permute-done.4.refs_1_), channel_id=1, source_target_pairs={{2,0},{4,2},{6,4},{7,6},{5,7},{3,5},{1,3},{0,1},{10,8},{12,10},{14... | collective-permute-start | bytes 1769480 | tf_op jit(solution)/shard_map/ppermute | solution.py:255
  37.3 0.0 collective-permute-done.10.refs_1_
  37.3 0.0 collective-permute-done.12.refs_3_
  37.3 0.0 copy-start.2
  37.3 0.7 copy-done.2
  38.0 0.8 assemble.1
  38.8 0.0 collective-permute-done.1.refs_0_
  38.8 0.8 collective-permute-start.2
  39.6 0.0 copy-start
  39.6 6.4 %copy-done = bf16[4096,2304]{1,0:T(8,128)(2,1)S(1)} copy-done((bf16[4096,2304]{1,0:T(8,128)(2,1)S(1)}, bf16[4096,2304]{1,0:T(8,128)(2,1)}, u32[]{:S(2)}) %copy-start) | copy-done | bytes 18874392
  46.0 17.2 %chunk.4 = (f32[3,256]{1,0:T(4,128)S(1)}, bf16[4096,2304]{1,0:T(8,128)(2,1)S(1)}) custom-call(bf16[2,64,2304]{2,1,0:T(8,128)(2,1)S(1)} %collective-permute-done.refs_0_, bf16[2,64,2304]{2,1,0:T(8,128)(2,1)S(1)} %collective-permute-done.4.refs_1_, bf16[4096,2304]{1,0:T(8,128)(2,1)S(1)} %copy-done, bf16[4096,64]{1,0:T(8,128)(2,1)S(1)} %get-tuple-element.7.refs_3_.refs_4_, ...), custom_call_target="tpu_custom_call" | custom-call | flops 5368709120 | bytes 19922944 | tf_op jit(solution)/shard_map/chunk/pallas_call | solution.py:286
  63.2 0.0 collective-permute-done.5.refs_1_
  63.2 1.3 %collective-permute-start.6 = (bf16[2,64,2304]{2,1,0:T(8,128)(2,1)S(1)}, bf16[2,64,2304]{2,1,0:T(8,128)(2,1)S(1)}, u32[]{:S(2)}, u32[]{:S(2)}) collective-permute-start(bf16[2,64,2304]{2,1,0:T(8,128)(2,1)S(1)} %collective-permute-done.5.refs_1_), channel_id=1, source_target_pairs={{2,0},{4,2},{6,4},{7,6},{5,7},{3,5},{1,3},{0,1},{10,8},{12,10},{14... | collective-permute-start | bytes 1769480 | tf_op jit(solution)/shard_map/ppermute | solution.py:255
  64.6 0.0 copy-start.1
  64.6 7.5 %chunk.5.refs_8_ = f32[3,256]{1,0:T(4,128)S(1)} custom-call(bf16[2,64,2304]{2,1,0:T(8,128)(2,1)S(1)} %collective-permute-done.1.refs_0_, bf16[2,64,2304]{2,1,0:T(8,128)(2,1)S(1)} %collective-permute-done.5.refs_1_, bf16[4096,2304]{1,0:T(8,128)(2,1)S(1)} %get-tuple-element.10.refs_2_.refs_3_, bf16[4096,64]{1,0:T(8,128)(2,1)S(1)} %get-tuple-element.7.refs_3_.refs_4_, ...), custom_call_target="tpu_custom_call" | custom-call | flops 5368709120 | bytes 19922944 | tf_op jit(solution)/shard_map/chunk/pallas_call | solution.py:286
  72.1 0.0 collective-permute-done.2.refs_0_
  72.1 1.3 %collective-permute-start.3 = (bf16[64,2304]{1,0:T(8,128)(2,1)S(1)}, bf16[64,2304]{1,0:T(8,128)(2,1)S(1)}, u32[]{:S(2)}, u32[]{:S(2)}) collective-permute-start(bf16[64,2304]{1,0:T(8,128)(2,1)S(1)} %slice_bitcast_fusion.1), channel_id=1, source_target_pairs={{0,2},{2,4},{4,6},{6,7},{7,5},{5,3},{3,1},{1,0},{8,10},{10,12},{12... | collective-permute-start | bytes 884744 | tf_op jit(solution)/shard_map/ppermute | solution.py:257
  73.4 5.2 %collective-permute-done.6.refs_1_ = bf16[2,64,2304]{2,1,0:T(8,128)(2,1)S(1)} collective-permute-done((bf16[2,64,2304]{2,1,0:T(8,128)(2,1)S(1)}, bf16[2,64,2304]{2,1,0:T(8,128)(2,1)S(1)}, u32[]{:S(2)}, u32[]{:S(2)}) %collective-permute-start.6) | collective-permute-done | bytes 589856 | tf_op jit(solution)/shard_map/ppermute | solution.py:255
  78.6 0.8 collective-permute-start.7
  79.4 7.5 %chunk.6.refs_9_ = f32[3,256]{1,0:T(4,128)S(1)} custom-call(bf16[2,64,2304]{2,1,0:T(8,128)(2,1)S(1)} %collective-permute-done.2.refs_0_, bf16[2,64,2304]{2,1,0:T(8,128)(2,1)S(1)} %collective-permute-done.6.refs_1_, bf16[4096,2304]{1,0:T(8,128)(2,1)S(1)} %get-tuple-element.10.refs_2_.refs_3_, bf16[4096,64]{1,0:T(8,128)(2,1)S(1)} %get-tuple-element.7.refs_3_.refs_4_, ...), custom_call_target="tpu_custom_call" | custom-call | flops 5368709120 | bytes 19922944 | tf_op jit(solution)/shard_map/chunk/pallas_call | solution.py:286
  86.8 0.0 collective-permute-done.3.refs_1_
  86.8 0.0 collective-permute-done.7.refs_2_
  86.9 0.0 copy-done.1
  86.9 8.0 %chunk.7.mine_ref = f32[3,8,128]{2,1,0:T(8,128)S(1)} custom-call(bf16[2,64,2304]{2,1,0:T(8,128)(2,1)S(1)} %copy-done.1, bf16[64,2304]{1,0:T(8,128)(2,1)S(1)} %collective-permute-done.3.refs_1_, bf16[64,2304]{1,0:T(8,128)(2,1)S(1)} %collective-permute-done.7.refs_2_, bf16[4096,2304]{1,0:T(8,128)(2,1)S(1)} %get-tuple-element.10.refs_2_.refs_3_, ...), custom_call_target="tpu_custom_call" | custom-call | flops 5368709120 | bytes 19922944 | tf_op jit(solution)/shard_map/chunk/pallas_call | solution.py:286
  94.9 1.8 %collective-permute-start.13 = (f32[3,8,128]{2,1,0:T(8,128)S(1)}, f32[3,8,128]{2,1,0:T(8,128)S(1)}, u32[]{:S(2)}, u32[]{:S(2)}) collective-permute-start(f32[3,8,128]{2,1,0:T(8,128)S(1)} %chunk.7.mine_ref), channel_id=1, source_target_pairs={{0,1},{1,0},{2,3},{3,2},{4,5},{5,4},{6,7},{7,6},{8,9},{9,8},{10,11... | collective-permute-start | bytes 36872 | tf_op jit(solution)/shard_map/ppermute | solution.py:250
  96.7 2.0 %collective-permute-done.13.other_ref = f32[3,8,128]{2,1,0:T(8,128)S(1)} collective-permute-done((f32[3,8,128]{2,1,0:T(8,128)S(1)}, f32[3,8,128]{2,1,0:T(8,128)S(1)}, u32[]{:S(2)}, u32[]{:S(2)}) %collective-permute-start.13) | collective-permute-done | bytes 12320 | tf_op jit(solution)/shard_map/ppermute | solution.py:250
  98.7 1.5 %collective-permute-start.14 = (f32[3,8,128]{2,1,0:T(8,128)S(1)}, f32[3,8,128]{2,1,0:T(8,128)S(1)}, u32[]{:S(2)}, u32[]{:S(2)}) collective-permute-start(f32[3,8,128]{2,1,0:T(8,128)S(1)} %combine.3.mine_ref), channel_id=1, source_target_pairs={{0,2},{1,3},{2,0},{3,1},{4,6},{5,7},{6,4},{7,5},{8,10},{9,11},{10,... | collective-permute-start | bytes 36872 | tf_op jit(solution)/shard_map/ppermute | solution.py:250
  100.2 2.2 %collective-permute-done.14.other_ref = f32[3,8,128]{2,1,0:T(8,128)S(1)} collective-permute-done((f32[3,8,128]{2,1,0:T(8,128)S(1)}, f32[3,8,128]{2,1,0:T(8,128)S(1)}, u32[]{:S(2)}, u32[]{:S(2)}) %collective-permute-start.14) | collective-permute-done | bytes 12320 | tf_op jit(solution)/shard_map/ppermute | solution.py:250
  102.4 2.6 %collective-permute-start.15 = (f32[3,8,128]{2,1,0:T(8,128)S(1)}, f32[3,8,128]{2,1,0:T(8,128)S(1)}, u32[]{:S(2)}, u32[]{:S(2)}) collective-permute-start(f32[3,8,128]{2,1,0:T(8,128)S(1)} %combine.4.mine_ref), channel_id=1, source_target_pairs={{0,4},{1,5},{2,6},{3,7},{4,0},{5,1},{6,2},{7,3},{8,12},{9,13},{10,... | collective-permute-start | bytes 36872 | tf_op jit(solution)/shard_map/ppermute | solution.py:250
  105.0 2.1 %collective-permute-done.15.other_ref = f32[3,8,128]{2,1,0:T(8,128)S(1)} collective-permute-done((f32[3,8,128]{2,1,0:T(8,128)S(1)}, f32[3,8,128]{2,1,0:T(8,128)S(1)}, u32[]{:S(2)}, u32[]{:S(2)}) %collective-permute-start.15) | collective-permute-done | bytes 12320 | tf_op jit(solution)/shard_map/ppermute | solution.py:250
  107.1 0.7 combine.5
  (7 shorter events, 0.1 us)
Async XLA Ops:
  0.6 19.9 %collective-permute-start = (bf16[2,64,2304]{2,1,0:T(8,128)(2,1)}, bf16[2,64,2304]{2,1,0:T(8,128)(2,1)S(1)}, u32[]{:S(2)}, u32[]{:S(2)}) collective-permute-start(bf16[2,64,2304]{2,1,0:T(8,128)(2,1)} %refs_0_.1), channel_id=1, source_target_pairs={{0,2},{2,4},{4,6},{6,7},{7,5},{5,3},{3,1},{1,0},{8,10},{10,12},{12... | collective-permute-start | bytes 1769480 | tf_op jit(solution)/shard_map/ppermute | solution.py:254
  4.7 3.2 %collective-permute-start.8 = (bf16[64,1408]{1,0:T(8,128)(2,1)S(1)}, bf16[64,1408]{1,0:T(8,128)(2,1)S(1)}, u32[]{:S(2)}, u32[]{:S(2)}) collective-permute-start(bf16[64,1408]{1,0:T(8,128)(2,1)S(1)} %fusion.1), channel_id=1, source_target_pairs={{0,0},{1,8},{2,16},{3,24},{4,1},{5,9},{6,17},{7,25},{8,2},{9,10},{... | collective-permute-start | bytes 540680 | tf_op jit(solution)/shard_map/ppermute | solution.py:265
  5.3 29.2 %collective-permute-start.4 = (bf16[2,64,2304]{2,1,0:T(8,128)(2,1)}, bf16[2,64,2304]{2,1,0:T(8,128)(2,1)S(1)}, u32[]{:S(2)}, u32[]{:S(2)}) collective-permute-start(bf16[2,64,2304]{2,1,0:T(8,128)(2,1)} %refs_0_.1), channel_id=1, source_target_pairs={{2,0},{4,2},{6,4},{7,6},{5,7},{3,5},{1,3},{0,1},{10,8},{12,10},{14... | collective-permute-start | bytes 1769480 | tf_op jit(solution)/shard_map/ppermute | solution.py:255
  7.8 18.3 %collective-permute-start.9 = (bf16[64,384]{1,0:T(8,128)(2,1)S(1)}, bf16[64,384]{1,0:T(8,128)(2,1)S(1)}, u32[]{:S(2)}, u32[]{:S(2)}) collective-permute-start(bf16[64,384]{1,0:T(8,128)(2,1)S(1)} %slice.14), channel_id=1, source_target_pairs={{0,1},{1,0},{2,3},{3,2},{4,5},{5,4},{6,7},{7,6},{8,9},{9,8},{10,11... | collective-permute-start | bytes 147464 | tf_op jit(solution)/shard_map/ppermute | solution.py:250
  20.6 18.3 %collective-permute-start.1 = (bf16[2,64,2304]{2,1,0:T(8,128)(2,1)S(1)}, bf16[2,64,2304]{2,1,0:T(8,128)(2,1)S(1)}, u32[]{:S(2)}, u32[]{:S(2)}) collective-permute-start(bf16[2,64,2304]{2,1,0:T(8,128)(2,1)S(1)} %collective-permute-done.refs_0_), channel_id=1, source_target_pairs={{0,2},{2,4},{4,6},{6,7},{7,5},{5,3},{3,1},{1,0},{8,10},{10,12},{12... | collective-permute-start | bytes 1769480 | tf_op jit(solution)/shard_map/ppermute | solution.py:254
  26.1 6.9 %collective-permute-start.11 = (bf16[64,1792]{1,0:T(8,128)(2,1)S(1)}, bf16[64,1792]{1,0:T(8,128)(2,1)S(1)}, u32[]{:S(2)}, u32[]{:S(2)}) collective-permute-start(bf16[64,1792]{1,0:T(8,128)(2,1)S(1)} %constant_dynamic-update-slice_fusion.refs_0_), channel_id=1, source_target_pairs={{0,16},{8,24},{16,0},{24,8},{1,17},{9,25},{17,1},{25,9},{2,18},{10... | collective-permute-start | bytes 688136 | tf_op jit(solution)/shard_map/ppermute | solution.py:250
  28.0 9.3 %collective-permute-start.10 = (bf16[64,1792]{1,0:T(8,128)(2,1)S(1)}, bf16[64,1792]{1,0:T(8,128)(2,1)S(1)}, u32[]{:S(2)}, u32[]{:S(2)}) collective-permute-start(bf16[64,1792]{1,0:T(8,128)(2,1)S(1)} %constant_dynamic-update-slice_fusion.refs_0_), channel_id=1, source_target_pairs={{0,8},{8,0},{16,24},{24,16},{1,9},{9,1},{17,25},{25,17},{2,10},{10... | collective-permute-start | bytes 688136 | tf_op jit(solution)/shard_map/ppermute | solution.py:250
  33.0 4.3 %collective-permute-start.12 = (bf16[64,1792]{1,0:T(8,128)(2,1)S(1)}, bf16[64,1792]{1,0:T(8,128)(2,1)S(1)}, u32[]{:S(2)}, u32[]{:S(2)}) collective-permute-start(bf16[64,1792]{1,0:T(8,128)(2,1)S(1)} %collective-permute-done.11.refs_2_), channel_id=1, source_target_pairs={{0,8},{8,0},{16,24},{24,16},{1,9},{9,1},{17,25},{25,17},{2,10},{10... | collective-permute-start | bytes 688136 | tf_op jit(solution)/shard_map/ppermute | solution.py:250
  34.6 28.7 %collective-permute-start.5 = (bf16[2,64,2304]{2,1,0:T(8,128)(2,1)S(1)}, bf16[2,64,2304]{2,1,0:T(8,128)(2,1)S(1)}, u32[]{:S(2)}, u32[]{:S(2)}) collective-permute-start(bf16[2,64,2304]{2,1,0:T(8,128)(2,1)S(1)} %collective-permute-done.4.refs_1_), channel_id=1, source_target_pairs={{2,0},{4,2},{6,4},{7,6},{5,7},{3,5},{1,3},{0,1},{10,8},{12,10},{14... | collective-permute-start | bytes 1769480 | tf_op jit(solution)/shard_map/ppermute | solution.py:255
  37.3 0.7 copy-start.2
  38.8 33.2 %collective-permute-start.2 = (bf16[2,64,2304]{2,1,0:T(8,128)(2,1)S(1)}, bf16[2,64,2304]{2,1,0:T(8,128)(2,1)S(1)}, u32[]{:S(2)}, u32[]{:S(2)}) collective-permute-start(bf16[2,64,2304]{2,1,0:T(8,128)(2,1)S(1)} %collective-permute-done.1.refs_0_), channel_id=1, source_target_pairs={{0,2},{2,4},{4,6},{6,7},{7,5},{5,3},{3,1},{1,0},{8,10},{10,12},{12... | collective-permute-start | bytes 1769480 | tf_op jit(solution)/shard_map/ppermute | solution.py:254
  39.6 6.4 %copy-start = (bf16[4096,2304]{1,0:T(8,128)(2,1)S(1)}, bf16[4096,2304]{1,0:T(8,128)(2,1)}, u32[]{:S(2)}) copy-start(bf16[4096,2304]{1,0:T(8,128)(2,1)} %refs_2_.1) | copy-start | bytes 56623108
  63.2 15.3 %collective-permute-start.6 = (bf16[2,64,2304]{2,1,0:T(8,128)(2,1)S(1)}, bf16[2,64,2304]{2,1,0:T(8,128)(2,1)S(1)}, u32[]{:S(2)}, u32[]{:S(2)}) collective-permute-start(bf16[2,64,2304]{2,1,0:T(8,128)(2,1)S(1)} %collective-permute-done.5.refs_1_), channel_id=1, source_target_pairs={{2,0},{4,2},{6,4},{7,6},{5,7},{3,5},{1,3},{0,1},{10,8},{12,10},{14... | collective-permute-start | bytes 1769480 | tf_op jit(solution)/shard_map/ppermute | solution.py:255
  64.6 22.3 %copy-start.1 = (bf16[2,64,2304]{2,1,0:T(8,128)(2,1)S(1)}, bf16[2,64,2304]{2,1,0:T(8,128)(2,1)}, u32[]{:S(2)}) copy-start(bf16[2,64,2304]{2,1,0:T(8,128)(2,1)} %refs_0_.1) | copy-start | bytes 1769476
  72.1 14.7 %collective-permute-start.3 = (bf16[64,2304]{1,0:T(8,128)(2,1)S(1)}, bf16[64,2304]{1,0:T(8,128)(2,1)S(1)}, u32[]{:S(2)}, u32[]{:S(2)}) collective-permute-start(bf16[64,2304]{1,0:T(8,128)(2,1)S(1)} %slice_bitcast_fusion.1), channel_id=1, source_target_pairs={{0,2},{2,4},{4,6},{6,7},{7,5},{5,3},{3,1},{1,0},{8,10},{10,12},{12... | collective-permute-start | bytes 884744 | tf_op jit(solution)/shard_map/ppermute | solution.py:257
  78.6 8.3 %collective-permute-start.7 = (bf16[64,2304]{1,0:T(8,128)(2,1)S(1)}, bf16[64,2304]{1,0:T(8,128)(2,1)S(1)}, u32[]{:S(2)}, u32[]{:S(2)}) collective-permute-start(bf16[64,2304]{1,0:T(8,128)(2,1)S(1)} %slice_bitcast_fusion), channel_id=1, source_target_pairs={{2,0},{4,2},{6,4},{7,6},{5,7},{3,5},{1,3},{0,1},{10,8},{12,10},{14... | collective-permute-start | bytes 884744 | tf_op jit(solution)/shard_map/ppermute | solution.py:258
  94.9 3.8 %collective-permute-start.13 = (f32[3,8,128]{2,1,0:T(8,128)S(1)}, f32[3,8,128]{2,1,0:T(8,128)S(1)}, u32[]{:S(2)}, u32[]{:S(2)}) collective-permute-start(f32[3,8,128]{2,1,0:T(8,128)S(1)} %chunk.7.mine_ref), channel_id=1, source_target_pairs={{0,1},{1,0},{2,3},{3,2},{4,5},{5,4},{6,7},{7,6},{8,9},{9,8},{10,11... | collective-permute-start | bytes 36872 | tf_op jit(solution)/shard_map/ppermute | solution.py:250
  98.7 3.8 %collective-permute-start.14 = (f32[3,8,128]{2,1,0:T(8,128)S(1)}, f32[3,8,128]{2,1,0:T(8,128)S(1)}, u32[]{:S(2)}, u32[]{:S(2)}) collective-permute-start(f32[3,8,128]{2,1,0:T(8,128)S(1)} %combine.3.mine_ref), channel_id=1, source_target_pairs={{0,2},{1,3},{2,0},{3,1},{4,6},{5,7},{6,4},{7,5},{8,10},{9,11},{10,... | collective-permute-start | bytes 36872 | tf_op jit(solution)/shard_map/ppermute | solution.py:250
  102.4 4.7 %collective-permute-start.15 = (f32[3,8,128]{2,1,0:T(8,128)S(1)}, f32[3,8,128]{2,1,0:T(8,128)S(1)}, u32[]{:S(2)}, u32[]{:S(2)}) collective-permute-start(f32[3,8,128]{2,1,0:T(8,128)S(1)} %combine.4.mine_ref), channel_id=1, source_target_pairs={{0,4},{1,5},{2,6},{3,7},{4,0},{5,1},{6,2},{7,3},{8,12},{9,13},{10,... | collective-permute-start | bytes 36872 | tf_op jit(solution)/shard_map/ppermute | solution.py:250

commit v5 on v4

--- a/solution.py
+++ b/solution.py
@@ -190,7 +190,7 @@
         + [WHOLE] * (3 + earlier),
         out_specs=out_specs,
         scratch_shapes=scratch,
-        compiler_params=pltpu.CompilerParams(vmem_limit_bytes=8 * MIB),
+        compiler_params=pltpu.CompilerParams(vmem_limit_bytes=(30 if first else 8) * MIB),
         cost_estimate=pl.CostEstimate(
             flops=2 * n * entries * (depth + 256),
             bytes_accessed=2 * entries * (depth + LANES),
@@ -249,6 +249,17 @@
     def trade(x, axis, size, bit):
         return lax.ppermute(x, axis, [(i, i ^ bit) for i in range(size)])
 
+    u_rows, v_rows = factor_u.shape[0], factor_v.shape[0]
+    shard = jnp.pad(factor_v.T, ((0, 0), (0, padded(v_rows) - v_rows)))
+    taken = []
+    for t in range(per):
+        sent = shard if t else jnp.concatenate([factor_u.T, shard], axis=1)
+        moves = [
+            ((v ^ t) * n_group + g, g * n_voc + v) for v in range(n_voc) for g in range(n_group)
+        ]
+        taken.append(lax.ppermute(sent, ("group", "vocab"), moves))
+
+    hidden, *taken = lax.optimization_barrier((hidden, *taken))
     up, down = [hidden], [hidden]
     for hop in range(1, half):
         up.append(lax.ppermute(up[-1], "vocab", ahead))
@@ -257,17 +268,7 @@
         lax.ppermute(up[-1][0], "vocab", ahead),
         lax.ppermute(down[-1][1], "vocab", behind),
     ]
-
-    u_rows, v_rows = factor_u.shape[0], factor_v.shape[0]
-    moves = [(v * n_group + g, g * n_voc + v) for v in range(n_voc) for g in range(n_group)]
-    shard = jnp.pad(factor_v.T, ((0, 0), (0, padded(v_rows) - v_rows)))
-    pack = jnp.concatenate([factor_u.T, shard], axis=1)
-    pack = lax.ppermute(pack, ("group", "vocab"), moves)
-    bit = 1
-    while bit < per:
-        other = trade(pack[:, u_rows:], "vocab", n_voc, bit)
-        pack = jnp.concatenate([pack, other], axis=1)
-        bit *= 2
+    pack = jnp.concatenate(taken, axis=1)
     packs = {0: pack}
     bit = n_group // 2
     while bit:

time: 108 us -> 107 us (level)
  waiting for transfers between devices: 19.9 us -> 49.3 us
  starting transfers between devices: 37.3 us -> 15.7 us
  local copies, waits for them, and re-layouts: 7.13 us -> 1.57 us
  Pallas kernels: 41.8 us -> 38.9 us
    ppermute x7 -> x6, starting transfers between devices: 23.8 us -> 2.2 us  [trade(): return lax.ppermute(x, axis, [(i, i ^ bit) for i in range(size)])]
    ppermute x3, waiting for transfers between devices: 0.01 us -> 16.3 us  [body(): up.append(lax.ppermute(up[-1], 'vocab', ahead))]
    ppermute x1 -> x2, waiting for transfers between devices: 0.01 us -> 13.2 us  [body(): taken.append(lax.ppermute(sent, ('group', 'vocab'), moves))]
    unnamed x7 -> x5, local copies, waits for them, and re-layouts: 7.07 us -> 0.7 us
    ppermute x1 -> x2, starting transfers between devices: 0.67 us -> 4.92 us  [body(): taken.append(lax.ppermute(sent, ('group', 'vocab'), moves))]
    ppermute x3, starting transfers between devices: 4.28 us -> 0.85 us  [body(): up.append(lax.ppermute(up[-1], 'vocab', ahead))]
    pallas_call x4, Pallas kernels: 40.2 us -> 37.3 us  [body(): out = chunk(*pieces, head, full_u, full_v, want, *before)]
    ppermute x7 -> x6, waiting for transfers between devices: 14.7 us -> 16.9 us  [trade(): return lax.ppermute(x, axis, [(i, i ^ bit) for i in range(size)])]
  transfers between devices with their start and end apart: 16 -> 16, of which waited for: 6 -> 9; matrix products, arithmetic and copies ran while one was open for 1% -> 0% of each run, Pallas kernels for 31% -> 28%
where the time goes in v5:
time: 107 us
  waiting for transfers between devices  49.3 us (46%)
  Pallas kernels  38.9 us (36%)
  starting transfers between devices  15.7 us (15%)
  local copies, waits for them, and re-layouts  1.57 us (1%)
    pallas_call x4, Pallas kernels, body(): out = chunk(*pieces, head, full_u, full_v, want, *before)  37.3 us
    ppermute x6, waiting for transfers between devices, trade(): return lax.ppermute(x, axis, [(i, i ^ bit) for i in range(size)])  16.9 us
    ppermute x3, waiting for transfers between devices, body(): up.append(lax.ppermute(up[-1], 'vocab', ahead))  16.3 us
    ppermute x2, waiting for transfers between devices, body(): taken.append(lax.ppermute(sent, ('group', 'vocab'), moves))  13.2 us
    ppermute x2, starting transfers between devices, body(): taken.append(lax.ppermute(sent, ('group', 'vocab'), moves))  4.92 us
    ppermute x3, starting transfers between devices, body(): down.append(lax.ppermute(down[-1], 'vocab', behind))  4.73 us
    ppermute x3, waiting for transfers between devices, body(): down.append(lax.ppermute(down[-1], 'vocab', behind))  2.99 us
    ppermute x1, starting transfers between devices, body(): lax.ppermute(down[-1][1], 'vocab', behind)  2.53 us
  transfers between devices with their start and end apart: 16, of which 9 were waited for; matrix products, arithmetic and copies ran while one was open for 0% of the time, Pallas kernels for 28%

profile of v5, /device:TPU:0, one launch (start us, length us, event | category | flops | bytes accessed | tf_op | source)
XLA Modules:
  0.0 107.2 jit_solution(5701339352605904489)
XLA Ops:
  0.6 0.8 pad.4
  1.4 0.9 pad_maximum_fusion
  2.4 0.7 collective-permute-start
  3.0 4.2 %collective-permute-start.1 = (bf16[64,384]{1,0:T(8,128)(2,1)S(1)}, bf16[64,384]{1,0:T(8,128)(2,1)S(1)}, u32[]{:S(2)}, u32[]{:S(2)}) collective-permute-start(bf16[64,384]{1,0:T(8,128)(2,1)S(1)} %pad.4), channel_id=1, source_target_pairs={{4,0},{5,8},{6,16},{7,24},{0,1},{1,9},{2,17},{3,25},{12,2},{13,10}... | collective-permute-start | bytes 147464 | tf_op jit(solution)/shard_map/ppermute | solution.py:260
  7.3 13.2 %collective-permute-done.1 = bf16[64,384]{1,0:T(8,128)(2,1)S(1)} collective-permute-done((bf16[64,384]{1,0:T(8,128)(2,1)S(1)}, bf16[64,384]{1,0:T(8,128)(2,1)S(1)}, u32[]{:S(2)}, u32[]{:S(2)}) %collective-permute-start.1) | collective-permute-done | bytes 49184 | tf_op jit(solution)/shard_map/ppermute | solution.py:260
  20.5 0.0 collective-permute-done
  20.5 0.2 collective-permute-start.2
  20.6 1.9 %collective-permute-start.6 = (bf16[2,64,2304]{2,1,0:T(8,128)(2,1)}, bf16[2,64,2304]{2,1,0:T(8,128)(2,1)S(1)}, u32[]{:S(2)}, u32[]{:S(2)}) collective-permute-start(bf16[2,64,2304]{2,1,0:T(8,128)(2,1)} %refs_0_), channel_id=1, source_target_pairs={{2,0},{4,2},{6,4},{7,6},{5,7},{3,5},{1,3},{0,1},{10,8},{12,10},{14... | collective-permute-start | bytes 1769480 | tf_op jit(solution)/shard_map/ppermute | solution.py:266
  22.5 12.7 %collective-permute-done.2.refs_0_ = bf16[2,64,2304]{2,1,0:T(8,128)(2,1)S(1)} collective-permute-done((bf16[2,64,2304]{2,1,0:T(8,128)(2,1)}, bf16[2,64,2304]{2,1,0:T(8,128)(2,1)S(1)}, u32[]{:S(2)}, u32[]{:S(2)}) %collective-permute-start.2) | collective-permute-done | bytes 589856 | tf_op jit(solution)/shard_map/ppermute | solution.py:265
  35.2 0.3 collective-permute-start.3
  35.5 1.5 %collective-permute-start.11 = (bf16[64,1792]{1,0:T(8,128)(2,1)S(1)}, bf16[64,1792]{1,0:T(8,128)(2,1)S(1)}, u32[]{:S(2)}, u32[]{:S(2)}) collective-permute-start(bf16[64,1792]{1,0:T(8,128)(2,1)S(1)} %constant_dynamic-update-slice_fusion.refs_0_), channel_id=1, source_target_pairs={{0,16},{8,24},{16,0},{24,8},{1,17},{9,25},{17,1},{25,9},{2,18},{10... | collective-permute-start | bytes 688136 | tf_op jit(solution)/shard_map/ppermute | solution.py:250
  37.0 0.0 collective-permute-start.10
  37.0 5.2 %collective-permute-done.11.refs_2_ = bf16[64,1792]{1,0:T(8,128)(2,1)S(1)} collective-permute-done((bf16[64,1792]{1,0:T(8,128)(2,1)S(1)}, bf16[64,1792]{1,0:T(8,128)(2,1)S(1)}, u32[]{:S(2)}, u32[]{:S(2)}) %collective-permute-start.11) | collective-permute-done | bytes 229408 | tf_op jit(solution)/shard_map/ppermute | solution.py:250
  42.1 0.0 collective-permute-start.12
  42.1 0.0 collective-permute-done.6.refs_1_
  42.1 1.2 %collective-permute-start.7 = (bf16[2,64,2304]{2,1,0:T(8,128)(2,1)S(1)}, bf16[2,64,2304]{2,1,0:T(8,128)(2,1)S(1)}, u32[]{:S(2)}, u32[]{:S(2)}) collective-permute-start(bf16[2,64,2304]{2,1,0:T(8,128)(2,1)S(1)} %collective-permute-done.6.refs_1_), channel_id=1, source_target_pairs={{2,0},{4,2},{6,4},{7,6},{5,7},{3,5},{1,3},{0,1},{10,8},{12,10},{14... | collective-permute-start | bytes 1769480 | tf_op jit(solution)/shard_map/ppermute | solution.py:266
  43.3 0.0 collective-permute-done.10.refs_1_
  43.3 0.3 collective-permute-done.12.refs_3_
  43.6 0.0 copy-start.1
  43.6 0.7 copy-done.1
  44.3 0.8 assemble.1
  45.1 3.6 %collective-permute-done.3.refs_0_ = bf16[2,64,2304]{2,1,0:T(8,128)(2,1)S(1)} collective-permute-done((bf16[2,64,2304]{2,1,0:T(8,128)(2,1)S(1)}, bf16[2,64,2304]{2,1,0:T(8,128)(2,1)S(1)}, u32[]{:S(2)}, u32[]{:S(2)}) %collective-permute-start.3) | collective-permute-done | bytes 589856 | tf_op jit(solution)/shard_map/ppermute | solution.py:265
  48.7 0.4 collective-permute-start.4
  49.1 14.4 %chunk.4 = (f32[3,256]{1,0:T(4,128)S(1)}, bf16[4096,2304]{1,0:T(8,128)(2,1)S(1)}) custom-call(bf16[2,64,2304]{2,1,0:T(8,128)(2,1)S(1)} %collective-permute-done.2.refs_0_, bf16[2,64,2304]{2,1,0:T(8,128)(2,1)S(1)} %collective-permute-done.6.refs_1_, bf16[4096,2304]{1,0:T(8,128)(2,1)} %refs_2_.1, bf16[4096,64]{1,0:T(8,128)(2,1)S(1)} %get-tuple-element.13.refs_3_.refs_4_, ...), custom_call_target="tpu_custom_call" | custom-call | flops 5368709120 | bytes 19922944 | tf_op jit(solution)/shard_map/chunk/pallas_call | solution.py:287
  63.5 0.0 collective-permute-done.7.refs_1_
  63.5 1.7 %collective-permute-start.8 = (bf16[2,64,2304]{2,1,0:T(8,128)(2,1)S(1)}, bf16[2,64,2304]{2,1,0:T(8,128)(2,1)S(1)}, u32[]{:S(2)}, u32[]{:S(2)}) collective-permute-start(bf16[2,64,2304]{2,1,0:T(8,128)(2,1)S(1)} %collective-permute-done.7.refs_1_), channel_id=1, source_target_pairs={{2,0},{4,2},{6,4},{7,6},{5,7},{3,5},{1,3},{0,1},{10,8},{12,10},{14... | collective-permute-start | bytes 1769480 | tf_op jit(solution)/shard_map/ppermute | solution.py:266
  65.2 0.0 copy-start
  65.2 7.5 %chunk.5.refs_8_ = f32[3,256]{1,0:T(4,128)S(1)} custom-call(bf16[2,64,2304]{2,1,0:T(8,128)(2,1)S(1)} %collective-permute-done.3.refs_0_, bf16[2,64,2304]{2,1,0:T(8,128)(2,1)S(1)} %collective-permute-done.7.refs_1_, bf16[4096,2304]{1,0:T(8,128)(2,1)S(1)} %get-tuple-element.16.refs_2_.refs_3_, bf16[4096,64]{1,0:T(8,128)(2,1)S(1)} %get-tuple-element.13.refs_3_.refs_4_, ...), custom_call_target="tpu_custom_call" | custom-call | flops 5368709120 | bytes 19922944 | tf_op jit(solution)/shard_map/chunk/pallas_call | solution.py:287
  72.7 0.0 collective-permute-done.4.refs_0_
  72.7 0.4 collective-permute-start.5
  73.2 3.0 %collective-permute-done.8.refs_1_ = bf16[2,64,2304]{2,1,0:T(8,128)(2,1)S(1)} collective-permute-done((bf16[2,64,2304]{2,1,0:T(8,128)(2,1)S(1)}, bf16[2,64,2304]{2,1,0:T(8,128)(2,1)S(1)}, u32[]{:S(2)}, u32[]{:S(2)}) %collective-permute-start.8) | collective-permute-done | bytes 589856 | tf_op jit(solution)/shard_map/ppermute | solution.py:266
  76.2 2.5 %collective-permute-start.9 = (bf16[64,2304]{1,0:T(8,128)(2,1)S(1)}, bf16[64,2304]{1,0:T(8,128)(2,1)S(1)}, u32[]{:S(2)}, u32[]{:S(2)}) collective-permute-start(bf16[64,2304]{1,0:T(8,128)(2,1)S(1)} %slice_bitcast_fusion), channel_id=1, source_target_pairs={{2,0},{4,2},{6,4},{7,6},{5,7},{3,5},{1,3},{0,1},{10,8},{12,10},{14... | collective-permute-start | bytes 884744 | tf_op jit(solution)/shard_map/ppermute | solution.py:269
  78.7 7.5 %chunk.6.refs_9_ = f32[3,256]{1,0:T(4,128)S(1)} custom-call(bf16[2,64,2304]{2,1,0:T(8,128)(2,1)S(1)} %collective-permute-done.4.refs_0_, bf16[2,64,2304]{2,1,0:T(8,128)(2,1)S(1)} %collective-permute-done.8.refs_1_, bf16[4096,2304]{1,0:T(8,128)(2,1)S(1)} %get-tuple-element.16.refs_2_.refs_3_, bf16[4096,64]{1,0:T(8,128)(2,1)S(1)} %get-tuple-element.13.refs_3_.refs_4_, ...), custom_call_target="tpu_custom_call" | custom-call | flops 5368709120 | bytes 19922944 | tf_op jit(solution)/shard_map/chunk/pallas_call | solution.py:287
  86.2 0.0 collective-permute-done.5.refs_1_
  86.2 0.0 collective-permute-done.9.refs_2_
  86.2 0.0 copy-done
  86.2 8.0 %chunk.7.mine_ref = f32[3,8,128]{2,1,0:T(8,128)S(1)} custom-call(bf16[2,64,2304]{2,1,0:T(8,128)(2,1)S(1)} %copy-done, bf16[64,2304]{1,0:T(8,128)(2,1)S(1)} %collective-permute-done.5.refs_1_, bf16[64,2304]{1,0:T(8,128)(2,1)S(1)} %collective-permute-done.9.refs_2_, bf16[4096,2304]{1,0:T(8,128)(2,1)S(1)} %get-tuple-element.16.refs_2_.refs_3_, ...), custom_call_target="tpu_custom_call" | custom-call | flops 5368709120 | bytes 19922944 | tf_op jit(solution)/shard_map/chunk/pallas_call | solution.py:287
  94.2 0.1 collective-permute-start.13
  94.3 3.7 %collective-permute-done.13.other_ref = f32[3,8,128]{2,1,0:T(8,128)S(1)} collective-permute-done((f32[3,8,128]{2,1,0:T(8,128)S(1)}, f32[3,8,128]{2,1,0:T(8,128)S(1)}, u32[]{:S(2)}, u32[]{:S(2)}) %collective-permute-start.13) | collective-permute-done | bytes 12320 | tf_op jit(solution)/shard_map/ppermute | solution.py:250
  98.0 0.1 collective-permute-start.14
  98.1 3.7 %collective-permute-done.14.other_ref = f32[3,8,128]{2,1,0:T(8,128)S(1)} collective-permute-done((f32[3,8,128]{2,1,0:T(8,128)S(1)}, f32[3,8,128]{2,1,0:T(8,128)S(1)}, u32[]{:S(2)}, u32[]{:S(2)}) %collective-permute-start.14) | collective-permute-done | bytes 12320 | tf_op jit(solution)/shard_map/ppermute | solution.py:250
  101.8 0.6 collective-permute-start.15
  102.4 4.1 %collective-permute-done.15.other_ref = f32[3,8,128]{2,1,0:T(8,128)S(1)} collective-permute-done((f32[3,8,128]{2,1,0:T(8,128)S(1)}, f32[3,8,128]{2,1,0:T(8,128)S(1)}, u32[]{:S(2)}, u32[]{:S(2)}) %collective-permute-start.15) | collective-permute-done | bytes 12320 | tf_op jit(solution)/shard_map/ppermute | solution.py:250
  106.5 0.7 combine.5
  (6 shorter events, 0.1 us)
Async XLA Ops:
  2.4 18.1 %collective-permute-start = (bf16[64,1408]{1,0:T(8,128)(2,1)S(1)}, bf16[64,1408]{1,0:T(8,128)(2,1)S(1)}, u32[]{:S(2)}, u32[]{:S(2)}) collective-permute-start(bf16[64,1408]{1,0:T(8,128)(2,1)S(1)} %pad_maximum_fusion), channel_id=1, source_target_pairs={{0,0},{1,8},{2,16},{3,24},{4,1},{5,9},{6,17},{7,25},{8,2},{9,10},{... | collective-permute-start | bytes 540680 | tf_op jit(solution)/shard_map/ppermute | solution.py:260
  3.0 17.4 %collective-permute-start.1 = (bf16[64,384]{1,0:T(8,128)(2,1)S(1)}, bf16[64,384]{1,0:T(8,128)(2,1)S(1)}, u32[]{:S(2)}, u32[]{:S(2)}) collective-permute-start(bf16[64,384]{1,0:T(8,128)(2,1)S(1)} %pad.4), channel_id=1, source_target_pairs={{4,0},{5,8},{6,16},{7,24},{0,1},{1,9},{2,17},{3,25},{12,2},{13,10}... | collective-permute-start | bytes 147464 | tf_op jit(solution)/shard_map/ppermute | solution.py:260
  20.5 14.7 %collective-permute-start.2 = (bf16[2,64,2304]{2,1,0:T(8,128)(2,1)}, bf16[2,64,2304]{2,1,0:T(8,128)(2,1)S(1)}, u32[]{:S(2)}, u32[]{:S(2)}) collective-permute-start(bf16[2,64,2304]{2,1,0:T(8,128)(2,1)} %refs_0_), channel_id=1, source_target_pairs={{0,2},{2,4},{4,6},{6,7},{7,5},{5,3},{3,1},{1,0},{8,10},{10,12},{12... | collective-permute-start | bytes 1769480 | tf_op jit(solution)/shard_map/ppermute | solution.py:265
  20.6 21.5 %collective-permute-start.6 = (bf16[2,64,2304]{2,1,0:T(8,128)(2,1)}, bf16[2,64,2304]{2,1,0:T(8,128)(2,1)S(1)}, u32[]{:S(2)}, u32[]{:S(2)}) collective-permute-start(bf16[2,64,2304]{2,1,0:T(8,128)(2,1)} %refs_0_), channel_id=1, source_target_pairs={{2,0},{4,2},{6,4},{7,6},{5,7},{3,5},{1,3},{0,1},{10,8},{12,10},{14... | collective-permute-start | bytes 1769480 | tf_op jit(solution)/shard_map/ppermute | solution.py:266
  35.2 13.6 %collective-permute-start.3 = (bf16[2,64,2304]{2,1,0:T(8,128)(2,1)S(1)}, bf16[2,64,2304]{2,1,0:T(8,128)(2,1)S(1)}, u32[]{:S(2)}, u32[]{:S(2)}) collective-permute-start(bf16[2,64,2304]{2,1,0:T(8,128)(2,1)S(1)} %collective-permute-done.2.refs_0_), channel_id=1, source_target_pairs={{0,2},{2,4},{4,6},{6,7},{7,5},{5,3},{3,1},{1,0},{8,10},{10,12},{12... | collective-permute-start | bytes 1769480 | tf_op jit(solution)/shard_map/ppermute | solution.py:265
  35.5 6.6 %collective-permute-start.11 = (bf16[64,1792]{1,0:T(8,128)(2,1)S(1)}, bf16[64,1792]{1,0:T(8,128)(2,1)S(1)}, u32[]{:S(2)}, u32[]{:S(2)}) collective-permute-start(bf16[64,1792]{1,0:T(8,128)(2,1)S(1)} %constant_dynamic-update-slice_fusion.refs_0_), channel_id=1, source_target_pairs={{0,16},{8,24},{16,0},{24,8},{1,17},{9,25},{17,1},{25,9},{2,18},{10... | collective-permute-start | bytes 688136 | tf_op jit(solution)/shard_map/ppermute | solution.py:250
  37.0 6.4 %collective-permute-start.10 = (bf16[64,1792]{1,0:T(8,128)(2,1)S(1)}, bf16[64,1792]{1,0:T(8,128)(2,1)S(1)}, u32[]{:S(2)}, u32[]{:S(2)}) collective-permute-start(bf16[64,1792]{1,0:T(8,128)(2,1)S(1)} %constant_dynamic-update-slice_fusion.refs_0_), channel_id=1, source_target_pairs={{0,8},{8,0},{16,24},{24,16},{1,9},{9,1},{17,25},{25,17},{2,10},{10... | collective-permute-start | bytes 688136 | tf_op jit(solution)/shard_map/ppermute | solution.py:250
  42.1 1.5 %collective-permute-start.12 = (bf16[64,1792]{1,0:T(8,128)(2,1)S(1)}, bf16[64,1792]{1,0:T(8,128)(2,1)S(1)}, u32[]{:S(2)}, u32[]{:S(2)}) collective-permute-start(bf16[64,1792]{1,0:T(8,128)(2,1)S(1)} %collective-permute-done.11.refs_2_), channel_id=1, source_target_pairs={{0,8},{8,0},{16,24},{24,16},{1,9},{9,1},{17,25},{25,17},{2,10},{10... | collective-permute-start | bytes 688136 | tf_op jit(solution)/shard_map/ppermute | solution.py:250
  42.1 21.4 %collective-permute-start.7 = (bf16[2,64,2304]{2,1,0:T(8,128)(2,1)S(1)}, bf16[2,64,2304]{2,1,0:T(8,128)(2,1)S(1)}, u32[]{:S(2)}, u32[]{:S(2)}) collective-permute-start(bf16[2,64,2304]{2,1,0:T(8,128)(2,1)S(1)} %collective-permute-done.6.refs_1_), channel_id=1, source_target_pairs={{2,0},{4,2},{6,4},{7,6},{5,7},{3,5},{1,3},{0,1},{10,8},{12,10},{14... | collective-permute-start | bytes 1769480 | tf_op jit(solution)/shard_map/ppermute | solution.py:266
  43.6 0.7 copy-start.1
  48.7 24.0 %collective-permute-start.4 = (bf16[2,64,2304]{2,1,0:T(8,128)(2,1)S(1)}, bf16[2,64,2304]{2,1,0:T(8,128)(2,1)S(1)}, u32[]{:S(2)}, u32[]{:S(2)}) collective-permute-start(bf16[2,64,2304]{2,1,0:T(8,128)(2,1)S(1)} %collective-permute-done.3.refs_0_), channel_id=1, source_target_pairs={{0,2},{2,4},{4,6},{6,7},{7,5},{5,3},{3,1},{1,0},{8,10},{10,12},{12... | collective-permute-start | bytes 1769480 | tf_op jit(solution)/shard_map/ppermute | solution.py:265
  63.5 12.6 %collective-permute-start.8 = (bf16[2,64,2304]{2,1,0:T(8,128)(2,1)S(1)}, bf16[2,64,2304]{2,1,0:T(8,128)(2,1)S(1)}, u32[]{:S(2)}, u32[]{:S(2)}) collective-permute-start(bf16[2,64,2304]{2,1,0:T(8,128)(2,1)S(1)} %collective-permute-done.7.refs_1_), channel_id=1, source_target_pairs={{2,0},{4,2},{6,4},{7,6},{5,7},{3,5},{1,3},{0,1},{10,8},{12,10},{14... | collective-permute-start | bytes 1769480 | tf_op jit(solution)/shard_map/ppermute | solution.py:266
  65.2 21.0 %copy-start = (bf16[2,64,2304]{2,1,0:T(8,128)(2,1)S(1)}, bf16[2,64,2304]{2,1,0:T(8,128)(2,1)}, u32[]{:S(2)}) copy-start(bf16[2,64,2304]{2,1,0:T(8,128)(2,1)} %refs_0_) | copy-start | bytes 1769476
  72.7 13.5 %collective-permute-start.5 = (bf16[64,2304]{1,0:T(8,128)(2,1)S(1)}, bf16[64,2304]{1,0:T(8,128)(2,1)S(1)}, u32[]{:S(2)}, u32[]{:S(2)}) collective-permute-start(bf16[64,2304]{1,0:T(8,128)(2,1)S(1)} %slice_bitcast_fusion.1), channel_id=1, source_target_pairs={{0,2},{2,4},{4,6},{6,7},{7,5},{5,3},{3,1},{1,0},{8,10},{10,12},{12... | collective-permute-start | bytes 884744 | tf_op jit(solution)/shard_map/ppermute | solution.py:268
  76.2 10.0 %collective-permute-start.9 = (bf16[64,2304]{1,0:T(8,128)(2,1)S(1)}, bf16[64,2304]{1,0:T(8,128)(2,1)S(1)}, u32[]{:S(2)}, u32[]{:S(2)}) collective-permute-start(bf16[64,2304]{1,0:T(8,128)(2,1)S(1)} %slice_bitcast_fusion), channel_id=1, source_target_pairs={{2,0},{4,2},{6,4},{7,6},{5,7},{3,5},{1,3},{0,1},{10,8},{12,10},{14... | collective-permute-start | bytes 884744 | tf_op jit(solution)/shard_map/ppermute | solution.py:269
  94.2 3.8 %collective-permute-start.13 = (f32[3,8,128]{2,1,0:T(8,128)S(1)}, f32[3,8,128]{2,1,0:T(8,128)S(1)}, u32[]{:S(2)}, u32[]{:S(2)}) collective-permute-start(f32[3,8,128]{2,1,0:T(8,128)S(1)} %chunk.7.mine_ref), channel_id=1, source_target_pairs={{0,1},{1,0},{2,3},{3,2},{4,5},{5,4},{6,7},{7,6},{8,9},{9,8},{10,11... | collective-permute-start | bytes 36872 | tf_op jit(solution)/shard_map/ppermute | solution.py:250
  98.0 3.8 %collective-permute-start.14 = (f32[3,8,128]{2,1,0:T(8,128)S(1)}, f32[3,8,128]{2,1,0:T(8,128)S(1)}, u32[]{:S(2)}, u32[]{:S(2)}) collective-permute-start(f32[3,8,128]{2,1,0:T(8,128)S(1)} %combine.3.mine_ref), channel_id=1, source_target_pairs={{0,2},{1,3},{2,0},{3,1},{4,6},{5,7},{6,4},{7,5},{8,10},{9,11},{10,... | collective-permute-start | bytes 36872 | tf_op jit(solution)/shard_map/ppermute | solution.py:250
  101.8 4.7 %collective-permute-start.15 = (f32[3,8,128]{2,1,0:T(8,128)S(1)}, f32[3,8,128]{2,1,0:T(8,128)S(1)}, u32[]{:S(2)}, u32[]{:S(2)}) collective-permute-start(f32[3,8,128]{2,1,0:T(8,128)S(1)} %combine.4.mine_ref), channel_id=1, source_target_pairs={{0,4},{1,5},{2,6},{3,7},{4,0},{5,1},{6,2},{7,3},{8,12},{9,13},{10,... | collective-permute-start | bytes 36872 | tf_op jit(solution)/shard_map/ppermute | solution.py:250

commit v6 on v5

--- a/solution.py
+++ b/solution.py
@@ -44,7 +44,7 @@
         group = lax.axis_index("group")
         voc = lax.axis_index("vocab")
         for k in range(n_group):
-            member = group ^ k
+            member = group ^ k ^ lax.rem(voc // per, n_group)
             start = pl.multiple_of(member * u_rows, u_rows)
             u_out[pl.ds(start, u_rows), :] = packs[k][:, :u_rows].T
             for t in range(per):
@@ -81,61 +81,112 @@
     return ring_device(position, n_voc), ring_device(position + hop, n_voc)
 
 
+def load_rows(rows, pieces):
+    at = 0
+    for ref in pieces:
+        block = ref[...].reshape(-1, ref.shape[-1])
+        rows[:, at : at + block.shape[0]] = block.T
+        at += block.shape[0]
+
+
+def make_base(r, depth, entries):
+    parts = 16 if entries % 4096 == 0 else 1
+    part = entries // parts
+    n = 4 * r
+
+    def kernel(up_ref, down_ref, head_ref, base_ref, rows, held, sems):
+        def fetch(t):
+            span = pl.ds(pl.multiple_of(t * part, part), part)
+            return pltpu.make_async_copy(head_ref.at[span, :], held.at[span, :], sems.at[t])
+
+        for t in range(parts):
+            fetch(t).start(priority=t % 2)
+        load_rows(rows, (up_ref, down_ref))
+
+        @pl.loop(0, parts // 2)
+        def _(i):
+            fetch(2 * i).wait()
+            fetch(2 * i + 1).wait()
+            span = pl.ds(pl.multiple_of(2 * i * part, 2 * part), 2 * part)
+            base_ref[span, :] = jnp.dot(
+                held[span, :], rows[...], preferred_element_type=jnp.float32
+            )
+
+    return pl.pallas_call(
+        kernel,
+        out_shape=(
+            jax.ShapeDtypeStruct((entries, n), jnp.float32),
+            jax.ShapeDtypeStruct((depth, n), jnp.bfloat16),
+            jax.ShapeDtypeStruct((entries, depth), jnp.bfloat16),
+        ),
+        in_specs=[WHOLE, WHOLE, pl.BlockSpec(memory_space=pltpu.HBM)],
+        out_specs=(WHOLE,) * 3,
+        scratch_shapes=[pltpu.SemaphoreType.DMA((parts,))],
+        compiler_params=pltpu.CompilerParams(vmem_limit_bytes=23 * MIB),
+        cost_estimate=pl.CostEstimate(
+            flops=2 * n * entries * depth,
+            bytes_accessed=2 * entries * depth,
+            transcendentals=0,
+        ),
+        name="base",
+    )
+
+
 def make_chunk(hop, pieces, r, depth, entries, rank, n_voc):
     tile = tile_rows(entries)
     tiles = entries // tile
     n = 4 * r
-    first, last = hop == 1, hop == n_voc // 2
+    carry, last = hop == 2, hop == n_voc // 2
     earlier = hop - 1 if last else 0
-    parts = 16 if entries % 4096 == 0 else tiles
-    part = entries // parts
 
     def kernel(*refs):
-        piece = refs[:pieces]
-        head_ref, u_ref, v_ref, want_ref = refs[pieces : pieces + 4]
-        before = refs[pieces + 4 : pieces + 4 + earlier]
-        out_ref, *rest = refs[pieces + 4 + earlier :]
-        held = head_ref
-        if first:
-            held, *rest, sems = rest
-        rows, proj, even, odd, top, total, pick = rest
-
-        def fetch(t):
-            span = pl.ds(pl.multiple_of(t * part, part), part)
-            return pltpu.make_async_copy(head_ref.at[span, :], held.at[span, :], sems.at[t])
-
-        if first:
-            for t in range(parts):
-                fetch(t).start()
-
-        at = 0
-        for ref in piece:
-            block = ref[...].reshape(-1, depth)
-            rows[:, at : at + block.shape[0]] = block.T
-            at += block.shape[0]
-        proj[...] = jnp.dot(v_ref[...], rows[...], preferred_element_type=jnp.float32).astype(
-            jnp.bfloat16
-        )
-        top[...] = jnp.full(top.shape, -1e30, jnp.float32)
+        piece, refs = refs[:pieces], refs[pieces:]
+        head_ref, u_ref, v_ref, want_ref, *refs = refs
+        if carry:
+            base_ref, base_rows, *refs = refs
+        before, refs = refs[:earlier], refs[earlier:]
+        out_ref, *refs = refs
+        if carry:
+            base_out, *refs = refs
+        rows, even, odd, proj, top, total, pick, *refs = refs
+        if carry:
+            base_proj, base_top, base_total, base_pick = refs
+            base_state = base_top, base_total, base_pick
+        state = top, total, pick
+
+        def project(source, into):
+            into[...] = jnp.dot(
+                v_ref[...], source[...], preferred_element_type=jnp.float32
+            ).astype(jnp.bfloat16)
+
+        def clear(top, total, pick):
+            top[...] = jnp.full(top.shape, -1e30, jnp.float32)
+            total[...] = jnp.zeros(total.shape, jnp.float32)
+            pick[...] = jnp.zeros(pick.shape, jnp.float32)
+
+        def wanted(k):
+            left, right = sources_of(k, n_voc)
+            return jnp.concatenate([want_ref[left], want_ref[right]], axis=1)
+
+        load_rows(rows, piece)
+        project(rows, proj)
+        clear(*state)
         odd[...] = jnp.full(odd.shape, -1e30, jnp.float32)
-        total[...] = jnp.zeros(total.shape, jnp.float32)
-        pick[...] = jnp.zeros(pick.shape, jnp.float32)
-        left, right = sources_of(hop, n_voc)
-        want = jnp.concatenate([want_ref[left], want_ref[right]], axis=1)
+        want = wanted(hop)
+        if carry:
+            project(base_rows, base_proj)
+            clear(*base_state)
+            base_want = wanted(1)
 
         def multiply(t, into):
-            if first:
-                for k in range(parts // tiles):
-                    fetch(t * (parts // tiles) + k).wait()
             span = pl.ds(pl.multiple_of(t * tile, tile), tile)
             into[...] = jnp.dot(
-                held[span, :], rows[...], preferred_element_type=jnp.float32
+                head_ref[span, :], rows[...], preferred_element_type=jnp.float32
             ) + jnp.dot(u_ref[span, :], proj[...], preferred_element_type=jnp.float32)
 
-        def reduce(start, values):
-            x = values[...]
+        def reduce(x, want, top, total, pick):
             entry = lax.broadcasted_iota(jnp.int32, (tile, n), 0)
-            hit = jnp.where(entry == want - start, x, 0.0)
+            hit = jnp.where(entry == want, x, 0.0)
             x3 = x.reshape(tile // 8, 8, n)
             new = jnp.maximum(top[...], jnp.max(x3, axis=0))
             total[...] = total[...] * jnp.exp(top[...] - new) + jnp.sum(
@@ -144,53 +195,58 @@
             pick[...] = pick[...] + jnp.sum(hit.reshape(tile // 8, 8, n), axis=0)
             top[...] = new
 
+        def finish_base(t):
+            if carry:
+                span = pl.ds(pl.multiple_of(t * tile, tile), tile)
+                x = base_ref[span, :] + jnp.dot(
+                    u_ref[span, :], base_proj[...], preferred_element_type=jnp.float32
+                )
+                reduce(x, base_want - t * tile, *base_state)
+
         @pl.loop(0, tiles // 2)
         def _(i):
             multiply(2 * i, even)
-            reduce(jnp.where(i == 0, 1 << 29, (2 * i - 1) * tile), odd)
+            reduce(odd[...], want - jnp.where(i == 0, 1 << 29, (2 * i - 1) * tile), *state)
+            finish_base(2 * i)
             multiply(2 * i + 1, odd)
-            reduce(2 * i * tile, even)
-
-        reduce(entries - tile, odd)
-        best = jnp.max(top[...], axis=0, keepdims=True)
-        sums = jnp.sum(total[...] * jnp.exp(top[...] - best), axis=0, keepdims=True)
-        picked = jnp.sum(pick[...], axis=0, keepdims=True)
-        if not last:
-            for q, value in enumerate((best, sums, picked)):
+            reduce(even[...], want - 2 * i * tile, *state)
+            finish_base(2 * i + 1)
+
+        reduce(odd[...], want - (entries - tile), *state)
+
+        def results(top, total, pick):
+            best = jnp.max(top[...], axis=0, keepdims=True)
+            sums = jnp.sum(total[...] * jnp.exp(top[...] - best), axis=0, keepdims=True)
+            return best, sums, jnp.sum(pick[...], axis=0, keepdims=True)
+
+        if carry:
+            for q, value in enumerate(results(*base_state)):
+                base_out[q : q + 1, :] = value
+        for q, value in enumerate(results(*state)):
+            if not last:
                 out_ref[q : q + 1, :] = value
-            return
-        for q, value in enumerate((best, sums, picked)):
-            out_ref[q, pl.ds(left, 1), :] = value[:, : 2 * r]
-            out_ref[q, pl.ds(right, 1), :] = value[:, 2 * r :]
-            for k in range(1, hop):
-                a, b = sources_of(k, n_voc)
-                out_ref[q, pl.ds(a, 1), :] = before[k - 1][q : q + 1, : 2 * r]
-                out_ref[q, pl.ds(b, 1), :] = before[k - 1][q : q + 1, 2 * r :]
+                continue
+            for k, lanes in [(hop, value)] + [
+                (k, before[k - 1][q : q + 1, :]) for k in range(1, hop)
+            ]:
+                left, right = sources_of(k, n_voc)
+                out_ref[q, pl.ds(left, 1), :] = lanes[:, : 2 * r]
+                out_ref[q, pl.ds(right, 1), :] = lanes[:, 2 * r :]
 
     out_shape = jax.ShapeDtypeStruct((3, n_voc, 2 * r) if last else (3, n), jnp.float32)
-    out_specs = WHOLE
-    scratch = [
-        pltpu.VMEM((depth, n), jnp.bfloat16),
-        pltpu.VMEM((rank, n), jnp.bfloat16),
-        pltpu.VMEM((tile, n), jnp.float32),
-        pltpu.VMEM((tile, n), jnp.float32),
-        pltpu.VMEM((8, n), jnp.float32),
-        pltpu.VMEM((8, n), jnp.float32),
-        pltpu.VMEM((8, n), jnp.float32),
-    ]
-    if first:
-        out_shape = (out_shape, jax.ShapeDtypeStruct((entries, depth), jnp.bfloat16))
-        out_specs = (WHOLE, WHOLE)
-        scratch.append(pltpu.SemaphoreType.DMA((parts,)))
+    small = [pltpu.VMEM((rank, n), jnp.bfloat16)] + [pltpu.VMEM((8, n), jnp.float32)] * 3
     return pl.pallas_call(
         kernel,
-        out_shape=out_shape,
-        in_specs=[WHOLE] * pieces
-        + [pl.BlockSpec(memory_space=pltpu.HBM) if first else WHOLE]
-        + [WHOLE] * (3 + earlier),
-        out_specs=out_specs,
-        scratch_shapes=scratch,
-        compiler_params=pltpu.CompilerParams(vmem_limit_bytes=(30 if first else 8) * MIB),
+        out_shape=(out_shape, out_shape) if carry else out_shape,
+        in_specs=[WHOLE] * (pieces + 4 + 2 * carry + earlier),
+        out_specs=(WHOLE, WHOLE) if carry else WHOLE,
+        scratch_shapes=[
+            pltpu.VMEM((depth, n), jnp.bfloat16),
+            pltpu.VMEM((tile, n), jnp.float32),
+            pltpu.VMEM((tile, n), jnp.float32),
+        ]
+        + small * (1 + carry),
+        compiler_params=pltpu.CompilerParams(vmem_limit_bytes=8 * MIB),
         cost_estimate=pl.CostEstimate(
             flops=2 * n * entries * (depth + 256),
             bytes_accessed=2 * entries * (depth + LANES),
@@ -255,21 +311,26 @@
     for t in range(per):
         sent = shard if t else jnp.concatenate([factor_u.T, shard], axis=1)
         moves = [
-            ((v ^ t) * n_group + g, g * n_voc + v) for v in range(n_voc) for g in range(n_group)
+            ((v ^ t) * n_group + (g ^ (v // per) % n_group), g * n_voc + v)
+            for v in range(n_voc)
+            for g in range(n_group)
         ]
         taken.append(lax.ppermute(sent, ("group", "vocab"), moves))
 
-    hidden, *taken = lax.optimization_barrier((hidden, *taken))
-    up, down = [hidden], [hidden]
-    for hop in range(1, half):
+    up = [hidden, lax.ppermute(hidden, "vocab", ahead)]
+    down = [hidden, lax.ppermute(hidden, "vocab", behind)]
+    up[1], down[1], *taken = lax.optimization_barrier((up[1], down[1], *taken))
+    base, base_rows, head = make_base(r, depth, entries)(up[1], down[1], head)
+    for hop in range(2, half):
         up.append(lax.ppermute(up[-1], "vocab", ahead))
         down.append(lax.ppermute(down[-1], "vocab", behind))
+        if hop == 2:
+            up[2], down[2], base = lax.optimization_barrier((up[2], down[2], base))
     ends = [
         lax.ppermute(up[-1][0], "vocab", ahead),
         lax.ppermute(down[-1][1], "vocab", behind),
     ]
-    pack = jnp.concatenate(taken, axis=1)
-    packs = {0: pack}
+    packs = {0: jnp.concatenate(taken, axis=1)}
     bit = n_group // 2
     while bit:
         for k in list(packs):
@@ -280,14 +341,12 @@
     )(sampled, *[packs[k] for k in range(n_group)])
 
     stats = []
-    for hop in range(1, half + 1):
+    for hop in range(2, half + 1):
         pieces = [up[hop], down[hop]] if hop < half else [hidden] + ends
+        extra = [base, base_rows] if hop == 2 else stats if hop == half else []
         chunk = make_chunk(hop, len(pieces), r, depth, entries, rank, n_voc)
-        before = stats if hop == half else []
-        out = chunk(*pieces, head, full_u, full_v, want, *before)
-        if hop == 1:
-            out, head = out
-        stats.append(out)
+        out = chunk(*pieces, head, full_u, full_v, want, *extra)
+        stats += [out[1], out[0]] if hop == 2 else [out]
     part = stats[-1]
     bit = 1
     while bit < n_voc:

time: 107 us -> 94.6 us (0.88)
  waiting for transfers between devices: 49.3 us -> 36.9 us
  starting transfers between devices: 15.7 us -> 18.6 us
  Pallas kernels: 38.9 us -> 36.2 us
    ppermute x3 -> x2, waiting for transfers between devices: 16.3 us -> 4.06 us  [body(): up.append(lax.ppermute(up[-1], 'vocab', ahead))]
    ppermute x2, waiting for transfers between devices: 13.2 us -> 18.3 us  [body(): taken.append(lax.ppermute(sent, ('group', 'vocab'), moves))]
    ppermute x6, waiting for transfers between devices: 16.9 us -> 12.9 us  [trade(): return lax.ppermute(x, axis, [(i, i ^ bit) for i in range(size)])]
    ppermute x0 -> x2, starting transfers between devices: none -> 3.08 us  [the longest x1 3.08 us: body(): up = [hidden, lax.ppermute(hidden, 'vocab', ahead)]]
    pallas_call x4, Pallas kernels: 37.3 us -> 34.7 us  [the longest x3 24.2 us: body(): out = chunk(*pieces, head, full_u, full_v, want, *extra)]
    ppermute x6, starting transfers between devices: 2.2 us -> 4.25 us  [trade(): return lax.ppermute(x, axis, [(i, i ^ bit) for i in range(size)])]
    ppermute x3 -> x2, waiting for transfers between devices: 2.99 us -> 1.28 us  [body(): down.append(lax.ppermute(down[-1], 'vocab', behind))]
    ppermute x1, starting transfers between devices: 2.53 us -> 0.85 us  [body(): lax.ppermute(down[-1][1], 'vocab', behind)]
  transfers between devices with their start and end apart: 16 -> 16, of which waited for: 9 -> 8; matrix products, arithmetic and copies ran while one was open for 0% -> 2% of each run, Pallas kernels for 28% -> 29%
where the time goes in v6:
time: 94.6 us; the launch traced here: 94.4 us
  waiting for transfers between devices  36.9 us (39%)
  Pallas kernels  36.2 us (38%)
  starting transfers between devices  18.6 us (20%)
    pallas_call x3, Pallas kernels, body(): out = chunk(*pieces, head, full_u, full_v, want, *extra)  24.2 us
    ppermute x2, waiting for transfers between devices, body(): taken.append(lax.ppermute(sent, ('group', 'vocab'), moves))  18.3 us
    ppermute x6, waiting for transfers between devices, trade(): return lax.ppermute(x, axis, [(i, i ^ bit) for i in range(size)])  12.9 us
    pallas_call x1, Pallas kernels, body(): base, base_rows, head = make_base(r, depth, entries)(up[1], down[1], head)  10.4 us
    ppermute x2, starting transfers between devices, body(): taken.append(lax.ppermute(sent, ('group', 'vocab'), moves))  5.77 us
    ppermute x6, starting transfers between devices, trade(): return lax.ppermute(x, axis, [(i, i ^ bit) for i in range(size)])  4.25 us
    ppermute x2, waiting for transfers between devices, body(): up.append(lax.ppermute(up[-1], 'vocab', ahead))  4.06 us
    ppermute x2, starting transfers between devices, body(): down.append(lax.ppermute(down[-1], 'vocab', behind))  4.04 us
  transfers between devices with their start and end apart: 16, of which 8 were waited for; matrix products, arithmetic and copies ran while one was open for 2% of the time, Pallas kernels for 29%

profile of v6, /device:TPU:0, one launch (start us, length us, event | category | flops | bytes accessed | tf_op | source)
XLA Modules:
  0.0 94.4 jit_solution(7914145901981708917)
XLA Ops:
  0.6 0.0 copy-start.1
  0.6 3.1 %collective-permute-start = (bf16[2,64,2304]{2,1,0:T(8,128)(2,1)}, bf16[2,64,2304]{2,1,0:T(8,128)(2,1)S(1)}, u32[]{:S(2)}, u32[]{:S(2)}) collective-permute-start(bf16[2,64,2304]{2,1,0:T(8,128)(2,1)} %refs_0_.1), channel_id=1, source_target_pairs={{0,2},{2,4},{4,6},{6,7},{7,5},{5,3},{3,1},{1,0},{8,10},{10,12},{12... | collective-permute-start | bytes 1769480 | tf_op jit(solution)/shard_map/ppermute | solution.py:320
  3.7 0.0 collective-permute-start.1
  3.7 0.8 pad.4
  4.5 0.9 pad_maximum_fusion
  5.4 0.7 collective-permute-start.2
  6.1 5.1 %collective-permute-start.3 = (bf16[64,384]{1,0:T(8,128)(2,1)S(1)}, bf16[64,384]{1,0:T(8,128)(2,1)S(1)}, u32[]{:S(2)}, u32[]{:S(2)}) collective-permute-start(bf16[64,384]{1,0:T(8,128)(2,1)S(1)} %pad.4), channel_id=1, source_target_pairs={{4,0},{5,8},{6,16},{7,24},{0,1},{1,9},{2,17},{3,25},{13,2},{12,10}... | collective-permute-start | bytes 147464 | tf_op jit(solution)/shard_map/ppermute | solution.py:318
  11.2 18.3 %collective-permute-done.3 = bf16[64,384]{1,0:T(8,128)(2,1)S(1)} collective-permute-done((bf16[64,384]{1,0:T(8,128)(2,1)S(1)}, bf16[64,384]{1,0:T(8,128)(2,1)S(1)}, u32[]{:S(2)}, u32[]{:S(2)}) %collective-permute-start.3) | collective-permute-done | bytes 49184 | tf_op jit(solution)/shard_map/ppermute | solution.py:318
  29.6 0.0 collective-permute-done.2
  29.6 0.0 collective-permute-done.up_ref
  29.6 0.0 collective-permute-done.1.down_ref
  29.6 0.1 collective-permute-start.11
  29.7 0.1 collective-permute-start.4
  29.8 2.0 %collective-permute-start.5 = (bf16[2,64,2304]{2,1,0:T(8,128)(2,1)S(1)}, bf16[2,64,2304]{2,1,0:T(8,128)(2,1)S(1)}, u32[]{:S(2)}, u32[]{:S(2)}) collective-permute-start(bf16[2,64,2304]{2,1,0:T(8,128)(2,1)S(1)} %collective-permute-done.1.down_ref), channel_id=1, source_target_pairs={{2,0},{4,2},{6,4},{7,6},{5,7},{3,5},{1,3},{0,1},{10,8},{12,10},{14... | collective-permute-start | bytes 1769480 | tf_op jit(solution)/shard_map/ppermute | solution.py:326
  31.8 0.0 collective-permute-start.10
  31.8 4.9 %collective-permute-done.11.refs_2_ = bf16[64,1792]{1,0:T(8,128)(2,1)S(1)} collective-permute-done((bf16[64,1792]{1,0:T(8,128)(2,1)S(1)}, bf16[64,1792]{1,0:T(8,128)(2,1)S(1)}, u32[]{:S(2)}, u32[]{:S(2)}) %collective-permute-start.11) | collective-permute-done | bytes 229408 | tf_op jit(solution)/shard_map/ppermute | solution.py:306
  36.6 0.0 collective-permute-start.12
  36.6 10.4 %base.1 = (f32[4096,256]{1,0:T(8,128)S(1)}, bf16[2304,256]{1,0:T(8,128)(2,1)S(1)}, bf16[4096,2304]{1,0:T(8,128)(2,1)S(1)}) custom-call(bf16[2,64,2304]{2,1,0:T(8,128)(2,1)S(1)} %collective-permute-done.up_ref, bf16[2,64,2304]{2,1,0:T(8,128)(2,1)S(1)} %collective-permute-done.1.down_ref, bf16[4096,2304]{1,0:T(8,128)(2,1)} %head_ref.1), custom_call_target="tpu_custom_call" | custom-call | flops 4831838208 | bytes 18874368 | tf_op jit(solution)/shard_map/base/pallas_call | solution.py:323
  47.1 0.0 collective-permute-done.4.refs_0_
  47.1 0.0 collective-permute-done.5.refs_1_
  47.1 0.1 collective-permute-start.6
  47.2 0.0 collective-permute-done.10.refs_1_
  47.2 0.0 collective-permute-done.12.refs_3_
  47.2 0.0 copy-done.1
  47.2 0.8 assemble.1
  48.0 2.0 %collective-permute-start.8 = (bf16[2,64,2304]{2,1,0:T(8,128)(2,1)S(1)}, bf16[2,64,2304]{2,1,0:T(8,128)(2,1)S(1)}, u32[]{:S(2)}, u32[]{:S(2)}) collective-permute-start(bf16[2,64,2304]{2,1,0:T(8,128)(2,1)S(1)} %collective-permute-done.5.refs_1_), channel_id=1, source_target_pairs={{2,0},{4,2},{6,4},{7,6},{5,7},{3,5},{1,3},{0,1},{10,8},{12,10},{14... | collective-permute-start | bytes 1769480 | tf_op jit(solution)/shard_map/ppermute | solution.py:326
  50.1 0.0 copy-start
  50.1 8.8 %chunk.3 = (f32[3,256]{1,0:T(4,128)S(1)}, f32[3,256]{1,0:T(4,128)S(1)}) custom-call(bf16[2,64,2304]{2,1,0:T(8,128)(2,1)S(1)} %collective-permute-done.4.refs_0_, bf16[2,64,2304]{2,1,0:T(8,128)(2,1)S(1)} %collective-permute-done.5.refs_1_, bf16[4096,2304]{1,0:T(8,128)(2,1)S(1)} %get-tuple-element.22.refs_2_.refs_3_, ...), custom_call_target="tpu_custom_call" | custom-call | flops 5368709120 | bytes 19922944 | tf_op jit(solution)/shard_map/chunk/pallas_call | solution.py:348
  58.8 4.1 %collective-permute-done.6.refs_0_ = bf16[2,64,2304]{2,1,0:T(8,128)(2,1)S(1)} collective-permute-done((bf16[2,64,2304]{2,1,0:T(8,128)(2,1)S(1)}, bf16[2,64,2304]{2,1,0:T(8,128)(2,1)S(1)}, u32[]{:S(2)}, u32[]{:S(2)}) %collective-permute-start.6) | collective-permute-done | bytes 589856 | tf_op jit(solution)/shard_map/ppermute | solution.py:325
  62.9 0.5 collective-permute-start.7
  63.5 1.3 %collective-permute-done.8.refs_1_ = bf16[2,64,2304]{2,1,0:T(8,128)(2,1)S(1)} collective-permute-done((bf16[2,64,2304]{2,1,0:T(8,128)(2,1)S(1)}, bf16[2,64,2304]{2,1,0:T(8,128)(2,1)S(1)}, u32[]{:S(2)}, u32[]{:S(2)}) %collective-permute-start.8) | collective-permute-done | bytes 589856 | tf_op jit(solution)/shard_map/ppermute | solution.py:326
  64.8 0.9 collective-permute-start.9
  65.6 7.5 %chunk.4.refs_9_ = f32[3,256]{1,0:T(4,128)S(1)} custom-call(bf16[2,64,2304]{2,1,0:T(8,128)(2,1)S(1)} %collective-permute-done.6.refs_0_, bf16[2,64,2304]{2,1,0:T(8,128)(2,1)S(1)} %collective-permute-done.8.refs_1_, bf16[4096,2304]{1,0:T(8,128)(2,1)S(1)} %get-tuple-element.22.refs_2_.refs_3_, bf16[4096,64]{1,0:T(8,128)(2,1)S(1)} %get-tuple-element.25.refs_3_.refs_4_, ...), custom_call_target="tpu_custom_call" | custom-call | flops 5368709120 | bytes 19922944 | tf_op jit(solution)/shard_map/chunk/pallas_call | solution.py:348
  73.1 0.0 collective-permute-done.7.refs_1_
  73.1 0.4 collective-permute-done.9.refs_2_
  73.4 0.0 copy-done
  73.4 8.0 %chunk.5.mine_ref = f32[3,8,128]{2,1,0:T(8,128)S(1)} custom-call(bf16[2,64,2304]{2,1,0:T(8,128)(2,1)S(1)} %copy-done, bf16[64,2304]{1,0:T(8,128)(2,1)S(1)} %collective-permute-done.7.refs_1_, bf16[64,2304]{1,0:T(8,128)(2,1)S(1)} %collective-permute-done.9.refs_2_, bf16[4096,2304]{1,0:T(8,128)(2,1)S(1)} %get-tuple-element.22.refs_2_.refs_3_, ...), custom_call_target="tpu_custom_call" | custom-call | flops 5368709120 | bytes 19922944 | tf_op jit(solution)/shard_map/chunk/pallas_call | solution.py:348
  81.5 0.5 collective-permute-start.13
  82.0 3.2 %collective-permute-done.13.other_ref = f32[3,8,128]{2,1,0:T(8,128)S(1)} collective-permute-done((f32[3,8,128]{2,1,0:T(8,128)S(1)}, f32[3,8,128]{2,1,0:T(8,128)S(1)}, u32[]{:S(2)}, u32[]{:S(2)}) %collective-permute-start.13) | collective-permute-done | bytes 12320 | tf_op jit(solution)/shard_map/ppermute | solution.py:306
  85.2 1.5 %collective-permute-start.14 = (f32[3,8,128]{2,1,0:T(8,128)S(1)}, f32[3,8,128]{2,1,0:T(8,128)S(1)}, u32[]{:S(2)}, u32[]{:S(2)}) collective-permute-start(f32[3,8,128]{2,1,0:T(8,128)S(1)} %combine.3.mine_ref), channel_id=1, source_target_pairs={{0,2},{1,3},{2,0},{3,1},{4,6},{5,7},{6,4},{7,5},{8,10},{9,11},{10,... | collective-permute-start | bytes 36872 | tf_op jit(solution)/shard_map/ppermute | solution.py:306
  86.7 2.3 %collective-permute-done.14.other_ref = f32[3,8,128]{2,1,0:T(8,128)S(1)} collective-permute-done((f32[3,8,128]{2,1,0:T(8,128)S(1)}, f32[3,8,128]{2,1,0:T(8,128)S(1)}, u32[]{:S(2)}, u32[]{:S(2)}) %collective-permute-start.14) | collective-permute-done | bytes 12320 | tf_op jit(solution)/shard_map/ppermute | solution.py:306
  89.0 2.1 %collective-permute-start.15 = (f32[3,8,128]{2,1,0:T(8,128)S(1)}, f32[3,8,128]{2,1,0:T(8,128)S(1)}, u32[]{:S(2)}, u32[]{:S(2)}) collective-permute-start(f32[3,8,128]{2,1,0:T(8,128)S(1)} %combine.4.mine_ref), channel_id=1, source_target_pairs={{0,4},{1,5},{2,6},{3,7},{4,0},{5,1},{6,2},{7,3},{8,12},{9,13},{10,... | collective-permute-start | bytes 36872 | tf_op jit(solution)/shard_map/ppermute | solution.py:306
  91.2 2.5 %collective-permute-done.15.other_ref = f32[3,8,128]{2,1,0:T(8,128)S(1)} collective-permute-done((f32[3,8,128]{2,1,0:T(8,128)S(1)}, f32[3,8,128]{2,1,0:T(8,128)S(1)}, u32[]{:S(2)}, u32[]{:S(2)}) %collective-permute-start.15) | collective-permute-done | bytes 12320 | tf_op jit(solution)/shard_map/ppermute | solution.py:306
  93.7 0.7 combine.5
  (6 shorter events, 0.1 us)
Async XLA Ops:
  0.6 46.6 %copy-start.1 = (s32[2,512]{1,0:T(2,128)S(1)}, s32[2,512]{1,0:T(2,128)}, u32[]{:S(2)}) copy-start(s32[2,512]{1,0:T(2,128)} %sampled_ref.1) | copy-start | bytes 12292
  0.6 28.9 %collective-permute-start = (bf16[2,64,2304]{2,1,0:T(8,128)(2,1)}, bf16[2,64,2304]{2,1,0:T(8,128)(2,1)S(1)}, u32[]{:S(2)}, u32[]{:S(2)}) collective-permute-start(bf16[2,64,2304]{2,1,0:T(8,128)(2,1)} %refs_0_.1), channel_id=1, source_target_pairs={{0,2},{2,4},{4,6},{6,7},{7,5},{5,3},{3,1},{1,0},{8,10},{10,12},{12... | collective-permute-start | bytes 1769480 | tf_op jit(solution)/shard_map/ppermute | solution.py:320
  3.7 25.9 %collective-permute-start.1 = (bf16[2,64,2304]{2,1,0:T(8,128)(2,1)}, bf16[2,64,2304]{2,1,0:T(8,128)(2,1)S(1)}, u32[]{:S(2)}, u32[]{:S(2)}) collective-permute-start(bf16[2,64,2304]{2,1,0:T(8,128)(2,1)} %refs_0_.1), channel_id=1, source_target_pairs={{2,0},{4,2},{6,4},{7,6},{5,7},{3,5},{1,3},{0,1},{10,8},{12,10},{14... | collective-permute-start | bytes 1769480 | tf_op jit(solution)/shard_map/ppermute | solution.py:321
  5.4 24.1 %collective-permute-start.2 = (bf16[64,1408]{1,0:T(8,128)(2,1)S(1)}, bf16[64,1408]{1,0:T(8,128)(2,1)S(1)}, u32[]{:S(2)}, u32[]{:S(2)}) collective-permute-start(bf16[64,1408]{1,0:T(8,128)(2,1)S(1)} %pad_maximum_fusion), channel_id=1, source_target_pairs={{0,0},{1,8},{2,16},{3,24},{4,1},{5,9},{6,17},{7,25},{9,2},{8,10},{... | collective-permute-start | bytes 540680 | tf_op jit(solution)/shard_map/ppermute | solution.py:318
  6.1 23.4 %collective-permute-start.3 = (bf16[64,384]{1,0:T(8,128)(2,1)S(1)}, bf16[64,384]{1,0:T(8,128)(2,1)S(1)}, u32[]{:S(2)}, u32[]{:S(2)}) collective-permute-start(bf16[64,384]{1,0:T(8,128)(2,1)S(1)} %pad.4), channel_id=1, source_target_pairs={{4,0},{5,8},{6,16},{7,24},{0,1},{1,9},{2,17},{3,25},{13,2},{12,10}... | collective-permute-start | bytes 147464 | tf_op jit(solution)/shard_map/ppermute | solution.py:318
  29.6 7.0 %collective-permute-start.11 = (bf16[64,1792]{1,0:T(8,128)(2,1)S(1)}, bf16[64,1792]{1,0:T(8,128)(2,1)S(1)}, u32[]{:S(2)}, u32[]{:S(2)}) collective-permute-start(bf16[64,1792]{1,0:T(8,128)(2,1)S(1)} %constant_dynamic-update-slice_fusion.refs_0_), channel_id=1, source_target_pairs={{0,16},{8,24},{16,0},{24,8},{1,17},{9,25},{17,1},{25,9},{2,18},{10... | collective-permute-start | bytes 688136 | tf_op jit(solution)/shard_map/ppermute | solution.py:306
  29.7 17.4 %collective-permute-start.4 = (bf16[2,64,2304]{2,1,0:T(8,128)(2,1)S(1)}, bf16[2,64,2304]{2,1,0:T(8,128)(2,1)S(1)}, u32[]{:S(2)}, u32[]{:S(2)}) collective-permute-start(bf16[2,64,2304]{2,1,0:T(8,128)(2,1)S(1)} %collective-permute-done.up_ref), channel_id=1, source_target_pairs={{0,2},{2,4},{4,6},{6,7},{7,5},{5,3},{3,1},{1,0},{8,10},{10,12},{12... | collective-permute-start | bytes 1769480 | tf_op jit(solution)/shard_map/ppermute | solution.py:325
  29.8 17.3 %collective-permute-start.5 = (bf16[2,64,2304]{2,1,0:T(8,128)(2,1)S(1)}, bf16[2,64,2304]{2,1,0:T(8,128)(2,1)S(1)}, u32[]{:S(2)}, u32[]{:S(2)}) collective-permute-start(bf16[2,64,2304]{2,1,0:T(8,128)(2,1)S(1)} %collective-permute-done.1.down_ref), channel_id=1, source_target_pairs={{2,0},{4,2},{6,4},{7,6},{5,7},{3,5},{1,3},{0,1},{10,8},{12,10},{14... | collective-permute-start | bytes 1769480 | tf_op jit(solution)/shard_map/ppermute | solution.py:326
  31.8 15.4 %collective-permute-start.10 = (bf16[64,1792]{1,0:T(8,128)(2,1)S(1)}, bf16[64,1792]{1,0:T(8,128)(2,1)S(1)}, u32[]{:S(2)}, u32[]{:S(2)}) collective-permute-start(bf16[64,1792]{1,0:T(8,128)(2,1)S(1)} %constant_dynamic-update-slice_fusion.refs_0_), channel_id=1, source_target_pairs={{0,8},{8,0},{16,24},{24,16},{1,9},{9,1},{17,25},{25,17},{2,10},{10... | collective-permute-start | bytes 688136 | tf_op jit(solution)/shard_map/ppermute | solution.py:306
  36.6 10.5 %collective-permute-start.12 = (bf16[64,1792]{1,0:T(8,128)(2,1)S(1)}, bf16[64,1792]{1,0:T(8,128)(2,1)S(1)}, u32[]{:S(2)}, u32[]{:S(2)}) collective-permute-start(bf16[64,1792]{1,0:T(8,128)(2,1)S(1)} %collective-permute-done.11.refs_2_), channel_id=1, source_target_pairs={{0,8},{8,0},{16,24},{24,16},{1,9},{9,1},{17,25},{25,17},{2,10},{10... | collective-permute-start | bytes 688136 | tf_op jit(solution)/shard_map/ppermute | solution.py:306
  47.1 15.8 %collective-permute-start.6 = (bf16[2,64,2304]{2,1,0:T(8,128)(2,1)S(1)}, bf16[2,64,2304]{2,1,0:T(8,128)(2,1)S(1)}, u32[]{:S(2)}, u32[]{:S(2)}) collective-permute-start(bf16[2,64,2304]{2,1,0:T(8,128)(2,1)S(1)} %collective-permute-done.4.refs_0_), channel_id=1, source_target_pairs={{0,2},{2,4},{4,6},{6,7},{7,5},{5,3},{3,1},{1,0},{8,10},{10,12},{12... | collective-permute-start | bytes 1769480 | tf_op jit(solution)/shard_map/ppermute | solution.py:325
  48.0 16.7 %collective-permute-start.8 = (bf16[2,64,2304]{2,1,0:T(8,128)(2,1)S(1)}, bf16[2,64,2304]{2,1,0:T(8,128)(2,1)S(1)}, u32[]{:S(2)}, u32[]{:S(2)}) collective-permute-start(bf16[2,64,2304]{2,1,0:T(8,128)(2,1)S(1)} %collective-permute-done.5.refs_1_), channel_id=1, source_target_pairs={{2,0},{4,2},{6,4},{7,6},{5,7},{3,5},{1,3},{0,1},{10,8},{12,10},{14... | collective-permute-start | bytes 1769480 | tf_op jit(solution)/shard_map/ppermute | solution.py:326
  50.1 23.4 %copy-start = (bf16[2,64,2304]{2,1,0:T(8,128)(2,1)S(1)}, bf16[2,64,2304]{2,1,0:T(8,128)(2,1)}, u32[]{:S(2)}) copy-start(bf16[2,64,2304]{2,1,0:T(8,128)(2,1)} %refs_0_.1) | copy-start | bytes 1769476
  62.9 10.2 %collective-permute-start.7 = (bf16[64,2304]{1,0:T(8,128)(2,1)S(1)}, bf16[64,2304]{1,0:T(8,128)(2,1)S(1)}, u32[]{:S(2)}, u32[]{:S(2)}) collective-permute-start(bf16[64,2304]{1,0:T(8,128)(2,1)S(1)} %slice_bitcast_fusion.1), channel_id=1, source_target_pairs={{0,2},{2,4},{4,6},{6,7},{7,5},{5,3},{3,1},{1,0},{8,10},{10,12},{12... | collective-permute-start | bytes 884744 | tf_op jit(solution)/shard_map/ppermute | solution.py:330
  64.8 8.7 %collective-permute-start.9 = (bf16[64,2304]{1,0:T(8,128)(2,1)S(1)}, bf16[64,2304]{1,0:T(8,128)(2,1)S(1)}, u32[]{:S(2)}, u32[]{:S(2)}) collective-permute-start(bf16[64,2304]{1,0:T(8,128)(2,1)S(1)} %slice_bitcast_fusion), channel_id=1, source_target_pairs={{2,0},{4,2},{6,4},{7,6},{5,7},{3,5},{1,3},{0,1},{10,8},{12,10},{14... | collective-permute-start | bytes 884744 | tf_op jit(solution)/shard_map/ppermute | solution.py:331
  81.5 3.8 %collective-permute-start.13 = (f32[3,8,128]{2,1,0:T(8,128)S(1)}, f32[3,8,128]{2,1,0:T(8,128)S(1)}, u32[]{:S(2)}, u32[]{:S(2)}) collective-permute-start(f32[3,8,128]{2,1,0:T(8,128)S(1)} %chunk.5.mine_ref), channel_id=1, source_target_pairs={{0,1},{1,0},{2,3},{3,2},{4,5},{5,4},{6,7},{7,6},{8,9},{9,8},{10,11... | collective-permute-start | bytes 36872 | tf_op jit(solution)/shard_map/ppermute | solution.py:306
  85.2 3.8 %collective-permute-start.14 = (f32[3,8,128]{2,1,0:T(8,128)S(1)}, f32[3,8,128]{2,1,0:T(8,128)S(1)}, u32[]{:S(2)}, u32[]{:S(2)}) collective-permute-start(f32[3,8,128]{2,1,0:T(8,128)S(1)} %combine.3.mine_ref), channel_id=1, source_target_pairs={{0,2},{1,3},{2,0},{3,1},{4,6},{5,7},{6,4},{7,5},{8,10},{9,11},{10,... | collective-permute-start | bytes 36872 | tf_op jit(solution)/shard_map/ppermute | solution.py:306
  89.0 4.7 %collective-permute-start.15 = (f32[3,8,128]{2,1,0:T(8,128)S(1)}, f32[3,8,128]{2,1,0:T(8,128)S(1)}, u32[]{:S(2)}, u32[]{:S(2)}) collective-permute-start(f32[3,8,128]{2,1,0:T(8,128)S(1)} %combine.4.mine_ref), channel_id=1, source_target_pairs={{0,4},{1,5},{2,6},{3,7},{4,0},{5,1},{6,2},{7,3},{8,12},{9,13},{10,... | collective-permute-start | bytes 36872 | tf_op jit(solution)/shard_map/ppermute | solution.py:306

commit v7 on v6

--- a/solution.py
+++ b/solution.py
@@ -25,7 +25,7 @@
 
 def tile_rows(entries):
     for rows in (512, 256, 128, 64, 32, 16):
-        if entries % (2 * rows) == 0:
+        if entries % (4 * rows) == 0:
             return rows
     raise ValueError(entries)
 
@@ -89,40 +89,75 @@
         at += block.shape[0]
 
 
+def fetch_rows(head_ref, first, held, sems, parts=8):
+    part = held.shape[0] // parts
+    return [
+        pltpu.make_async_copy(
+            head_ref.at[pl.ds(first + t * part, part), :],
+            held.at[pl.ds(t * part, part), :],
+            sems.at[t],
+        )
+        for t in range(parts)
+    ]
+
+
+def make_load(depth, entries):
+    def kernel(head_ref, held, sems):
+        copies = fetch_rows(head_ref, 0, held, sems)
+        for t, copy in enumerate(copies):
+            copy.start(priority=t % 2)
+        for copy in copies:
+            copy.wait()
+
+    return pl.pallas_call(
+        kernel,
+        out_shape=jax.ShapeDtypeStruct((entries // 2, depth), jnp.bfloat16),
+        in_specs=[pl.BlockSpec(memory_space=pltpu.HBM)],
+        out_specs=WHOLE,
+        scratch_shapes=[pltpu.SemaphoreType.DMA((8,))],
+        compiler_params=pltpu.CompilerParams(vmem_limit_bytes=40 * MIB),
+        cost_estimate=pl.CostEstimate(
+            flops=0, bytes_accessed=depth * entries, transcendentals=0
+        ),
+        name="load",
+    )
+
+
 def make_base(r, depth, entries):
-    parts = 16 if entries % 4096 == 0 else 1
-    part = entries // parts
     n = 4 * r
-
-    def kernel(up_ref, down_ref, head_ref, base_ref, rows, held, sems):
-        def fetch(t):
-            span = pl.ds(pl.multiple_of(t * part, part), part)
-            return pltpu.make_async_copy(head_ref.at[span, :], held.at[span, :], sems.at[t])
-
-        for t in range(parts):
-            fetch(t).start(priority=t % 2)
+    half = entries // 2
+    tile = 2 * half // 8
+
+    def kernel(up_ref, down_ref, head_ref, low, base_ref, rows, high, sems):
+        copies = fetch_rows(head_ref, half, high, sems)
+        for t, copy in enumerate(copies):
+            copy.start(priority=t % 2)
         load_rows(rows, (up_ref, down_ref))
 
-        @pl.loop(0, parts // 2)
-        def _(i):
-            fetch(2 * i).wait()
-            fetch(2 * i + 1).wait()
-            span = pl.ds(pl.multiple_of(2 * i * part, 2 * part), 2 * part)
-            base_ref[span, :] = jnp.dot(
+        def multiply(i, held, first):
+            span = pl.ds(pl.multiple_of(i * tile, tile), tile)
+            at = pl.ds(pl.multiple_of(first + i * tile, tile), tile)
+            base_ref[at, :] = jnp.dot(
                 held[span, :], rows[...], preferred_element_type=jnp.float32
             )
+
+        pl.loop(0, half // tile)(lambda i: multiply(i, low, 0))
+        for i in range(half // tile):
+            for copy in copies[2 * i : 2 * i + 2]:
+                copy.wait()
+            multiply(i, high, half)
 
     return pl.pallas_call(
         kernel,
         out_shape=(
             jax.ShapeDtypeStruct((entries, n), jnp.float32),
             jax.ShapeDtypeStruct((depth, n), jnp.bfloat16),
-            jax.ShapeDtypeStruct((entries, depth), jnp.bfloat16),
+            jax.ShapeDtypeStruct((half, depth), jnp.bfloat16),
         ),
-        in_specs=[WHOLE, WHOLE, pl.BlockSpec(memory_space=pltpu.HBM)],
+        in_specs=[WHOLE, WHOLE, pl.BlockSpec(memory_space=pltpu.HBM), WHOLE],
         out_specs=(WHOLE,) * 3,
-        scratch_shapes=[pltpu.SemaphoreType.DMA((parts,))],
-        compiler_params=pltpu.CompilerParams(vmem_limit_bytes=23 * MIB),
+        scratch_shapes=[pltpu.SemaphoreType.DMA((8,))],
+        compiler_params=pltpu.CompilerParams(vmem_limit_bytes=24 * MIB),
         cost_estimate=pl.CostEstimate(
             flops=2 * n * entries * depth,
             bytes_accessed=2 * entries * depth,
@@ -141,7 +176,7 @@
 
     def kernel(*refs):
         piece, refs = refs[:pieces], refs[pieces:]
-        head_ref, u_ref, v_ref, want_ref, *refs = refs
+        low_ref, high_ref, u_ref, v_ref, want_ref, *refs = refs
         if carry:
             base_ref, base_rows, *refs = refs
         before, refs = refs[:earlier], refs[earlier:]
@@ -178,10 +213,11 @@
             clear(*base_state)
             base_want = wanted(1)
 
-        def multiply(t, into):
+        def multiply(t, into, head_ref, first):
             span = pl.ds(pl.multiple_of(t * tile, tile), tile)
+            at = pl.ds(pl.multiple_of((t - first) * tile, tile), tile)
             into[...] = jnp.dot(
-                head_ref[span, :], rows[...], preferred_element_type=jnp.float32
+                head_ref[at, :], rows[...], preferred_element_type=jnp.float32
             ) + jnp.dot(u_ref[span, :], proj[...], preferred_element_type=jnp.float32)
 
         def reduce(x, want, top, total, pick):
@@ -203,14 +239,16 @@
                 )
                 reduce(x, base_want - t * tile, *base_state)
 
-        @pl.loop(0, tiles // 2)
-        def _(i):
-            multiply(2 * i, even)
+        def step(i, head_ref, first):
+            multiply(2 * i, even, head_ref, first)
             reduce(odd[...], want - jnp.where(i == 0, 1 << 29, (2 * i - 1) * tile), *state)
             finish_base(2 * i)
-            multiply(2 * i + 1, odd)
+            multiply(2 * i + 1, odd, head_ref, first)
             reduce(even[...], want - 2 * i * tile, *state)
             finish_base(2 * i + 1)
+
+        pl.loop(0, tiles // 4)(lambda i: step(i, low_ref, 0))
+        pl.loop(tiles // 4, tiles // 2)(lambda i: step(i, high_ref, tiles // 2))
 
         reduce(odd[...], want - (entries - tile), *state)
 
@@ -238,7 +276,7 @@
     return pl.pallas_call(
         kernel,
         out_shape=(out_shape, out_shape) if carry else out_shape,
-        in_specs=[WHOLE] * (pieces + 4 + 2 * carry + earlier),
+        in_specs=[WHOLE] * (pieces + 5 + 2 * carry + earlier),
         out_specs=(WHOLE, WHOLE) if carry else WHOLE,
         scratch_shapes=[
             pltpu.VMEM((depth, n), jnp.bfloat16),
@@ -256,14 +294,23 @@
     )
 
 
-def make_combine(bit, r, n_voc, finish):
-    def kernel(mine_ref, other_ref, *outs):
-        high = (lax.axis_index("vocab") & bit) != 0
-        low = [jnp.where(high, other_ref[q], mine_ref[q]) for q in range(3)]
-        up = [jnp.where(high, mine_ref[q], other_ref[q]) for q in range(3)]
-        top = jnp.maximum(low[0], up[0])
-        total = low[1] * jnp.exp(low[0] - top) + up[1] * jnp.exp(up[0] - top)
-        pick = low[2] + up[2]
+def make_combine(bits, r, n_voc, finish):
+    low = bits & -bits
+    count = bits // low + 1
+
+    def kernel(*refs):
+        parts, outs, held = refs[:count], refs[count:-1], refs[-1]
+        slot = lax.rem(lax.axis_index("vocab") // low, count)
+        for k in range(count):
+            held[slot ^ k] = parts[k][...]
+        top = held[0, 0]
+        for k in range(1, count):
+            top = jnp.maximum(top, held[k, 0])
+        total = held[0, 1] * jnp.exp(held[0, 0] - top)
+        pick = held[0, 2]
+        for k in range(1, count):
+            total = total + held[k, 1] * jnp.exp(held[k, 0] - top)
+            pick = pick + held[k, 2]
         if not finish:
             for q, value in enumerate((top, total, pick)):
                 outs[0][q] = value
@@ -282,8 +329,9 @@
     return pl.pallas_call(
         kernel,
         out_shape=shape,
-        in_specs=[WHOLE, WHOLE],
+        in_specs=[WHOLE] * count,
         out_specs=specs,
+        scratch_shapes=[pltpu.VMEM((count, 3, n_voc, 2 * r), jnp.float32)],
         compiler_params=pltpu.CompilerParams(vmem_limit_bytes=MIB),
         name="combine",
     )
@@ -319,8 +367,8 @@
 
     up = [hidden, lax.ppermute(hidden, "vocab", ahead)]
     down = [hidden, lax.ppermute(hidden, "vocab", behind)]
-    up[1], down[1], *taken = lax.optimization_barrier((up[1], down[1], *taken))
-    base, base_rows, head = make_base(r, depth, entries)(up[1], down[1], head)
+    low, *taken = lax.optimization_barrier((make_load(depth, entries)(head), *taken))
+    base, base_rows, high = make_base(r, depth, entries)(up[1], down[1], head, low)
     for hop in range(2, half):
         up.append(lax.ppermute(up[-1], "vocab", ahead))
         down.append(lax.ppermute(down[-1], "vocab", behind))
@@ -345,14 +393,16 @@
         pieces = [up[hop], down[hop]] if hop < half else [hidden] + ends
         extra = [base, base_rows] if hop == 2 else stats if hop == half else []
         chunk = make_chunk(hop, len(pieces), r, depth, entries, rank, n_voc)
-        out = chunk(*pieces, head, full_u, full_v, want, *extra)
+        out = chunk(*pieces, low, high, full_u, full_v, want, *extra)
         stats += [out[1], out[0]] if hop == 2 else [out]
     part = stats[-1]
-    bit = 1
-    while bit < n_voc:
-        other = trade(part, "vocab", n_voc, bit)
-        part = make_combine(bit, r, n_voc, 2 * bit == n_voc)(part, other)
-        bit *= 2
+    low = 1
+    while low < n_voc:
+        count = 2 if low == 1 else min(4, n_voc // low)
+        bits = low * (count - 1)
+        others = [trade(part, "vocab", n_voc, low * k) for k in range(1, count)]
+        part = make_combine(bits, r, n_voc, low * count == n_voc)(part, *others)
+        low *= count
     return part
 
 

time: 94.6 us -> 96.4 us (1.019)
  waiting for transfers between devices: 36.9 us -> 34 us
  starting transfers between devices: 18.6 us -> 21.1 us
  Pallas kernels: 36.2 us -> 38.5 us
    ppermute x1, starting transfers between devices: 3.08 us -> 5.72 us  [body(): up = [hidden, lax.ppermute(hidden, 'vocab', ahead)]]
    pallas_call x7, Pallas kernels: 35.4 us -> 37.7 us  [the longest x3 24 us: body(): out = chunk(*pieces, low, high, full_u, full_v, want, *extra)]
    ppermute x2, starting transfers between devices: 5.77 us -> 3.54 us  [body(): taken.append(lax.ppermute(sent, ('group', 'vocab'), moves))]
    ppermute x2, waiting for transfers between devices: 18.3 us -> 17.1 us  [body(): taken.append(lax.ppermute(sent, ('group', 'vocab'), moves))]
    ppermute x6 -> x7, starting transfers between devices: 4.25 us -> 5.4 us  [trade(): return lax.ppermute(x, axis, [(i, i ^ bit) for i in range(size)])]
    ppermute x2, starting transfers between devices: 0.12 us -> 1.24 us  [body(): up.append(lax.ppermute(up[-1], 'vocab', ahead))]
    ppermute x2, starting transfers between devices: 4.04 us -> 2.94 us  [body(): down.append(lax.ppermute(down[-1], 'vocab', behind))]
    ppermute x1, starting transfers between devices: 0.85 us -> 1.95 us  [body(): lax.ppermute(down[-1][1], 'vocab', behind)]
  transfers between devices with their start and end apart: 16 -> 17, of which waited for: 8 -> 7; matrix products, arithmetic and copies ran while one was open for 2% -> 0% of each run, Pallas kernels for 29% -> 31%
where the time goes in v7:
time: 96.4 us; the launch traced here: 96.2 us
  Pallas kernels  38.5 us (40%)
  waiting for transfers between devices  34 us (35%)
  starting transfers between devices  21.1 us (22%)
    pallas_call x3, Pallas kernels, body(): out = chunk(*pieces, low, high, full_u, full_v, want, *extra)  24 us
    ppermute x2, waiting for transfers between devices, body(): taken.append(lax.ppermute(sent, ('group', 'vocab'), moves))  17.1 us
    ppermute x7, waiting for transfers between devices, trade(): return lax.ppermute(x, axis, [(i, i ^ bit) for i in range(size)])  12 us
    pallas_call x1, Pallas kernels, body(): make_base(r, depth, entries)(up[1], down[1], head, low)  9.07 us
    ppermute x1, starting transfers between devices, body(): up = [hidden, lax.ppermute(hidden, 'vocab', ahead)]  5.72 us
    ppermute x7, starting transfers between devices, trade(): return lax.ppermute(x, axis, [(i, i ^ bit) for i in range(size)])  5.4 us
    ppermute x2, waiting for transfers between devices, body(): up.append(lax.ppermute(up[-1], 'vocab', ahead))  4.32 us
    pallas_call x1, Pallas kernels, body(): make_load(depth, entries)(head)  3.83 us
  transfers between devices with their start and end apart: 17, of which 7 were waited for; matrix products, arithmetic and copies ran while one was open for 0% of the time, Pallas kernels for 31%

profile of v7, /device:TPU:0, one launch (start us, length us, event | category | flops | bytes accessed | tf_op | source)
XLA Modules:
  0.0 96.2 jit_solution(15014363098829239876)
XLA Ops:
  0.6 0.8 pad.4
  1.4 0.9 pad_maximum_fusion
  2.4 0.7 collective-permute-start.4
  3.0 5.7 %collective-permute-start = (bf16[2,64,2304]{2,1,0:T(8,128)(2,1)}, bf16[2,64,2304]{2,1,0:T(8,128)(2,1)S(1)}, u32[]{:S(2)}, u32[]{:S(2)}) collective-permute-start(bf16[2,64,2304]{2,1,0:T(8,128)(2,1)} %refs_0_.1), channel_id=1, source_target_pairs={{0,2},{2,4},{4,6},{6,7},{7,5},{5,3},{3,1},{1,0},{8,10},{10,12},{12... | collective-permute-start | bytes 1769480 | tf_op jit(solution)/shard_map/ppermute | solution.py:368
  8.8 0.0 collective-permute-start.2
  8.8 2.9 %collective-permute-start.5 = (bf16[64,384]{1,0:T(8,128)(2,1)S(1)}, bf16[64,384]{1,0:T(8,128)(2,1)S(1)}, u32[]{:S(2)}, u32[]{:S(2)}) collective-permute-start(bf16[64,384]{1,0:T(8,128)(2,1)S(1)} %pad.4), channel_id=1, source_target_pairs={{4,0},{5,8},{6,16},{7,24},{0,1},{1,9},{2,17},{3,25},{13,2},{12,10}... | collective-permute-start | bytes 147464 | tf_op jit(solution)/shard_map/ppermute | solution.py:366
  11.6 3.8 %load.1.low.refs_2_.refs_3_ = bf16[2048,2304]{1,0:T(8,128)(2,1)S(1)} custom-call(bf16[4096,2304]{1,0:T(8,128)(2,1)} %head_ref.3), custom_call_target="tpu_custom_call" | custom-call | bytes 9437184 | tf_op jit(solution)/shard_map/load/pallas_call | solution.py:370
  15.5 17.1 %collective-permute-done.5 = bf16[64,384]{1,0:T(8,128)(2,1)S(1)} collective-permute-done((bf16[64,384]{1,0:T(8,128)(2,1)S(1)}, bf16[64,384]{1,0:T(8,128)(2,1)S(1)}, u32[]{:S(2)}, u32[]{:S(2)}) %collective-permute-start.5) | collective-permute-done | bytes 49184 | tf_op jit(solution)/shard_map/ppermute | solution.py:366
  32.5 0.0 collective-permute-done.4
  32.6 0.0 copy-start.1
  32.6 0.1 collective-permute-start.11
  32.7 0.0 collective-permute-done.up_ref
  32.7 1.2 %collective-permute-start.1 = (bf16[2,64,2304]{2,1,0:T(8,128)(2,1)S(1)}, bf16[2,64,2304]{2,1,0:T(8,128)(2,1)S(1)}, u32[]{:S(2)}, u32[]{:S(2)}) collective-permute-start(bf16[2,64,2304]{2,1,0:T(8,128)(2,1)S(1)} %collective-permute-done.up_ref), channel_id=1, source_target_pairs={{0,2},{2,4},{4,6},{6,7},{7,5},{5,3},{3,1},{1,0},{8,10},{10,12},{12... | collective-permute-start | bytes 1769480 | tf_op jit(solution)/shard_map/ppermute | solution.py:373
  33.9 0.0 collective-permute-done.2.down_ref
  33.9 0.9 collective-permute-start.3
  34.8 0.0 collective-permute-start.10
  34.8 5.8 %collective-permute-done.11.refs_2_ = bf16[64,1792]{1,0:T(8,128)(2,1)S(1)} collective-permute-done((bf16[64,1792]{1,0:T(8,128)(2,1)S(1)}, bf16[64,1792]{1,0:T(8,128)(2,1)S(1)}, u32[]{:S(2)}, u32[]{:S(2)}) %collective-permute-start.11) | collective-permute-done | bytes 229408 | tf_op jit(solution)/shard_map/ppermute | solution.py:354
  40.5 0.0 collective-permute-start.12
  40.6 9.1 %base.1 = (f32[4096,256]{1,0:T(8,128)S(1)}, bf16[2304,256]{1,0:T(8,128)(2,1)S(1)}, bf16[2048,2304]{1,0:T(8,128)(2,1)S(1)}) custom-call(bf16[2,64,2304]{2,1,0:T(8,128)(2,1)S(1)} %collective-permute-done.up_ref, bf16[2,64,2304]{2,1,0:T(8,128)(2,1)S(1)} %collective-permute-done.2.down_ref, bf16[4096,2304]{1,0:T(8,128)(2,1)} %head_ref.3, ...), custom_call_target="tpu_custom_call" | custom-call | flops 4831838208 | bytes 18874368 | tf_op jit(solution)/shard_map/base/pallas_call | solution.py:371
  49.6 0.0 collective-permute-done.1.refs_0_
  49.6 0.0 collective-permute-done.3.refs_1_
  49.7 0.1 collective-permute-start.6
  49.7 0.0 collective-permute-done.10.refs_1_
  49.7 0.0 collective-permute-done.12.refs_3_
  49.7 0.0 copy-done.1
  49.7 0.8 assemble.1
  50.6 2.0 %collective-permute-start.8 = (bf16[2,64,2304]{2,1,0:T(8,128)(2,1)S(1)}, bf16[2,64,2304]{2,1,0:T(8,128)(2,1)S(1)}, u32[]{:S(2)}, u32[]{:S(2)}) collective-permute-start(bf16[2,64,2304]{2,1,0:T(8,128)(2,1)S(1)} %collective-permute-done.3.refs_1_), channel_id=1, source_target_pairs={{2,0},{4,2},{6,4},{7,6},{5,7},{3,5},{1,3},{0,1},{10,8},{12,10},{14... | collective-permute-start | bytes 1769480 | tf_op jit(solution)/shard_map/ppermute | solution.py:374
  52.6 8.5 %chunk.3 = (f32[3,256]{1,0:T(4,128)S(1)}, f32[3,256]{1,0:T(4,128)S(1)}) custom-call(bf16[2,64,2304]{2,1,0:T(8,128)(2,1)S(1)} %collective-permute-done.1.refs_0_, bf16[2,64,2304]{2,1,0:T(8,128)(2,1)S(1)} %collective-permute-done.3.refs_1_, bf16[2048,2304]{1,0:T(8,128)(2,1)S(1)} %load.1.low.refs_2_.refs_3_, ...), custom_call_target="tpu_custom_call" | custom-call | flops 5368709120 | bytes 19922944 | tf_op jit(solution)/shard_map/chunk/pallas_call | solution.py:396
  61.1 4.3 %collective-permute-done.6.refs_0_ = bf16[2,64,2304]{2,1,0:T(8,128)(2,1)S(1)} collective-permute-done((bf16[2,64,2304]{2,1,0:T(8,128)(2,1)S(1)}, bf16[2,64,2304]{2,1,0:T(8,128)(2,1)S(1)}, u32[]{:S(2)}, u32[]{:S(2)}) %collective-permute-start.6) | collective-permute-done | bytes 589856 | tf_op jit(solution)/shard_map/ppermute | solution.py:373
  65.5 0.3 collective-permute-start.7
  65.8 0.6 collective-permute-done.8.refs_1_
  66.4 0.0 copy-start
  66.4 1.9 %collective-permute-start.9 = (bf16[64,2304]{1,0:T(8,128)(2,1)S(1)}, bf16[64,2304]{1,0:T(8,128)(2,1)S(1)}, u32[]{:S(2)}, u32[]{:S(2)}) collective-permute-start(bf16[64,2304]{1,0:T(8,128)(2,1)S(1)} %slice_bitcast_fusion), channel_id=1, source_target_pairs={{2,0},{4,2},{6,4},{7,6},{5,7},{3,5},{1,3},{0,1},{10,8},{12,10},{14... | collective-permute-start | bytes 884744 | tf_op jit(solution)/shard_map/ppermute | solution.py:379
  68.4 7.5 %chunk.4.refs_10_ = f32[3,256]{1,0:T(4,128)S(1)} custom-call(bf16[2,64,2304]{2,1,0:T(8,128)(2,1)S(1)} %collective-permute-done.6.refs_0_, bf16[2,64,2304]{2,1,0:T(8,128)(2,1)S(1)} %collective-permute-done.8.refs_1_, bf16[2048,2304]{1,0:T(8,128)(2,1)S(1)} %load.1.low.refs_2_.refs_3_, bf16[2048,2304]{1,0:T(8,128)(2,1)S(1)} %get-tuple-element.20.refs_3_.refs_4_, ...), custom_call_target="tpu_custom_call" | custom-call | flops 5368709120 | bytes 19922944 | tf_op jit(solution)/shard_map/chunk/pallas_call | solution.py:396
  75.8 0.0 collective-permute-done.7.refs_1_
  75.9 0.0 collective-permute-done.9.refs_2_
  75.9 0.0 copy-done
  75.9 8.0 %chunk.5.refs_0_ = f32[3,8,128]{2,1,0:T(8,128)S(1)} custom-call(bf16[2,64,2304]{2,1,0:T(8,128)(2,1)S(1)} %copy-done, bf16[64,2304]{1,0:T(8,128)(2,1)S(1)} %collective-permute-done.7.refs_1_, bf16[64,2304]{1,0:T(8,128)(2,1)S(1)} %collective-permute-done.9.refs_2_, bf16[2048,2304]{1,0:T(8,128)(2,1)S(1)} %load.1.low.refs_2_.refs_3_, ...), custom_call_target="tpu_custom_call" | custom-call | flops 5368709120 | bytes 19922944 | tf_op jit(solution)/shard_map/chunk/pallas_call | solution.py:396
  83.9 0.9 collective-permute-start.13
  84.8 2.9 %collective-permute-done.13.refs_1_ = f32[3,8,128]{2,1,0:T(8,128)S(1)} collective-permute-done((f32[3,8,128]{2,1,0:T(8,128)S(1)}, f32[3,8,128]{2,1,0:T(8,128)S(1)}, u32[]{:S(2)}, u32[]{:S(2)}) %collective-permute-start.13) | collective-permute-done | bytes 12320 | tf_op jit(solution)/shard_map/ppermute | solution.py:354
  87.7 3.2 %collective-permute-start.16 = (f32[3,8,128]{2,1,0:T(8,128)S(1)}, f32[3,8,128]{2,1,0:T(8,128)S(1)}, u32[]{:S(2)}, u32[]{:S(2)}) collective-permute-start(f32[3,8,128]{2,1,0:T(8,128)S(1)} %combine.2.refs_0_), channel_id=1, source_target_pairs={{0,6},{1,7},{2,4},{3,5},{4,2},{5,3},{6,0},{7,1},{8,14},{9,15},{10,... | collective-permute-start | bytes 36872 | tf_op jit(solution)/shard_map/ppermute | solution.py:354
  90.9 0.0 collective-permute-start.15
  90.9 1.3 %collective-permute-start.14 = (f32[3,8,128]{2,1,0:T(8,128)S(1)}, f32[3,8,128]{2,1,0:T(8,128)S(1)}, u32[]{:S(2)}, u32[]{:S(2)}) collective-permute-start(f32[3,8,128]{2,1,0:T(8,128)S(1)} %combine.2.refs_0_), channel_id=1, source_target_pairs={{0,2},{1,3},{2,0},{3,1},{4,6},{5,7},{6,4},{7,5},{8,10},{9,11},{10,... | collective-permute-start | bytes 36872 | tf_op jit(solution)/shard_map/ppermute | solution.py:354
  92.2 1.1 %collective-permute-done.16.refs_3_ = f32[3,8,128]{2,1,0:T(8,128)S(1)} collective-permute-done((f32[3,8,128]{2,1,0:T(8,128)S(1)}, f32[3,8,128]{2,1,0:T(8,128)S(1)}, u32[]{:S(2)}, u32[]{:S(2)}) %collective-permute-start.16) | collective-permute-done | bytes 12320 | tf_op jit(solution)/shard_map/ppermute | solution.py:354
  93.3 2.2 %collective-permute-done.15.refs_2_ = f32[3,8,128]{2,1,0:T(8,128)S(1)} collective-permute-done((f32[3,8,128]{2,1,0:T(8,128)S(1)}, f32[3,8,128]{2,1,0:T(8,128)S(1)}, u32[]{:S(2)}, u32[]{:S(2)}) %collective-permute-start.15) | collective-permute-done | bytes 12320 | tf_op jit(solution)/shard_map/ppermute | solution.py:354
  95.5 0.0 collective-permute-done.14.refs_1_
  95.5 0.7 combine.3
  (5 shorter events, 0.1 us)
Async XLA Ops:
  2.4 30.2 %collective-permute-start.4 = (bf16[64,1408]{1,0:T(8,128)(2,1)S(1)}, bf16[64,1408]{1,0:T(8,128)(2,1)S(1)}, u32[]{:S(2)}, u32[]{:S(2)}) collective-permute-start(bf16[64,1408]{1,0:T(8,128)(2,1)S(1)} %pad_maximum_fusion), channel_id=1, source_target_pairs={{0,0},{1,8},{2,16},{3,24},{4,1},{5,9},{6,17},{7,25},{9,2},{8,10},{... | collective-permute-start | bytes 540680 | tf_op jit(solution)/shard_map/ppermute | solution.py:366
  3.0 29.6 %collective-permute-start = (bf16[2,64,2304]{2,1,0:T(8,128)(2,1)}, bf16[2,64,2304]{2,1,0:T(8,128)(2,1)S(1)}, u32[]{:S(2)}, u32[]{:S(2)}) collective-permute-start(bf16[2,64,2304]{2,1,0:T(8,128)(2,1)} %refs_0_.1), channel_id=1, source_target_pairs={{0,2},{2,4},{4,6},{6,7},{7,5},{5,3},{3,1},{1,0},{8,10},{10,12},{12... | collective-permute-start | bytes 1769480 | tf_op jit(solution)/shard_map/ppermute | solution.py:368
  8.8 25.1 %collective-permute-start.2 = (bf16[2,64,2304]{2,1,0:T(8,128)(2,1)}, bf16[2,64,2304]{2,1,0:T(8,128)(2,1)S(1)}, u32[]{:S(2)}, u32[]{:S(2)}) collective-permute-start(bf16[2,64,2304]{2,1,0:T(8,128)(2,1)} %refs_0_.1), channel_id=1, source_target_pairs={{2,0},{4,2},{6,4},{7,6},{5,7},{3,5},{1,3},{0,1},{10,8},{12,10},{14... | collective-permute-start | bytes 1769480 | tf_op jit(solution)/shard_map/ppermute | solution.py:369
  8.8 23.8 %collective-permute-start.5 = (bf16[64,384]{1,0:T(8,128)(2,1)S(1)}, bf16[64,384]{1,0:T(8,128)(2,1)S(1)}, u32[]{:S(2)}, u32[]{:S(2)}) collective-permute-start(bf16[64,384]{1,0:T(8,128)(2,1)S(1)} %pad.4), channel_id=1, source_target_pairs={{4,0},{5,8},{6,16},{7,24},{0,1},{1,9},{2,17},{3,25},{13,2},{12,10}... | collective-permute-start | bytes 147464 | tf_op jit(solution)/shard_map/ppermute | solution.py:366
  32.6 17.2 %copy-start.1 = (s32[2,512]{1,0:T(2,128)S(1)}, s32[2,512]{1,0:T(2,128)}, u32[]{:S(2)}) copy-start(s32[2,512]{1,0:T(2,128)} %sampled_ref.1) | copy-start | bytes 12292
  32.6 8.0 %collective-permute-start.11 = (bf16[64,1792]{1,0:T(8,128)(2,1)S(1)}, bf16[64,1792]{1,0:T(8,128)(2,1)S(1)}, u32[]{:S(2)}, u32[]{:S(2)}) collective-permute-start(bf16[64,1792]{1,0:T(8,128)(2,1)S(1)} %constant_dynamic-update-slice_fusion.refs_0_), channel_id=1, source_target_pairs={{0,16},{8,24},{16,0},{24,8},{1,17},{9,25},{17,1},{25,9},{2,18},{10... | collective-permute-start | bytes 688136 | tf_op jit(solution)/shard_map/ppermute | solution.py:354
  32.7 17.0 %collective-permute-start.1 = (bf16[2,64,2304]{2,1,0:T(8,128)(2,1)S(1)}, bf16[2,64,2304]{2,1,0:T(8,128)(2,1)S(1)}, u32[]{:S(2)}, u32[]{:S(2)}) collective-permute-start(bf16[2,64,2304]{2,1,0:T(8,128)(2,1)S(1)} %collective-permute-done.up_ref), channel_id=1, source_target_pairs={{0,2},{2,4},{4,6},{6,7},{7,5},{5,3},{3,1},{1,0},{8,10},{10,12},{12... | collective-permute-start | bytes 1769480 | tf_op jit(solution)/shard_map/ppermute | solution.py:373
  33.9 15.8 %collective-permute-start.3 = (bf16[2,64,2304]{2,1,0:T(8,128)(2,1)S(1)}, bf16[2,64,2304]{2,1,0:T(8,128)(2,1)S(1)}, u32[]{:S(2)}, u32[]{:S(2)}) collective-permute-start(bf16[2,64,2304]{2,1,0:T(8,128)(2,1)S(1)} %collective-permute-done.2.down_ref), channel_id=1, source_target_pairs={{2,0},{4,2},{6,4},{7,6},{5,7},{3,5},{1,3},{0,1},{10,8},{12,10},{14... | collective-permute-start | bytes 1769480 | tf_op jit(solution)/shard_map/ppermute | solution.py:374
  34.8 14.9 %collective-permute-start.10 = (bf16[64,1792]{1,0:T(8,128)(2,1)S(1)}, bf16[64,1792]{1,0:T(8,128)(2,1)S(1)}, u32[]{:S(2)}, u32[]{:S(2)}) collective-permute-start(bf16[64,1792]{1,0:T(8,128)(2,1)S(1)} %constant_dynamic-update-slice_fusion.refs_0_), channel_id=1, source_target_pairs={{0,8},{8,0},{16,24},{24,16},{1,9},{9,1},{17,25},{25,17},{2,10},{10... | collective-permute-start | bytes 688136 | tf_op jit(solution)/shard_map/ppermute | solution.py:354
  40.5 9.2 %collective-permute-start.12 = (bf16[64,1792]{1,0:T(8,128)(2,1)S(1)}, bf16[64,1792]{1,0:T(8,128)(2,1)S(1)}, u32[]{:S(2)}, u32[]{:S(2)}) collective-permute-start(bf16[64,1792]{1,0:T(8,128)(2,1)S(1)} %collective-permute-done.11.refs_2_), channel_id=1, source_target_pairs={{0,8},{8,0},{16,24},{24,16},{1,9},{9,1},{17,25},{25,17},{2,10},{10... | collective-permute-start | bytes 688136 | tf_op jit(solution)/shard_map/ppermute | solution.py:354
  49.7 15.8 %collective-permute-start.6 = (bf16[2,64,2304]{2,1,0:T(8,128)(2,1)S(1)}, bf16[2,64,2304]{2,1,0:T(8,128)(2,1)S(1)}, u32[]{:S(2)}, u32[]{:S(2)}) collective-permute-start(bf16[2,64,2304]{2,1,0:T(8,128)(2,1)S(1)} %collective-permute-done.1.refs_0_), channel_id=1, source_target_pairs={{0,2},{2,4},{4,6},{6,7},{7,5},{5,3},{3,1},{1,0},{8,10},{10,12},{12... | collective-permute-start | bytes 1769480 | tf_op jit(solution)/shard_map/ppermute | solution.py:373
  50.6 15.8 %collective-permute-start.8 = (bf16[2,64,2304]{2,1,0:T(8,128)(2,1)S(1)}, bf16[2,64,2304]{2,1,0:T(8,128)(2,1)S(1)}, u32[]{:S(2)}, u32[]{:S(2)}) collective-permute-start(bf16[2,64,2304]{2,1,0:T(8,128)(2,1)S(1)} %collective-permute-done.3.refs_1_), channel_id=1, source_target_pairs={{2,0},{4,2},{6,4},{7,6},{5,7},{3,5},{1,3},{0,1},{10,8},{12,10},{14... | collective-permute-start | bytes 1769480 | tf_op jit(solution)/shard_map/ppermute | solution.py:374
  65.5 10.4 %collective-permute-start.7 = (bf16[64,2304]{1,0:T(8,128)(2,1)S(1)}, bf16[64,2304]{1,0:T(8,128)(2,1)S(1)}, u32[]{:S(2)}, u32[]{:S(2)}) collective-permute-start(bf16[64,2304]{1,0:T(8,128)(2,1)S(1)} %slice_bitcast_fusion.1), channel_id=1, source_target_pairs={{0,2},{2,4},{4,6},{6,7},{7,5},{5,3},{3,1},{1,0},{8,10},{10,12},{12... | collective-permute-start | bytes 884744 | tf_op jit(solution)/shard_map/ppermute | solution.py:378
  66.4 9.5 %copy-start = (bf16[2,64,2304]{2,1,0:T(8,128)(2,1)S(1)}, bf16[2,64,2304]{2,1,0:T(8,128)(2,1)}, u32[]{:S(2)}) copy-start(bf16[2,64,2304]{2,1,0:T(8,128)(2,1)} %refs_0_.1) | copy-start | bytes 1769476
  66.4 9.5 %collective-permute-start.9 = (bf16[64,2304]{1,0:T(8,128)(2,1)S(1)}, bf16[64,2304]{1,0:T(8,128)(2,1)S(1)}, u32[]{:S(2)}, u32[]{:S(2)}) collective-permute-start(bf16[64,2304]{1,0:T(8,128)(2,1)S(1)} %slice_bitcast_fusion), channel_id=1, source_target_pairs={{2,0},{4,2},{6,4},{7,6},{5,7},{3,5},{1,3},{0,1},{10,8},{12,10},{14... | collective-permute-start | bytes 884744 | tf_op jit(solution)/shard_map/ppermute | solution.py:379
  83.9 3.8 %collective-permute-start.13 = (f32[3,8,128]{2,1,0:T(8,128)S(1)}, f32[3,8,128]{2,1,0:T(8,128)S(1)}, u32[]{:S(2)}, u32[]{:S(2)}) collective-permute-start(f32[3,8,128]{2,1,0:T(8,128)S(1)} %chunk.5.refs_0_), channel_id=1, source_target_pairs={{0,1},{1,0},{2,3},{3,2},{4,5},{5,4},{6,7},{7,6},{8,9},{9,8},{10,11... | collective-permute-start | bytes 36872 | tf_op jit(solution)/shard_map/ppermute | solution.py:354
  87.7 5.6 %collective-permute-start.16 = (f32[3,8,128]{2,1,0:T(8,128)S(1)}, f32[3,8,128]{2,1,0:T(8,128)S(1)}, u32[]{:S(2)}, u32[]{:S(2)}) collective-permute-start(f32[3,8,128]{2,1,0:T(8,128)S(1)} %combine.2.refs_0_), channel_id=1, source_target_pairs={{0,6},{1,7},{2,4},{3,5},{4,2},{5,3},{6,0},{7,1},{8,14},{9,15},{10,... | collective-permute-start | bytes 36872 | tf_op jit(solution)/shard_map/ppermute | solution.py:354
  90.9 4.6 %collective-permute-start.15 = (f32[3,8,128]{2,1,0:T(8,128)S(1)}, f32[3,8,128]{2,1,0:T(8,128)S(1)}, u32[]{:S(2)}, u32[]{:S(2)}) collective-permute-start(f32[3,8,128]{2,1,0:T(8,128)S(1)} %combine.2.refs_0_), channel_id=1, source_target_pairs={{0,4},{1,5},{2,6},{3,7},{4,0},{5,1},{6,2},{7,3},{8,12},{9,13},{10,... | collective-permute-start | bytes 36872 | tf_op jit(solution)/shard_map/ppermute | solution.py:354
  90.9 4.6 %collective-permute-start.14 = (f32[3,8,128]{2,1,0:T(8,128)S(1)}, f32[3,8,128]{2,1,0:T(8,128)S(1)}, u32[]{:S(2)}, u32[]{:S(2)}) collective-permute-start(f32[3,8,128]{2,1,0:T(8,128)S(1)} %combine.2.refs_0_), channel_id=1, source_target_pairs={{0,2},{1,3},{2,0},{3,1},{4,6},{5,7},{6,4},{7,5},{8,10},{9,11},{10,... | collective-permute-start | bytes 36872 | tf_op jit(solution)/shard_map/ppermute | solution.py:354

commit v8 on v7

--- a/solution.py
+++ b/solution.py
@@ -25,7 +25,7 @@
 
 def tile_rows(entries):
     for rows in (512, 256, 128, 64, 32, 16):
-        if entries % (4 * rows) == 0:
+        if entries % (2 * rows) == 0:
             return rows
     raise ValueError(entries)
 
@@ -44,14 +44,15 @@
         group = lax.axis_index("group")
         voc = lax.axis_index("vocab")
         for k in range(n_group):
-            member = group ^ k ^ lax.rem(voc // per, n_group)
-            start = pl.multiple_of(member * u_rows, u_rows)
+            member = group ^ k
+            block = member ^ lax.rem(voc // per, n_group)
+            start = pl.multiple_of(block * u_rows, u_rows)
             u_out[pl.ds(start, u_rows), :] = packs[k][:, :u_rows].T
             for t in range(per):
-                shard = n_group * (lax.rem(voc, per) ^ t) + member
+                shard = member * per + (lax.rem(voc, per) ^ t)
                 at = u_rows + t * wide
-                block = packs[k][:, at : at + wide].astype(jnp.float32).T
-                v_wide[pl.ds(pl.multiple_of(shard * v_rows, 8), v_rows), :] = block[:v_rows]
+                rows = packs[k][:, at : at + wide].astype(jnp.float32).T
+                v_wide[pl.ds(pl.multiple_of(shard * v_rows, 8), v_rows), :] = rows[:v_rows]
         v_out[...] = v_wide[...].T.astype(jnp.bfloat16)
         for k in range(n_voc):
             for s in range(2):
@@ -89,21 +90,16 @@
         at += block.shape[0]
 
 
-def fetch_rows(head_ref, first, held, sems, parts=8):
-    part = held.shape[0] // parts
-    return [
-        pltpu.make_async_copy(
-            head_ref.at[pl.ds(first + t * part, part), :],
-            held.at[pl.ds(t * part, part), :],
-            sems.at[t],
-        )
-        for t in range(parts)
-    ]
-
-
 def make_load(depth, entries):
+    parts = 16 if entries % 4096 == 0 else 1
+    part = entries // parts
+
     def kernel(head_ref, held, sems):
-        copies = fetch_rows(head_ref, 0, held, sems)
+        spans = [pl.ds(t * part, part) for t in range(parts)]
+        copies = [
+            pltpu.make_async_copy(head_ref.at[span, :], held.at[span, :], sems.at[t])
+            for t, span in enumerate(spans)
+        ]
         for t, copy in enumerate(copies):
             copy.start(priority=t % 2)
         for copy in copies:
@@ -111,13 +107,13 @@
 
     return pl.pallas_call(
         kernel,
-        out_shape=jax.ShapeDtypeStruct((entries // 2, depth), jnp.bfloat16),
+        out_shape=jax.ShapeDtypeStruct((entries, depth), jnp.bfloat16),
         in_specs=[pl.BlockSpec(memory_space=pltpu.HBM)],
         out_specs=WHOLE,
-        scratch_shapes=[pltpu.SemaphoreType.DMA((8,))],
-        compiler_params=pltpu.CompilerParams(vmem_limit_bytes=40 * MIB),
+        scratch_shapes=[pltpu.SemaphoreType.DMA((parts,))],
+        compiler_params=pltpu.CompilerParams(vmem_limit_bytes=32 * MIB),
         cost_estimate=pl.CostEstimate(
-            flops=0, bytes_accessed=depth * entries, transcendentals=0
+            flops=0, bytes_accessed=2 * depth * entries, transcendentals=0
         ),
         name="load",
     )
@@ -125,39 +121,27 @@
 
 def make_base(r, depth, entries):
     n = 4 * r
-    half = entries // 2
-    tile = 2 * half // 8
-
-    def kernel(up_ref, down_ref, head_ref, low, base_ref, rows, high, sems):
-        copies = fetch_rows(head_ref, half, high, sems)
-        for t, copy in enumerate(copies):
-            copy.start(priority=t % 2)
+    tile = tile_rows(entries)
+
+    def kernel(up_ref, down_ref, head_ref, base_ref, rows):
         load_rows(rows, (up_ref, down_ref))
 
-        def multiply(i, held, first):
+        @pl.loop(0, entries // tile)
+        def _(i):
             span = pl.ds(pl.multiple_of(i * tile, tile), tile)
-            at = pl.ds(pl.multiple_of(first + i * tile, tile), tile)
-            base_ref[at, :] = jnp.dot(
-                held[span, :], rows[...], preferred_element_type=jnp.float32
+            base_ref[span, :] = jnp.dot(
+                head_ref[span, :], rows[...], preferred_element_type=jnp.float32
             )
-
-        pl.loop(0, half // tile)(lambda i: multiply(i, low, 0))
-        for i in range(half // tile):
-            for copy in copies[2 * i : 2 * i + 2]:
-                copy.wait()
-            multiply(i, high, half)
 
     return pl.pallas_call(
         kernel,
         out_shape=(
             jax.ShapeDtypeStruct((entries, n), jnp.float32),
             jax.ShapeDtypeStruct((depth, n), jnp.bfloat16),
-            jax.ShapeDtypeStruct((half, depth), jnp.bfloat16),
         ),
-        in_specs=[WHOLE, WHOLE, pl.BlockSpec(memory_space=pltpu.HBM), WHOLE],
-        out_specs=(WHOLE,) * 3,
-        scratch_shapes=[pltpu.SemaphoreType.DMA((8,))],
-        compiler_params=pltpu.CompilerParams(vmem_limit_bytes=24 * MIB),
+        in_specs=[WHOLE] * 3,
+        out_specs=(WHOLE,) * 2,
+        compiler_params=pltpu.CompilerParams(vmem_limit_bytes=8 * MIB),
         cost_estimate=pl.CostEstimate(
             flops=2 * n * entries * depth,
             bytes_accessed=2 * entries * depth,
@@ -176,7 +160,7 @@
 
     def kernel(*refs):
         piece, refs = refs[:pieces], refs[pieces:]
-        low_ref, high_ref, u_ref, v_ref, want_ref, *refs = refs
+        head_ref, u_ref, v_ref, want_ref, *refs = refs
         if carry:
             base_ref, base_rows, *refs = refs
         before, refs = refs[:earlier], refs[earlier:]
@@ -213,11 +197,10 @@
             clear(*base_state)
             base_want = wanted(1)
 
-        def multiply(t, into, head_ref, first):
+        def multiply(t, into):
             span = pl.ds(pl.multiple_of(t * tile, tile), tile)
-            at = pl.ds(pl.multiple_of((t - first) * tile, tile), tile)
             into[...] = jnp.dot(
-                head_ref[at, :], rows[...], preferred_element_type=jnp.float32
+                head_ref[span, :], rows[...], preferred_element_type=jnp.float32
             ) + jnp.dot(u_ref[span, :], proj[...], preferred_element_type=jnp.float32)
 
         def reduce(x, want, top, total, pick):
@@ -239,16 +222,14 @@
                 )
                 reduce(x, base_want - t * tile, *base_state)
 
-        def step(i, head_ref, first):
-            multiply(2 * i, even, head_ref, first)
+        @pl.loop(0, tiles // 2)
+        def _(i):
+            multiply(2 * i, even)
             reduce(odd[...], want - jnp.where(i == 0, 1 << 29, (2 * i - 1) * tile), *state)
             finish_base(2 * i)
-            multiply(2 * i + 1, odd, head_ref, first)
+            multiply(2 * i + 1, odd)
             reduce(even[...], want - 2 * i * tile, *state)
             finish_base(2 * i + 1)
-
-        pl.loop(0, tiles // 4)(lambda i: step(i, low_ref, 0))
-        pl.loop(tiles // 4, tiles // 2)(lambda i: step(i, high_ref, tiles // 2))
 
         reduce(odd[...], want - (entries - tile), *state)
 
@@ -276,7 +257,7 @@
     return pl.pallas_call(
         kernel,
         out_shape=(out_shape, out_shape) if carry else out_shape,
-        in_specs=[WHOLE] * (pieces + 5 + 2 * carry + earlier),
+        in_specs=[WHOLE] * (pieces + 4 + 2 * carry + earlier),
         out_specs=(WHOLE, WHOLE) if carry else WHOLE,
         scratch_shapes=[
             pltpu.VMEM((depth, n), jnp.bfloat16),
@@ -354,21 +335,24 @@
         return lax.ppermute(x, axis, [(i, i ^ bit) for i in range(size)])
 
     u_rows, v_rows = factor_u.shape[0], factor_v.shape[0]
-    shard = jnp.pad(factor_v.T, ((0, 0), (0, padded(v_rows) - v_rows)))
-    taken = []
+    everyone = [(g, v) for g in range(n_group) for v in range(n_voc)]
+    moves = [
+        (v * n_group + (g ^ (v // per) % n_group), g * n_voc + v) for g, v in everyone
+    ]
+    block = lax.ppermute(factor_u.T, ("group", "vocab"), moves)
+    shards = []
     for t in range(per):
-        sent = shard if t else jnp.concatenate([factor_u.T, shard], axis=1)
         moves = [
-            ((v ^ t) * n_group + (g ^ (v // per) % n_group), g * n_voc + v)
-            for v in range(n_voc)
-            for g in range(n_group)
+            ((v // per) % n_group * n_voc + g * per + (v % per ^ t), g * n_voc + v)
+            for g, v in everyone
         ]
-        taken.append(lax.ppermute(sent, ("group", "vocab"), moves))
-
+        shards.append(lax.ppermute(factor_v.T, ("group", "vocab"), moves))
+
+    hidden, *shards = lax.optimization_barrier((hidden, *shards))
     up = [hidden, lax.ppermute(hidden, "vocab", ahead)]
     down = [hidden, lax.ppermute(hidden, "vocab", behind)]
-    low, *taken = lax.optimization_barrier((make_load(depth, entries)(head), *taken))
-    base, base_rows, high = make_base(r, depth, entries)(up[1], down[1], head, low)
+    head, block = lax.optimization_barrier((make_load(depth, entries)(head), block))
+    base, base_rows = make_base(r, depth, entries)(up[1], down[1], head)
     for hop in range(2, half):
         up.append(lax.ppermute(up[-1], "vocab", ahead))
         down.append(lax.ppermute(down[-1], "vocab", behind))
@@ -378,7 +362,8 @@
         lax.ppermute(up[-1][0], "vocab", ahead),
         lax.ppermute(down[-1][1], "vocab", behind),
     ]
-    packs = {0: jnp.concatenate(taken, axis=1)}
+    gap = ((0, 0), (0, padded(v_rows) - v_rows))
+    packs = {0: jnp.concatenate([block] + [jnp.pad(x, gap) for x in shards], axis=1)}
     bit = n_group // 2
     while bit:
         for k in list(packs):
@@ -393,7 +378,7 @@
         pieces = [up[hop], down[hop]] if hop < half else [hidden] + ends
         extra = [base, base_rows] if hop == 2 else stats if hop == half else []
         chunk = make_chunk(hop, len(pieces), r, depth, entries, rank, n_voc)
-        out = chunk(*pieces, low, high, full_u, full_v, want, *extra)
+        out = chunk(*pieces, head, full_u, full_v, want, *extra)
         stats += [out[1], out[0]] if hop == 2 else [out]
     part = stats[-1]
     low = 1

time: 96.4 us -> 96.9 us (level)
  starting transfers between devices: 21.1 us -> 38.1 us
  waiting for transfers between devices: 34 us -> 18.8 us
    ppermute x2 -> x3, waiting for transfers between devices: 17.1 us -> 0.84 us  [the longest x2 0.84 us: body(): shards.append(lax.ppermute(factor_v.T, ('group', 'vocab'), moves))]
    ppermute x7, starting transfers between devices: 5.4 us -> 20.6 us  [trade(): return lax.ppermute(x, axis, [(i, i ^ bit) for i in range(size)])]
    ppermute x1, starting transfers between devices: 5.72 us -> 2.09 us  [body(): up = [hidden, lax.ppermute(hidden, 'vocab', ahead)]]
    ppermute x2, waiting for transfers between devices: 0.57 us -> 4.16 us  [body(): down.append(lax.ppermute(down[-1], 'vocab', behind))]
    pallas_call x1, Pallas kernels: 3.83 us -> 6.61 us  [body(): make_load(depth, entries)(head)]
    ppermute x1, starting transfers between devices: 0.01 us -> 2.55 us  [body(): down = [hidden, lax.ppermute(hidden, 'vocab', behind)]]
    ppermute x2 -> x3, starting transfers between devices: 3.54 us -> 6 us  [the longest x2 4.45 us: body(): shards.append(lax.ppermute(factor_v.T, ('group', 'vocab'), moves))]
    pallas_call x4, Pallas kernels: 33.1 us -> 30.8 us  [the longest x3 24.2 us: body(): out = chunk(*pieces, head, full_u, full_v, want, *extra)]
  transfers between devices with their start and end apart: 17 -> 18, of which waited for: 7 -> 9; matrix products, arithmetic and copies ran while one was open for 0% -> 0% of each run, Pallas kernels for 31% -> 31%
where the time goes in v8:
time: 96.9 us; the launch traced here: 96.7 us
  Pallas kernels  39 us (40%)
  starting transfers between devices  38.1 us (39%)
  waiting for transfers between devices  18.8 us (19%)
    pallas_call x3, Pallas kernels, body(): out = chunk(*pieces, head, full_u, full_v, want, *extra)  24.2 us
    ppermute x7, starting transfers between devices, trade(): return lax.ppermute(x, axis, [(i, i ^ bit) for i in range(size)])  20.6 us
    ppermute x7, waiting for transfers between devices, trade(): return lax.ppermute(x, axis, [(i, i ^ bit) for i in range(size)])  10.7 us
    pallas_call x1, Pallas kernels, body(): make_load(depth, entries)(head)  6.61 us
    pallas_call x1, Pallas kernels, body(): base, base_rows = make_base(r, depth, entries)(up[1], down[1], head)  6.57 us
    ppermute x2, starting transfers between devices, body(): shards.append(lax.ppermute(factor_v.T, ('group', 'vocab'), moves))  4.45 us
    ppermute x2, waiting for transfers between devices, body(): down.append(lax.ppermute(down[-1], 'vocab', behind))  4.16 us
    ppermute x2, waiting for transfers between devices, body(): up.append(lax.ppermute(up[-1], 'vocab', ahead))  3.11 us
  transfers between devices with their start and end apart: 18, of which 9 were waited for; matrix products, arithmetic and copies ran while one was open for 0% of the time, Pallas kernels for 31%

profile of v8, /device:TPU:0, one launch (start us, length us, event | category | flops | bytes accessed | tf_op | source)
XLA Modules:
  0.0 96.7 jit_solution(505380318610921546)
XLA Ops:
  0.6 3.0 %collective-permute-start.1 = (bf16[64,288]{1,0:T(8,128)(2,1)}, bf16[64,288]{1,0:T(8,128)(2,1)S(1)}, u32[]{:S(2)}, u32[]{:S(2)}) collective-permute-start(bf16[64,288]{1,0:T(8,128)(2,1)} %bitcast.7), channel_id=1, source_target_pairs={{1,0},{0,1},{9,2},{8,3},{17,4},{16,5},{25,6},{24,7},{3,8},{2,9},{1... | collective-permute-start | bytes 110600 | tf_op jit(solution)/shard_map/ppermute | solution.py:349
  3.6 1.4 %collective-permute-start = (bf16[64,288]{1,0:T(8,128)(2,1)}, bf16[64,288]{1,0:T(8,128)(2,1)S(1)}, u32[]{:S(2)}, u32[]{:S(2)}) collective-permute-start(bf16[64,288]{1,0:T(8,128)(2,1)} %bitcast.8), channel_id=1, source_target_pairs={{0,0},{1,1},{8,2},{9,3},{16,4},{17,5},{24,6},{25,7},{2,8},{3,9},{1... | collective-permute-start | bytes 110600 | tf_op jit(solution)/shard_map/ppermute | solution.py:349
  5.1 0.8 collective-permute-done.1
  5.9 0.0 collective-permute-done
  5.9 2.5 %collective-permute-start.4 = (bf16[2,64,2304]{2,1,0:T(8,128)(2,1)}, bf16[2,64,2304]{2,1,0:T(8,128)(2,1)S(1)}, u32[]{:S(2)}, u32[]{:S(2)}) collective-permute-start(bf16[2,64,2304]{2,1,0:T(8,128)(2,1)} %refs_0_), channel_id=1, source_target_pairs={{2,0},{4,2},{6,4},{7,6},{5,7},{3,5},{1,3},{0,1},{10,8},{12,10},{14... | collective-permute-start | bytes 1769480 | tf_op jit(solution)/shard_map/ppermute | solution.py:353
  8.5 2.1 %collective-permute-start.2 = (bf16[2,64,2304]{2,1,0:T(8,128)(2,1)}, bf16[2,64,2304]{2,1,0:T(8,128)(2,1)S(1)}, u32[]{:S(2)}, u32[]{:S(2)}) collective-permute-start(bf16[2,64,2304]{2,1,0:T(8,128)(2,1)} %refs_0_), channel_id=1, source_target_pairs={{0,2},{2,4},{4,6},{6,7},{7,5},{5,3},{3,1},{1,0},{8,10},{10,12},{12... | collective-permute-start | bytes 1769480 | tf_op jit(solution)/shard_map/ppermute | solution.py:352
  10.6 1.6 %collective-permute-start.6 = (bf16[64,1024]{1,0:T(8,128)(2,1)}, bf16[64,1024]{1,0:T(8,128)(2,1)S(1)}, u32[]{:S(2)}, u32[]{:S(2)}) collective-permute-start(bf16[64,1024]{1,0:T(8,128)(2,1)} %bitcast.6), channel_id=1, source_target_pairs={{0,0},{4,1},{9,2},{13,3},{18,4},{22,5},{27,6},{31,7},{1,8},{5,9},{... | collective-permute-start | bytes 393224 | tf_op jit(solution)/shard_map/ppermute | solution.py:342
  12.1 6.6 %load.1.head_ref.refs_2_.refs_3_ = bf16[4096,2304]{1,0:T(8,128)(2,1)S(1)} custom-call(bf16[4096,2304]{1,0:T(8,128)(2,1)} %head_ref.1), custom_call_target="tpu_custom_call" | custom-call | bytes 18874368 | tf_op jit(solution)/shard_map/load/pallas_call | solution.py:354
  18.7 0.0 copy-start.1
  18.7 0.0 collective-permute-done.6
  18.8 15.5 %collective-permute-start.12 = (bf16[64,1792]{1,0:T(8,128)(2,1)S(1)}, bf16[64,1792]{1,0:T(8,128)(2,1)S(1)}, u32[]{:S(2)}, u32[]{:S(2)}) collective-permute-start(bf16[64,1792]{1,0:T(8,128)(2,1)S(1)} %fusion.4.refs_0_), channel_id=1, source_target_pairs={{0,16},{8,24},{16,0},{24,8},{1,17},{9,25},{17,1},{25,9},{2,18},{10... | collective-permute-start | bytes 688136 | tf_op jit(solution)/shard_map/ppermute | solution.py:335
  34.3 0.0 collective-permute-done.4.down_ref
  34.3 1.9 %collective-permute-start.5 = (bf16[2,64,2304]{2,1,0:T(8,128)(2,1)S(1)}, bf16[2,64,2304]{2,1,0:T(8,128)(2,1)S(1)}, u32[]{:S(2)}, u32[]{:S(2)}) collective-permute-start(bf16[2,64,2304]{2,1,0:T(8,128)(2,1)S(1)} %collective-permute-done.4.down_ref), channel_id=1, source_target_pairs={{2,0},{4,2},{6,4},{7,6},{5,7},{3,5},{1,3},{0,1},{10,8},{12,10},{14... | collective-permute-start | bytes 1769480 | tf_op jit(solution)/shard_map/ppermute | solution.py:358
  36.2 0.0 collective-permute-done.2.up_ref
  36.2 0.8 collective-permute-start.3
  37.0 0.0 collective-permute-start.11
  37.0 3.3 %collective-permute-done.12.refs_2_ = bf16[64,1792]{1,0:T(8,128)(2,1)S(1)} collective-permute-done((bf16[64,1792]{1,0:T(8,128)(2,1)S(1)}, bf16[64,1792]{1,0:T(8,128)(2,1)S(1)}, u32[]{:S(2)}, u32[]{:S(2)}) %collective-permute-start.12) | collective-permute-done | bytes 229408 | tf_op jit(solution)/shard_map/ppermute | solution.py:335
  40.3 0.0 collective-permute-start.13
  40.3 6.6 %base.1 = (f32[4096,256]{1,0:T(8,128)S(1)}, bf16[2304,256]{1,0:T(8,128)(2,1)S(1)}) custom-call(bf16[2,64,2304]{2,1,0:T(8,128)(2,1)S(1)} %collective-permute-done.2.up_ref, bf16[2,64,2304]{2,1,0:T(8,128)(2,1)S(1)} %collective-permute-done.4.down_ref, bf16[4096,2304]{1,0:T(8,128)(2,1)S(1)} %load.1.head_ref.refs_2_.refs_3_), custom_call_target="tpu_custom_call" | custom-call | flops 4831838208 | bytes 18874368 | tf_op jit(solution)/shard_map/base/pallas_call | solution.py:355
  46.8 3.6 %collective-permute-done.5.refs_1_ = bf16[2,64,2304]{2,1,0:T(8,128)(2,1)S(1)} collective-permute-done((bf16[2,64,2304]{2,1,0:T(8,128)(2,1)S(1)}, bf16[2,64,2304]{2,1,0:T(8,128)(2,1)S(1)}, u32[]{:S(2)}, u32[]{:S(2)}) %collective-permute-start.5) | collective-permute-done | bytes 589856 | tf_op jit(solution)/shard_map/ppermute | solution.py:358
  50.5 0.2 collective-permute-done.3.refs_0_
  50.7 1.6 %collective-permute-start.7 = (bf16[2,64,2304]{2,1,0:T(8,128)(2,1)S(1)}, bf16[2,64,2304]{2,1,0:T(8,128)(2,1)S(1)}, u32[]{:S(2)}, u32[]{:S(2)}) collective-permute-start(bf16[2,64,2304]{2,1,0:T(8,128)(2,1)S(1)} %collective-permute-done.3.refs_0_), channel_id=1, source_target_pairs={{0,2},{2,4},{4,6},{6,7},{7,5},{5,3},{3,1},{1,0},{8,10},{10,12},{12... | collective-permute-start | bytes 1769480 | tf_op jit(solution)/shard_map/ppermute | solution.py:357
  52.3 0.0 collective-permute-done.11.refs_1_
  52.3 0.0 collective-permute-done.13.refs_3_
  52.3 0.0 copy-done.1
  52.3 0.8 assemble.1
  53.1 0.5 collective-permute-start.9
  53.6 0.0 copy-start
  53.6 8.8 %chunk.3 = (f32[3,256]{1,0:T(4,128)S(1)}, f32[3,256]{1,0:T(4,128)S(1)}) custom-call(bf16[2,64,2304]{2,1,0:T(8,128)(2,1)S(1)} %collective-permute-done.3.refs_0_, bf16[2,64,2304]{2,1,0:T(8,128)(2,1)S(1)} %collective-permute-done.5.refs_1_, bf16[4096,2304]{1,0:T(8,128)(2,1)S(1)} %load.1.head_ref.refs_2_.refs_3_, ...), custom_call_target="tpu_custom_call" | custom-call | flops 5368709120 | bytes 19922944 | tf_op jit(solution)/shard_map/chunk/pallas_call | solution.py:381
  62.4 2.9 %collective-permute-done.7.refs_0_ = bf16[2,64,2304]{2,1,0:T(8,128)(2,1)S(1)} collective-permute-done((bf16[2,64,2304]{2,1,0:T(8,128)(2,1)S(1)}, bf16[2,64,2304]{2,1,0:T(8,128)(2,1)S(1)}, u32[]{:S(2)}, u32[]{:S(2)}) %collective-permute-start.7) | collective-permute-done | bytes 589856 | tf_op jit(solution)/shard_map/ppermute | solution.py:357
  65.3 1.5 %collective-permute-start.8 = (bf16[64,2304]{1,0:T(8,128)(2,1)S(1)}, bf16[64,2304]{1,0:T(8,128)(2,1)S(1)}, u32[]{:S(2)}, u32[]{:S(2)}) collective-permute-start(bf16[64,2304]{1,0:T(8,128)(2,1)S(1)} %slice_bitcast_fusion.1), channel_id=1, source_target_pairs={{0,2},{2,4},{4,6},{6,7},{7,5},{5,3},{3,1},{1,0},{8,10},{10,12},{12... | collective-permute-start | bytes 884744 | tf_op jit(solution)/shard_map/ppermute | solution.py:362
  66.8 0.5 collective-permute-done.9.refs_1_
  67.4 0.6 collective-permute-start.10
  68.0 7.5 %chunk.4.refs_9_ = f32[3,256]{1,0:T(4,128)S(1)} custom-call(bf16[2,64,2304]{2,1,0:T(8,128)(2,1)S(1)} %collective-permute-done.7.refs_0_, bf16[2,64,2304]{2,1,0:T(8,128)(2,1)S(1)} %collective-permute-done.9.refs_1_, bf16[4096,2304]{1,0:T(8,128)(2,1)S(1)} %load.1.head_ref.refs_2_.refs_3_, bf16[4096,64]{1,0:T(8,128)(2,1)S(1)} %get-tuple-element.25.refs_3_.refs_4_, ...), custom_call_target="tpu_custom_call" | custom-call | flops 5368709120 | bytes 19922944 | tf_op jit(solution)/shard_map/chunk/pallas_call | solution.py:381
  75.4 0.0 collective-permute-done.8.refs_1_
  75.5 0.0 collective-permute-done.10.refs_2_
  75.5 0.0 copy-done
  75.5 8.0 %chunk.5.refs_0_ = f32[3,8,128]{2,1,0:T(8,128)S(1)} custom-call(bf16[2,64,2304]{2,1,0:T(8,128)(2,1)S(1)} %copy-done, bf16[64,2304]{1,0:T(8,128)(2,1)S(1)} %collective-permute-done.8.refs_1_, bf16[64,2304]{1,0:T(8,128)(2,1)S(1)} %collective-permute-done.10.refs_2_, bf16[4096,2304]{1,0:T(8,128)(2,1)S(1)} %load.1.head_ref.refs_2_.refs_3_, ...), custom_call_target="tpu_custom_call" | custom-call | flops 5368709120 | bytes 19922944 | tf_op jit(solution)/shard_map/chunk/pallas_call | solution.py:381
  83.5 0.3 collective-permute-start.14
  83.9 3.4 %collective-permute-done.14.refs_1_ = f32[3,8,128]{2,1,0:T(8,128)S(1)} collective-permute-done((f32[3,8,128]{2,1,0:T(8,128)S(1)}, f32[3,8,128]{2,1,0:T(8,128)S(1)}, u32[]{:S(2)}, u32[]{:S(2)}) %collective-permute-start.14) | collective-permute-done | bytes 12320 | tf_op jit(solution)/shard_map/ppermute | solution.py:335
  87.3 4.1 %collective-permute-start.17 = (f32[3,8,128]{2,1,0:T(8,128)S(1)}, f32[3,8,128]{2,1,0:T(8,128)S(1)}, u32[]{:S(2)}, u32[]{:S(2)}) collective-permute-start(f32[3,8,128]{2,1,0:T(8,128)S(1)} %combine.2.refs_0_), channel_id=1, source_target_pairs={{0,6},{1,7},{2,4},{3,5},{4,2},{5,3},{6,0},{7,1},{8,14},{9,15},{10,... | collective-permute-start | bytes 36872 | tf_op jit(solution)/shard_map/ppermute | solution.py:335
  91.4 0.0 collective-permute-start.16
  91.4 0.6 collective-permute-start.15
  92.0 1.0 %collective-permute-done.17.refs_3_ = f32[3,8,128]{2,1,0:T(8,128)S(1)} collective-permute-done((f32[3,8,128]{2,1,0:T(8,128)S(1)}, f32[3,8,128]{2,1,0:T(8,128)S(1)}, u32[]{:S(2)}, u32[]{:S(2)}) %collective-permute-start.17) | collective-permute-done | bytes 12320 | tf_op jit(solution)/shard_map/ppermute | solution.py:335
  93.1 2.9 %collective-permute-done.16.refs_2_ = f32[3,8,128]{2,1,0:T(8,128)S(1)} collective-permute-done((f32[3,8,128]{2,1,0:T(8,128)S(1)}, f32[3,8,128]{2,1,0:T(8,128)S(1)}, u32[]{:S(2)}, u32[]{:S(2)}) %collective-permute-start.16) | collective-permute-done | bytes 12320 | tf_op jit(solution)/shard_map/ppermute | solution.py:335
  96.0 0.0 collective-permute-done.15.refs_1_
  96.0 0.7 combine.3
  (4 shorter events, 0.1 us)
Async XLA Ops:
  0.6 5.3 %collective-permute-start.1 = (bf16[64,288]{1,0:T(8,128)(2,1)}, bf16[64,288]{1,0:T(8,128)(2,1)S(1)}, u32[]{:S(2)}, u32[]{:S(2)}) collective-permute-start(bf16[64,288]{1,0:T(8,128)(2,1)} %bitcast.7), channel_id=1, source_target_pairs={{1,0},{0,1},{9,2},{8,3},{17,4},{16,5},{25,6},{24,7},{3,8},{2,9},{1... | collective-permute-start | bytes 110600 | tf_op jit(solution)/shard_map/ppermute | solution.py:349
  3.6 2.3 %collective-permute-start = (bf16[64,288]{1,0:T(8,128)(2,1)}, bf16[64,288]{1,0:T(8,128)(2,1)S(1)}, u32[]{:S(2)}, u32[]{:S(2)}) collective-permute-start(bf16[64,288]{1,0:T(8,128)(2,1)} %bitcast.8), channel_id=1, source_target_pairs={{0,0},{1,1},{8,2},{9,3},{16,4},{17,5},{24,6},{25,7},{2,8},{3,9},{1... | collective-permute-start | bytes 110600 | tf_op jit(solution)/shard_map/ppermute | solution.py:349
  5.9 28.3 %collective-permute-start.4 = (bf16[2,64,2304]{2,1,0:T(8,128)(2,1)}, bf16[2,64,2304]{2,1,0:T(8,128)(2,1)S(1)}, u32[]{:S(2)}, u32[]{:S(2)}) collective-permute-start(bf16[2,64,2304]{2,1,0:T(8,128)(2,1)} %refs_0_), channel_id=1, source_target_pairs={{2,0},{4,2},{6,4},{7,6},{5,7},{3,5},{1,3},{0,1},{10,8},{12,10},{14... | collective-permute-start | bytes 1769480 | tf_op jit(solution)/shard_map/ppermute | solution.py:353
  8.5 27.7 %collective-permute-start.2 = (bf16[2,64,2304]{2,1,0:T(8,128)(2,1)}, bf16[2,64,2304]{2,1,0:T(8,128)(2,1)S(1)}, u32[]{:S(2)}, u32[]{:S(2)}) collective-permute-start(bf16[2,64,2304]{2,1,0:T(8,128)(2,1)} %refs_0_), channel_id=1, source_target_pairs={{0,2},{2,4},{4,6},{6,7},{7,5},{5,3},{3,1},{1,0},{8,10},{10,12},{12... | collective-permute-start | bytes 1769480 | tf_op jit(solution)/shard_map/ppermute | solution.py:352
  10.6 8.2 %collective-permute-start.6 = (bf16[64,1024]{1,0:T(8,128)(2,1)}, bf16[64,1024]{1,0:T(8,128)(2,1)S(1)}, u32[]{:S(2)}, u32[]{:S(2)}) collective-permute-start(bf16[64,1024]{1,0:T(8,128)(2,1)} %bitcast.6), channel_id=1, source_target_pairs={{0,0},{4,1},{9,2},{13,3},{18,4},{22,5},{27,6},{31,7},{1,8},{5,9},{... | collective-permute-start | bytes 393224 | tf_op jit(solution)/shard_map/ppermute | solution.py:342
  18.7 33.6 %copy-start.1 = (s32[2,512]{1,0:T(2,128)S(1)}, s32[2,512]{1,0:T(2,128)}, u32[]{:S(2)}) copy-start(s32[2,512]{1,0:T(2,128)} %sampled_ref.1) | copy-start | bytes 12292
  18.8 21.5 %collective-permute-start.12 = (bf16[64,1792]{1,0:T(8,128)(2,1)S(1)}, bf16[64,1792]{1,0:T(8,128)(2,1)S(1)}, u32[]{:S(2)}, u32[]{:S(2)}) collective-permute-start(bf16[64,1792]{1,0:T(8,128)(2,1)S(1)} %fusion.4.refs_0_), channel_id=1, source_target_pairs={{0,16},{8,24},{16,0},{24,8},{1,17},{9,25},{17,1},{25,9},{2,18},{10... | collective-permute-start | bytes 688136 | tf_op jit(solution)/shard_map/ppermute | solution.py:335
  34.3 16.2 %collective-permute-start.5 = (bf16[2,64,2304]{2,1,0:T(8,128)(2,1)S(1)}, bf16[2,64,2304]{2,1,0:T(8,128)(2,1)S(1)}, u32[]{:S(2)}, u32[]{:S(2)}) collective-permute-start(bf16[2,64,2304]{2,1,0:T(8,128)(2,1)S(1)} %collective-permute-done.4.down_ref), channel_id=1, source_target_pairs={{2,0},{4,2},{6,4},{7,6},{5,7},{3,5},{1,3},{0,1},{10,8},{12,10},{14... | collective-permute-start | bytes 1769480 | tf_op jit(solution)/shard_map/ppermute | solution.py:358
  36.2 14.5 %collective-permute-start.3 = (bf16[2,64,2304]{2,1,0:T(8,128)(2,1)S(1)}, bf16[2,64,2304]{2,1,0:T(8,128)(2,1)S(1)}, u32[]{:S(2)}, u32[]{:S(2)}) collective-permute-start(bf16[2,64,2304]{2,1,0:T(8,128)(2,1)S(1)} %collective-permute-done.2.up_ref), channel_id=1, source_target_pairs={{0,2},{2,4},{4,6},{6,7},{7,5},{5,3},{3,1},{1,0},{8,10},{10,12},{12... | collective-permute-start | bytes 1769480 | tf_op jit(solution)/shard_map/ppermute | solution.py:357
  37.0 15.3 %collective-permute-start.11 = (bf16[64,1792]{1,0:T(8,128)(2,1)S(1)}, bf16[64,1792]{1,0:T(8,128)(2,1)S(1)}, u32[]{:S(2)}, u32[]{:S(2)}) collective-permute-start(bf16[64,1792]{1,0:T(8,128)(2,1)S(1)} %fusion.4.refs_0_), channel_id=1, source_target_pairs={{0,8},{8,0},{16,24},{24,16},{1,9},{9,1},{17,25},{25,17},{2,10},{10... | collective-permute-start | bytes 688136 | tf_op jit(solution)/shard_map/ppermute | solution.py:335
  40.3 12.0 %collective-permute-start.13 = (bf16[64,1792]{1,0:T(8,128)(2,1)S(1)}, bf16[64,1792]{1,0:T(8,128)(2,1)S(1)}, u32[]{:S(2)}, u32[]{:S(2)}) collective-permute-start(bf16[64,1792]{1,0:T(8,128)(2,1)S(1)} %collective-permute-done.12.refs_2_), channel_id=1, source_target_pairs={{0,8},{8,0},{16,24},{24,16},{1,9},{9,1},{17,25},{25,17},{2,10},{10... | collective-permute-start | bytes 688136 | tf_op jit(solution)/shard_map/ppermute | solution.py:335
  50.7 14.6 %collective-permute-start.7 = (bf16[2,64,2304]{2,1,0:T(8,128)(2,1)S(1)}, bf16[2,64,2304]{2,1,0:T(8,128)(2,1)S(1)}, u32[]{:S(2)}, u32[]{:S(2)}) collective-permute-start(bf16[2,64,2304]{2,1,0:T(8,128)(2,1)S(1)} %collective-permute-done.3.refs_0_), channel_id=1, source_target_pairs={{0,2},{2,4},{4,6},{6,7},{7,5},{5,3},{3,1},{1,0},{8,10},{10,12},{12... | collective-permute-start | bytes 1769480 | tf_op jit(solution)/shard_map/ppermute | solution.py:357
  53.1 14.2 %collective-permute-start.9 = (bf16[2,64,2304]{2,1,0:T(8,128)(2,1)S(1)}, bf16[2,64,2304]{2,1,0:T(8,128)(2,1)S(1)}, u32[]{:S(2)}, u32[]{:S(2)}) collective-permute-start(bf16[2,64,2304]{2,1,0:T(8,128)(2,1)S(1)} %collective-permute-done.5.refs_1_), channel_id=1, source_target_pairs={{2,0},{4,2},{6,4},{7,6},{5,7},{3,5},{1,3},{0,1},{10,8},{12,10},{14... | collective-permute-start | bytes 1769480 | tf_op jit(solution)/shard_map/ppermute | solution.py:358
  53.6 21.9 %copy-start = (bf16[2,64,2304]{2,1,0:T(8,128)(2,1)S(1)}, bf16[2,64,2304]{2,1,0:T(8,128)(2,1)}, u32[]{:S(2)}) copy-start(bf16[2,64,2304]{2,1,0:T(8,128)(2,1)} %refs_0_) | copy-start | bytes 1769476
  65.3 10.2 %collective-permute-start.8 = (bf16[64,2304]{1,0:T(8,128)(2,1)S(1)}, bf16[64,2304]{1,0:T(8,128)(2,1)S(1)}, u32[]{:S(2)}, u32[]{:S(2)}) collective-permute-start(bf16[64,2304]{1,0:T(8,128)(2,1)S(1)} %slice_bitcast_fusion.1), channel_id=1, source_target_pairs={{0,2},{2,4},{4,6},{6,7},{7,5},{5,3},{3,1},{1,0},{8,10},{10,12},{12... | collective-permute-start | bytes 884744 | tf_op jit(solution)/shard_map/ppermute | solution.py:362
  67.4 8.1 %collective-permute-start.10 = (bf16[64,2304]{1,0:T(8,128)(2,1)S(1)}, bf16[64,2304]{1,0:T(8,128)(2,1)S(1)}, u32[]{:S(2)}, u32[]{:S(2)}) collective-permute-start(bf16[64,2304]{1,0:T(8,128)(2,1)S(1)} %slice_bitcast_fusion), channel_id=1, source_target_pairs={{2,0},{4,2},{6,4},{7,6},{5,7},{3,5},{1,3},{0,1},{10,8},{12,10},{14... | collective-permute-start | bytes 884744 | tf_op jit(solution)/shard_map/ppermute | solution.py:363
  83.5 3.8 %collective-permute-start.14 = (f32[3,8,128]{2,1,0:T(8,128)S(1)}, f32[3,8,128]{2,1,0:T(8,128)S(1)}, u32[]{:S(2)}, u32[]{:S(2)}) collective-permute-start(f32[3,8,128]{2,1,0:T(8,128)S(1)} %chunk.5.refs_0_), channel_id=1, source_target_pairs={{0,1},{1,0},{2,3},{3,2},{4,5},{5,4},{6,7},{7,6},{8,9},{9,8},{10,11... | collective-permute-start | bytes 36872 | tf_op jit(solution)/shard_map/ppermute | solution.py:335
  87.3 5.8 %collective-permute-start.17 = (f32[3,8,128]{2,1,0:T(8,128)S(1)}, f32[3,8,128]{2,1,0:T(8,128)S(1)}, u32[]{:S(2)}, u32[]{:S(2)}) collective-permute-start(f32[3,8,128]{2,1,0:T(8,128)S(1)} %combine.2.refs_0_), channel_id=1, source_target_pairs={{0,6},{1,7},{2,4},{3,5},{4,2},{5,3},{6,0},{7,1},{8,14},{9,15},{10,... | collective-permute-start | bytes 36872 | tf_op jit(solution)/shard_map/ppermute | solution.py:335
  91.4 4.6 %collective-permute-start.16 = (f32[3,8,128]{2,1,0:T(8,128)S(1)}, f32[3,8,128]{2,1,0:T(8,128)S(1)}, u32[]{:S(2)}, u32[]{:S(2)}) collective-permute-start(f32[3,8,128]{2,1,0:T(8,128)S(1)} %combine.2.refs_0_), channel_id=1, source_target_pairs={{0,4},{1,5},{2,6},{3,7},{4,0},{5,1},{6,2},{7,3},{8,12},{9,13},{10,... | collective-permute-start | bytes 36872 | tf_op jit(solution)/shard_map/ppermute | solution.py:335
  91.4 4.6 %collective-permute-start.15 = (f32[3,8,128]{2,1,0:T(8,128)S(1)}, f32[3,8,128]{2,1,0:T(8,128)S(1)}, u32[]{:S(2)}, u32[]{:S(2)}) collective-permute-start(f32[3,8,128]{2,1,0:T(8,128)S(1)} %combine.2.refs_0_), channel_id=1, source_target_pairs={{0,2},{1,3},{2,0},{3,1},{4,6},{5,7},{6,4},{7,5},{8,10},{9,11},{10,... | collective-permute-start | bytes 36872 | tf_op jit(solution)/shard_map/ppermute | solution.py:335

commit v9 on v8

--- a/solution.py
+++ b/solution.py
@@ -348,20 +348,10 @@
         ]
         shards.append(lax.ppermute(factor_v.T, ("group", "vocab"), moves))
 
-    hidden, *shards = lax.optimization_barrier((hidden, *shards))
+    hidden, block, *shards = lax.optimization_barrier((hidden, block, *shards))
     up = [hidden, lax.ppermute(hidden, "vocab", ahead)]
     down = [hidden, lax.ppermute(hidden, "vocab", behind)]
     head, block = lax.optimization_barrier((make_load(depth, entries)(head), block))
-    base, base_rows = make_base(r, depth, entries)(up[1], down[1], head)
-    for hop in range(2, half):
-        up.append(lax.ppermute(up[-1], "vocab", ahead))
-        down.append(lax.ppermute(down[-1], "vocab", behind))
-        if hop == 2:
-            up[2], down[2], base = lax.optimization_barrier((up[2], down[2], base))
-    ends = [
-        lax.ppermute(up[-1][0], "vocab", ahead),
-        lax.ppermute(down[-1][1], "vocab", behind),
-    ]
     gap = ((0, 0), (0, padded(v_rows) - v_rows))
     packs = {0: jnp.concatenate([block] + [jnp.pad(x, gap) for x in shards], axis=1)}
     bit = n_group // 2
@@ -372,7 +362,18 @@
     full_u, full_v, want = make_assemble(
         n_group, n_voc, u_rows, v_rows, rank, r, entries
     )(sampled, *[packs[k] for k in range(n_group)])
-
+    base, base_rows = make_base(r, depth, entries)(up[1], down[1], head)
+    for hop in range(2, half):
+        up.append(lax.ppermute(up[-1], "vocab", ahead))
+        down.append(lax.ppermute(down[-1], "vocab", behind))
+        if hop == 2:
+            up[2], down[2], base, full_u = lax.optimization_barrier(
+                (up[2], down[2], base, full_u)
+            )
+    ends = [
+        lax.ppermute(up[-1][0], "vocab", ahead),
+        lax.ppermute(down[-1][1], "vocab", behind),
+    ]
     stats = []
     for hop in range(2, half + 1):
         pieces = [up[hop], down[hop]] if hop < half else [hidden] + ends

time: 96.9 us -> 95.5 us (0.986)
  starting transfers between devices: 38.1 us -> 31 us
  waiting for transfers between devices: 18.8 us -> 24.5 us
    ppermute x7, starting transfers between devices: 20.6 us -> 10.4 us  [trade(): return lax.ppermute(x, axis, [(i, i ^ bit) for i in range(size)])]
    ppermute x1, starting transfers between devices: 2.55 us -> 8.01 us  [body(): down = [hidden, lax.ppermute(hidden, 'vocab', behind)]]
    ppermute x2, waiting for transfers between devices: 3.11 us -> 5.28 us  [body(): up.append(lax.ppermute(up[-1], 'vocab', ahead))]
    ppermute x2, waiting for transfers between devices: 4.16 us -> 6.29 us  [body(): down.append(lax.ppermute(down[-1], 'vocab', behind))]
    ppermute x1, starting transfers between devices: 2.09 us -> 0.01 us  [body(): up = [hidden, lax.ppermute(hidden, 'vocab', ahead)]]
    ppermute x2, waiting for transfers between devices: 0.84 us -> 2.45 us  [body(): shards.append(lax.ppermute(factor_v.T, ('group', 'vocab'), moves))]
    ppermute x2, starting transfers between devices: 2.39 us -> 0.94 us  [body(): up.append(lax.ppermute(up[-1], 'vocab', ahead))]
  transfers between devices with their start and end apart: 18 -> 18, of which waited for: 9 -> 8; matrix products, arithmetic and copies ran while one was open for 0% -> 0% of each run, Pallas kernels for 31% -> 32%
where the time goes in v9:
time: 95.5 us; the launch traced here: 95.3 us
  Pallas kernels  39 us (41%)
  starting transfers between devices  31 us (32%)
  waiting for transfers between devices  24.5 us (26%)
    pallas_call x3, Pallas kernels, body(): out = chunk(*pieces, head, full_u, full_v, want, *extra)  24.3 us
    ppermute x7, waiting for transfers between devices, trade(): return lax.ppermute(x, axis, [(i, i ^ bit) for i in range(size)])  10.5 us
    ppermute x7, starting transfers between devices, trade(): return lax.ppermute(x, axis, [(i, i ^ bit) for i in range(size)])  10.4 us
    ppermute x1, starting transfers between devices, body(): down = [hidden, lax.ppermute(hidden, 'vocab', behind)]  8.01 us
    pallas_call x1, Pallas kernels, body(): make_load(depth, entries)(head)  6.61 us
    pallas_call x1, Pallas kernels, body(): base, base_rows = make_base(r, depth, entries)(up[1], down[1], head)  6.58 us
    ppermute x2, waiting for transfers between devices, body(): down.append(lax.ppermute(down[-1], 'vocab', behind))  6.29 us
    ppermute x2, waiting for transfers between devices, body(): up.append(lax.ppermute(up[-1], 'vocab', ahead))  5.28 us
  transfers between devices with their start and end apart: 18, of which 8 were waited for; matrix products, arithmetic and copies ran while one was open for 0% of the time, Pallas kernels for 32%

profile of v9, /device:TPU:0, one launch (start us, length us, event | category | flops | bytes accessed | tf_op | source)
XLA Modules:
  0.0 95.3 jit_solution(7099623863740315397)
XLA Ops:
  0.6 1.6 %collective-permute-start = (bf16[64,1024]{1,0:T(8,128)(2,1)}, bf16[64,1024]{1,0:T(8,128)(2,1)S(1)}, u32[]{:S(2)}, u32[]{:S(2)}) collective-permute-start(bf16[64,1024]{1,0:T(8,128)(2,1)} %bitcast.6), channel_id=1, source_target_pairs={{0,0},{4,1},{9,2},{13,3},{18,4},{22,5},{27,6},{31,7},{1,8},{5,9},{... | collective-permute-start | bytes 393224 | tf_op jit(solution)/shard_map/ppermute | solution.py:342
  2.2 0.0 copy-start.1
  2.2 3.4 %collective-permute-start.2 = (bf16[64,288]{1,0:T(8,128)(2,1)}, bf16[64,288]{1,0:T(8,128)(2,1)S(1)}, u32[]{:S(2)}, u32[]{:S(2)}) collective-permute-start(bf16[64,288]{1,0:T(8,128)(2,1)} %bitcast.7), channel_id=1, source_target_pairs={{1,0},{0,1},{9,2},{8,3},{17,4},{16,5},{25,6},{24,7},{3,8},{2,9},{1... | collective-permute-start | bytes 110600 | tf_op jit(solution)/shard_map/ppermute | solution.py:349
  5.6 1.4 %collective-permute-start.1 = (bf16[64,288]{1,0:T(8,128)(2,1)}, bf16[64,288]{1,0:T(8,128)(2,1)S(1)}, u32[]{:S(2)}, u32[]{:S(2)}) collective-permute-start(bf16[64,288]{1,0:T(8,128)(2,1)} %bitcast.8), channel_id=1, source_target_pairs={{0,0},{1,1},{8,2},{9,3},{16,4},{17,5},{24,6},{25,7},{2,8},{3,9},{1... | collective-permute-start | bytes 110600 | tf_op jit(solution)/shard_map/ppermute | solution.py:349
  7.0 2.4 %collective-permute-done.2 = bf16[64,288]{1,0:T(8,128)(2,1)S(1)} collective-permute-done((bf16[64,288]{1,0:T(8,128)(2,1)}, bf16[64,288]{1,0:T(8,128)(2,1)S(1)}, u32[]{:S(2)}, u32[]{:S(2)}) %collective-permute-start.2) | collective-permute-done | bytes 36896 | tf_op jit(solution)/shard_map/ppermute | solution.py:349
  9.5 0.0 collective-permute-done.1
  9.5 0.0 collective-permute-done
  9.5 8.0 %collective-permute-start.5 = (bf16[2,64,2304]{2,1,0:T(8,128)(2,1)}, bf16[2,64,2304]{2,1,0:T(8,128)(2,1)S(1)}, u32[]{:S(2)}, u32[]{:S(2)}) collective-permute-start(bf16[2,64,2304]{2,1,0:T(8,128)(2,1)} %refs_0_), channel_id=1, source_target_pairs={{2,0},{4,2},{6,4},{7,6},{5,7},{3,5},{1,3},{0,1},{10,8},{12,10},{14... | collective-permute-start | bytes 1769480 | tf_op jit(solution)/shard_map/ppermute | solution.py:353
  17.5 0.0 collective-permute-start.3
  17.5 6.6 %load.1.head_ref.refs_2_.refs_3_ = bf16[4096,2304]{1,0:T(8,128)(2,1)S(1)} custom-call(bf16[4096,2304]{1,0:T(8,128)(2,1)} %head_ref.1), custom_call_target="tpu_custom_call" | custom-call | bytes 18874368 | tf_op jit(solution)/shard_map/load/pallas_call | solution.py:354
  24.1 4.6 %collective-permute-start.8 = (bf16[64,1792]{1,0:T(8,128)(2,1)S(1)}, bf16[64,1792]{1,0:T(8,128)(2,1)S(1)}, u32[]{:S(2)}, u32[]{:S(2)}) collective-permute-start(bf16[64,1792]{1,0:T(8,128)(2,1)S(1)} %fusion.4.refs_0_), channel_id=1, source_target_pairs={{0,16},{8,24},{16,0},{24,8},{1,17},{9,25},{17,1},{25,9},{2,18},{10... | collective-permute-start | bytes 688136 | tf_op jit(solution)/shard_map/ppermute | solution.py:335
  28.7 0.0 collective-permute-start.7
  28.7 4.6 %collective-permute-done.8.refs_2_ = bf16[64,1792]{1,0:T(8,128)(2,1)S(1)} collective-permute-done((bf16[64,1792]{1,0:T(8,128)(2,1)S(1)}, bf16[64,1792]{1,0:T(8,128)(2,1)S(1)}, u32[]{:S(2)}, u32[]{:S(2)}) %collective-permute-start.8) | collective-permute-done | bytes 229408 | tf_op jit(solution)/shard_map/ppermute | solution.py:335
  33.3 0.0 collective-permute-start.9
  33.3 0.0 collective-permute-done.5.down_ref
  33.3 1.7 %collective-permute-start.6 = (bf16[2,64,2304]{2,1,0:T(8,128)(2,1)S(1)}, bf16[2,64,2304]{2,1,0:T(8,128)(2,1)S(1)}, u32[]{:S(2)}, u32[]{:S(2)}) collective-permute-start(bf16[2,64,2304]{2,1,0:T(8,128)(2,1)S(1)} %collective-permute-done.5.down_ref), channel_id=1, source_target_pairs={{2,0},{4,2},{6,4},{7,6},{5,7},{3,5},{1,3},{0,1},{10,8},{12,10},{14... | collective-permute-start | bytes 1769480 | tf_op jit(solution)/shard_map/ppermute | solution.py:368
  35.1 0.0 collective-permute-done.3.up_ref
  35.1 0.3 collective-permute-start.4
  35.4 0.0 collective-permute-done.7.refs_1_
  35.4 0.0 collective-permute-done.9.refs_3_
  35.4 0.0 copy-done.1
  35.4 0.8 assemble.1
  36.2 6.6 %base.1 = (f32[4096,256]{1,0:T(8,128)S(1)}, bf16[2304,256]{1,0:T(8,128)(2,1)S(1)}) custom-call(bf16[2,64,2304]{2,1,0:T(8,128)(2,1)S(1)} %collective-permute-done.3.up_ref, bf16[2,64,2304]{2,1,0:T(8,128)(2,1)S(1)} %collective-permute-done.5.down_ref, bf16[4096,2304]{1,0:T(8,128)(2,1)S(1)} %load.1.head_ref.refs_2_.refs_3_), custom_call_target="tpu_custom_call" | custom-call | flops 4831838208 | bytes 18874368 | tf_op jit(solution)/shard_map/base/pallas_call | solution.py:365
  42.8 6.3 %collective-permute-done.6.refs_1_ = bf16[2,64,2304]{2,1,0:T(8,128)(2,1)S(1)} collective-permute-done((bf16[2,64,2304]{2,1,0:T(8,128)(2,1)S(1)}, bf16[2,64,2304]{2,1,0:T(8,128)(2,1)S(1)}, u32[]{:S(2)}, u32[]{:S(2)}) %collective-permute-start.6) | collective-permute-done | bytes 589856 | tf_op jit(solution)/shard_map/ppermute | solution.py:368
  49.1 1.4 %collective-permute-done.4.refs_0_ = bf16[2,64,2304]{2,1,0:T(8,128)(2,1)S(1)} collective-permute-done((bf16[2,64,2304]{2,1,0:T(8,128)(2,1)S(1)}, bf16[2,64,2304]{2,1,0:T(8,128)(2,1)S(1)}, u32[]{:S(2)}, u32[]{:S(2)}) %collective-permute-start.4) | collective-permute-done | bytes 589856 | tf_op jit(solution)/shard_map/ppermute | solution.py:367
  50.6 0.7 collective-permute-start.10
  51.2 1.4 %collective-permute-start.12 = (bf16[2,64,2304]{2,1,0:T(8,128)(2,1)S(1)}, bf16[2,64,2304]{2,1,0:T(8,128)(2,1)S(1)}, u32[]{:S(2)}, u32[]{:S(2)}) collective-permute-start(bf16[2,64,2304]{2,1,0:T(8,128)(2,1)S(1)} %collective-permute-done.6.refs_1_), channel_id=1, source_target_pairs={{2,0},{4,2},{6,4},{7,6},{5,7},{3,5},{1,3},{0,1},{10,8},{12,10},{14... | collective-permute-start | bytes 1769480 | tf_op jit(solution)/shard_map/ppermute | solution.py:368
  52.6 0.0 copy-start
  52.6 8.8 %chunk.3 = (f32[3,256]{1,0:T(4,128)S(1)}, f32[3,256]{1,0:T(4,128)S(1)}) custom-call(bf16[2,64,2304]{2,1,0:T(8,128)(2,1)S(1)} %collective-permute-done.4.refs_0_, bf16[2,64,2304]{2,1,0:T(8,128)(2,1)S(1)} %collective-permute-done.6.refs_1_, bf16[4096,2304]{1,0:T(8,128)(2,1)S(1)} %load.1.head_ref.refs_2_.refs_3_, ...), custom_call_target="tpu_custom_call" | custom-call | flops 5368709120 | bytes 19922944 | tf_op jit(solution)/shard_map/chunk/pallas_call | solution.py:382
  61.4 3.8 %collective-permute-done.10.refs_0_ = bf16[2,64,2304]{2,1,0:T(8,128)(2,1)S(1)} collective-permute-done((bf16[2,64,2304]{2,1,0:T(8,128)(2,1)S(1)}, bf16[2,64,2304]{2,1,0:T(8,128)(2,1)S(1)}, u32[]{:S(2)}, u32[]{:S(2)}) %collective-permute-start.10) | collective-permute-done | bytes 589856 | tf_op jit(solution)/shard_map/ppermute | solution.py:367
  65.2 1.2 %collective-permute-start.11 = (bf16[64,2304]{1,0:T(8,128)(2,1)S(1)}, bf16[64,2304]{1,0:T(8,128)(2,1)S(1)}, u32[]{:S(2)}, u32[]{:S(2)}) collective-permute-start(bf16[64,2304]{1,0:T(8,128)(2,1)S(1)} %slice_bitcast_fusion.1), channel_id=1, source_target_pairs={{0,2},{2,4},{4,6},{6,7},{7,5},{5,3},{3,1},{1,0},{8,10},{10,12},{12... | collective-permute-start | bytes 884744 | tf_op jit(solution)/shard_map/ppermute | solution.py:374
  66.4 0.0 collective-permute-done.12.refs_1_
  66.4 1.0 %collective-permute-start.13 = (bf16[64,2304]{1,0:T(8,128)(2,1)S(1)}, bf16[64,2304]{1,0:T(8,128)(2,1)S(1)}, u32[]{:S(2)}, u32[]{:S(2)}) collective-permute-start(bf16[64,2304]{1,0:T(8,128)(2,1)S(1)} %slice_bitcast_fusion), channel_id=1, source_target_pairs={{2,0},{4,2},{6,4},{7,6},{5,7},{3,5},{1,3},{0,1},{10,8},{12,10},{14... | collective-permute-start | bytes 884744 | tf_op jit(solution)/shard_map/ppermute | solution.py:375
  67.4 7.5 %chunk.4.refs_9_ = f32[3,256]{1,0:T(4,128)S(1)} custom-call(bf16[2,64,2304]{2,1,0:T(8,128)(2,1)S(1)} %collective-permute-done.10.refs_0_, bf16[2,64,2304]{2,1,0:T(8,128)(2,1)S(1)} %collective-permute-done.12.refs_1_, bf16[4096,2304]{1,0:T(8,128)(2,1)S(1)} %load.1.head_ref.refs_2_.refs_3_, bf16[4096,64]{1,0:T(8,128)(2,1)S(1)} %get-tuple-element.29.refs_3_.refs_4_, ...), custom_call_target="tpu_custom_call" | custom-call | flops 5368709120 | bytes 19922944 | tf_op jit(solution)/shard_map/chunk/pallas_call | solution.py:382
  74.8 0.0 collective-permute-done.11.refs_1_
  74.9 0.0 collective-permute-done.13.refs_2_
  74.9 0.0 copy-done
  74.9 8.0 %chunk.5.refs_0_ = f32[3,8,128]{2,1,0:T(8,128)S(1)} custom-call(bf16[2,64,2304]{2,1,0:T(8,128)(2,1)S(1)} %copy-done, bf16[64,2304]{1,0:T(8,128)(2,1)S(1)} %collective-permute-done.11.refs_1_, bf16[64,2304]{1,0:T(8,128)(2,1)S(1)} %collective-permute-done.13.refs_2_, bf16[4096,2304]{1,0:T(8,128)(2,1)S(1)} %load.1.head_ref.refs_2_.refs_3_, ...), custom_call_target="tpu_custom_call" | custom-call | flops 5368709120 | bytes 19922944 | tf_op jit(solution)/shard_map/chunk/pallas_call | solution.py:382
  82.9 1.4 %collective-permute-start.14 = (f32[3,8,128]{2,1,0:T(8,128)S(1)}, f32[3,8,128]{2,1,0:T(8,128)S(1)}, u32[]{:S(2)}, u32[]{:S(2)}) collective-permute-start(f32[3,8,128]{2,1,0:T(8,128)S(1)} %chunk.5.refs_0_), channel_id=1, source_target_pairs={{0,1},{1,0},{2,3},{3,2},{4,5},{5,4},{6,7},{7,6},{8,9},{9,8},{10,11... | collective-permute-start | bytes 36872 | tf_op jit(solution)/shard_map/ppermute | solution.py:335
  84.3 2.4 %collective-permute-done.14.refs_1_ = f32[3,8,128]{2,1,0:T(8,128)S(1)} collective-permute-done((f32[3,8,128]{2,1,0:T(8,128)S(1)}, f32[3,8,128]{2,1,0:T(8,128)S(1)}, u32[]{:S(2)}, u32[]{:S(2)}) %collective-permute-start.14) | collective-permute-done | bytes 12320 | tf_op jit(solution)/shard_map/ppermute | solution.py:335
  86.7 3.3 %collective-permute-start.17 = (f32[3,8,128]{2,1,0:T(8,128)S(1)}, f32[3,8,128]{2,1,0:T(8,128)S(1)}, u32[]{:S(2)}, u32[]{:S(2)}) collective-permute-start(f32[3,8,128]{2,1,0:T(8,128)S(1)} %combine.2.refs_0_), channel_id=1, source_target_pairs={{0,6},{1,7},{2,4},{3,5},{4,2},{5,3},{6,0},{7,1},{8,14},{9,15},{10,... | collective-permute-start | bytes 36872 | tf_op jit(solution)/shard_map/ppermute | solution.py:335
  90.0 0.0 collective-permute-start.16
  90.0 1.1 %collective-permute-start.15 = (f32[3,8,128]{2,1,0:T(8,128)S(1)}, f32[3,8,128]{2,1,0:T(8,128)S(1)}, u32[]{:S(2)}, u32[]{:S(2)}) collective-permute-start(f32[3,8,128]{2,1,0:T(8,128)S(1)} %combine.2.refs_0_), channel_id=1, source_target_pairs={{0,2},{1,3},{2,0},{3,1},{4,6},{5,7},{6,4},{7,5},{8,10},{9,11},{10,... | collective-permute-start | bytes 36872 | tf_op jit(solution)/shard_map/ppermute | solution.py:335
  91.1 1.1 %collective-permute-done.17.refs_3_ = f32[3,8,128]{2,1,0:T(8,128)S(1)} collective-permute-done((f32[3,8,128]{2,1,0:T(8,128)S(1)}, f32[3,8,128]{2,1,0:T(8,128)S(1)}, u32[]{:S(2)}, u32[]{:S(2)}) %collective-permute-start.17) | collective-permute-done | bytes 12320 | tf_op jit(solution)/shard_map/ppermute | solution.py:335
  92.2 2.4 %collective-permute-done.16.refs_2_ = f32[3,8,128]{2,1,0:T(8,128)S(1)} collective-permute-done((f32[3,8,128]{2,1,0:T(8,128)S(1)}, f32[3,8,128]{2,1,0:T(8,128)S(1)}, u32[]{:S(2)}, u32[]{:S(2)}) %collective-permute-start.16) | collective-permute-done | bytes 12320 | tf_op jit(solution)/shard_map/ppermute | solution.py:335
  94.6 0.0 collective-permute-done.15.refs_1_
  94.6 0.7 combine.3
  (4 shorter events, 0.1 us)
Async XLA Ops:
  0.6 8.8 %collective-permute-start = (bf16[64,1024]{1,0:T(8,128)(2,1)}, bf16[64,1024]{1,0:T(8,128)(2,1)S(1)}, u32[]{:S(2)}, u32[]{:S(2)}) collective-permute-start(bf16[64,1024]{1,0:T(8,128)(2,1)} %bitcast.6), channel_id=1, source_target_pairs={{0,0},{4,1},{9,2},{13,3},{18,4},{22,5},{27,6},{31,7},{1,8},{5,9},{... | collective-permute-start | bytes 393224 | tf_op jit(solution)/shard_map/ppermute | solution.py:342
  2.2 33.2 %copy-start.1 = (s32[2,512]{1,0:T(2,128)S(1)}, s32[2,512]{1,0:T(2,128)}, u32[]{:S(2)}) copy-start(s32[2,512]{1,0:T(2,128)} %sampled_ref.1) | copy-start | bytes 12292
  2.2 7.3 %collective-permute-start.2 = (bf16[64,288]{1,0:T(8,128)(2,1)}, bf16[64,288]{1,0:T(8,128)(2,1)S(1)}, u32[]{:S(2)}, u32[]{:S(2)}) collective-permute-start(bf16[64,288]{1,0:T(8,128)(2,1)} %bitcast.7), channel_id=1, source_target_pairs={{1,0},{0,1},{9,2},{8,3},{17,4},{16,5},{25,6},{24,7},{3,8},{2,9},{1... | collective-permute-start | bytes 110600 | tf_op jit(solution)/shard_map/ppermute | solution.py:349
  5.6 3.9 %collective-permute-start.1 = (bf16[64,288]{1,0:T(8,128)(2,1)}, bf16[64,288]{1,0:T(8,128)(2,1)S(1)}, u32[]{:S(2)}, u32[]{:S(2)}) collective-permute-start(bf16[64,288]{1,0:T(8,128)(2,1)} %bitcast.8), channel_id=1, source_target_pairs={{0,0},{1,1},{8,2},{9,3},{16,4},{17,5},{24,6},{25,7},{2,8},{3,9},{1... | collective-permute-start | bytes 110600 | tf_op jit(solution)/shard_map/ppermute | solution.py:349
  9.5 23.9 %collective-permute-start.5 = (bf16[2,64,2304]{2,1,0:T(8,128)(2,1)}, bf16[2,64,2304]{2,1,0:T(8,128)(2,1)S(1)}, u32[]{:S(2)}, u32[]{:S(2)}) collective-permute-start(bf16[2,64,2304]{2,1,0:T(8,128)(2,1)} %refs_0_), channel_id=1, source_target_pairs={{2,0},{4,2},{6,4},{7,6},{5,7},{3,5},{1,3},{0,1},{10,8},{12,10},{14... | collective-permute-start | bytes 1769480 | tf_op jit(solution)/shard_map/ppermute | solution.py:353
  17.5 17.6 %collective-permute-start.3 = (bf16[2,64,2304]{2,1,0:T(8,128)(2,1)}, bf16[2,64,2304]{2,1,0:T(8,128)(2,1)S(1)}, u32[]{:S(2)}, u32[]{:S(2)}) collective-permute-start(bf16[2,64,2304]{2,1,0:T(8,128)(2,1)} %refs_0_), channel_id=1, source_target_pairs={{0,2},{2,4},{4,6},{6,7},{7,5},{5,3},{3,1},{1,0},{8,10},{10,12},{12... | collective-permute-start | bytes 1769480 | tf_op jit(solution)/shard_map/ppermute | solution.py:352
  24.1 9.2 %collective-permute-start.8 = (bf16[64,1792]{1,0:T(8,128)(2,1)S(1)}, bf16[64,1792]{1,0:T(8,128)(2,1)S(1)}, u32[]{:S(2)}, u32[]{:S(2)}) collective-permute-start(bf16[64,1792]{1,0:T(8,128)(2,1)S(1)} %fusion.4.refs_0_), channel_id=1, source_target_pairs={{0,16},{8,24},{16,0},{24,8},{1,17},{9,25},{17,1},{25,9},{2,18},{10... | collective-permute-start | bytes 688136 | tf_op jit(solution)/shard_map/ppermute | solution.py:335
  28.7 6.6 %collective-permute-start.7 = (bf16[64,1792]{1,0:T(8,128)(2,1)S(1)}, bf16[64,1792]{1,0:T(8,128)(2,1)S(1)}, u32[]{:S(2)}, u32[]{:S(2)}) collective-permute-start(bf16[64,1792]{1,0:T(8,128)(2,1)S(1)} %fusion.4.refs_0_), channel_id=1, source_target_pairs={{0,8},{8,0},{16,24},{24,16},{1,9},{9,1},{17,25},{25,17},{2,10},{10... | collective-permute-start | bytes 688136 | tf_op jit(solution)/shard_map/ppermute | solution.py:335
  33.3 2.0 %collective-permute-start.9 = (bf16[64,1792]{1,0:T(8,128)(2,1)S(1)}, bf16[64,1792]{1,0:T(8,128)(2,1)S(1)}, u32[]{:S(2)}, u32[]{:S(2)}) collective-permute-start(bf16[64,1792]{1,0:T(8,128)(2,1)S(1)} %collective-permute-done.8.refs_2_), channel_id=1, source_target_pairs={{0,8},{8,0},{16,24},{24,16},{1,9},{9,1},{17,25},{25,17},{2,10},{10... | collective-permute-start | bytes 688136 | tf_op jit(solution)/shard_map/ppermute | solution.py:335
  33.3 15.8 %collective-permute-start.6 = (bf16[2,64,2304]{2,1,0:T(8,128)(2,1)S(1)}, bf16[2,64,2304]{2,1,0:T(8,128)(2,1)S(1)}, u32[]{:S(2)}, u32[]{:S(2)}) collective-permute-start(bf16[2,64,2304]{2,1,0:T(8,128)(2,1)S(1)} %collective-permute-done.5.down_ref), channel_id=1, source_target_pairs={{2,0},{4,2},{6,4},{7,6},{5,7},{3,5},{1,3},{0,1},{10,8},{12,10},{14... | collective-permute-start | bytes 1769480 | tf_op jit(solution)/shard_map/ppermute | solution.py:368
  35.1 15.5 %collective-permute-start.4 = (bf16[2,64,2304]{2,1,0:T(8,128)(2,1)S(1)}, bf16[2,64,2304]{2,1,0:T(8,128)(2,1)S(1)}, u32[]{:S(2)}, u32[]{:S(2)}) collective-permute-start(bf16[2,64,2304]{2,1,0:T(8,128)(2,1)S(1)} %collective-permute-done.3.up_ref), channel_id=1, source_target_pairs={{0,2},{2,4},{4,6},{6,7},{7,5},{5,3},{3,1},{1,0},{8,10},{10,12},{12... | collective-permute-start | bytes 1769480 | tf_op jit(solution)/shard_map/ppermute | solution.py:367
  50.6 14.6 %collective-permute-start.10 = (bf16[2,64,2304]{2,1,0:T(8,128)(2,1)S(1)}, bf16[2,64,2304]{2,1,0:T(8,128)(2,1)S(1)}, u32[]{:S(2)}, u32[]{:S(2)}) collective-permute-start(bf16[2,64,2304]{2,1,0:T(8,128)(2,1)S(1)} %collective-permute-done.4.refs_0_), channel_id=1, source_target_pairs={{0,2},{2,4},{4,6},{6,7},{7,5},{5,3},{3,1},{1,0},{8,10},{10,12},{12... | collective-permute-start | bytes 1769480 | tf_op jit(solution)/shard_map/ppermute | solution.py:367
  51.2 15.2 %collective-permute-start.12 = (bf16[2,64,2304]{2,1,0:T(8,128)(2,1)S(1)}, bf16[2,64,2304]{2,1,0:T(8,128)(2,1)S(1)}, u32[]{:S(2)}, u32[]{:S(2)}) collective-permute-start(bf16[2,64,2304]{2,1,0:T(8,128)(2,1)S(1)} %collective-permute-done.6.refs_1_), channel_id=1, source_target_pairs={{2,0},{4,2},{6,4},{7,6},{5,7},{3,5},{1,3},{0,1},{10,8},{12,10},{14... | collective-permute-start | bytes 1769480 | tf_op jit(solution)/shard_map/ppermute | solution.py:368
  52.6 22.3 %copy-start = (bf16[2,64,2304]{2,1,0:T(8,128)(2,1)S(1)}, bf16[2,64,2304]{2,1,0:T(8,128)(2,1)}, u32[]{:S(2)}) copy-start(bf16[2,64,2304]{2,1,0:T(8,128)(2,1)} %refs_0_) | copy-start | bytes 1769476
  65.2 9.6 %collective-permute-start.11 = (bf16[64,2304]{1,0:T(8,128)(2,1)S(1)}, bf16[64,2304]{1,0:T(8,128)(2,1)S(1)}, u32[]{:S(2)}, u32[]{:S(2)}) collective-permute-start(bf16[64,2304]{1,0:T(8,128)(2,1)S(1)} %slice_bitcast_fusion.1), channel_id=1, source_target_pairs={{0,2},{2,4},{4,6},{6,7},{7,5},{5,3},{3,1},{1,0},{8,10},{10,12},{12... | collective-permute-start | bytes 884744 | tf_op jit(solution)/shard_map/ppermute | solution.py:374
  66.4 8.4 %collective-permute-start.13 = (bf16[64,2304]{1,0:T(8,128)(2,1)S(1)}, bf16[64,2304]{1,0:T(8,128)(2,1)S(1)}, u32[]{:S(2)}, u32[]{:S(2)}) collective-permute-start(bf16[64,2304]{1,0:T(8,128)(2,1)S(1)} %slice_bitcast_fusion), channel_id=1, source_target_pairs={{2,0},{4,2},{6,4},{7,6},{5,7},{3,5},{1,3},{0,1},{10,8},{12,10},{14... | collective-permute-start | bytes 884744 | tf_op jit(solution)/shard_map/ppermute | solution.py:375
  82.9 3.8 %collective-permute-start.14 = (f32[3,8,128]{2,1,0:T(8,128)S(1)}, f32[3,8,128]{2,1,0:T(8,128)S(1)}, u32[]{:S(2)}, u32[]{:S(2)}) collective-permute-start(f32[3,8,128]{2,1,0:T(8,128)S(1)} %chunk.5.refs_0_), channel_id=1, source_target_pairs={{0,1},{1,0},{2,3},{3,2},{4,5},{5,4},{6,7},{7,6},{8,9},{9,8},{10,11... | collective-permute-start | bytes 36872 | tf_op jit(solution)/shard_map/ppermute | solution.py:335
  86.7 5.6 %collective-permute-start.17 = (f32[3,8,128]{2,1,0:T(8,128)S(1)}, f32[3,8,128]{2,1,0:T(8,128)S(1)}, u32[]{:S(2)}, u32[]{:S(2)}) collective-permute-start(f32[3,8,128]{2,1,0:T(8,128)S(1)} %combine.2.refs_0_), channel_id=1, source_target_pairs={{0,6},{1,7},{2,4},{3,5},{4,2},{5,3},{6,0},{7,1},{8,14},{9,15},{10,... | collective-permute-start | bytes 36872 | tf_op jit(solution)/shard_map/ppermute | solution.py:335
  90.0 4.6 %collective-permute-start.16 = (f32[3,8,128]{2,1,0:T(8,128)S(1)}, f32[3,8,128]{2,1,0:T(8,128)S(1)}, u32[]{:S(2)}, u32[]{:S(2)}) collective-permute-start(f32[3,8,128]{2,1,0:T(8,128)S(1)} %combine.2.refs_0_), channel_id=1, source_target_pairs={{0,4},{1,5},{2,6},{3,7},{4,0},{5,1},{6,2},{7,3},{8,12},{9,13},{10,... | collective-permute-start | bytes 36872 | tf_op jit(solution)/shard_map/ppermute | solution.py:335
  90.0 4.6 %collective-permute-start.15 = (f32[3,8,128]{2,1,0:T(8,128)S(1)}, f32[3,8,128]{2,1,0:T(8,128)S(1)}, u32[]{:S(2)}, u32[]{:S(2)}) collective-permute-start(f32[3,8,128]{2,1,0:T(8,128)S(1)} %combine.2.refs_0_), channel_id=1, source_target_pairs={{0,2},{1,3},{2,0},{3,1},{4,6},{5,7},{6,4},{7,5},{8,10},{9,11},{10,... | collective-permute-start | bytes 36872 | tf_op jit(solution)/shard_map/ppermute | solution.py:335

commit v10 on v8

--- a/solution.py
+++ b/solution.py
@@ -77,9 +77,7 @@
 
 def sources_of(hop, n_voc):
     position = ring_position(lax.axis_index("vocab"), n_voc)
-    if hop < n_voc // 2:
-        return ring_device(position - hop, n_voc), ring_device(position + hop, n_voc)
-    return ring_device(position, n_voc), ring_device(position + hop, n_voc)
+    return ring_device(position + hop, n_voc), ring_device(position - hop + 1, n_voc)
 
 
 def load_rows(rows, pieces):
@@ -348,20 +346,11 @@
         ]
         shards.append(lax.ppermute(factor_v.T, ("group", "vocab"), moves))
 
-    hidden, *shards = lax.optimization_barrier((hidden, *shards))
-    up = [hidden, lax.ppermute(hidden, "vocab", ahead)]
-    down = [hidden, lax.ppermute(hidden, "vocab", behind)]
-    head, block = lax.optimization_barrier((make_load(depth, entries)(head), block))
-    base, base_rows = make_base(r, depth, entries)(up[1], down[1], head)
-    for hop in range(2, half):
-        up.append(lax.ppermute(up[-1], "vocab", ahead))
-        down.append(lax.ppermute(down[-1], "vocab", behind))
-        if hop == 2:
-            up[2], down[2], base = lax.optimization_barrier((up[2], down[2], base))
-    ends = [
-        lax.ppermute(up[-1][0], "vocab", ahead),
-        lax.ppermute(down[-1][1], "vocab", behind),
-    ]
+    up = [hidden, lax.ppermute(hidden, "vocab", behind)]
+    head = make_load(depth, entries)(head)
+    first, head, block, *shards = lax.optimization_barrier((hidden, head, block, *shards))
+    down = [hidden, lax.ppermute(first, "vocab", ahead)]
+    _, block, *shards = lax.optimization_barrier((up[1], block, *shards))
     gap = ((0, 0), (0, padded(v_rows) - v_rows))
     packs = {0: jnp.concatenate([block] + [jnp.pad(x, gap) for x in shards], axis=1)}
     bit = n_group // 2
@@ -372,14 +361,19 @@
     full_u, full_v, want = make_assemble(
         n_group, n_voc, u_rows, v_rows, rank, r, entries
     )(sampled, *[packs[k] for k in range(n_group)])
-
+    base, base_rows = make_base(r, depth, entries)(up[1], hidden, head)
+    up.append(lax.ppermute(up[1], "vocab", behind))
+    up[2], down[1], base, full_u = lax.optimization_barrier((up[2], down[1], base, full_u))
     stats = []
     for hop in range(2, half + 1):
-        pieces = [up[hop], down[hop]] if hop < half else [hidden] + ends
         extra = [base, base_rows] if hop == 2 else stats if hop == half else []
-        chunk = make_chunk(hop, len(pieces), r, depth, entries, rank, n_voc)
-        out = chunk(*pieces, head, full_u, full_v, want, *extra)
+        chunk = make_chunk(hop, 2, r, depth, entries, rank, n_voc)
+        out = chunk(up[hop], down[hop - 1], head, full_u, full_v, want, *extra)
         stats += [out[1], out[0]] if hop == 2 else [out]
+        if hop < half:
+            up.append(lax.ppermute(up[-1], "vocab", behind))
+            down.append(lax.ppermute(down[-1], "vocab", ahead))
+            up[-1], down[-1], stats[-1] = lax.optimization_barrier((up[-1], down[-1], stats[-1]))
     part = stats[-1]
     low = 1
     while low < n_voc:

time: 96.9 us -> 94.1 us (0.971)
  starting transfers between devices: 38.1 us -> 34 us
  waiting for transfers between devices: 18.8 us -> 20.6 us
    ppermute x8 -> x7, waiting for transfers between devices: 7.28 us -> 12.2 us  [the longest x2 8.53 us: body(): up.append(lax.ppermute(up[-1], 'vocab', behind))]
    ppermute x7, waiting for transfers between devices: 10.7 us -> 6.59 us  [trade(): return lax.ppermute(x, axis, [(i, i ^ bit) for i in range(size)])]
    ppermute x8 -> x7, starting transfers between devices: 11.5 us -> 9.07 us  [the longest x1 2.99 us: body(): up = [hidden, lax.ppermute(hidden, 'vocab', behind)]]
    ppermute x2, starting transfers between devices: 4.45 us -> 3.46 us  [body(): shards.append(lax.ppermute(factor_v.T, ('group', 'vocab'), moves))]
  transfers between devices with their start and end apart: 18 -> 17, of which waited for: 9 -> 9; matrix products, arithmetic and copies ran while one was open for 0% -> 0% of each run, Pallas kernels for 31% -> 32%
where the time goes in v10:
time: 94.1 us; the launch traced here: 93.9 us
  Pallas kernels  38.5 us (41%)
  starting transfers between devices  34 us (36%)
  waiting for transfers between devices  20.6 us (22%)
    pallas_call x3, Pallas kernels, body(): out = chunk(up[hop], down[hop - 1], head, full_u, full_v, want, *extra)  23.7 us
    ppermute x7, starting transfers between devices, trade(): return lax.ppermute(x, axis, [(i, i ^ bit) for i in range(size)])  19.9 us
    ppermute x2, waiting for transfers between devices, body(): up.append(lax.ppermute(up[-1], 'vocab', behind))  8.53 us
    pallas_call x1, Pallas kernels, body(): base, base_rows = make_base(r, depth, entries)(up[1], hidden, head)  6.68 us
    pallas_call x1, Pallas kernels, body(): head = make_load(depth, entries)(head)  6.61 us
    ppermute x7, waiting for transfers between devices, trade(): return lax.ppermute(x, axis, [(i, i ^ bit) for i in range(size)])  6.59 us
    ppermute x1, waiting for transfers between devices, body(): up.append(lax.ppermute(up[1], 'vocab', behind))  3.46 us
    ppermute x2, starting transfers between devices, body(): shards.append(lax.ppermute(factor_v.T, ('group', 'vocab'), moves))  3.46 us
  transfers between devices with their start and end apart: 17, of which 9 were waited for; matrix products, arithmetic and copies ran while one was open for 0% of the time, Pallas kernels for 32%

profile of v10, /device:TPU:0, one launch (start us, length us, event | category | flops | bytes accessed | tf_op | source)
XLA Modules:
  0.0 93.9 jit_solution(17679810884848413789)
XLA Ops:
  0.6 3.0 %collective-permute-start = (bf16[2,64,2304]{2,1,0:T(8,128)(2,1)}, bf16[2,64,2304]{2,1,0:T(8,128)(2,1)S(1)}, u32[]{:S(2)}, u32[]{:S(2)}) collective-permute-start(bf16[2,64,2304]{2,1,0:T(8,128)(2,1)} %down_ref.1), channel_id=1, source_target_pairs={{2,0},{4,2},{6,4},{7,6},{5,7},{3,5},{1,3},{0,1},{10,8},{12,10},{14... | collective-permute-start | bytes 1769480 | tf_op jit(solution)/shard_map/ppermute | solution.py:349
  3.6 1.6 %collective-permute-start.2 = (bf16[64,1024]{1,0:T(8,128)(2,1)}, bf16[64,1024]{1,0:T(8,128)(2,1)S(1)}, u32[]{:S(2)}, u32[]{:S(2)}) collective-permute-start(bf16[64,1024]{1,0:T(8,128)(2,1)} %bitcast.2), channel_id=1, source_target_pairs={{0,0},{4,1},{9,2},{13,3},{18,4},{22,5},{27,6},{31,7},{1,8},{5,9},{... | collective-permute-start | bytes 393224 | tf_op jit(solution)/shard_map/ppermute | solution.py:340
  5.2 0.0 copy-start
  5.2 2.0 %collective-permute-start.4 = (bf16[64,288]{1,0:T(8,128)(2,1)}, bf16[64,288]{1,0:T(8,128)(2,1)S(1)}, u32[]{:S(2)}, u32[]{:S(2)}) collective-permute-start(bf16[64,288]{1,0:T(8,128)(2,1)} %bitcast.3), channel_id=1, source_target_pairs={{1,0},{0,1},{9,2},{8,3},{17,4},{16,5},{25,6},{24,7},{3,8},{2,9},{1... | collective-permute-start | bytes 110600 | tf_op jit(solution)/shard_map/ppermute | solution.py:347
  7.2 1.4 %collective-permute-start.3 = (bf16[64,288]{1,0:T(8,128)(2,1)}, bf16[64,288]{1,0:T(8,128)(2,1)S(1)}, u32[]{:S(2)}, u32[]{:S(2)}) collective-permute-start(bf16[64,288]{1,0:T(8,128)(2,1)} %bitcast.4), channel_id=1, source_target_pairs={{0,0},{1,1},{8,2},{9,3},{16,4},{17,5},{24,6},{25,7},{2,8},{3,9},{1... | collective-permute-start | bytes 110600 | tf_op jit(solution)/shard_map/ppermute | solution.py:347
  8.6 6.6 %load.1.head_ref.refs_2_ = bf16[4096,2304]{1,0:T(8,128)(2,1)S(1)} custom-call(bf16[4096,2304]{1,0:T(8,128)(2,1)} %head_ref.1), custom_call_target="tpu_custom_call" | custom-call | bytes 18874368 | tf_op jit(solution)/shard_map/load/pallas_call | solution.py:350
  15.3 0.0 copy-start.1
  15.3 1.8 %collective-permute-done.4 = bf16[64,288]{1,0:T(8,128)(2,1)S(1)} collective-permute-done((bf16[64,288]{1,0:T(8,128)(2,1)}, bf16[64,288]{1,0:T(8,128)(2,1)S(1)}, u32[]{:S(2)}, u32[]{:S(2)}) %collective-permute-start.4) | collective-permute-done | bytes 36896 | tf_op jit(solution)/shard_map/ppermute | solution.py:347
  17.1 0.0 collective-permute-done.3
  17.1 0.0 collective-permute-done.2
  17.1 0.2 collective-permute-done.up_ref
  17.3 12.7 %collective-permute-start.7 = (bf16[64,1792]{1,0:T(8,128)(2,1)S(1)}, bf16[64,1792]{1,0:T(8,128)(2,1)S(1)}, u32[]{:S(2)}, u32[]{:S(2)}) collective-permute-start(bf16[64,1792]{1,0:T(8,128)(2,1)S(1)} %fusion.4.refs_0_), channel_id=1, source_target_pairs={{0,16},{8,24},{16,0},{24,8},{1,17},{9,25},{17,1},{25,9},{2,18},{10... | collective-permute-start | bytes 688136 | tf_op jit(solution)/shard_map/ppermute | solution.py:333
  29.9 0.0 copy-done
  29.9 0.0 collective-permute-start.5
  29.9 2.0 %collective-permute-start.1 = (bf16[2,64,2304]{2,1,0:T(8,128)(2,1)S(1)}, bf16[2,64,2304]{2,1,0:T(8,128)(2,1)S(1)}, u32[]{:S(2)}, u32[]{:S(2)}) collective-permute-start(bf16[2,64,2304]{2,1,0:T(8,128)(2,1)S(1)} %collective-permute-done.up_ref), channel_id=1, source_target_pairs={{2,0},{4,2},{6,4},{7,6},{5,7},{3,5},{1,3},{0,1},{10,8},{12,10},{14... | collective-permute-start | bytes 1769480 | tf_op jit(solution)/shard_map/ppermute | solution.py:365
  31.9 0.0 collective-permute-start.6
  32.0 2.0 %collective-permute-done.7.refs_2_ = bf16[64,1792]{1,0:T(8,128)(2,1)S(1)} collective-permute-done((bf16[64,1792]{1,0:T(8,128)(2,1)S(1)}, bf16[64,1792]{1,0:T(8,128)(2,1)S(1)}, u32[]{:S(2)}, u32[]{:S(2)}) %collective-permute-start.7) | collective-permute-done | bytes 229408 | tf_op jit(solution)/shard_map/ppermute | solution.py:333
  33.9 0.0 collective-permute-start.8
  33.9 6.7 %base.1 = (f32[4096,256]{1,0:T(8,128)S(1)}, bf16[2304,256]{1,0:T(8,128)(2,1)S(1)}) custom-call(bf16[2,64,2304]{2,1,0:T(8,128)(2,1)S(1)} %collective-permute-done.up_ref, bf16[2,64,2304]{2,1,0:T(8,128)(2,1)S(1)} %copy-done, bf16[4096,2304]{1,0:T(8,128)(2,1)S(1)} %load.1.head_ref.refs_2_), custom_call_target="tpu_custom_call" | custom-call | flops 4831838208 | bytes 18874368 | tf_op jit(solution)/shard_map/base/pallas_call | solution.py:364
  40.6 0.0 collective-permute-done.6.refs_1_
  40.6 0.0 collective-permute-done.8.refs_3_
  40.6 0.0 copy-done.1
  40.6 0.8 assemble.1
  41.5 0.0 collective-permute-done.5.refs_1_
  41.5 3.5 %collective-permute-done.1.refs_0_ = bf16[2,64,2304]{2,1,0:T(8,128)(2,1)S(1)} collective-permute-done((bf16[2,64,2304]{2,1,0:T(8,128)(2,1)S(1)}, bf16[2,64,2304]{2,1,0:T(8,128)(2,1)S(1)}, u32[]{:S(2)}, u32[]{:S(2)}) %collective-permute-start.1) | collective-permute-done | bytes 589856 | tf_op jit(solution)/shard_map/ppermute | solution.py:365
  45.0 0.0 collective-permute-start.9
  45.0 2.0 %collective-permute-start.10 = (bf16[2,64,2304]{2,1,0:T(8,128)(2,1)S(1)}, bf16[2,64,2304]{2,1,0:T(8,128)(2,1)S(1)}, u32[]{:S(2)}, u32[]{:S(2)}) collective-permute-start(bf16[2,64,2304]{2,1,0:T(8,128)(2,1)S(1)} %collective-permute-done.5.refs_1_), channel_id=1, source_target_pairs={{0,2},{2,4},{4,6},{6,7},{7,5},{5,3},{3,1},{1,0},{8,10},{10,12},{12... | collective-permute-start | bytes 1769480 | tf_op jit(solution)/shard_map/ppermute | solution.py:375
  47.0 8.7 %chunk.3 = (f32[3,256]{1,0:T(4,128)S(1)}, f32[3,256]{1,0:T(4,128)S(1)}) custom-call(bf16[2,64,2304]{2,1,0:T(8,128)(2,1)S(1)} %collective-permute-done.1.refs_0_, bf16[2,64,2304]{2,1,0:T(8,128)(2,1)S(1)} %collective-permute-done.5.refs_1_, bf16[4096,2304]{1,0:T(8,128)(2,1)S(1)} %load.1.head_ref.refs_2_, bf16[4096,64]{1,0:T(8,128)(2,1)S(1)} %get-tuple-element.39.refs_3_, ...), custom_call_target="tpu_custom_call" | custom-call | flops 5368709120 | bytes 19922944 | tf_op jit(solution)/shard_map/chunk/pallas_call | solution.py:371
  55.7 3.4 %collective-permute-done.9.refs_0_ = bf16[2,64,2304]{2,1,0:T(8,128)(2,1)S(1)} collective-permute-done((bf16[2,64,2304]{2,1,0:T(8,128)(2,1)S(1)}, bf16[2,64,2304]{2,1,0:T(8,128)(2,1)S(1)}, u32[]{:S(2)}, u32[]{:S(2)}) %collective-permute-start.9) | collective-permute-done | bytes 589856 | tf_op jit(solution)/shard_map/ppermute | solution.py:374
  59.1 0.0 collective-permute-done.10.refs_1_
  59.1 1.5 %collective-permute-start.11 = (bf16[2,64,2304]{2,1,0:T(8,128)(2,1)S(1)}, bf16[2,64,2304]{2,1,0:T(8,128)(2,1)S(1)}, u32[]{:S(2)}, u32[]{:S(2)}) collective-permute-start(bf16[2,64,2304]{2,1,0:T(8,128)(2,1)S(1)} %collective-permute-done.9.refs_0_), channel_id=1, source_target_pairs={{2,0},{4,2},{6,4},{7,6},{5,7},{3,5},{1,3},{0,1},{10,8},{12,10},{14... | collective-permute-start | bytes 1769480 | tf_op jit(solution)/shard_map/ppermute | solution.py:374
  60.6 0.5 collective-permute-start.12
  61.2 7.5 %chunk.4.refs_8_ = f32[3,256]{1,0:T(4,128)S(1)} custom-call(bf16[2,64,2304]{2,1,0:T(8,128)(2,1)S(1)} %collective-permute-done.9.refs_0_, bf16[2,64,2304]{2,1,0:T(8,128)(2,1)S(1)} %collective-permute-done.10.refs_1_, bf16[4096,2304]{1,0:T(8,128)(2,1)S(1)} %load.1.head_ref.refs_2_, bf16[4096,64]{1,0:T(8,128)(2,1)S(1)} %get-tuple-element.39.refs_3_, ...), custom_call_target="tpu_custom_call" | custom-call | flops 5368709120 | bytes 19922944 | tf_op jit(solution)/shard_map/chunk/pallas_call | solution.py:371
  68.6 5.1 %collective-permute-done.11.refs_0_ = bf16[2,64,2304]{2,1,0:T(8,128)(2,1)S(1)} collective-permute-done((bf16[2,64,2304]{2,1,0:T(8,128)(2,1)S(1)}, bf16[2,64,2304]{2,1,0:T(8,128)(2,1)S(1)}, u32[]{:S(2)}, u32[]{:S(2)}) %collective-permute-start.11) | collective-permute-done | bytes 589856 | tf_op jit(solution)/shard_map/ppermute | solution.py:374
  73.8 0.0 collective-permute-done.12.refs_1_
  73.8 7.5 %chunk.5.refs_0_ = f32[3,8,128]{2,1,0:T(8,128)S(1)} custom-call(bf16[2,64,2304]{2,1,0:T(8,128)(2,1)S(1)} %collective-permute-done.11.refs_0_, bf16[2,64,2304]{2,1,0:T(8,128)(2,1)S(1)} %collective-permute-done.12.refs_1_, bf16[4096,2304]{1,0:T(8,128)(2,1)S(1)} %load.1.head_ref.refs_2_, bf16[4096,64]{1,0:T(8,128)(2,1)S(1)} %get-tuple-element.39.refs_3_, ...), custom_call_target="tpu_custom_call" | custom-call | flops 5368709120 | bytes 19922944 | tf_op jit(solution)/shard_map/chunk/pallas_call | solution.py:371
  81.2 2.8 %collective-permute-start.13 = (f32[3,8,128]{2,1,0:T(8,128)S(1)}, f32[3,8,128]{2,1,0:T(8,128)S(1)}, u32[]{:S(2)}, u32[]{:S(2)}) collective-permute-start(f32[3,8,128]{2,1,0:T(8,128)S(1)} %chunk.5.refs_0_), channel_id=1, source_target_pairs={{0,1},{1,0},{2,3},{3,2},{4,5},{5,4},{6,7},{7,6},{8,9},{9,8},{10,11... | collective-permute-start | bytes 36872 | tf_op jit(solution)/shard_map/ppermute | solution.py:333
  84.1 1.7 %collective-permute-done.13.refs_1_ = f32[3,8,128]{2,1,0:T(8,128)S(1)} collective-permute-done((f32[3,8,128]{2,1,0:T(8,128)S(1)}, f32[3,8,128]{2,1,0:T(8,128)S(1)}, u32[]{:S(2)}, u32[]{:S(2)}) %collective-permute-start.13) | collective-permute-done | bytes 12320 | tf_op jit(solution)/shard_map/ppermute | solution.py:333
  85.8 2.8 %collective-permute-start.16 = (f32[3,8,128]{2,1,0:T(8,128)S(1)}, f32[3,8,128]{2,1,0:T(8,128)S(1)}, u32[]{:S(2)}, u32[]{:S(2)}) collective-permute-start(f32[3,8,128]{2,1,0:T(8,128)S(1)} %combine.2.refs_0_), channel_id=1, source_target_pairs={{0,6},{1,7},{2,4},{3,5},{4,2},{5,3},{6,0},{7,1},{8,14},{9,15},{10,... | collective-permute-start | bytes 36872 | tf_op jit(solution)/shard_map/ppermute | solution.py:333
  88.6 0.5 collective-permute-start.15
  89.0 1.2 %collective-permute-start.14 = (f32[3,8,128]{2,1,0:T(8,128)S(1)}, f32[3,8,128]{2,1,0:T(8,128)S(1)}, u32[]{:S(2)}, u32[]{:S(2)}) collective-permute-start(f32[3,8,128]{2,1,0:T(8,128)S(1)} %combine.2.refs_0_), channel_id=1, source_target_pairs={{0,2},{1,3},{2,0},{3,1},{4,6},{5,7},{6,4},{7,5},{8,10},{9,11},{10,... | collective-permute-start | bytes 36872 | tf_op jit(solution)/shard_map/ppermute | solution.py:333
  90.2 1.1 %collective-permute-done.16.refs_3_ = f32[3,8,128]{2,1,0:T(8,128)S(1)} collective-permute-done((f32[3,8,128]{2,1,0:T(8,128)S(1)}, f32[3,8,128]{2,1,0:T(8,128)S(1)}, u32[]{:S(2)}, u32[]{:S(2)}) %collective-permute-start.16) | collective-permute-done | bytes 12320 | tf_op jit(solution)/shard_map/ppermute | solution.py:333
  91.3 1.8 %collective-permute-done.15.refs_2_ = f32[3,8,128]{2,1,0:T(8,128)S(1)} collective-permute-done((f32[3,8,128]{2,1,0:T(8,128)S(1)}, f32[3,8,128]{2,1,0:T(8,128)S(1)}, u32[]{:S(2)}, u32[]{:S(2)}) %collective-permute-start.15) | collective-permute-done | bytes 12320 | tf_op jit(solution)/shard_map/ppermute | solution.py:333
  93.2 0.0 collective-permute-done.14.refs_1_
  93.2 0.7 combine.3
  (2 shorter events, 0.0 us)
Async XLA Ops:
  0.6 16.6 %collective-permute-start = (bf16[2,64,2304]{2,1,0:T(8,128)(2,1)}, bf16[2,64,2304]{2,1,0:T(8,128)(2,1)S(1)}, u32[]{:S(2)}, u32[]{:S(2)}) collective-permute-start(bf16[2,64,2304]{2,1,0:T(8,128)(2,1)} %down_ref.1), channel_id=1, source_target_pairs={{2,0},{4,2},{6,4},{7,6},{5,7},{3,5},{1,3},{0,1},{10,8},{12,10},{14... | collective-permute-start | bytes 1769480 | tf_op jit(solution)/shard_map/ppermute | solution.py:349
  3.6 13.4 %collective-permute-start.2 = (bf16[64,1024]{1,0:T(8,128)(2,1)}, bf16[64,1024]{1,0:T(8,128)(2,1)S(1)}, u32[]{:S(2)}, u32[]{:S(2)}) collective-permute-start(bf16[64,1024]{1,0:T(8,128)(2,1)} %bitcast.2), channel_id=1, source_target_pairs={{0,0},{4,1},{9,2},{13,3},{18,4},{22,5},{27,6},{31,7},{1,8},{5,9},{... | collective-permute-start | bytes 393224 | tf_op jit(solution)/shard_map/ppermute | solution.py:340
  5.2 24.8 %copy-start = (bf16[2,64,2304]{2,1,0:T(8,128)(2,1)S(1)}, bf16[2,64,2304]{2,1,0:T(8,128)(2,1)}, u32[]{:S(2)}) copy-start(bf16[2,64,2304]{2,1,0:T(8,128)(2,1)} %down_ref.1) | copy-start | bytes 1769476
  5.2 11.9 %collective-permute-start.4 = (bf16[64,288]{1,0:T(8,128)(2,1)}, bf16[64,288]{1,0:T(8,128)(2,1)S(1)}, u32[]{:S(2)}, u32[]{:S(2)}) collective-permute-start(bf16[64,288]{1,0:T(8,128)(2,1)} %bitcast.3), channel_id=1, source_target_pairs={{1,0},{0,1},{9,2},{8,3},{17,4},{16,5},{25,6},{24,7},{3,8},{2,9},{1... | collective-permute-start | bytes 110600 | tf_op jit(solution)/shard_map/ppermute | solution.py:347
  7.2 9.9 %collective-permute-start.3 = (bf16[64,288]{1,0:T(8,128)(2,1)}, bf16[64,288]{1,0:T(8,128)(2,1)S(1)}, u32[]{:S(2)}, u32[]{:S(2)}) collective-permute-start(bf16[64,288]{1,0:T(8,128)(2,1)} %bitcast.4), channel_id=1, source_target_pairs={{0,0},{1,1},{8,2},{9,3},{16,4},{17,5},{24,6},{25,7},{2,8},{3,9},{1... | collective-permute-start | bytes 110600 | tf_op jit(solution)/shard_map/ppermute | solution.py:347
  15.3 25.4 %copy-start.1 = (s32[2,512]{1,0:T(2,128)S(1)}, s32[2,512]{1,0:T(2,128)}, u32[]{:S(2)}) copy-start(s32[2,512]{1,0:T(2,128)} %sampled_ref.1) | copy-start | bytes 12292
  17.3 16.7 %collective-permute-start.7 = (bf16[64,1792]{1,0:T(8,128)(2,1)S(1)}, bf16[64,1792]{1,0:T(8,128)(2,1)S(1)}, u32[]{:S(2)}, u32[]{:S(2)}) collective-permute-start(bf16[64,1792]{1,0:T(8,128)(2,1)S(1)} %fusion.4.refs_0_), channel_id=1, source_target_pairs={{0,16},{8,24},{16,0},{24,8},{1,17},{9,25},{17,1},{25,9},{2,18},{10... | collective-permute-start | bytes 688136 | tf_op jit(solution)/shard_map/ppermute | solution.py:333
  29.9 11.6 %collective-permute-start.5 = (bf16[2,64,2304]{2,1,0:T(8,128)(2,1)S(1)}, bf16[2,64,2304]{2,1,0:T(8,128)(2,1)S(1)}, u32[]{:S(2)}, u32[]{:S(2)}) collective-permute-start(bf16[2,64,2304]{2,1,0:T(8,128)(2,1)S(1)} %copy-done), channel_id=1, source_target_pairs={{0,2},{2,4},{4,6},{6,7},{7,5},{5,3},{3,1},{1,0},{8,10},{10,12},{12... | collective-permute-start | bytes 1769480 | tf_op jit(solution)/shard_map/ppermute | solution.py:352
  29.9 15.0 %collective-permute-start.1 = (bf16[2,64,2304]{2,1,0:T(8,128)(2,1)S(1)}, bf16[2,64,2304]{2,1,0:T(8,128)(2,1)S(1)}, u32[]{:S(2)}, u32[]{:S(2)}) collective-permute-start(bf16[2,64,2304]{2,1,0:T(8,128)(2,1)S(1)} %collective-permute-done.up_ref), channel_id=1, source_target_pairs={{2,0},{4,2},{6,4},{7,6},{5,7},{3,5},{1,3},{0,1},{10,8},{12,10},{14... | collective-permute-start | bytes 1769480 | tf_op jit(solution)/shard_map/ppermute | solution.py:365
  31.9 8.7 %collective-permute-start.6 = (bf16[64,1792]{1,0:T(8,128)(2,1)S(1)}, bf16[64,1792]{1,0:T(8,128)(2,1)S(1)}, u32[]{:S(2)}, u32[]{:S(2)}) collective-permute-start(bf16[64,1792]{1,0:T(8,128)(2,1)S(1)} %fusion.4.refs_0_), channel_id=1, source_target_pairs={{0,8},{8,0},{16,24},{24,16},{1,9},{9,1},{17,25},{25,17},{2,10},{10... | collective-permute-start | bytes 688136 | tf_op jit(solution)/shard_map/ppermute | solution.py:333
  33.9 6.7 %collective-permute-start.8 = (bf16[64,1792]{1,0:T(8,128)(2,1)S(1)}, bf16[64,1792]{1,0:T(8,128)(2,1)S(1)}, u32[]{:S(2)}, u32[]{:S(2)}) collective-permute-start(bf16[64,1792]{1,0:T(8,128)(2,1)S(1)} %collective-permute-done.7.refs_2_), channel_id=1, source_target_pairs={{0,8},{8,0},{16,24},{24,16},{1,9},{9,1},{17,25},{25,17},{2,10},{10... | collective-permute-start | bytes 688136 | tf_op jit(solution)/shard_map/ppermute | solution.py:333
  45.0 14.2 %collective-permute-start.9 = (bf16[2,64,2304]{2,1,0:T(8,128)(2,1)S(1)}, bf16[2,64,2304]{2,1,0:T(8,128)(2,1)S(1)}, u32[]{:S(2)}, u32[]{:S(2)}) collective-permute-start(bf16[2,64,2304]{2,1,0:T(8,128)(2,1)S(1)} %collective-permute-done.1.refs_0_), channel_id=1, source_target_pairs={{2,0},{4,2},{6,4},{7,6},{5,7},{3,5},{1,3},{0,1},{10,8},{12,10},{14... | collective-permute-start | bytes 1769480 | tf_op jit(solution)/shard_map/ppermute | solution.py:374
  45.0 14.2 %collective-permute-start.10 = (bf16[2,64,2304]{2,1,0:T(8,128)(2,1)S(1)}, bf16[2,64,2304]{2,1,0:T(8,128)(2,1)S(1)}, u32[]{:S(2)}, u32[]{:S(2)}) collective-permute-start(bf16[2,64,2304]{2,1,0:T(8,128)(2,1)S(1)} %collective-permute-done.5.refs_1_), channel_id=1, source_target_pairs={{0,2},{2,4},{4,6},{6,7},{7,5},{5,3},{3,1},{1,0},{8,10},{10,12},{12... | collective-permute-start | bytes 1769480 | tf_op jit(solution)/shard_map/ppermute | solution.py:375
  59.1 14.6 %collective-permute-start.11 = (bf16[2,64,2304]{2,1,0:T(8,128)(2,1)S(1)}, bf16[2,64,2304]{2,1,0:T(8,128)(2,1)S(1)}, u32[]{:S(2)}, u32[]{:S(2)}) collective-permute-start(bf16[2,64,2304]{2,1,0:T(8,128)(2,1)S(1)} %collective-permute-done.9.refs_0_), channel_id=1, source_target_pairs={{2,0},{4,2},{6,4},{7,6},{5,7},{3,5},{1,3},{0,1},{10,8},{12,10},{14... | collective-permute-start | bytes 1769480 | tf_op jit(solution)/shard_map/ppermute | solution.py:374
  60.6 13.1 %collective-permute-start.12 = (bf16[2,64,2304]{2,1,0:T(8,128)(2,1)S(1)}, bf16[2,64,2304]{2,1,0:T(8,128)(2,1)S(1)}, u32[]{:S(2)}, u32[]{:S(2)}) collective-permute-start(bf16[2,64,2304]{2,1,0:T(8,128)(2,1)S(1)} %collective-permute-done.10.refs_1_), channel_id=1, source_target_pairs={{0,2},{2,4},{4,6},{6,7},{7,5},{5,3},{3,1},{1,0},{8,10},{10,12},{12... | collective-permute-start | bytes 1769480 | tf_op jit(solution)/shard_map/ppermute | solution.py:375
  81.2 4.5 %collective-permute-start.13 = (f32[3,8,128]{2,1,0:T(8,128)S(1)}, f32[3,8,128]{2,1,0:T(8,128)S(1)}, u32[]{:S(2)}, u32[]{:S(2)}) collective-permute-start(f32[3,8,128]{2,1,0:T(8,128)S(1)} %chunk.5.refs_0_), channel_id=1, source_target_pairs={{0,1},{1,0},{2,3},{3,2},{4,5},{5,4},{6,7},{7,6},{8,9},{9,8},{10,11... | collective-permute-start | bytes 36872 | tf_op jit(solution)/shard_map/ppermute | solution.py:333
  85.8 5.6 %collective-permute-start.16 = (f32[3,8,128]{2,1,0:T(8,128)S(1)}, f32[3,8,128]{2,1,0:T(8,128)S(1)}, u32[]{:S(2)}, u32[]{:S(2)}) collective-permute-start(f32[3,8,128]{2,1,0:T(8,128)S(1)} %combine.2.refs_0_), channel_id=1, source_target_pairs={{0,6},{1,7},{2,4},{3,5},{4,2},{5,3},{6,0},{7,1},{8,14},{9,15},{10,... | collective-permute-start | bytes 36872 | tf_op jit(solution)/shard_map/ppermute | solution.py:333
  88.6 4.6 %collective-permute-start.15 = (f32[3,8,128]{2,1,0:T(8,128)S(1)}, f32[3,8,128]{2,1,0:T(8,128)S(1)}, u32[]{:S(2)}, u32[]{:S(2)}) collective-permute-start(f32[3,8,128]{2,1,0:T(8,128)S(1)} %combine.2.refs_0_), channel_id=1, source_target_pairs={{0,4},{1,5},{2,6},{3,7},{4,0},{5,1},{6,2},{7,3},{8,12},{9,13},{10,... | collective-permute-start | bytes 36872 | tf_op jit(solution)/shard_map/ppermute | solution.py:333
  89.0 4.1 %collective-permute-start.14 = (f32[3,8,128]{2,1,0:T(8,128)S(1)}, f32[3,8,128]{2,1,0:T(8,128)S(1)}, u32[]{:S(2)}, u32[]{:S(2)}) collective-permute-start(f32[3,8,128]{2,1,0:T(8,128)S(1)} %combine.2.refs_0_), channel_id=1, source_target_pairs={{0,2},{1,3},{2,0},{3,1},{4,6},{5,7},{6,4},{7,5},{8,10},{9,11},{10,... | collective-permute-start | bytes 36872 | tf_op jit(solution)/shard_map/ppermute | solution.py:333

commit v11 on v10

--- a/solution.py
+++ b/solution.py
@@ -149,27 +149,21 @@
     )
 
 
-def make_chunk(hop, pieces, r, depth, entries, rank, n_voc):
+def make_chunk(hop, r, depth, entries, rank, n_voc):
     tile = tile_rows(entries)
     tiles = entries // tile
     n = 4 * r
-    carry, last = hop == 2, hop == n_voc // 2
+    carry, last = 2 * (hop == 3), hop == n_voc // 2
     earlier = hop - 1 if last else 0
 
     def kernel(*refs):
-        piece, refs = refs[:pieces], refs[pieces:]
+        piece, refs = refs[:2], refs[2:]
         head_ref, u_ref, v_ref, want_ref, *refs = refs
-        if carry:
-            base_ref, base_rows, *refs = refs
+        bases, refs = refs[: 2 * carry], refs[2 * carry :]
         before, refs = refs[:earlier], refs[earlier:]
-        out_ref, *refs = refs
-        if carry:
-            base_out, *refs = refs
-        rows, even, odd, proj, top, total, pick, *refs = refs
-        if carry:
-            base_proj, base_top, base_total, base_pick = refs
-            base_state = base_top, base_total, base_pick
-        state = top, total, pick
+        (out_ref, *base_outs), refs = refs[: 1 + carry], refs[1 + carry :]
+        rows, even, odd, *refs = refs
+        (proj, *state), *base_scratch = [refs[4 * k : 4 * k + 4] for k in range(1 + carry)]
 
         def project(source, into):
             into[...] = jnp.dot(
@@ -190,10 +184,11 @@
         clear(*state)
         odd[...] = jnp.full(odd.shape, -1e30, jnp.float32)
         want = wanted(hop)
-        if carry:
-            project(base_rows, base_proj)
-            clear(*base_state)
-            base_want = wanted(1)
+        base_wants = []
+        for k in range(carry):
+            project(bases[2 * k + 1], base_scratch[k][0])
+            clear(*base_scratch[k][1:])
+            base_wants.append(wanted(k + 1))
 
         def multiply(t, into):
             span = pl.ds(pl.multiple_of(t * tile, tile), tile)
@@ -212,22 +207,23 @@
             pick[...] = pick[...] + jnp.sum(hit.reshape(tile // 8, 8, n), axis=0)
             top[...] = new
 
-        def finish_base(t):
-            if carry:
-                span = pl.ds(pl.multiple_of(t * tile, tile), tile)
-                x = base_ref[span, :] + jnp.dot(
+        def finish_bases(t):
+            span = pl.ds(pl.multiple_of(t * tile, tile), tile)
+            for k in range(carry):
+                base_proj, *base_state = base_scratch[k]
+                x = bases[2 * k][span, :] + jnp.dot(
                     u_ref[span, :], base_proj[...], preferred_element_type=jnp.float32
                 )
-                reduce(x, base_want - t * tile, *base_state)
+                reduce(x, base_wants[k] - t * tile, *base_state)
 
         @pl.loop(0, tiles // 2)
         def _(i):
             multiply(2 * i, even)
             reduce(odd[...], want - jnp.where(i == 0, 1 << 29, (2 * i - 1) * tile), *state)
-            finish_base(2 * i)
+            finish_bases(2 * i)
             multiply(2 * i + 1, odd)
             reduce(even[...], want - 2 * i * tile, *state)
-            finish_base(2 * i + 1)
+            finish_bases(2 * i + 1)
 
         reduce(odd[...], want - (entries - tile), *state)
 
@@ -236,9 +232,9 @@
             sums = jnp.sum(total[...] * jnp.exp(top[...] - best), axis=0, keepdims=True)
             return best, sums, jnp.sum(pick[...], axis=0, keepdims=True)
 
-        if carry:
-            for q, value in enumerate(results(*base_state)):
-                base_out[q : q + 1, :] = value
+        for k in range(carry):
+            for q, value in enumerate(results(*base_scratch[k][1:])):
+                base_outs[k][q : q + 1, :] = value
         for q, value in enumerate(results(*state)):
             if not last:
                 out_ref[q : q + 1, :] = value
@@ -254,9 +250,9 @@
     small = [pltpu.VMEM((rank, n), jnp.bfloat16)] + [pltpu.VMEM((8, n), jnp.float32)] * 3
     return pl.pallas_call(
         kernel,
-        out_shape=(out_shape, out_shape) if carry else out_shape,
-        in_specs=[WHOLE] * (pieces + 4 + 2 * carry + earlier),
-        out_specs=(WHOLE, WHOLE) if carry else WHOLE,
+        out_shape=(out_shape,) * (1 + carry) if carry else out_shape,
+        in_specs=[WHOLE] * (6 + 2 * carry + earlier),
+        out_specs=(WHOLE,) * (1 + carry) if carry else WHOLE,
         scratch_shapes=[
             pltpu.VMEM((depth, n), jnp.bfloat16),
             pltpu.VMEM((tile, n), jnp.float32),
@@ -346,13 +342,21 @@
         ]
         shards.append(lax.ppermute(factor_v.T, ("group", "vocab"), moves))
 
+    head = make_load(depth, entries)(head)
     up = [hidden, lax.ppermute(hidden, "vocab", behind)]
-    head = make_load(depth, entries)(head)
-    first, head, block, *shards = lax.optimization_barrier((hidden, head, block, *shards))
+    first, _ = lax.optimization_barrier((hidden, up[1]))
     down = [hidden, lax.ppermute(first, "vocab", ahead)]
-    _, block, *shards = lax.optimization_barrier((up[1], block, *shards))
+    up.append(lax.ppermute(up[1], "vocab", behind))
+    base, base_rows = make_base(r, depth, entries)(up[1], hidden, head)
+    base, block, *shards = lax.optimization_barrier((base, block, *shards))
+    held = [base, base_rows]
     gap = ((0, 0), (0, padded(v_rows) - v_rows))
-    packs = {0: jnp.concatenate([block] + [jnp.pad(x, gap) for x in shards], axis=1)}
+    pack = jnp.concatenate([block] + [jnp.pad(x, gap) for x in shards], axis=1)
+    up[2], down[1], held[0], pack = lax.optimization_barrier((up[2], down[1], held[0], pack))
+
+    up.append(lax.ppermute(up[2], "vocab", behind))
+    down.append(lax.ppermute(down[1], "vocab", ahead))
+    packs = {0: pack}
     bit = n_group // 2
     while bit:
         for k in list(packs):
@@ -361,15 +365,15 @@
     full_u, full_v, want = make_assemble(
         n_group, n_voc, u_rows, v_rows, rank, r, entries
     )(sampled, *[packs[k] for k in range(n_group)])
-    base, base_rows = make_base(r, depth, entries)(up[1], hidden, head)
-    up.append(lax.ppermute(up[1], "vocab", behind))
-    up[2], down[1], base, full_u = lax.optimization_barrier((up[2], down[1], base, full_u))
+    held += make_base(r, depth, entries)(up[2], down[1], head)
+    up[3], down[2], held[2], full_u = lax.optimization_barrier((up[3], down[2], held[2], full_u))
+
     stats = []
-    for hop in range(2, half + 1):
-        extra = [base, base_rows] if hop == 2 else stats if hop == half else []
-        chunk = make_chunk(hop, 2, r, depth, entries, rank, n_voc)
+    for hop in range(3, half + 1):
+        extra = held if hop == 3 else stats if hop == half else []
+        chunk = make_chunk(hop, r, depth, entries, rank, n_voc)
         out = chunk(up[hop], down[hop - 1], head, full_u, full_v, want, *extra)
-        stats += [out[1], out[0]] if hop == 2 else [out]
+        stats += [out[1], out[2], out[0]] if hop == 3 else [out]
         if hop < half:
             up.append(lax.ppermute(up[-1], "vocab", behind))
             down.append(lax.ppermute(down[-1], "vocab", ahead))

time: 94.1 us -> 90.5 us (0.962)
  starting transfers between devices: 34 us -> 25.7 us
  waiting for transfers between devices: 20.6 us -> 24.6 us
    ppermute x7, starting transfers between devices: 19.9 us -> 6.01 us  [trade(): return lax.ppermute(x, axis, [(i, i ^ bit) for i in range(size)])]
    ppermute x1, starting transfers between devices: 0.01 us -> 7.48 us  [body(): down = [hidden, lax.ppermute(first, 'vocab', ahead)]]
    ppermute x2 -> x1, waiting for transfers between devices: 8.53 us -> 1.39 us  [body(): up.append(lax.ppermute(up[-1], 'vocab', behind))]
    pallas_call x0 -> x1, Pallas kernels: none -> 6.69 us  [body(): held += make_base(r, depth, entries)(up[2], down[1], head)]
    pallas_call x3 -> x2, Pallas kernels: 23.7 us -> 17.7 us  [body(): out = chunk(up[hop], down[hop - 1], head, full_u, full_v, want, *extra)]
    ppermute x7, waiting for transfers between devices: 6.59 us -> 9.45 us  [trade(): return lax.ppermute(x, axis, [(i, i ^ bit) for i in range(size)])]
    ppermute x2 -> x1, starting transfers between devices: 2.55 us -> 0.01 us  [body(): down.append(lax.ppermute(down[-1], 'vocab', ahead))]
    ppermute x1, waiting for transfers between devices: 0.01 us -> 2.43 us  [body(): down = [hidden, lax.ppermute(first, 'vocab', ahead)]]
  transfers between devices with their start and end apart: 17 -> 17, of which waited for: 9 -> 11; matrix products, arithmetic and copies ran while one was open for 0% -> 0% of each run, Pallas kernels for 32% -> 34%
where the time goes in v11:
time: 90.5 us; the launch traced here: 90.3 us
  Pallas kernels  39.3 us (43%)
  starting transfers between devices  25.7 us (28%)
  waiting for transfers between devices  24.6 us (27%)
    pallas_call x2, Pallas kernels, body(): out = chunk(up[hop], down[hop - 1], head, full_u, full_v, want, *extra)  17.7 us
    ppermute x7, waiting for transfers between devices, trade(): return lax.ppermute(x, axis, [(i, i ^ bit) for i in range(size)])  9.45 us
    ppermute x1, starting transfers between devices, body(): down = [hidden, lax.ppermute(first, 'vocab', ahead)]  7.48 us
    pallas_call x1, Pallas kernels, body(): held += make_base(r, depth, entries)(up[2], down[1], head)  6.69 us
    pallas_call x1, Pallas kernels, body(): base, base_rows = make_base(r, depth, entries)(up[1], hidden, head)  6.69 us
    pallas_call x1, Pallas kernels, body(): head = make_load(depth, entries)(head)  6.61 us
    ppermute x7, starting transfers between devices, trade(): return lax.ppermute(x, axis, [(i, i ^ bit) for i in range(size)])  6.01 us
    ppermute x1, waiting for transfers between devices, body(): up.append(lax.ppermute(up[1], 'vocab', behind))  5.61 us
  transfers between devices with their start and end apart: 17, of which 11 were waited for; matrix products, arithmetic and copies ran while one was open for 0% of the time, Pallas kernels for 34%

profile of v11, /device:TPU:0, one launch (start us, length us, event | category | flops | bytes accessed | tf_op | source)
XLA Modules:
  0.0 90.3 jit_solution(15139458009023490644)
XLA Ops:
  0.6 3.0 %collective-permute-start = (bf16[2,64,2304]{2,1,0:T(8,128)(2,1)}, bf16[2,64,2304]{2,1,0:T(8,128)(2,1)S(1)}, u32[]{:S(2)}, u32[]{:S(2)}) collective-permute-start(bf16[2,64,2304]{2,1,0:T(8,128)(2,1)} %down_ref.1), channel_id=1, source_target_pairs={{2,0},{4,2},{6,4},{7,6},{5,7},{3,5},{1,3},{0,1},{10,8},{12,10},{14... | collective-permute-start | bytes 1769480 | tf_op jit(solution)/shard_map/ppermute | solution.py:346
  3.6 1.4 %collective-permute-start.4 = (bf16[64,288]{1,0:T(8,128)(2,1)}, bf16[64,288]{1,0:T(8,128)(2,1)S(1)}, u32[]{:S(2)}, u32[]{:S(2)}) collective-permute-start(bf16[64,288]{1,0:T(8,128)(2,1)} %bitcast.3), channel_id=1, source_target_pairs={{0,0},{1,1},{8,2},{9,3},{16,4},{17,5},{24,6},{25,7},{2,8},{3,9},{1... | collective-permute-start | bytes 110600 | tf_op jit(solution)/shard_map/ppermute | solution.py:343
  5.1 1.6 %collective-permute-start.5 = (bf16[64,288]{1,0:T(8,128)(2,1)}, bf16[64,288]{1,0:T(8,128)(2,1)S(1)}, u32[]{:S(2)}, u32[]{:S(2)}) collective-permute-start(bf16[64,288]{1,0:T(8,128)(2,1)} %bitcast.4), channel_id=1, source_target_pairs={{1,0},{0,1},{9,2},{8,3},{17,4},{16,5},{25,6},{24,7},{3,8},{2,9},{1... | collective-permute-start | bytes 110600 | tf_op jit(solution)/shard_map/ppermute | solution.py:343
  6.6 0.0 copy-start
  6.6 1.7 %collective-permute-start.3 = (bf16[64,1024]{1,0:T(8,128)(2,1)}, bf16[64,1024]{1,0:T(8,128)(2,1)S(1)}, u32[]{:S(2)}, u32[]{:S(2)}) collective-permute-start(bf16[64,1024]{1,0:T(8,128)(2,1)} %bitcast.2), channel_id=1, source_target_pairs={{0,0},{4,1},{9,2},{13,3},{18,4},{22,5},{27,6},{31,7},{1,8},{5,9},{... | collective-permute-start | bytes 393224 | tf_op jit(solution)/shard_map/ppermute | solution.py:336
  8.3 6.6 %load.1.head_ref.refs_2_ = bf16[4096,2304]{1,0:T(8,128)(2,1)S(1)} custom-call(bf16[4096,2304]{1,0:T(8,128)(2,1)} %head_ref.1), custom_call_target="tpu_custom_call" | custom-call | bytes 18874368 | tf_op jit(solution)/shard_map/load/pallas_call | solution.py:345
  14.9 2.3 %collective-permute-done.up_ref = bf16[2,64,2304]{2,1,0:T(8,128)(2,1)S(1)} collective-permute-done((bf16[2,64,2304]{2,1,0:T(8,128)(2,1)}, bf16[2,64,2304]{2,1,0:T(8,128)(2,1)S(1)}, u32[]{:S(2)}, u32[]{:S(2)}) %collective-permute-start) | collective-permute-done | bytes 589856 | tf_op jit(solution)/shard_map/ppermute | solution.py:346
  17.2 0.0 copy-done
  17.2 7.5 %collective-permute-start.2 = (bf16[2,64,2304]{2,1,0:T(8,128)(2,1)S(1)}, bf16[2,64,2304]{2,1,0:T(8,128)(2,1)S(1)}, u32[]{:S(2)}, u32[]{:S(2)}) collective-permute-start(bf16[2,64,2304]{2,1,0:T(8,128)(2,1)S(1)} %copy-done), channel_id=1, source_target_pairs={{0,2},{2,4},{4,6},{6,7},{7,5},{5,3},{3,1},{1,0},{8,10},{10,12},{12... | collective-permute-start | bytes 1769480 | tf_op jit(solution)/shard_map/ppermute | solution.py:348
  24.7 0.0 collective-permute-start.1
  24.7 6.7 %base.2 = (f32[4096,256]{1,0:T(8,128)S(1)}, bf16[2304,256]{1,0:T(8,128)(2,1)S(1)}) custom-call(bf16[2,64,2304]{2,1,0:T(8,128)(2,1)S(1)} %collective-permute-done.up_ref, bf16[2,64,2304]{2,1,0:T(8,128)(2,1)S(1)} %copy-done, bf16[4096,2304]{1,0:T(8,128)(2,1)S(1)} %load.1.head_ref.refs_2_), custom_call_target="tpu_custom_call" | custom-call | flops 4831838208 | bytes 18874368 | tf_op jit(solution)/shard_map/base/pallas_call | solution.py:350
  31.4 0.0 collective-permute-done.4
  31.4 0.0 collective-permute-done.5
  31.5 0.0 collective-permute-done.3
  31.5 0.0 copy-start.1
  31.5 2.4 %collective-permute-done.2.down_ref = bf16[2,64,2304]{2,1,0:T(8,128)(2,1)S(1)} collective-permute-done((bf16[2,64,2304]{2,1,0:T(8,128)(2,1)S(1)}, bf16[2,64,2304]{2,1,0:T(8,128)(2,1)S(1)}, u32[]{:S(2)}, u32[]{:S(2)}) %collective-permute-start.2) | collective-permute-done | bytes 589856 | tf_op jit(solution)/shard_map/ppermute | solution.py:348
  33.9 5.6 %collective-permute-done.1.up_ref = bf16[2,64,2304]{2,1,0:T(8,128)(2,1)S(1)} collective-permute-done((bf16[2,64,2304]{2,1,0:T(8,128)(2,1)S(1)}, bf16[2,64,2304]{2,1,0:T(8,128)(2,1)S(1)}, u32[]{:S(2)}, u32[]{:S(2)}) %collective-permute-start.1) | collective-permute-done | bytes 589856 | tf_op jit(solution)/shard_map/ppermute | solution.py:349
  39.5 0.0 collective-permute-start.9
  39.5 0.3 collective-permute-start.6
  39.9 1.7 %collective-permute-start.7 = (bf16[2,64,2304]{2,1,0:T(8,128)(2,1)S(1)}, bf16[2,64,2304]{2,1,0:T(8,128)(2,1)S(1)}, u32[]{:S(2)}, u32[]{:S(2)}) collective-permute-start(bf16[2,64,2304]{2,1,0:T(8,128)(2,1)S(1)} %collective-permute-done.2.down_ref), channel_id=1, source_target_pairs={{0,2},{2,4},{4,6},{6,7},{7,5},{5,3},{3,1},{1,0},{8,10},{10,12},{12... | collective-permute-start | bytes 1769480 | tf_op jit(solution)/shard_map/ppermute | solution.py:358
  41.6 0.0 collective-permute-start.8
  41.6 4.0 %collective-permute-done.9.refs_2_ = bf16[64,1792]{1,0:T(8,128)(2,1)S(1)} collective-permute-done((bf16[64,1792]{1,0:T(8,128)(2,1)S(1)}, bf16[64,1792]{1,0:T(8,128)(2,1)S(1)}, u32[]{:S(2)}, u32[]{:S(2)}) %collective-permute-start.9) | collective-permute-done | bytes 229408 | tf_op jit(solution)/shard_map/ppermute | solution.py:329
  45.6 0.0 collective-permute-start.10
  45.6 6.7 %base.3 = (f32[4096,256]{1,0:T(8,128)S(1)}, bf16[2304,256]{1,0:T(8,128)(2,1)S(1)}) custom-call(bf16[2,64,2304]{2,1,0:T(8,128)(2,1)S(1)} %collective-permute-done.1.up_ref, bf16[2,64,2304]{2,1,0:T(8,128)(2,1)S(1)} %collective-permute-done.2.down_ref, bf16[4096,2304]{1,0:T(8,128)(2,1)S(1)} %load.1.head_ref.refs_2_), custom_call_target="tpu_custom_call" | custom-call | flops 4831838208 | bytes 18874368 | tf_op jit(solution)/shard_map/base/pallas_call | solution.py:368
  52.3 0.0 collective-permute-done.8.refs_1_
  52.3 0.0 collective-permute-done.10.refs_3_
  52.3 0.0 copy-done.1
  52.3 0.8 assemble.1
  53.1 0.8 collective-permute-done.6.refs_0_
  53.9 1.5 %collective-permute-done.7.refs_1_ = bf16[2,64,2304]{2,1,0:T(8,128)(2,1)S(1)} collective-permute-done((bf16[2,64,2304]{2,1,0:T(8,128)(2,1)S(1)}, bf16[2,64,2304]{2,1,0:T(8,128)(2,1)S(1)}, u32[]{:S(2)}, u32[]{:S(2)}) %collective-permute-start.7) | collective-permute-done | bytes 589856 | tf_op jit(solution)/shard_map/ppermute | solution.py:358
  55.5 2.5 %collective-permute-start.11 = (bf16[2,64,2304]{2,1,0:T(8,128)(2,1)S(1)}, bf16[2,64,2304]{2,1,0:T(8,128)(2,1)S(1)}, u32[]{:S(2)}, u32[]{:S(2)}) collective-permute-start(bf16[2,64,2304]{2,1,0:T(8,128)(2,1)S(1)} %collective-permute-done.6.refs_0_), channel_id=1, source_target_pairs={{2,0},{4,2},{6,4},{7,6},{5,7},{3,5},{1,3},{0,1},{10,8},{12,10},{14... | collective-permute-start | bytes 1769480 | tf_op jit(solution)/shard_map/ppermute | solution.py:378
  57.9 0.0 collective-permute-start.12
  57.9 10.2 %chunk.2 = (f32[3,256]{1,0:T(4,128)S(1)}, f32[3,256]{1,0:T(4,128)S(1)}, f32[3,256]{1,0:T(4,128)S(1)}) custom-call(bf16[2,64,2304]{2,1,0:T(8,128)(2,1)S(1)} %collective-permute-done.6.refs_0_, bf16[2,64,2304]{2,1,0:T(8,128)(2,1)S(1)} %collective-permute-done.7.refs_1_, bf16[4096,2304]{1,0:T(8,128)(2,1)S(1)} %load.1.head_ref.refs_2_, ...), custom_call_target="tpu_custom_call" | custom-call | flops 5368709120 | bytes 19922944 | tf_op jit(solution)/shard_map/chunk/pallas_call | solution.py:375
  68.2 1.4 %collective-permute-done.11.refs_0_ = bf16[2,64,2304]{2,1,0:T(8,128)(2,1)S(1)} collective-permute-done((bf16[2,64,2304]{2,1,0:T(8,128)(2,1)S(1)}, bf16[2,64,2304]{2,1,0:T(8,128)(2,1)S(1)}, u32[]{:S(2)}, u32[]{:S(2)}) %collective-permute-start.11) | collective-permute-done | bytes 589856 | tf_op jit(solution)/shard_map/ppermute | solution.py:378
  69.6 1.1 %collective-permute-done.12.refs_1_ = bf16[2,64,2304]{2,1,0:T(8,128)(2,1)S(1)} collective-permute-done((bf16[2,64,2304]{2,1,0:T(8,128)(2,1)S(1)}, bf16[2,64,2304]{2,1,0:T(8,128)(2,1)S(1)}, u32[]{:S(2)}, u32[]{:S(2)}) %collective-permute-start.12) | collective-permute-done | bytes 589856 | tf_op jit(solution)/shard_map/ppermute | solution.py:379
  70.7 7.5 %chunk.3.refs_0_ = f32[3,8,128]{2,1,0:T(8,128)S(1)} custom-call(bf16[2,64,2304]{2,1,0:T(8,128)(2,1)S(1)} %collective-permute-done.11.refs_0_, bf16[2,64,2304]{2,1,0:T(8,128)(2,1)S(1)} %collective-permute-done.12.refs_1_, bf16[4096,2304]{1,0:T(8,128)(2,1)S(1)} %load.1.head_ref.refs_2_, bf16[4096,64]{1,0:T(8,128)(2,1)S(1)} %get-tuple-element.41.refs_3_, ...), custom_call_target="tpu_custom_call" | custom-call | flops 5368709120 | bytes 19922944 | tf_op jit(solution)/shard_map/chunk/pallas_call | solution.py:375
  78.1 1.6 %collective-permute-start.13 = (f32[3,8,128]{2,1,0:T(8,128)S(1)}, f32[3,8,128]{2,1,0:T(8,128)S(1)}, u32[]{:S(2)}, u32[]{:S(2)}) collective-permute-start(f32[3,8,128]{2,1,0:T(8,128)S(1)} %chunk.3.refs_0_), channel_id=1, source_target_pairs={{0,1},{1,0},{2,3},{3,2},{4,5},{5,4},{6,7},{7,6},{8,9},{9,8},{10,11... | collective-permute-start | bytes 36872 | tf_op jit(solution)/shard_map/ppermute | solution.py:329
  79.7 2.2 %collective-permute-done.13.refs_1_ = f32[3,8,128]{2,1,0:T(8,128)S(1)} collective-permute-done((f32[3,8,128]{2,1,0:T(8,128)S(1)}, f32[3,8,128]{2,1,0:T(8,128)S(1)}, u32[]{:S(2)}, u32[]{:S(2)}) %collective-permute-start.13) | collective-permute-done | bytes 12320 | tf_op jit(solution)/shard_map/ppermute | solution.py:329
  81.9 1.3 %collective-permute-start.14 = (f32[3,8,128]{2,1,0:T(8,128)S(1)}, f32[3,8,128]{2,1,0:T(8,128)S(1)}, u32[]{:S(2)}, u32[]{:S(2)}) collective-permute-start(f32[3,8,128]{2,1,0:T(8,128)S(1)} %combine.2.refs_0_), channel_id=1, source_target_pairs={{0,2},{1,3},{2,0},{3,1},{4,6},{5,7},{6,4},{7,5},{8,10},{9,11},{10,... | collective-permute-start | bytes 36872 | tf_op jit(solution)/shard_map/ppermute | solution.py:329
  83.2 0.9 %collective-permute-start.15 = (f32[3,8,128]{2,1,0:T(8,128)S(1)}, f32[3,8,128]{2,1,0:T(8,128)S(1)}, u32[]{:S(2)}, u32[]{:S(2)}) collective-permute-start(f32[3,8,128]{2,1,0:T(8,128)S(1)} %combine.2.refs_0_), channel_id=1, source_target_pairs={{0,4},{1,5},{2,6},{3,7},{4,0},{5,1},{6,2},{7,3},{8,12},{9,13},{10,... | collective-permute-start | bytes 36872 | tf_op jit(solution)/shard_map/ppermute | solution.py:329
  84.1 2.2 %collective-permute-start.16 = (f32[3,8,128]{2,1,0:T(8,128)S(1)}, f32[3,8,128]{2,1,0:T(8,128)S(1)}, u32[]{:S(2)}, u32[]{:S(2)}) collective-permute-start(f32[3,8,128]{2,1,0:T(8,128)S(1)} %combine.2.refs_0_), channel_id=1, source_target_pairs={{0,6},{1,7},{2,4},{3,5},{4,2},{5,3},{6,0},{7,1},{8,14},{9,15},{10,... | collective-permute-start | bytes 36872 | tf_op jit(solution)/shard_map/ppermute | solution.py:329
  86.4 0.0 collective-permute-done.14.refs_1_
  86.4 1.4 %collective-permute-done.15.refs_2_ = f32[3,8,128]{2,1,0:T(8,128)S(1)} collective-permute-done((f32[3,8,128]{2,1,0:T(8,128)S(1)}, f32[3,8,128]{2,1,0:T(8,128)S(1)}, u32[]{:S(2)}, u32[]{:S(2)}) %collective-permute-start.15) | collective-permute-done | bytes 12320 | tf_op jit(solution)/shard_map/ppermute | solution.py:329
  87.8 1.8 %collective-permute-done.16.refs_3_ = f32[3,8,128]{2,1,0:T(8,128)S(1)} collective-permute-done((f32[3,8,128]{2,1,0:T(8,128)S(1)}, f32[3,8,128]{2,1,0:T(8,128)S(1)}, u32[]{:S(2)}, u32[]{:S(2)}) %collective-permute-start.16) | collective-permute-done | bytes 12320 | tf_op jit(solution)/shard_map/ppermute | solution.py:329
  89.6 0.7 combine.3
  (2 shorter events, 0.0 us)
Async XLA Ops:
  0.6 16.6 %collective-permute-start = (bf16[2,64,2304]{2,1,0:T(8,128)(2,1)}, bf16[2,64,2304]{2,1,0:T(8,128)(2,1)S(1)}, u32[]{:S(2)}, u32[]{:S(2)}) collective-permute-start(bf16[2,64,2304]{2,1,0:T(8,128)(2,1)} %down_ref.1), channel_id=1, source_target_pairs={{2,0},{4,2},{6,4},{7,6},{5,7},{3,5},{1,3},{0,1},{10,8},{12,10},{14... | collective-permute-start | bytes 1769480 | tf_op jit(solution)/shard_map/ppermute | solution.py:346
  3.6 27.8 %collective-permute-start.4 = (bf16[64,288]{1,0:T(8,128)(2,1)}, bf16[64,288]{1,0:T(8,128)(2,1)S(1)}, u32[]{:S(2)}, u32[]{:S(2)}) collective-permute-start(bf16[64,288]{1,0:T(8,128)(2,1)} %bitcast.3), channel_id=1, source_target_pairs={{0,0},{1,1},{8,2},{9,3},{16,4},{17,5},{24,6},{25,7},{2,8},{3,9},{1... | collective-permute-start | bytes 110600 | tf_op jit(solution)/shard_map/ppermute | solution.py:343
  5.1 26.4 %collective-permute-start.5 = (bf16[64,288]{1,0:T(8,128)(2,1)}, bf16[64,288]{1,0:T(8,128)(2,1)S(1)}, u32[]{:S(2)}, u32[]{:S(2)}) collective-permute-start(bf16[64,288]{1,0:T(8,128)(2,1)} %bitcast.4), channel_id=1, source_target_pairs={{1,0},{0,1},{9,2},{8,3},{17,4},{16,5},{25,6},{24,7},{3,8},{2,9},{1... | collective-permute-start | bytes 110600 | tf_op jit(solution)/shard_map/ppermute | solution.py:343
  6.6 10.6 %copy-start = (bf16[2,64,2304]{2,1,0:T(8,128)(2,1)S(1)}, bf16[2,64,2304]{2,1,0:T(8,128)(2,1)}, u32[]{:S(2)}) copy-start(bf16[2,64,2304]{2,1,0:T(8,128)(2,1)} %down_ref.1) | copy-start | bytes 1769476
  6.6 24.8 %collective-permute-start.3 = (bf16[64,1024]{1,0:T(8,128)(2,1)}, bf16[64,1024]{1,0:T(8,128)(2,1)S(1)}, u32[]{:S(2)}, u32[]{:S(2)}) collective-permute-start(bf16[64,1024]{1,0:T(8,128)(2,1)} %bitcast.2), channel_id=1, source_target_pairs={{0,0},{4,1},{9,2},{13,3},{18,4},{22,5},{27,6},{31,7},{1,8},{5,9},{... | collective-permute-start | bytes 393224 | tf_op jit(solution)/shard_map/ppermute | solution.py:336
  17.2 16.7 %collective-permute-start.2 = (bf16[2,64,2304]{2,1,0:T(8,128)(2,1)S(1)}, bf16[2,64,2304]{2,1,0:T(8,128)(2,1)S(1)}, u32[]{:S(2)}, u32[]{:S(2)}) collective-permute-start(bf16[2,64,2304]{2,1,0:T(8,128)(2,1)S(1)} %copy-done), channel_id=1, source_target_pairs={{0,2},{2,4},{4,6},{6,7},{7,5},{5,3},{3,1},{1,0},{8,10},{10,12},{12... | collective-permute-start | bytes 1769480 | tf_op jit(solution)/shard_map/ppermute | solution.py:348
  24.7 14.8 %collective-permute-start.1 = (bf16[2,64,2304]{2,1,0:T(8,128)(2,1)S(1)}, bf16[2,64,2304]{2,1,0:T(8,128)(2,1)S(1)}, u32[]{:S(2)}, u32[]{:S(2)}) collective-permute-start(bf16[2,64,2304]{2,1,0:T(8,128)(2,1)S(1)} %collective-permute-done.up_ref), channel_id=1, source_target_pairs={{2,0},{4,2},{6,4},{7,6},{5,7},{3,5},{1,3},{0,1},{10,8},{12,10},{14... | collective-permute-start | bytes 1769480 | tf_op jit(solution)/shard_map/ppermute | solution.py:349
  31.5 20.8 %copy-start.1 = (s32[2,512]{1,0:T(2,128)S(1)}, s32[2,512]{1,0:T(2,128)}, u32[]{:S(2)}) copy-start(s32[2,512]{1,0:T(2,128)} %sampled_ref.1) | copy-start | bytes 12292
  39.5 6.0 %collective-permute-start.9 = (bf16[64,1792]{1,0:T(8,128)(2,1)S(1)}, bf16[64,1792]{1,0:T(8,128)(2,1)S(1)}, u32[]{:S(2)}, u32[]{:S(2)}) collective-permute-start(bf16[64,1792]{1,0:T(8,128)(2,1)S(1)} %fusion.4.refs_0_), channel_id=1, source_target_pairs={{0,16},{8,24},{16,0},{24,8},{1,17},{9,25},{17,1},{25,9},{2,18},{10... | collective-permute-start | bytes 688136 | tf_op jit(solution)/shard_map/ppermute | solution.py:329
  39.5 14.4 %collective-permute-start.6 = (bf16[2,64,2304]{2,1,0:T(8,128)(2,1)S(1)}, bf16[2,64,2304]{2,1,0:T(8,128)(2,1)S(1)}, u32[]{:S(2)}, u32[]{:S(2)}) collective-permute-start(bf16[2,64,2304]{2,1,0:T(8,128)(2,1)S(1)} %collective-permute-done.1.up_ref), channel_id=1, source_target_pairs={{2,0},{4,2},{6,4},{7,6},{5,7},{3,5},{1,3},{0,1},{10,8},{12,10},{14... | collective-permute-start | bytes 1769480 | tf_op jit(solution)/shard_map/ppermute | solution.py:357
  39.9 15.6 %collective-permute-start.7 = (bf16[2,64,2304]{2,1,0:T(8,128)(2,1)S(1)}, bf16[2,64,2304]{2,1,0:T(8,128)(2,1)S(1)}, u32[]{:S(2)}, u32[]{:S(2)}) collective-permute-start(bf16[2,64,2304]{2,1,0:T(8,128)(2,1)S(1)} %collective-permute-done.2.down_ref), channel_id=1, source_target_pairs={{0,2},{2,4},{4,6},{6,7},{7,5},{5,3},{3,1},{1,0},{8,10},{10,12},{12... | collective-permute-start | bytes 1769480 | tf_op jit(solution)/shard_map/ppermute | solution.py:358
  41.6 10.7 %collective-permute-start.8 = (bf16[64,1792]{1,0:T(8,128)(2,1)S(1)}, bf16[64,1792]{1,0:T(8,128)(2,1)S(1)}, u32[]{:S(2)}, u32[]{:S(2)}) collective-permute-start(bf16[64,1792]{1,0:T(8,128)(2,1)S(1)} %fusion.4.refs_0_), channel_id=1, source_target_pairs={{0,8},{8,0},{16,24},{24,16},{1,9},{9,1},{17,25},{25,17},{2,10},{10... | collective-permute-start | bytes 688136 | tf_op jit(solution)/shard_map/ppermute | solution.py:329
  45.6 6.7 %collective-permute-start.10 = (bf16[64,1792]{1,0:T(8,128)(2,1)S(1)}, bf16[64,1792]{1,0:T(8,128)(2,1)S(1)}, u32[]{:S(2)}, u32[]{:S(2)}) collective-permute-start(bf16[64,1792]{1,0:T(8,128)(2,1)S(1)} %collective-permute-done.9.refs_2_), channel_id=1, source_target_pairs={{0,8},{8,0},{16,24},{24,16},{1,9},{9,1},{17,25},{25,17},{2,10},{10... | collective-permute-start | bytes 688136 | tf_op jit(solution)/shard_map/ppermute | solution.py:329
  55.5 14.1 %collective-permute-start.11 = (bf16[2,64,2304]{2,1,0:T(8,128)(2,1)S(1)}, bf16[2,64,2304]{2,1,0:T(8,128)(2,1)S(1)}, u32[]{:S(2)}, u32[]{:S(2)}) collective-permute-start(bf16[2,64,2304]{2,1,0:T(8,128)(2,1)S(1)} %collective-permute-done.6.refs_0_), channel_id=1, source_target_pairs={{2,0},{4,2},{6,4},{7,6},{5,7},{3,5},{1,3},{0,1},{10,8},{12,10},{14... | collective-permute-start | bytes 1769480 | tf_op jit(solution)/shard_map/ppermute | solution.py:378
  57.9 12.7 %collective-permute-start.12 = (bf16[2,64,2304]{2,1,0:T(8,128)(2,1)S(1)}, bf16[2,64,2304]{2,1,0:T(8,128)(2,1)S(1)}, u32[]{:S(2)}, u32[]{:S(2)}) collective-permute-start(bf16[2,64,2304]{2,1,0:T(8,128)(2,1)S(1)} %collective-permute-done.7.refs_1_), channel_id=1, source_target_pairs={{0,2},{2,4},{4,6},{6,7},{7,5},{5,3},{3,1},{1,0},{8,10},{10,12},{12... | collective-permute-start | bytes 1769480 | tf_op jit(solution)/shard_map/ppermute | solution.py:379
  78.1 3.8 %collective-permute-start.13 = (f32[3,8,128]{2,1,0:T(8,128)S(1)}, f32[3,8,128]{2,1,0:T(8,128)S(1)}, u32[]{:S(2)}, u32[]{:S(2)}) collective-permute-start(f32[3,8,128]{2,1,0:T(8,128)S(1)} %chunk.3.refs_0_), channel_id=1, source_target_pairs={{0,1},{1,0},{2,3},{3,2},{4,5},{5,4},{6,7},{7,6},{8,9},{9,8},{10,11... | collective-permute-start | bytes 36872 | tf_op jit(solution)/shard_map/ppermute | solution.py:329
  81.9 4.5 %collective-permute-start.14 = (f32[3,8,128]{2,1,0:T(8,128)S(1)}, f32[3,8,128]{2,1,0:T(8,128)S(1)}, u32[]{:S(2)}, u32[]{:S(2)}) collective-permute-start(f32[3,8,128]{2,1,0:T(8,128)S(1)} %combine.2.refs_0_), channel_id=1, source_target_pairs={{0,2},{1,3},{2,0},{3,1},{4,6},{5,7},{6,4},{7,5},{8,10},{9,11},{10,... | collective-permute-start | bytes 36872 | tf_op jit(solution)/shard_map/ppermute | solution.py:329
  83.2 4.6 %collective-permute-start.15 = (f32[3,8,128]{2,1,0:T(8,128)S(1)}, f32[3,8,128]{2,1,0:T(8,128)S(1)}, u32[]{:S(2)}, u32[]{:S(2)}) collective-permute-start(f32[3,8,128]{2,1,0:T(8,128)S(1)} %combine.2.refs_0_), channel_id=1, source_target_pairs={{0,4},{1,5},{2,6},{3,7},{4,0},{5,1},{6,2},{7,3},{8,12},{9,13},{10,... | collective-permute-start | bytes 36872 | tf_op jit(solution)/shard_map/ppermute | solution.py:329
  84.1 5.5 %collective-permute-start.16 = (f32[3,8,128]{2,1,0:T(8,128)S(1)}, f32[3,8,128]{2,1,0:T(8,128)S(1)}, u32[]{:S(2)}, u32[]{:S(2)}) collective-permute-start(f32[3,8,128]{2,1,0:T(8,128)S(1)} %combine.2.refs_0_), channel_id=1, source_target_pairs={{0,6},{1,7},{2,4},{3,5},{4,2},{5,3},{6,0},{7,1},{8,14},{9,15},{10,... | collective-permute-start | bytes 36872 | tf_op jit(solution)/shard_map/ppermute | solution.py:329

commit v12 on v11

--- a/solution.py
+++ b/solution.py
@@ -24,7 +24,7 @@
 
 
 def tile_rows(entries):
-    for rows in (512, 256, 128, 64, 32, 16):
+    for rows in (1024, 512, 256, 128, 64, 32, 16):
         if entries % (2 * rows) == 0:
             return rows
     raise ValueError(entries)
@@ -88,58 +88,50 @@
         at += block.shape[0]
 
 
-def make_load(depth, entries):
-    parts = 16 if entries % 4096 == 0 else 1
-    part = entries // parts
-
-    def kernel(head_ref, held, sems):
-        spans = [pl.ds(t * part, part) for t in range(parts)]
-        copies = [
-            pltpu.make_async_copy(head_ref.at[span, :], held.at[span, :], sems.at[t])
-            for t, span in enumerate(spans)
-        ]
-        for t, copy in enumerate(copies):
-            copy.start(priority=t % 2)
-        for copy in copies:
-            copy.wait()
-
+def make_base(r, depth, entries, load):
+    n = 4 * r
+    tile = tile_rows(entries)
+    tiles = entries // tile
+    split = 2 if tile % 32 == 0 else 1
+    part = tile // split
+
+    def kernel(up_ref, down_ref, head_ref, base_ref, rows, *refs):
+        held = head_ref
+        if load:
+            held, sems = refs
+
+        def fetch(t):
+            span = pl.ds(pl.multiple_of(t * part, part), part)
+            return pltpu.make_async_copy(head_ref.at[span, :], held.at[span, :], sems.at[t])
+
+        if load:
+            for t in range(split * tiles):
+                fetch(t).start(priority=t % 2)
+        load_rows(rows, (up_ref, down_ref))
+
+        @pl.loop(0, tiles)
+        def _(i):
+            if load:
+                for k in range(split):
+                    fetch(split * i + k).wait()
+            span = pl.ds(pl.multiple_of(i * tile, tile), tile)
+            base_ref[span, :] = jnp.dot(
+                held[span, :], rows[...], preferred_element_type=jnp.float32
+            )
+
+    out_shape = [
+        jax.ShapeDtypeStruct((entries, n), jnp.float32),
+        jax.ShapeDtypeStruct((depth, n), jnp.bfloat16),
+    ]
+    if load:
+        out_shape.append(jax.ShapeDtypeStruct((entries, depth), jnp.bfloat16))
     return pl.pallas_call(
         kernel,
-        out_shape=jax.ShapeDtypeStruct((entries, depth), jnp.bfloat16),
-        in_specs=[pl.BlockSpec(memory_space=pltpu.HBM)],
-        out_specs=WHOLE,
-        scratch_shapes=[pltpu.SemaphoreType.DMA((parts,))],
-        compiler_params=pltpu.CompilerParams(vmem_limit_bytes=32 * MIB),
-        cost_estimate=pl.CostEstimate(
-            flops=0, bytes_accessed=2 * depth * entries, transcendentals=0
-        ),
-        name="load",
-    )
-
-
-def make_base(r, depth, entries):
-    n = 4 * r
-    tile = tile_rows(entries)
-
-    def kernel(up_ref, down_ref, head_ref, base_ref, rows):
-        load_rows(rows, (up_ref, down_ref))
-
-        @pl.loop(0, entries // tile)
-        def _(i):
-            span = pl.ds(pl.multiple_of(i * tile, tile), tile)
-            base_ref[span, :] = jnp.dot(
-                head_ref[span, :], rows[...], preferred_element_type=jnp.float32
-            )
-
-    return pl.pallas_call(
-        kernel,
-        out_shape=(
-            jax.ShapeDtypeStruct((entries, n), jnp.float32),
-            jax.ShapeDtypeStruct((depth, n), jnp.bfloat16),
-        ),
-        in_specs=[WHOLE] * 3,
-        out_specs=(WHOLE,) * 2,
-        compiler_params=pltpu.CompilerParams(vmem_limit_bytes=8 * MIB),
+        out_shape=tuple(out_shape),
+        in_specs=[WHOLE, WHOLE, pl.BlockSpec(memory_space=pltpu.HBM) if load else WHOLE],
+        out_specs=(WHOLE,) * len(out_shape),
+        scratch_shapes=[pltpu.SemaphoreType.DMA((split * tiles,))] * load,
+        compiler_params=pltpu.CompilerParams(vmem_limit_bytes=(23 if load else 8) * MIB),
         cost_estimate=pl.CostEstimate(
             flops=2 * n * entries * depth,
             bytes_accessed=2 * entries * depth,
@@ -342,17 +334,18 @@
         ]
         shards.append(lax.ppermute(factor_v.T, ("group", "vocab"), moves))
 
-    head = make_load(depth, entries)(head)
     up = [hidden, lax.ppermute(hidden, "vocab", behind)]
     first, _ = lax.optimization_barrier((hidden, up[1]))
     down = [hidden, lax.ppermute(first, "vocab", ahead)]
     up.append(lax.ppermute(up[1], "vocab", behind))
-    base, base_rows = make_base(r, depth, entries)(up[1], hidden, head)
+    base, base_rows, head = make_base(r, depth, entries, True)(up[1], hidden, head)
     base, block, *shards = lax.optimization_barrier((base, block, *shards))
     held = [base, base_rows]
     gap = ((0, 0), (0, padded(v_rows) - v_rows))
     pack = jnp.concatenate([block] + [jnp.pad(x, gap) for x in shards], axis=1)
-    up[2], down[1], held[0], pack = lax.optimization_barrier((up[2], down[1], held[0], pack))
+    up[2], down[1], held[0] = lax.optimization_barrier((up[2], down[1], held[0]))
+    held += make_base(r, depth, entries, False)(up[2], down[1], head)
+    held[2], pack = lax.optimization_barrier((held[2], pack))
 
     up.append(lax.ppermute(up[2], "vocab", behind))
     down.append(lax.ppermute(down[1], "vocab", ahead))
@@ -365,7 +358,6 @@
     full_u, full_v, want = make_assemble(
         n_group, n_voc, u_rows, v_rows, rank, r, entries
     )(sampled, *[packs[k] for k in range(n_group)])
-    held += make_base(r, depth, entries)(up[2], down[1], head)
     up[3], down[2], held[2], full_u = lax.optimization_barrier((up[3], down[2], held[2], full_u))
 
     stats = []

time: 90.5 us -> 91.3 us (level)
  Pallas kernels: 39.3 us -> 35 us
  waiting for transfers between devices: 24.6 us -> 27.6 us
  local copies, waits for them, and re-layouts: 0.01 us -> 1.1 us
    ppermute x1, waiting for transfers between devices: 2.3 us -> 9.05 us  [body(): up = [hidden, lax.ppermute(hidden, 'vocab', behind)]]
    pallas_call x3 -> x2, Pallas kernels: 20 us -> 16 us  [the longest x1 10.1 us: body(): make_base(r, depth, entries, True)(up[1], hidden, head)]
    ppermute x1, waiting for transfers between devices: 5.61 us -> 2.59 us  [body(): up.append(lax.ppermute(up[1], 'vocab', behind))]
    ppermute x1, waiting for transfers between devices: 2.43 us -> 0.01 us  [body(): down = [hidden, lax.ppermute(first, 'vocab', ahead)]]
    ppermute x7, waiting for transfers between devices: 9.45 us -> 11.8 us  [trade(): return lax.ppermute(x, axis, [(i, i ^ bit) for i in range(size)])]
    ppermute x1, starting transfers between devices: 2.48 us -> 0.42 us  [body(): up.append(lax.ppermute(up[-1], 'vocab', behind))]
    ppermute x1, waiting for transfers between devices: 1.39 us -> 3.43 us  [body(): up.append(lax.ppermute(up[-1], 'vocab', behind))]
    ppermute x1, starting transfers between devices: 1.68 us -> 3.64 us  [body(): down.append(lax.ppermute(down[1], 'vocab', ahead))]
  transfers between devices with their start and end apart: 17 -> 17, of which waited for: 11 -> 10; matrix products, arithmetic and copies ran while one was open for 0% -> 0% of each run, Pallas kernels for 34% -> 29%
where the time goes in v12:
time: 91.3 us; the launch traced here: 91 us
  Pallas kernels  35 us (38%)
  waiting for transfers between devices  27.6 us (30%)
  starting transfers between devices  26.5 us (29%)
  local copies, waits for them, and re-layouts  1.1 us (1%)
    pallas_call x2, Pallas kernels, body(): out = chunk(up[hop], down[hop - 1], head, full_u, full_v, want, *extra)  17.5 us
    ppermute x7, waiting for transfers between devices, trade(): return lax.ppermute(x, axis, [(i, i ^ bit) for i in range(size)])  11.8 us
    pallas_call x1, Pallas kernels, body(): make_base(r, depth, entries, True)(up[1], hidden, head)  10.1 us
    ppermute x1, waiting for transfers between devices, body(): up = [hidden, lax.ppermute(hidden, 'vocab', behind)]  9.05 us
    ppermute x1, starting transfers between devices, body(): down = [hidden, lax.ppermute(first, 'vocab', ahead)]  6.74 us
    ppermute x7, starting transfers between devices, trade(): return lax.ppermute(x, axis, [(i, i ^ bit) for i in range(size)])  6.41 us
    pallas_call x1, Pallas kernels, body(): held += make_base(r, depth, entries, False)(up[2], down[1], head)  5.92 us
    ppermute x1, starting transfers between devices, body(): down.append(lax.ppermute(down[1], 'vocab', ahead))  3.64 us
  transfers between devices with their start and end apart: 17, of which 10 were waited for; matrix products, arithmetic and copies ran while one was open for 0% of the time, Pallas kernels for 29%

profile of v12, /device:TPU:0, one launch (start us, length us, event | category | flops | bytes accessed | tf_op | source)
XLA Modules:
  0.0 91.0 jit_solution(56925164816316)
XLA Ops:
  0.6 3.0 %collective-permute-start = (bf16[2,64,2304]{2,1,0:T(8,128)(2,1)}, bf16[2,64,2304]{2,1,0:T(8,128)(2,1)S(1)}, u32[]{:S(2)}, u32[]{:S(2)}) collective-permute-start(bf16[2,64,2304]{2,1,0:T(8,128)(2,1)} %down_ref.1), channel_id=1, source_target_pairs={{2,0},{4,2},{6,4},{7,6},{5,7},{3,5},{1,3},{0,1},{10,8},{12,10},{14... | collective-permute-start | bytes 1769480 | tf_op jit(solution)/shard_map/ppermute | solution.py:337
  3.6 1.6 %collective-permute-start.5 = (bf16[64,288]{1,0:T(8,128)(2,1)}, bf16[64,288]{1,0:T(8,128)(2,1)S(1)}, u32[]{:S(2)}, u32[]{:S(2)}) collective-permute-start(bf16[64,288]{1,0:T(8,128)(2,1)} %bitcast.3), channel_id=1, source_target_pairs={{1,0},{0,1},{9,2},{8,3},{17,4},{16,5},{25,6},{24,7},{3,8},{2,9},{1... | collective-permute-start | bytes 110600 | tf_op jit(solution)/shard_map/ppermute | solution.py:335
  5.2 1.4 %collective-permute-start.4 = (bf16[64,288]{1,0:T(8,128)(2,1)}, bf16[64,288]{1,0:T(8,128)(2,1)S(1)}, u32[]{:S(2)}, u32[]{:S(2)}) collective-permute-start(bf16[64,288]{1,0:T(8,128)(2,1)} %bitcast.4), channel_id=1, source_target_pairs={{0,0},{1,1},{8,2},{9,3},{16,4},{17,5},{24,6},{25,7},{2,8},{3,9},{1... | collective-permute-start | bytes 110600 | tf_op jit(solution)/shard_map/ppermute | solution.py:335
  6.6 1.6 %collective-permute-start.3 = (bf16[64,1024]{1,0:T(8,128)(2,1)}, bf16[64,1024]{1,0:T(8,128)(2,1)S(1)}, u32[]{:S(2)}, u32[]{:S(2)}) collective-permute-start(bf16[64,1024]{1,0:T(8,128)(2,1)} %bitcast.2), channel_id=1, source_target_pairs={{0,0},{4,1},{9,2},{13,3},{18,4},{22,5},{27,6},{31,7},{1,8},{5,9},{... | collective-permute-start | bytes 393224 | tf_op jit(solution)/shard_map/ppermute | solution.py:328
  8.2 9.1 %collective-permute-done.up_ref = bf16[2,64,2304]{2,1,0:T(8,128)(2,1)S(1)} collective-permute-done((bf16[2,64,2304]{2,1,0:T(8,128)(2,1)}, bf16[2,64,2304]{2,1,0:T(8,128)(2,1)S(1)}, u32[]{:S(2)}, u32[]{:S(2)}) %collective-permute-start) | collective-permute-done | bytes 589856 | tf_op jit(solution)/shard_map/ppermute | solution.py:337
  17.2 6.7 %collective-permute-start.2 = (bf16[2,64,2304]{2,1,0:T(8,128)(2,1)}, bf16[2,64,2304]{2,1,0:T(8,128)(2,1)S(1)}, u32[]{:S(2)}, u32[]{:S(2)}) collective-permute-start(bf16[2,64,2304]{2,1,0:T(8,128)(2,1)} %down_ref.1), channel_id=1, source_target_pairs={{0,2},{2,4},{4,6},{6,7},{7,5},{5,3},{3,1},{1,0},{8,10},{10,12},{12... | collective-permute-start | bytes 1769480 | tf_op jit(solution)/shard_map/ppermute | solution.py:339
  24.0 0.0 collective-permute-start.1
  24.0 0.0 copy-start
  24.0 1.1 %copy-done = bf16[2,64,2304]{2,1,0:T(8,128)(2,1)S(1)} copy-done((bf16[2,64,2304]{2,1,0:T(8,128)(2,1)S(1)}, bf16[2,64,2304]{2,1,0:T(8,128)(2,1)}, u32[]{:S(2)}) %copy-start) | copy-done | bytes 589848
  25.1 10.1 %base.2 = (f32[4096,256]{1,0:T(8,128)S(1)}, bf16[2304,256]{1,0:T(8,128)(2,1)S(1)}, bf16[4096,2304]{1,0:T(8,128)(2,1)S(1)}) custom-call(bf16[2,64,2304]{2,1,0:T(8,128)(2,1)S(1)} %collective-permute-done.up_ref, bf16[2,64,2304]{2,1,0:T(8,128)(2,1)S(1)} %copy-done, bf16[4096,2304]{1,0:T(8,128)(2,1)} %head_ref.1), custom_call_target="tpu_custom_call" | custom-call | flops 4831838208 | bytes 18874368 | tf_op jit(solution)/shard_map/base/pallas_call | solution.py:341
  35.2 0.0 collective-permute-done.5
  35.2 0.0 collective-permute-done.4
  35.2 0.0 collective-permute-done.3
  35.2 0.0 collective-permute-done.2.down_ref
  35.2 2.6 %collective-permute-done.1.up_ref = bf16[2,64,2304]{2,1,0:T(8,128)(2,1)S(1)} collective-permute-done((bf16[2,64,2304]{2,1,0:T(8,128)(2,1)S(1)}, bf16[2,64,2304]{2,1,0:T(8,128)(2,1)S(1)}, u32[]{:S(2)}, u32[]{:S(2)}) %collective-permute-start.1) | collective-permute-done | bytes 589856 | tf_op jit(solution)/shard_map/ppermute | solution.py:340
  37.8 0.0 collective-permute-start.6
  37.8 3.6 %collective-permute-start.7 = (bf16[2,64,2304]{2,1,0:T(8,128)(2,1)S(1)}, bf16[2,64,2304]{2,1,0:T(8,128)(2,1)S(1)}, u32[]{:S(2)}, u32[]{:S(2)}) collective-permute-start(bf16[2,64,2304]{2,1,0:T(8,128)(2,1)S(1)} %collective-permute-done.2.down_ref), channel_id=1, source_target_pairs={{0,2},{2,4},{4,6},{6,7},{7,5},{5,3},{3,1},{1,0},{8,10},{10,12},{12... | collective-permute-start | bytes 1769480 | tf_op jit(solution)/shard_map/ppermute | solution.py:351
  41.5 0.0 copy-start.1
  41.5 5.9 %base.3 = (f32[4096,256]{1,0:T(8,128)S(1)}, bf16[2304,256]{1,0:T(8,128)(2,1)S(1)}) custom-call(bf16[2,64,2304]{2,1,0:T(8,128)(2,1)S(1)} %collective-permute-done.1.up_ref, bf16[2,64,2304]{2,1,0:T(8,128)(2,1)S(1)} %collective-permute-done.2.down_ref, bf16[4096,2304]{1,0:T(8,128)(2,1)S(1)} %get-tuple-element.35.head_ref.refs_2_), custom_call_target="tpu_custom_call" | custom-call | flops 4831838208 | bytes 18874368 | tf_op jit(solution)/shard_map/base/pallas_call | solution.py:347
  47.4 0.1 collective-permute-start.9
  47.5 0.1 collective-permute-start.8
  47.5 6.1 %collective-permute-done.9.refs_2_ = bf16[64,1792]{1,0:T(8,128)(2,1)S(1)} collective-permute-done((bf16[64,1792]{1,0:T(8,128)(2,1)S(1)}, bf16[64,1792]{1,0:T(8,128)(2,1)S(1)}, u32[]{:S(2)}, u32[]{:S(2)}) %collective-permute-start.9) | collective-permute-done | bytes 229408 | tf_op jit(solution)/shard_map/ppermute | solution.py:321
  53.6 0.0 collective-permute-start.10
  53.6 0.0 collective-permute-done.8.refs_1_
  53.7 1.5 %collective-permute-done.10.refs_3_ = bf16[64,1792]{1,0:T(8,128)(2,1)S(1)} collective-permute-done((bf16[64,1792]{1,0:T(8,128)(2,1)S(1)}, bf16[64,1792]{1,0:T(8,128)(2,1)S(1)}, u32[]{:S(2)}, u32[]{:S(2)}) %collective-permute-start.10) | collective-permute-done | bytes 229408 | tf_op jit(solution)/shard_map/ppermute | solution.py:321
  55.1 0.0 copy-done.1
  55.1 0.8 assemble.1
  56.0 0.0 collective-permute-done.6.refs_0_
  56.0 0.0 collective-permute-done.7.refs_1_
  56.0 0.4 collective-permute-start.11
  56.4 1.7 %collective-permute-start.12 = (bf16[2,64,2304]{2,1,0:T(8,128)(2,1)S(1)}, bf16[2,64,2304]{2,1,0:T(8,128)(2,1)S(1)}, u32[]{:S(2)}, u32[]{:S(2)}) collective-permute-start(bf16[2,64,2304]{2,1,0:T(8,128)(2,1)S(1)} %collective-permute-done.7.refs_1_), channel_id=1, source_target_pairs={{0,2},{2,4},{4,6},{6,7},{7,5},{5,3},{3,1},{1,0},{8,10},{10,12},{12... | collective-permute-start | bytes 1769480 | tf_op jit(solution)/shard_map/ppermute | solution.py:371
  58.2 9.9 %chunk.2 = (f32[3,256]{1,0:T(4,128)S(1)}, f32[3,256]{1,0:T(4,128)S(1)}, f32[3,256]{1,0:T(4,128)S(1)}) custom-call(bf16[2,64,2304]{2,1,0:T(8,128)(2,1)S(1)} %collective-permute-done.6.refs_0_, bf16[2,64,2304]{2,1,0:T(8,128)(2,1)S(1)} %collective-permute-done.7.refs_1_, bf16[4096,2304]{1,0:T(8,128)(2,1)S(1)} %get-tuple-element.35.head_ref.refs_2_, ...), custom_call_target="tpu_custom_call" | custom-call | flops 5368709120 | bytes 19922944 | tf_op jit(solution)/shard_map/chunk/pallas_call | solution.py:367
  68.1 3.4 %collective-permute-done.11.refs_0_ = bf16[2,64,2304]{2,1,0:T(8,128)(2,1)S(1)} collective-permute-done((bf16[2,64,2304]{2,1,0:T(8,128)(2,1)S(1)}, bf16[2,64,2304]{2,1,0:T(8,128)(2,1)S(1)}, u32[]{:S(2)}, u32[]{:S(2)}) %collective-permute-start.11) | collective-permute-done | bytes 589856 | tf_op jit(solution)/shard_map/ppermute | solution.py:370
  71.5 0.7 collective-permute-done.12.refs_1_
  72.2 7.5 %chunk.3.refs_0_ = f32[3,8,128]{2,1,0:T(8,128)S(1)} custom-call(bf16[2,64,2304]{2,1,0:T(8,128)(2,1)S(1)} %collective-permute-done.11.refs_0_, bf16[2,64,2304]{2,1,0:T(8,128)(2,1)S(1)} %collective-permute-done.12.refs_1_, bf16[4096,2304]{1,0:T(8,128)(2,1)S(1)} %get-tuple-element.35.head_ref.refs_2_, bf16[4096,64]{1,0:T(8,128)(2,1)S(1)} %get-tuple-element.45.refs_3_, ...), custom_call_target="tpu_custom_call" | custom-call | flops 5368709120 | bytes 19922944 | tf_op jit(solution)/shard_map/chunk/pallas_call | solution.py:367
  79.8 1.8 %collective-permute-start.13 = (f32[3,8,128]{2,1,0:T(8,128)S(1)}, f32[3,8,128]{2,1,0:T(8,128)S(1)}, u32[]{:S(2)}, u32[]{:S(2)}) collective-permute-start(f32[3,8,128]{2,1,0:T(8,128)S(1)} %chunk.3.refs_0_), channel_id=1, source_target_pairs={{0,1},{1,0},{2,3},{3,2},{4,5},{5,4},{6,7},{7,6},{8,9},{9,8},{10,11... | collective-permute-start | bytes 36872 | tf_op jit(solution)/shard_map/ppermute | solution.py:321
  81.6 1.9 %collective-permute-done.13.refs_1_ = f32[3,8,128]{2,1,0:T(8,128)S(1)} collective-permute-done((f32[3,8,128]{2,1,0:T(8,128)S(1)}, f32[3,8,128]{2,1,0:T(8,128)S(1)}, u32[]{:S(2)}, u32[]{:S(2)}) %collective-permute-start.13) | collective-permute-done | bytes 12320 | tf_op jit(solution)/shard_map/ppermute | solution.py:321
  83.6 2.0 %collective-permute-start.16 = (f32[3,8,128]{2,1,0:T(8,128)S(1)}, f32[3,8,128]{2,1,0:T(8,128)S(1)}, u32[]{:S(2)}, u32[]{:S(2)}) collective-permute-start(f32[3,8,128]{2,1,0:T(8,128)S(1)} %combine.2.refs_0_), channel_id=1, source_target_pairs={{0,6},{1,7},{2,4},{3,5},{4,2},{5,3},{6,0},{7,1},{8,14},{9,15},{10,... | collective-permute-start | bytes 36872 | tf_op jit(solution)/shard_map/ppermute | solution.py:321
  85.6 1.0 %collective-permute-start.15 = (f32[3,8,128]{2,1,0:T(8,128)S(1)}, f32[3,8,128]{2,1,0:T(8,128)S(1)}, u32[]{:S(2)}, u32[]{:S(2)}) collective-permute-start(f32[3,8,128]{2,1,0:T(8,128)S(1)} %combine.2.refs_0_), channel_id=1, source_target_pairs={{0,4},{1,5},{2,6},{3,7},{4,0},{5,1},{6,2},{7,3},{8,12},{9,13},{10,... | collective-permute-start | bytes 36872 | tf_op jit(solution)/shard_map/ppermute | solution.py:321
  86.6 1.4 %collective-permute-start.14 = (f32[3,8,128]{2,1,0:T(8,128)S(1)}, f32[3,8,128]{2,1,0:T(8,128)S(1)}, u32[]{:S(2)}, u32[]{:S(2)}) collective-permute-start(f32[3,8,128]{2,1,0:T(8,128)S(1)} %combine.2.refs_0_), channel_id=1, source_target_pairs={{0,2},{1,3},{2,0},{3,1},{4,6},{5,7},{6,4},{7,5},{8,10},{9,11},{10,... | collective-permute-start | bytes 36872 | tf_op jit(solution)/shard_map/ppermute | solution.py:321
  88.0 1.1 %collective-permute-done.16.refs_3_ = f32[3,8,128]{2,1,0:T(8,128)S(1)} collective-permute-done((f32[3,8,128]{2,1,0:T(8,128)S(1)}, f32[3,8,128]{2,1,0:T(8,128)S(1)}, u32[]{:S(2)}, u32[]{:S(2)}) %collective-permute-start.16) | collective-permute-done | bytes 12320 | tf_op jit(solution)/shard_map/ppermute | solution.py:321
  89.1 1.0 %collective-permute-done.15.refs_2_ = f32[3,8,128]{2,1,0:T(8,128)S(1)} collective-permute-done((f32[3,8,128]{2,1,0:T(8,128)S(1)}, f32[3,8,128]{2,1,0:T(8,128)S(1)}, u32[]{:S(2)}, u32[]{:S(2)}) %collective-permute-start.15) | collective-permute-done | bytes 12320 | tf_op jit(solution)/shard_map/ppermute | solution.py:321
  90.2 0.1 collective-permute-done.14.refs_1_
  90.3 0.7 combine.3
  (2 shorter events, 0.0 us)
Async XLA Ops:
  0.6 16.6 %collective-permute-start = (bf16[2,64,2304]{2,1,0:T(8,128)(2,1)}, bf16[2,64,2304]{2,1,0:T(8,128)(2,1)S(1)}, u32[]{:S(2)}, u32[]{:S(2)}) collective-permute-start(bf16[2,64,2304]{2,1,0:T(8,128)(2,1)} %down_ref.1), channel_id=1, source_target_pairs={{2,0},{4,2},{6,4},{7,6},{5,7},{3,5},{1,3},{0,1},{10,8},{12,10},{14... | collective-permute-start | bytes 1769480 | tf_op jit(solution)/shard_map/ppermute | solution.py:337
  3.6 31.5 %collective-permute-start.5 = (bf16[64,288]{1,0:T(8,128)(2,1)}, bf16[64,288]{1,0:T(8,128)(2,1)S(1)}, u32[]{:S(2)}, u32[]{:S(2)}) collective-permute-start(bf16[64,288]{1,0:T(8,128)(2,1)} %bitcast.3), channel_id=1, source_target_pairs={{1,0},{0,1},{9,2},{8,3},{17,4},{16,5},{25,6},{24,7},{3,8},{2,9},{1... | collective-permute-start | bytes 110600 | tf_op jit(solution)/shard_map/ppermute | solution.py:335
  5.2 30.0 %collective-permute-start.4 = (bf16[64,288]{1,0:T(8,128)(2,1)}, bf16[64,288]{1,0:T(8,128)(2,1)S(1)}, u32[]{:S(2)}, u32[]{:S(2)}) collective-permute-start(bf16[64,288]{1,0:T(8,128)(2,1)} %bitcast.4), channel_id=1, source_target_pairs={{0,0},{1,1},{8,2},{9,3},{16,4},{17,5},{24,6},{25,7},{2,8},{3,9},{1... | collective-permute-start | bytes 110600 | tf_op jit(solution)/shard_map/ppermute | solution.py:335
  6.6 28.5 %collective-permute-start.3 = (bf16[64,1024]{1,0:T(8,128)(2,1)}, bf16[64,1024]{1,0:T(8,128)(2,1)S(1)}, u32[]{:S(2)}, u32[]{:S(2)}) collective-permute-start(bf16[64,1024]{1,0:T(8,128)(2,1)} %bitcast.2), channel_id=1, source_target_pairs={{0,0},{4,1},{9,2},{13,3},{18,4},{22,5},{27,6},{31,7},{1,8},{5,9},{... | collective-permute-start | bytes 393224 | tf_op jit(solution)/shard_map/ppermute | solution.py:328
  17.2 18.0 %collective-permute-start.2 = (bf16[2,64,2304]{2,1,0:T(8,128)(2,1)}, bf16[2,64,2304]{2,1,0:T(8,128)(2,1)S(1)}, u32[]{:S(2)}, u32[]{:S(2)}) collective-permute-start(bf16[2,64,2304]{2,1,0:T(8,128)(2,1)} %down_ref.1), channel_id=1, source_target_pairs={{0,2},{2,4},{4,6},{6,7},{7,5},{5,3},{3,1},{1,0},{8,10},{10,12},{12... | collective-permute-start | bytes 1769480 | tf_op jit(solution)/shard_map/ppermute | solution.py:339
  24.0 13.8 %collective-permute-start.1 = (bf16[2,64,2304]{2,1,0:T(8,128)(2,1)S(1)}, bf16[2,64,2304]{2,1,0:T(8,128)(2,1)S(1)}, u32[]{:S(2)}, u32[]{:S(2)}) collective-permute-start(bf16[2,64,2304]{2,1,0:T(8,128)(2,1)S(1)} %collective-permute-done.up_ref), channel_id=1, source_target_pairs={{2,0},{4,2},{6,4},{7,6},{5,7},{3,5},{1,3},{0,1},{10,8},{12,10},{14... | collective-permute-start | bytes 1769480 | tf_op jit(solution)/shard_map/ppermute | solution.py:340
  24.0 1.1 %copy-start = (bf16[2,64,2304]{2,1,0:T(8,128)(2,1)S(1)}, bf16[2,64,2304]{2,1,0:T(8,128)(2,1)}, u32[]{:S(2)}) copy-start(bf16[2,64,2304]{2,1,0:T(8,128)(2,1)} %down_ref.1) | copy-start | bytes 1769476
  37.8 18.2 %collective-permute-start.6 = (bf16[2,64,2304]{2,1,0:T(8,128)(2,1)S(1)}, bf16[2,64,2304]{2,1,0:T(8,128)(2,1)S(1)}, u32[]{:S(2)}, u32[]{:S(2)}) collective-permute-start(bf16[2,64,2304]{2,1,0:T(8,128)(2,1)S(1)} %collective-permute-done.1.up_ref), channel_id=1, source_target_pairs={{2,0},{4,2},{6,4},{7,6},{5,7},{3,5},{1,3},{0,1},{10,8},{12,10},{14... | collective-permute-start | bytes 1769480 | tf_op jit(solution)/shard_map/ppermute | solution.py:350
  37.8 18.2 %collective-permute-start.7 = (bf16[2,64,2304]{2,1,0:T(8,128)(2,1)S(1)}, bf16[2,64,2304]{2,1,0:T(8,128)(2,1)S(1)}, u32[]{:S(2)}, u32[]{:S(2)}) collective-permute-start(bf16[2,64,2304]{2,1,0:T(8,128)(2,1)S(1)} %collective-permute-done.2.down_ref), channel_id=1, source_target_pairs={{0,2},{2,4},{4,6},{6,7},{7,5},{5,3},{3,1},{1,0},{8,10},{10,12},{12... | collective-permute-start | bytes 1769480 | tf_op jit(solution)/shard_map/ppermute | solution.py:351
  41.5 13.7 %copy-start.1 = (s32[2,512]{1,0:T(2,128)S(1)}, s32[2,512]{1,0:T(2,128)}, u32[]{:S(2)}) copy-start(s32[2,512]{1,0:T(2,128)} %sampled_ref.1) | copy-start | bytes 12292
  47.4 6.3 %collective-permute-start.9 = (bf16[64,1792]{1,0:T(8,128)(2,1)S(1)}, bf16[64,1792]{1,0:T(8,128)(2,1)S(1)}, u32[]{:S(2)}, u32[]{:S(2)}) collective-permute-start(bf16[64,1792]{1,0:T(8,128)(2,1)S(1)} %fusion.4.refs_0_), channel_id=1, source_target_pairs={{0,16},{8,24},{16,0},{24,8},{1,17},{9,25},{17,1},{25,9},{2,18},{10... | collective-permute-start | bytes 688136 | tf_op jit(solution)/shard_map/ppermute | solution.py:321
  47.5 6.2 %collective-permute-start.8 = (bf16[64,1792]{1,0:T(8,128)(2,1)S(1)}, bf16[64,1792]{1,0:T(8,128)(2,1)S(1)}, u32[]{:S(2)}, u32[]{:S(2)}) collective-permute-start(bf16[64,1792]{1,0:T(8,128)(2,1)S(1)} %fusion.4.refs_0_), channel_id=1, source_target_pairs={{0,8},{8,0},{16,24},{24,16},{1,9},{9,1},{17,25},{25,17},{2,10},{10... | collective-permute-start | bytes 688136 | tf_op jit(solution)/shard_map/ppermute | solution.py:321
  53.6 1.5 %collective-permute-start.10 = (bf16[64,1792]{1,0:T(8,128)(2,1)S(1)}, bf16[64,1792]{1,0:T(8,128)(2,1)S(1)}, u32[]{:S(2)}, u32[]{:S(2)}) collective-permute-start(bf16[64,1792]{1,0:T(8,128)(2,1)S(1)} %collective-permute-done.9.refs_2_), channel_id=1, source_target_pairs={{0,8},{8,0},{16,24},{24,16},{1,9},{9,1},{17,25},{25,17},{2,10},{10... | collective-permute-start | bytes 688136 | tf_op jit(solution)/shard_map/ppermute | solution.py:321
  56.0 15.5 %collective-permute-start.11 = (bf16[2,64,2304]{2,1,0:T(8,128)(2,1)S(1)}, bf16[2,64,2304]{2,1,0:T(8,128)(2,1)S(1)}, u32[]{:S(2)}, u32[]{:S(2)}) collective-permute-start(bf16[2,64,2304]{2,1,0:T(8,128)(2,1)S(1)} %collective-permute-done.6.refs_0_), channel_id=1, source_target_pairs={{2,0},{4,2},{6,4},{7,6},{5,7},{3,5},{1,3},{0,1},{10,8},{12,10},{14... | collective-permute-start | bytes 1769480 | tf_op jit(solution)/shard_map/ppermute | solution.py:370
  56.4 15.8 %collective-permute-start.12 = (bf16[2,64,2304]{2,1,0:T(8,128)(2,1)S(1)}, bf16[2,64,2304]{2,1,0:T(8,128)(2,1)S(1)}, u32[]{:S(2)}, u32[]{:S(2)}) collective-permute-start(bf16[2,64,2304]{2,1,0:T(8,128)(2,1)S(1)} %collective-permute-done.7.refs_1_), channel_id=1, source_target_pairs={{0,2},{2,4},{4,6},{6,7},{7,5},{5,3},{3,1},{1,0},{8,10},{10,12},{12... | collective-permute-start | bytes 1769480 | tf_op jit(solution)/shard_map/ppermute | solution.py:371
  79.8 3.8 %collective-permute-start.13 = (f32[3,8,128]{2,1,0:T(8,128)S(1)}, f32[3,8,128]{2,1,0:T(8,128)S(1)}, u32[]{:S(2)}, u32[]{:S(2)}) collective-permute-start(f32[3,8,128]{2,1,0:T(8,128)S(1)} %chunk.3.refs_0_), channel_id=1, source_target_pairs={{0,1},{1,0},{2,3},{3,2},{4,5},{5,4},{6,7},{7,6},{8,9},{9,8},{10,11... | collective-permute-start | bytes 36872 | tf_op jit(solution)/shard_map/ppermute | solution.py:321
  83.6 5.6 %collective-permute-start.16 = (f32[3,8,128]{2,1,0:T(8,128)S(1)}, f32[3,8,128]{2,1,0:T(8,128)S(1)}, u32[]{:S(2)}, u32[]{:S(2)}) collective-permute-start(f32[3,8,128]{2,1,0:T(8,128)S(1)} %combine.2.refs_0_), channel_id=1, source_target_pairs={{0,6},{1,7},{2,4},{3,5},{4,2},{5,3},{6,0},{7,1},{8,14},{9,15},{10,... | collective-permute-start | bytes 36872 | tf_op jit(solution)/shard_map/ppermute | solution.py:321
  85.6 4.6 %collective-permute-start.15 = (f32[3,8,128]{2,1,0:T(8,128)S(1)}, f32[3,8,128]{2,1,0:T(8,128)S(1)}, u32[]{:S(2)}, u32[]{:S(2)}) collective-permute-start(f32[3,8,128]{2,1,0:T(8,128)S(1)} %combine.2.refs_0_), channel_id=1, source_target_pairs={{0,4},{1,5},{2,6},{3,7},{4,0},{5,1},{6,2},{7,3},{8,12},{9,13},{10,... | collective-permute-start | bytes 36872 | tf_op jit(solution)/shard_map/ppermute | solution.py:321
  86.6 3.7 %collective-permute-start.14 = (f32[3,8,128]{2,1,0:T(8,128)S(1)}, f32[3,8,128]{2,1,0:T(8,128)S(1)}, u32[]{:S(2)}, u32[]{:S(2)}) collective-permute-start(f32[3,8,128]{2,1,0:T(8,128)S(1)} %combine.2.refs_0_), channel_id=1, source_target_pairs={{0,2},{1,3},{2,0},{3,1},{4,6},{5,7},{6,4},{7,5},{8,10},{9,11},{10,... | collective-permute-start | bytes 36872 | tf_op jit(solution)/shard_map/ppermute | solution.py:321

commit v13 on v12

--- a/solution.py
+++ b/solution.py
@@ -12,6 +12,10 @@
 
 def ring_order(n):
     return [2 * i for i in range(n // 2)] + [2 * i + 1 for i in reversed(range(n // 2))]
+
+
+def plane_of(member, n_group):
+    return member // 2 + member % 2 * (n_group // 2)
 
 
 def ring_position(device, n):
@@ -45,11 +49,12 @@
         voc = lax.axis_index("vocab")
         for k in range(n_group):
             member = group ^ k
+            plane = lax.div(member, 2) + lax.rem(member, 2) * (n_group // 2)
             block = member ^ lax.rem(voc // per, n_group)
             start = pl.multiple_of(block * u_rows, u_rows)
             u_out[pl.ds(start, u_rows), :] = packs[k][:, :u_rows].T
             for t in range(per):
-                shard = member * per + (lax.rem(voc, per) ^ t)
+                shard = plane * per + (lax.rem(voc, per) ^ t)
                 at = u_rows + t * wide
                 rows = packs[k][:, at : at + wide].astype(jnp.float32).T
                 v_wide[pl.ds(pl.multiple_of(shard * v_rows, 8), v_rows), :] = rows[:v_rows]
@@ -143,7 +148,7 @@
 
 def make_chunk(hop, r, depth, entries, rank, n_voc):
     tile = tile_rows(entries)
-    tiles = entries // tile
+    sizes = [tile] * (entries // tile - 1) + [tile // 2] * 2
     n = 4 * r
     carry, last = 2 * (hop == 3), hop == n_voc // 2
     earlier = hop - 1 if last else 0
@@ -174,7 +179,6 @@
         load_rows(rows, piece)
         project(rows, proj)
         clear(*state)
-        odd[...] = jnp.full(odd.shape, -1e30, jnp.float32)
         want = wanted(hop)
         base_wants = []
         for k in range(carry):
@@ -182,42 +186,42 @@
             clear(*base_scratch[k][1:])
             base_wants.append(wanted(k + 1))
 
-        def multiply(t, into):
-            span = pl.ds(pl.multiple_of(t * tile, tile), tile)
-            into[...] = jnp.dot(
+        def multiply(start, size, into):
+            span = slice(start, start + size)
+            into[:size, :] = jnp.dot(
                 head_ref[span, :], rows[...], preferred_element_type=jnp.float32
             ) + jnp.dot(u_ref[span, :], proj[...], preferred_element_type=jnp.float32)
 
         def reduce(x, want, top, total, pick):
-            entry = lax.broadcasted_iota(jnp.int32, (tile, n), 0)
+            size = x.shape[0]
+            entry = lax.broadcasted_iota(jnp.int32, (size, n), 0)
             hit = jnp.where(entry == want, x, 0.0)
-            x3 = x.reshape(tile // 8, 8, n)
+            x3 = x.reshape(size // 8, 8, n)
             new = jnp.maximum(top[...], jnp.max(x3, axis=0))
             total[...] = total[...] * jnp.exp(top[...] - new) + jnp.sum(
                 jnp.exp(x3 - new[None]), axis=0
             )
-            pick[...] = pick[...] + jnp.sum(hit.reshape(tile // 8, 8, n), axis=0)
+            pick[...] = pick[...] + jnp.sum(hit.reshape(size // 8, 8, n), axis=0)
             top[...] = new
 
-        def finish_bases(t):
-            span = pl.ds(pl.multiple_of(t * tile, tile), tile)
+        def finish_bases(start, size):
+            span = slice(start, start + size)
             for k in range(carry):
                 base_proj, *base_state = base_scratch[k]
                 x = bases[2 * k][span, :] + jnp.dot(
                     u_ref[span, :], base_proj[...], preferred_element_type=jnp.float32
                 )
-                reduce(x, base_wants[k] - t * tile, *base_state)
-
-        @pl.loop(0, tiles // 2)
-        def _(i):
-            multiply(2 * i, even)
-            reduce(odd[...], want - jnp.where(i == 0, 1 << 29, (2 * i - 1) * tile), *state)
-            finish_bases(2 * i)
-            multiply(2 * i + 1, odd)
-            reduce(even[...], want - 2 * i * tile, *state)
-            finish_bases(2 * i + 1)
-
-        reduce(odd[...], want - (entries - tile), *state)
+                reduce(x, base_wants[k] - start, *base_state)
+
+        start = 0
+        for i, size in enumerate(sizes):
+            multiply(start, size, (even, odd)[i % 2])
+            if i:
+                ahead = sizes[i - 1]
+                reduce((even, odd)[(i - 1) % 2][:ahead, :], want - (start - ahead), *state)
+            finish_bases(start, size)
+            start += size
+        reduce((even, odd)[(len(sizes) - 1) % 2][:size, :], want - (start - size), *state)
 
         def results(top, total, pick):
             best = jnp.max(top[...], axis=0, keepdims=True)
@@ -329,10 +333,10 @@
     shards = []
     for t in range(per):
         moves = [
-            ((v // per) % n_group * n_voc + g * per + (v % per ^ t), g * n_voc + v)
+            ((v // per) % n_group * n_voc + plane_of(g, n_group) * per + (v % per ^ t), g * n_voc + v)
             for g, v in everyone
         ]
-        shards.append(lax.ppermute(factor_v.T, ("group", "vocab"), moves))
+        shards.append(lax.ppermute(factor_v.T.reshape(16, -1), ("group", "vocab"), moves))
 
     up = [hidden, lax.ppermute(hidden, "vocab", behind)]
     first, _ = lax.optimization_barrier((hidden, up[1]))
@@ -342,8 +346,9 @@
     base, block, *shards = lax.optimization_barrier((base, block, *shards))
     held = [base, base_rows]
     gap = ((0, 0), (0, padded(v_rows) - v_rows))
-    pack = jnp.concatenate([block] + [jnp.pad(x, gap) for x in shards], axis=1)
-    up[2], down[1], held[0] = lax.optimization_barrier((up[2], down[1], held[0]))
+    pack = jnp.concatenate([block] + [jnp.pad(x.reshape(rank, -1), gap) for x in shards], axis=1)
+    up[2], held[0] = lax.optimization_barrier((up[2], held[0]))
+    down[1], held[0] = lax.optimization_barrier((down[1], held[0]))
     held += make_base(r, depth, entries, False)(up[2], down[1], head)
     held[2], pack = lax.optimization_barrier((held[2], pack))
 
@@ -358,7 +363,8 @@
     full_u, full_v, want = make_assemble(
         n_group, n_voc, u_rows, v_rows, rank, r, entries
     )(sampled, *[packs[k] for k in range(n_group)])
-    up[3], down[2], held[2], full_u = lax.optimization_barrier((up[3], down[2], held[2], full_u))
+    up[3], held[2], full_u = lax.optimization_barrier((up[3], held[2], full_u))
+    down[2], full_u = lax.optimization_barrier((down[2], full_u))
 
     stats = []
     for hop in range(3, half + 1):
@@ -369,7 +375,8 @@
         if hop < half:
             up.append(lax.ppermute(up[-1], "vocab", behind))
             down.append(lax.ppermute(down[-1], "vocab", ahead))
-            up[-1], down[-1], stats[-1] = lax.optimization_barrier((up[-1], down[-1], stats[-1]))
+            up[-1], stats[-1] = lax.optimization_barrier((up[-1], stats[-1]))
+            down[-1], stats[-1] = lax.optimization_barrier((down[-1], stats[-1]))
     part = stats[-1]
     low = 1
     while low < n_voc:

time: 91.3 us -> 102 us (1.12)
  local copies, waits for them, and re-layouts: 1.1 us -> 19.3 us
  waiting for transfers between devices: 27.6 us -> 22.5 us
  starting transfers between devices: 26.5 us -> 24.8 us
    unnamed x4 -> x14, local copies, waits for them, and re-layouts: 1.1 us -> 18.1 us
    ppermute x1, waiting for transfers between devices: 2.59 us -> 0.01 us  [body(): up.append(lax.ppermute(up[1], 'vocab', behind))]
    ppermute x1, waiting for transfers between devices: 3.43 us -> 1.36 us  [body(): up.append(lax.ppermute(up[-1], 'vocab', behind))]
    ppermute x1, starting transfers between devices: 3.64 us -> 2.05 us  [body(): down.append(lax.ppermute(down[1], 'vocab', ahead))]
    ppermute x1, starting transfers between devices: 0.42 us -> 1.69 us  [body(): up.append(lax.ppermute(up[-1], 'vocab', behind))]
    reshape x0 -> x3, local copies, waits for them, and re-layouts: none -> 1.16 us  [the longest x1 0.91 us: body(): factor_v.T.reshape(16, -1)]
    ppermute x1, starting transfers between devices: 1.73 us -> 0.61 us  [body(): down.append(lax.ppermute(down[-1], 'vocab', ahead))]
  transfers between devices with their start and end apart: 17 -> 17, of which waited for: 10 -> 9; matrix products, arithmetic and copies ran while one was open for 0% -> 1% of each run, Pallas kernels for 29% -> 26%
where the time goes in v13:
time: 102 us; the launch traced here: 101 us
  Pallas kernels  34.1 us (33%)
  starting transfers between devices  24.8 us (24%)
  waiting for transfers between devices  22.5 us (22%)
  local copies, waits for them, and re-layouts  19.3 us (19%)
    unnamed x14, local copies, waits for them, and re-layouts  18.1 us
    pallas_call x2, Pallas kernels, body(): out = chunk(up[hop], down[hop - 1], head, full_u, full_v, want, *extra)  16.6 us
    ppermute x7, waiting for transfers between devices, trade(): return lax.ppermute(x, axis, [(i, i ^ bit) for i in range(size)])  10.8 us
    pallas_call x1, Pallas kernels, body(): make_base(r, depth, entries, True)(up[1], hidden, head)  10.1 us
    ppermute x1, waiting for transfers between devices, body(): up = [hidden, lax.ppermute(hidden, 'vocab', behind)]  8.85 us
    ppermute x7, starting transfers between devices, trade(): return lax.ppermute(x, axis, [(i, i ^ bit) for i in range(size)])  7.4 us
    ppermute x1, starting transfers between devices, body(): down = [hidden, lax.ppermute(first, 'vocab', ahead)]  6.21 us
    pallas_call x1, Pallas kernels, body(): held += make_base(r, depth, entries, False)(up[2], down[1], head)  5.9 us
  transfers between devices with their start and end apart: 17, of which 9 were waited for; matrix products, arithmetic and copies ran while one was open for 1% of the time, Pallas kernels for 26%

profile of v13, /device:TPU:0, one launch (start us, length us, event | category | flops | bytes accessed | tf_op | source)
XLA Modules:
  0.0 101.4 jit_solution(18062392273003688527)
XLA Ops:
  0.6 3.0 %collective-permute-start = (bf16[2,64,2304]{2,1,0:T(8,128)(2,1)}, bf16[2,64,2304]{2,1,0:T(8,128)(2,1)S(1)}, u32[]{:S(2)}, u32[]{:S(2)}) collective-permute-start(bf16[2,64,2304]{2,1,0:T(8,128)(2,1)} %down_ref.1), channel_id=1, source_target_pairs={{2,0},{4,2},{6,4},{7,6},{5,7},{3,5},{1,3},{0,1},{10,8},{12,10},{14... | collective-permute-start | bytes 1769480 | tf_op jit(solution)/shard_map/ppermute | solution.py:341
  3.6 0.9 reshape.14
  4.5 1.6 %collective-permute-start.4 = (bf16[16,1152]{1,0:T(8,128)(2,1)S(1)}, bf16[16,1152]{1,0:T(8,128)(2,1)S(1)}, u32[]{:S(2)}, u32[]{:S(2)}) collective-permute-start(bf16[16,1152]{1,0:T(8,128)(2,1)S(1)} %reshape.14), channel_id=1, source_target_pairs={{1,0},{0,1},{9,2},{8,3},{17,4},{16,5},{25,6},{24,7},{5,8},{4,9},{1... | collective-permute-start | bytes 110600 | tf_op jit(solution)/shard_map/ppermute | solution.py:339
  6.2 0.7 collective-permute-start.3
  6.8 1.6 %collective-permute-start.2 = (bf16[64,1024]{1,0:T(8,128)(2,1)}, bf16[64,1024]{1,0:T(8,128)(2,1)S(1)}, u32[]{:S(2)}, u32[]{:S(2)}) collective-permute-start(bf16[64,1024]{1,0:T(8,128)(2,1)} %bitcast.3), channel_id=1, source_target_pairs={{0,0},{4,1},{9,2},{13,3},{18,4},{22,5},{27,6},{31,7},{1,8},{5,9},{... | collective-permute-start | bytes 393224 | tf_op jit(solution)/shard_map/ppermute | solution.py:332
  8.4 8.9 %collective-permute-done.up_ref = bf16[2,64,2304]{2,1,0:T(8,128)(2,1)S(1)} collective-permute-done((bf16[2,64,2304]{2,1,0:T(8,128)(2,1)}, bf16[2,64,2304]{2,1,0:T(8,128)(2,1)S(1)}, u32[]{:S(2)}, u32[]{:S(2)}) %collective-permute-start) | collective-permute-done | bytes 589856 | tf_op jit(solution)/shard_map/ppermute | solution.py:341
  17.2 6.2 %collective-permute-start.6 = (bf16[2,64,2304]{2,1,0:T(8,128)(2,1)}, bf16[2,64,2304]{2,1,0:T(8,128)(2,1)S(1)}, u32[]{:S(2)}, u32[]{:S(2)}) collective-permute-start(bf16[2,64,2304]{2,1,0:T(8,128)(2,1)} %down_ref.1), channel_id=1, source_target_pairs={{0,2},{2,4},{4,6},{6,7},{7,5},{5,3},{3,1},{1,0},{8,10},{10,12},{12... | collective-permute-start | bytes 1769480 | tf_op jit(solution)/shard_map/ppermute | solution.py:343
  23.5 0.0 collective-permute-start.1
  23.5 1.1 %copy-done.5 = bf16[2,64,2304]{2,1,0:T(8,128)(2,1)S(1)} copy-done((bf16[2,64,2304]{2,1,0:T(8,128)(2,1)S(1)}, bf16[2,64,2304]{2,1,0:T(8,128)(2,1)}, u32[]{:S(2)}) %copy-start.5) | copy-done | bytes 589848
  24.6 10.1 %base.2 = (f32[4096,256]{1,0:T(8,128)S(1)}, bf16[2304,256]{1,0:T(8,128)(2,1)S(1)}, bf16[4096,2304]{1,0:T(8,128)(2,1)S(1)}) custom-call(bf16[2,64,2304]{2,1,0:T(8,128)(2,1)S(1)} %collective-permute-done.up_ref, bf16[2,64,2304]{2,1,0:T(8,128)(2,1)S(1)} %copy-done.5, bf16[4096,2304]{1,0:T(8,128)(2,1)} %head_ref.1), custom_call_target="tpu_custom_call" | custom-call | flops 4831838208 | bytes 18874368 | tf_op jit(solution)/shard_map/base/pallas_call | solution.py:345
  34.6 6.4 %copy-done = bf16[4096,2304]{1,0:T(8,128)(2,1)} copy-done((bf16[4096,2304]{1,0:T(8,128)(2,1)}, bf16[4096,2304]{1,0:T(8,128)(2,1)S(1)}, u32[]{:S(2)}) %copy-start) | copy-done | bytes 18874392
  41.1 2.0 %copy-done.3 = f32[4096,256]{1,0:T(8,128)} copy-done((f32[4096,256]{1,0:T(8,128)}, f32[4096,256]{1,0:T(8,128)S(1)}, u32[]{:S(2)}) %copy-start.3) | copy-done | bytes 4194328
  43.1 0.0 collective-permute-done.4
  43.1 0.0 collective-permute-done.3
  43.1 0.0 collective-permute-done.2
  43.1 0.1 reshape.15
  43.2 0.1 reshape.16
  43.4 0.0 collective-permute-done.1.up_ref
  43.4 0.0 collective-permute-done.6.down_ref
  43.4 2.0 %collective-permute-start.11 = (bf16[2,64,2304]{2,1,0:T(8,128)(2,1)S(1)}, bf16[2,64,2304]{2,1,0:T(8,128)(2,1)S(1)}, u32[]{:S(2)}, u32[]{:S(2)}) collective-permute-start(bf16[2,64,2304]{2,1,0:T(8,128)(2,1)S(1)} %collective-permute-done.6.down_ref), channel_id=1, source_target_pairs={{0,2},{2,4},{4,6},{6,7},{7,5},{5,3},{3,1},{1,0},{8,10},{10,12},{12... | collective-permute-start | bytes 1769480 | tf_op jit(solution)/shard_map/ppermute | solution.py:356
  45.5 0.0 collective-permute-start.5
  45.5 6.4 %copy-done.1 = bf16[4096,2304]{1,0:T(8,128)(2,1)S(1)} copy-done((bf16[4096,2304]{1,0:T(8,128)(2,1)S(1)}, bf16[4096,2304]{1,0:T(8,128)(2,1)}, u32[]{:S(2)}) %copy-start.1) | copy-done | bytes 18874392
  51.9 5.9 %base.3 = (f32[4096,256]{1,0:T(8,128)S(1)}, bf16[2304,256]{1,0:T(8,128)(2,1)S(1)}) custom-call(bf16[2,64,2304]{2,1,0:T(8,128)(2,1)S(1)} %collective-permute-done.1.up_ref, bf16[2,64,2304]{2,1,0:T(8,128)(2,1)S(1)} %collective-permute-done.6.down_ref, bf16[4096,2304]{1,0:T(8,128)(2,1)S(1)} %copy-done.1), custom_call_target="tpu_custom_call" | custom-call | flops 4831838208 | bytes 18874368 | tf_op jit(solution)/shard_map/base/pallas_call | solution.py:352
  57.8 0.9 collective-permute-start.8
  58.7 0.0 collective-permute-start.7
  58.7 5.2 %collective-permute-done.8.refs_2_ = bf16[64,1792]{1,0:T(8,128)(2,1)S(1)} collective-permute-done((bf16[64,1792]{1,0:T(8,128)(2,1)S(1)}, bf16[64,1792]{1,0:T(8,128)(2,1)S(1)}, u32[]{:S(2)}, u32[]{:S(2)}) %collective-permute-start.8) | collective-permute-done | bytes 229408 | tf_op jit(solution)/shard_map/ppermute | solution.py:325
  63.9 0.0 collective-permute-start.9
  63.9 0.0 collective-permute-done.7.refs_1_
  63.9 1.5 %collective-permute-done.9.refs_3_ = bf16[64,1792]{1,0:T(8,128)(2,1)S(1)} collective-permute-done((bf16[64,1792]{1,0:T(8,128)(2,1)S(1)}, bf16[64,1792]{1,0:T(8,128)(2,1)S(1)}, u32[]{:S(2)}, u32[]{:S(2)}) %collective-permute-start.9) | collective-permute-done | bytes 229408 | tf_op jit(solution)/shard_map/ppermute | solution.py:325
  65.3 0.8 assemble.1
  66.2 0.0 collective-permute-done.5.refs_0_
  66.2 1.7 %collective-permute-start.10 = (bf16[2,64,2304]{2,1,0:T(8,128)(2,1)S(1)}, bf16[2,64,2304]{2,1,0:T(8,128)(2,1)S(1)}, u32[]{:S(2)}, u32[]{:S(2)}) collective-permute-start(bf16[2,64,2304]{2,1,0:T(8,128)(2,1)S(1)} %collective-permute-done.5.refs_0_), channel_id=1, source_target_pairs={{2,0},{4,2},{6,4},{7,6},{5,7},{3,5},{1,3},{0,1},{10,8},{12,10},{14... | collective-permute-start | bytes 1769480 | tf_op jit(solution)/shard_map/ppermute | solution.py:376
  67.9 0.0 collective-permute-done.11.refs_1_
  67.9 0.6 collective-permute-start.12
  68.5 2.2 %copy-done.4 = f32[4096,256]{1,0:T(8,128)S(1)} copy-done((f32[4096,256]{1,0:T(8,128)S(1)}, f32[4096,256]{1,0:T(8,128)}, u32[]{:S(2)}) %copy-start.4) | copy-done | bytes 4194328
  70.7 9.8 %chunk.2 = (f32[3,256]{1,0:T(4,128)S(1)}, f32[3,256]{1,0:T(4,128)S(1)}, f32[3,256]{1,0:T(4,128)S(1)}) custom-call(bf16[2,64,2304]{2,1,0:T(8,128)(2,1)S(1)} %collective-permute-done.5.refs_0_, bf16[2,64,2304]{2,1,0:T(8,128)(2,1)S(1)} %collective-permute-done.11.refs_1_, bf16[4096,2304]{1,0:T(8,128)(2,1)S(1)} %copy-done.2, ...), custom_call_target="tpu_custom_call" | custom-call | flops 5368709120 | bytes 19922944 | tf_op jit(solution)/shard_map/chunk/pallas_call | solution.py:373
  80.5 1.4 %collective-permute-done.10.refs_0_ = bf16[2,64,2304]{2,1,0:T(8,128)(2,1)S(1)} collective-permute-done((bf16[2,64,2304]{2,1,0:T(8,128)(2,1)S(1)}, bf16[2,64,2304]{2,1,0:T(8,128)(2,1)S(1)}, u32[]{:S(2)}, u32[]{:S(2)}) %collective-permute-start.10) | collective-permute-done | bytes 589856 | tf_op jit(solution)/shard_map/ppermute | solution.py:376
  81.9 1.4 %collective-permute-done.12.refs_1_ = bf16[2,64,2304]{2,1,0:T(8,128)(2,1)S(1)} collective-permute-done((bf16[2,64,2304]{2,1,0:T(8,128)(2,1)S(1)}, bf16[2,64,2304]{2,1,0:T(8,128)(2,1)S(1)}, u32[]{:S(2)}, u32[]{:S(2)}) %collective-permute-start.12) | collective-permute-done | bytes 589856 | tf_op jit(solution)/shard_map/ppermute | solution.py:377
  83.3 6.7 %chunk.3.refs_0_ = f32[3,8,128]{2,1,0:T(8,128)S(1)} custom-call(bf16[2,64,2304]{2,1,0:T(8,128)(2,1)S(1)} %collective-permute-done.10.refs_0_, bf16[2,64,2304]{2,1,0:T(8,128)(2,1)S(1)} %collective-permute-done.12.refs_1_, bf16[4096,2304]{1,0:T(8,128)(2,1)S(1)} %copy-done.2, bf16[4096,64]{1,0:T(8,128)(2,1)S(1)} %get-tuple-element.50.refs_3_, ...), custom_call_target="tpu_custom_call" | custom-call | flops 5368709120 | bytes 19922944 | tf_op jit(solution)/shard_map/chunk/pallas_call | solution.py:373
  90.0 2.0 %collective-permute-start.13 = (f32[3,8,128]{2,1,0:T(8,128)S(1)}, f32[3,8,128]{2,1,0:T(8,128)S(1)}, u32[]{:S(2)}, u32[]{:S(2)}) collective-permute-start(f32[3,8,128]{2,1,0:T(8,128)S(1)} %chunk.3.refs_0_), channel_id=1, source_target_pairs={{0,1},{1,0},{2,3},{3,2},{4,5},{5,4},{6,7},{7,6},{8,9},{9,8},{10,11... | collective-permute-start | bytes 36872 | tf_op jit(solution)/shard_map/ppermute | solution.py:325
  92.0 1.7 %collective-permute-done.13.refs_1_ = f32[3,8,128]{2,1,0:T(8,128)S(1)} collective-permute-done((f32[3,8,128]{2,1,0:T(8,128)S(1)}, f32[3,8,128]{2,1,0:T(8,128)S(1)}, u32[]{:S(2)}, u32[]{:S(2)}) %collective-permute-start.13) | collective-permute-done | bytes 12320 | tf_op jit(solution)/shard_map/ppermute | solution.py:325
  93.8 1.4 %collective-permute-start.16 = (f32[3,8,128]{2,1,0:T(8,128)S(1)}, f32[3,8,128]{2,1,0:T(8,128)S(1)}, u32[]{:S(2)}, u32[]{:S(2)}) collective-permute-start(f32[3,8,128]{2,1,0:T(8,128)S(1)} %combine.2.refs_0_), channel_id=1, source_target_pairs={{0,6},{1,7},{2,4},{3,5},{4,2},{5,3},{6,0},{7,1},{8,14},{9,15},{10,... | collective-permute-start | bytes 36872 | tf_op jit(solution)/shard_map/ppermute | solution.py:325
  95.2 1.8 %collective-permute-start.15 = (f32[3,8,128]{2,1,0:T(8,128)S(1)}, f32[3,8,128]{2,1,0:T(8,128)S(1)}, u32[]{:S(2)}, u32[]{:S(2)}) collective-permute-start(f32[3,8,128]{2,1,0:T(8,128)S(1)} %combine.2.refs_0_), channel_id=1, source_target_pairs={{0,4},{1,5},{2,6},{3,7},{4,0},{5,1},{6,2},{7,3},{8,12},{9,13},{10,... | collective-permute-start | bytes 36872 | tf_op jit(solution)/shard_map/ppermute | solution.py:325
  97.0 1.2 %collective-permute-start.14 = (f32[3,8,128]{2,1,0:T(8,128)S(1)}, f32[3,8,128]{2,1,0:T(8,128)S(1)}, u32[]{:S(2)}, u32[]{:S(2)}) collective-permute-start(f32[3,8,128]{2,1,0:T(8,128)S(1)} %combine.2.refs_0_), channel_id=1, source_target_pairs={{0,2},{1,3},{2,0},{3,1},{4,6},{5,7},{6,4},{7,5},{8,10},{9,11},{10,... | collective-permute-start | bytes 36872 | tf_op jit(solution)/shard_map/ppermute | solution.py:325
  98.2 1.1 %collective-permute-done.16.refs_3_ = f32[3,8,128]{2,1,0:T(8,128)S(1)} collective-permute-done((f32[3,8,128]{2,1,0:T(8,128)S(1)}, f32[3,8,128]{2,1,0:T(8,128)S(1)}, u32[]{:S(2)}, u32[]{:S(2)}) %collective-permute-start.16) | collective-permute-done | bytes 12320 | tf_op jit(solution)/shard_map/ppermute | solution.py:325
  99.3 0.4 collective-permute-done.15.refs_2_
  99.8 0.9 collective-permute-done.14.refs_1_
  100.7 0.7 combine.3
  (11 shorter events, 0.1 us)
Async XLA Ops:
  0.6 16.6 %collective-permute-start = (bf16[2,64,2304]{2,1,0:T(8,128)(2,1)}, bf16[2,64,2304]{2,1,0:T(8,128)(2,1)S(1)}, u32[]{:S(2)}, u32[]{:S(2)}) collective-permute-start(bf16[2,64,2304]{2,1,0:T(8,128)(2,1)} %down_ref.1), channel_id=1, source_target_pairs={{2,0},{4,2},{6,4},{7,6},{5,7},{3,5},{1,3},{0,1},{10,8},{12,10},{14... | collective-permute-start | bytes 1769480 | tf_op jit(solution)/shard_map/ppermute | solution.py:341
  4.5 38.6 %collective-permute-start.4 = (bf16[16,1152]{1,0:T(8,128)(2,1)S(1)}, bf16[16,1152]{1,0:T(8,128)(2,1)S(1)}, u32[]{:S(2)}, u32[]{:S(2)}) collective-permute-start(bf16[16,1152]{1,0:T(8,128)(2,1)S(1)} %reshape.14), channel_id=1, source_target_pairs={{1,0},{0,1},{9,2},{8,3},{17,4},{16,5},{25,6},{24,7},{5,8},{4,9},{1... | collective-permute-start | bytes 110600 | tf_op jit(solution)/shard_map/ppermute | solution.py:339
  6.2 36.9 %collective-permute-start.3 = (bf16[16,1152]{1,0:T(8,128)(2,1)S(1)}, bf16[16,1152]{1,0:T(8,128)(2,1)S(1)}, u32[]{:S(2)}, u32[]{:S(2)}) collective-permute-start(bf16[16,1152]{1,0:T(8,128)(2,1)S(1)} %reshape.14), channel_id=1, source_target_pairs={{0,0},{1,1},{8,2},{9,3},{16,4},{17,5},{24,6},{25,7},{4,8},{5,9},{1... | collective-permute-start | bytes 110600 | tf_op jit(solution)/shard_map/ppermute | solution.py:339
  6.8 36.3 %collective-permute-start.2 = (bf16[64,1024]{1,0:T(8,128)(2,1)}, bf16[64,1024]{1,0:T(8,128)(2,1)S(1)}, u32[]{:S(2)}, u32[]{:S(2)}) collective-permute-start(bf16[64,1024]{1,0:T(8,128)(2,1)} %bitcast.3), channel_id=1, source_target_pairs={{0,0},{4,1},{9,2},{13,3},{18,4},{22,5},{27,6},{31,7},{1,8},{5,9},{... | collective-permute-start | bytes 393224 | tf_op jit(solution)/shard_map/ppermute | solution.py:332
  17.2 26.2 %collective-permute-start.6 = (bf16[2,64,2304]{2,1,0:T(8,128)(2,1)}, bf16[2,64,2304]{2,1,0:T(8,128)(2,1)S(1)}, u32[]{:S(2)}, u32[]{:S(2)}) collective-permute-start(bf16[2,64,2304]{2,1,0:T(8,128)(2,1)} %down_ref.1), channel_id=1, source_target_pairs={{0,2},{2,4},{4,6},{6,7},{7,5},{5,3},{3,1},{1,0},{8,10},{10,12},{12... | collective-permute-start | bytes 1769480 | tf_op jit(solution)/shard_map/ppermute | solution.py:343
  23.5 19.9 %collective-permute-start.1 = (bf16[2,64,2304]{2,1,0:T(8,128)(2,1)S(1)}, bf16[2,64,2304]{2,1,0:T(8,128)(2,1)S(1)}, u32[]{:S(2)}, u32[]{:S(2)}) collective-permute-start(bf16[2,64,2304]{2,1,0:T(8,128)(2,1)S(1)} %collective-permute-done.up_ref), channel_id=1, source_target_pairs={{2,0},{4,2},{6,4},{7,6},{5,7},{3,5},{1,3},{0,1},{10,8},{12,10},{14... | collective-permute-start | bytes 1769480 | tf_op jit(solution)/shard_map/ppermute | solution.py:344
  23.5 1.1 %copy-start.5 = (bf16[2,64,2304]{2,1,0:T(8,128)(2,1)S(1)}, bf16[2,64,2304]{2,1,0:T(8,128)(2,1)}, u32[]{:S(2)}) copy-start(bf16[2,64,2304]{2,1,0:T(8,128)(2,1)} %down_ref.1) | copy-start | bytes 1769476
  34.6 6.4 %copy-start = (bf16[4096,2304]{1,0:T(8,128)(2,1)}, bf16[4096,2304]{1,0:T(8,128)(2,1)S(1)}, u32[]{:S(2)}) copy-start(bf16[4096,2304]{1,0:T(8,128)(2,1)S(1)} %get-tuple-element.39.head_ref.refs_2_) | copy-start | bytes 56623108
  41.1 2.0 %copy-start.3 = (f32[4096,256]{1,0:T(8,128)}, f32[4096,256]{1,0:T(8,128)S(1)}, u32[]{:S(2)}) copy-start(f32[4096,256]{1,0:T(8,128)S(1)} %get-tuple-element.53.refs_6_) | copy-start | bytes 12582916
  43.4 24.5 %collective-permute-start.11 = (bf16[2,64,2304]{2,1,0:T(8,128)(2,1)S(1)}, bf16[2,64,2304]{2,1,0:T(8,128)(2,1)S(1)}, u32[]{:S(2)}, u32[]{:S(2)}) collective-permute-start(bf16[2,64,2304]{2,1,0:T(8,128)(2,1)S(1)} %collective-permute-done.6.down_ref), channel_id=1, source_target_pairs={{0,2},{2,4},{4,6},{6,7},{7,5},{5,3},{3,1},{1,0},{8,10},{10,12},{12... | collective-permute-start | bytes 1769480 | tf_op jit(solution)/shard_map/ppermute | solution.py:356
  45.5 20.7 %collective-permute-start.5 = (bf16[2,64,2304]{2,1,0:T(8,128)(2,1)S(1)}, bf16[2,64,2304]{2,1,0:T(8,128)(2,1)S(1)}, u32[]{:S(2)}, u32[]{:S(2)}) collective-permute-start(bf16[2,64,2304]{2,1,0:T(8,128)(2,1)S(1)} %collective-permute-done.1.up_ref), channel_id=1, source_target_pairs={{2,0},{4,2},{6,4},{7,6},{5,7},{3,5},{1,3},{0,1},{10,8},{12,10},{14... | collective-permute-start | bytes 1769480 | tf_op jit(solution)/shard_map/ppermute | solution.py:355
  45.5 6.4 %copy-start.1 = (bf16[4096,2304]{1,0:T(8,128)(2,1)S(1)}, bf16[4096,2304]{1,0:T(8,128)(2,1)}, u32[]{:S(2)}) copy-start(bf16[4096,2304]{1,0:T(8,128)(2,1)} %copy-done) | copy-start | bytes 56623108
  51.9 13.5 %copy-start.6 = (s32[2,512]{1,0:T(2,128)S(1)}, s32[2,512]{1,0:T(2,128)}, u32[]{:S(2)}) copy-start(s32[2,512]{1,0:T(2,128)} %sampled_ref.1) | copy-start | bytes 12292
  51.9 16.7 %copy-start.2 = (bf16[4096,2304]{1,0:T(8,128)(2,1)S(1)}, bf16[4096,2304]{1,0:T(8,128)(2,1)}, u32[]{:S(2)}) copy-start(bf16[4096,2304]{1,0:T(8,128)(2,1)} %copy-done) | copy-start | bytes 56623108
  57.8 6.1 %collective-permute-start.8 = (bf16[64,1792]{1,0:T(8,128)(2,1)S(1)}, bf16[64,1792]{1,0:T(8,128)(2,1)S(1)}, u32[]{:S(2)}, u32[]{:S(2)}) collective-permute-start(bf16[64,1792]{1,0:T(8,128)(2,1)S(1)} %fusion.4.refs_0_), channel_id=1, source_target_pairs={{0,16},{8,24},{16,0},{24,8},{1,17},{9,25},{17,1},{25,9},{2,18},{10... | collective-permute-start | bytes 688136 | tf_op jit(solution)/shard_map/ppermute | solution.py:325
  58.7 5.2 %collective-permute-start.7 = (bf16[64,1792]{1,0:T(8,128)(2,1)S(1)}, bf16[64,1792]{1,0:T(8,128)(2,1)S(1)}, u32[]{:S(2)}, u32[]{:S(2)}) collective-permute-start(bf16[64,1792]{1,0:T(8,128)(2,1)S(1)} %fusion.4.refs_0_), channel_id=1, source_target_pairs={{0,8},{8,0},{16,24},{24,16},{1,9},{9,1},{17,25},{25,17},{2,10},{10... | collective-permute-start | bytes 688136 | tf_op jit(solution)/shard_map/ppermute | solution.py:325
  63.9 1.5 %collective-permute-start.9 = (bf16[64,1792]{1,0:T(8,128)(2,1)S(1)}, bf16[64,1792]{1,0:T(8,128)(2,1)S(1)}, u32[]{:S(2)}, u32[]{:S(2)}) collective-permute-start(bf16[64,1792]{1,0:T(8,128)(2,1)S(1)} %collective-permute-done.8.refs_2_), channel_id=1, source_target_pairs={{0,8},{8,0},{16,24},{24,16},{1,9},{9,1},{17,25},{25,17},{2,10},{10... | collective-permute-start | bytes 688136 | tf_op jit(solution)/shard_map/ppermute | solution.py:325
  66.2 15.7 %collective-permute-start.10 = (bf16[2,64,2304]{2,1,0:T(8,128)(2,1)S(1)}, bf16[2,64,2304]{2,1,0:T(8,128)(2,1)S(1)}, u32[]{:S(2)}, u32[]{:S(2)}) collective-permute-start(bf16[2,64,2304]{2,1,0:T(8,128)(2,1)S(1)} %collective-permute-done.5.refs_0_), channel_id=1, source_target_pairs={{2,0},{4,2},{6,4},{7,6},{5,7},{3,5},{1,3},{0,1},{10,8},{12,10},{14... | collective-permute-start | bytes 1769480 | tf_op jit(solution)/shard_map/ppermute | solution.py:376
  67.9 15.4 %collective-permute-start.12 = (bf16[2,64,2304]{2,1,0:T(8,128)(2,1)S(1)}, bf16[2,64,2304]{2,1,0:T(8,128)(2,1)S(1)}, u32[]{:S(2)}, u32[]{:S(2)}) collective-permute-start(bf16[2,64,2304]{2,1,0:T(8,128)(2,1)S(1)} %collective-permute-done.11.refs_1_), channel_id=1, source_target_pairs={{0,2},{2,4},{4,6},{6,7},{7,5},{5,3},{3,1},{1,0},{8,10},{10,12},{12... | collective-permute-start | bytes 1769480 | tf_op jit(solution)/shard_map/ppermute | solution.py:377
  68.5 2.2 %copy-start.4 = (f32[4096,256]{1,0:T(8,128)S(1)}, f32[4096,256]{1,0:T(8,128)}, u32[]{:S(2)}) copy-start(f32[4096,256]{1,0:T(8,128)} %copy-done.3) | copy-start | bytes 12582916
  90.0 3.8 %collective-permute-start.13 = (f32[3,8,128]{2,1,0:T(8,128)S(1)}, f32[3,8,128]{2,1,0:T(8,128)S(1)}, u32[]{:S(2)}, u32[]{:S(2)}) collective-permute-start(f32[3,8,128]{2,1,0:T(8,128)S(1)} %chunk.3.refs_0_), channel_id=1, source_target_pairs={{0,1},{1,0},{2,3},{3,2},{4,5},{5,4},{6,7},{7,6},{8,9},{9,8},{10,11... | collective-permute-start | bytes 36872 | tf_op jit(solution)/shard_map/ppermute | solution.py:325
  93.8 5.6 %collective-permute-start.16 = (f32[3,8,128]{2,1,0:T(8,128)S(1)}, f32[3,8,128]{2,1,0:T(8,128)S(1)}, u32[]{:S(2)}, u32[]{:S(2)}) collective-permute-start(f32[3,8,128]{2,1,0:T(8,128)S(1)} %combine.2.refs_0_), channel_id=1, source_target_pairs={{0,6},{1,7},{2,4},{3,5},{4,2},{5,3},{6,0},{7,1},{8,14},{9,15},{10,... | collective-permute-start | bytes 36872 | tf_op jit(solution)/shard_map/ppermute | solution.py:325
  95.2 4.6 %collective-permute-start.15 = (f32[3,8,128]{2,1,0:T(8,128)S(1)}, f32[3,8,128]{2,1,0:T(8,128)S(1)}, u32[]{:S(2)}, u32[]{:S(2)}) collective-permute-start(f32[3,8,128]{2,1,0:T(8,128)S(1)} %combine.2.refs_0_), channel_id=1, source_target_pairs={{0,4},{1,5},{2,6},{3,7},{4,0},{5,1},{6,2},{7,3},{8,12},{9,13},{10,... | collective-permute-start | bytes 36872 | tf_op jit(solution)/shard_map/ppermute | solution.py:325
  97.0 3.7 %collective-permute-start.14 = (f32[3,8,128]{2,1,0:T(8,128)S(1)}, f32[3,8,128]{2,1,0:T(8,128)S(1)}, u32[]{:S(2)}, u32[]{:S(2)}) collective-permute-start(f32[3,8,128]{2,1,0:T(8,128)S(1)} %combine.2.refs_0_), channel_id=1, source_target_pairs={{0,2},{1,3},{2,0},{3,1},{4,6},{5,7},{6,4},{7,5},{8,10},{9,11},{10,... | collective-permute-start | bytes 36872 | tf_op jit(solution)/shard_map/ppermute | solution.py:325

commit v14 on v13

--- a/solution.py
+++ b/solution.py
@@ -14,7 +14,7 @@
     return [2 * i for i in range(n // 2)] + [2 * i + 1 for i in reversed(range(n // 2))]
 
 
-def plane_of(member, n_group):
+def swapped(member, n_group):
     return member // 2 + member % 2 * (n_group // 2)
 
 
@@ -49,8 +49,8 @@
         voc = lax.axis_index("vocab")
         for k in range(n_group):
             member = group ^ k
-            plane = lax.div(member, 2) + lax.rem(member, 2) * (n_group // 2)
-            block = member ^ lax.rem(voc // per, n_group)
+            plane = member ^ swapped(voc // per, n_group)
+            block = swapped(member, n_group)
             start = pl.multiple_of(block * u_rows, u_rows)
             u_out[pl.ds(start, u_rows), :] = packs[k][:, :u_rows].T
             for t in range(per):
@@ -327,28 +327,28 @@
     u_rows, v_rows = factor_u.shape[0], factor_v.shape[0]
     everyone = [(g, v) for g in range(n_group) for v in range(n_voc)]
     moves = [
-        (v * n_group + (g ^ (v // per) % n_group), g * n_voc + v) for g, v in everyone
+        (v * n_group + swapped(g, n_group), g * n_voc + v) for g, v in everyone
     ]
     block = lax.ppermute(factor_u.T, ("group", "vocab"), moves)
     shards = []
     for t in range(per):
-        moves = [
-            ((v // per) % n_group * n_voc + plane_of(g, n_group) * per + (v % per ^ t), g * n_voc + v)
-            for g, v in everyone
-        ]
-        shards.append(lax.ppermute(factor_v.T.reshape(16, -1), ("group", "vocab"), moves))
+        moves = []
+        for g, v in everyone:
+            z = v // per
+            plane = g ^ swapped(z, n_group)
+            moves.append((z * n_voc + plane * per + (v % per ^ t), g * n_voc + v))
+        shards.append(lax.ppermute(factor_v.T, ("group", "vocab"), moves))
 
     up = [hidden, lax.ppermute(hidden, "vocab", behind)]
-    first, _ = lax.optimization_barrier((hidden, up[1]))
-    down = [hidden, lax.ppermute(first, "vocab", ahead)]
+    down = [hidden, lax.ppermute(hidden, "vocab", ahead)]
     up.append(lax.ppermute(up[1], "vocab", behind))
     base, base_rows, head = make_base(r, depth, entries, True)(up[1], hidden, head)
     base, block, *shards = lax.optimization_barrier((base, block, *shards))
     held = [base, base_rows]
     gap = ((0, 0), (0, padded(v_rows) - v_rows))
-    pack = jnp.concatenate([block] + [jnp.pad(x.reshape(rank, -1), gap) for x in shards], axis=1)
+    pack = jnp.concatenate([block] + [jnp.pad(x, gap) for x in shards], axis=1)
+    down[1], held[0] = lax.optimization_barrier((down[1], held[0]))
     up[2], held[0] = lax.optimization_barrier((up[2], held[0]))
-    down[1], held[0] = lax.optimization_barrier((down[1], held[0]))
     held += make_base(r, depth, entries, False)(up[2], down[1], head)
     held[2], pack = lax.optimization_barrier((held[2], pack))
 
@@ -363,8 +363,8 @@
     full_u, full_v, want = make_assemble(
         n_group, n_voc, u_rows, v_rows, rank, r, entries
     )(sampled, *[packs[k] for k in range(n_group)])
+    down[2], full_u = lax.optimization_barrier((down[2], full_u))
     up[3], held[2], full_u = lax.optimization_barrier((up[3], held[2], full_u))
-    down[2], full_u = lax.optimization_barrier((down[2], full_u))
 
     stats = []
     for hop in range(3, half + 1):
@@ -375,8 +375,8 @@
         if hop < half:
             up.append(lax.ppermute(up[-1], "vocab", behind))
             down.append(lax.ppermute(down[-1], "vocab", ahead))
+            down[-1], stats[-1] = lax.optimization_barrier((down[-1], stats[-1]))
             up[-1], stats[-1] = lax.optimization_barrier((up[-1], stats[-1]))
-            down[-1], stats[-1] = lax.optimization_barrier((down[-1], stats[-1]))
     part = stats[-1]
     low = 1
     while low < n_voc:

time: 102 us -> 89.9 us (0.88)
  local copies, waits for them, and re-layouts: 19.3 us -> 1.07 us
  waiting for transfers between devices: 22.5 us -> 27.2 us
  starting transfers between devices: 24.8 us -> 26.4 us
    unnamed x14 -> x4, local copies, waits for them, and re-layouts: 18.1 us -> 1.07 us
    ppermute x3, starting transfers between devices: 8.49 us -> 3.47 us  [the longest x2 3.32 us: body(): shards.append(lax.ppermute(factor_v.T, ('group', 'vocab'), moves))]
    ppermute x1, starting transfers between devices: 0.61 us -> 4.7 us  [body(): down.append(lax.ppermute(down[-1], 'vocab', ahead))]
    ppermute x1, starting transfers between devices: 2.05 us -> 4.61 us  [body(): down.append(lax.ppermute(down[1], 'vocab', ahead))]
    ppermute x1, starting transfers between devices: 0.01 us -> 2.18 us  [body(): up.append(lax.ppermute(up[1], 'vocab', behind))]
    ppermute x1, waiting for transfers between devices: 1.39 us -> 3.5 us  [body(): down.append(lax.ppermute(down[-1], 'vocab', ahead))]
    ppermute x1, waiting for transfers between devices: 0.01 us -> 2.02 us  [body(): up.append(lax.ppermute(up[1], 'vocab', behind))]
    ppermute x1, starting transfers between devices: 1.69 us -> 0.34 us  [body(): up.append(lax.ppermute(up[-1], 'vocab', behind))]
  transfers between devices with their start and end apart: 17 -> 17, of which waited for: 9 -> 10; matrix products, arithmetic and copies ran while one was open for 1% -> 0% of each run, Pallas kernels for 26% -> 30%
where the time goes in v14:
time: 89.9 us; the launch traced here: 89.6 us
  Pallas kernels  34.2 us (38%)
  waiting for transfers between devices  27.2 us (30%)
  starting transfers between devices  26.4 us (29%)
  local copies, waits for them, and re-layouts  1.07 us (1%)
    pallas_call x2, Pallas kernels, body(): out = chunk(up[hop], down[hop - 1], head, full_u, full_v, want, *extra)  16.6 us
    ppermute x7, waiting for transfers between devices, trade(): return lax.ppermute(x, axis, [(i, i ^ bit) for i in range(size)])  11.7 us
    pallas_call x1, Pallas kernels, body(): make_base(r, depth, entries, True)(up[1], hidden, head)  10.1 us
    ppermute x1, waiting for transfers between devices, body(): up = [hidden, lax.ppermute(hidden, 'vocab', behind)]  8.6 us
    ppermute x7, starting transfers between devices, trade(): return lax.ppermute(x, axis, [(i, i ^ bit) for i in range(size)])  6.59 us
    pallas_call x1, Pallas kernels, body(): held += make_base(r, depth, entries, False)(up[2], down[1], head)  5.92 us
    ppermute x1, starting transfers between devices, body(): down.append(lax.ppermute(down[-1], 'vocab', ahead))  4.7 us
    ppermute x1, starting transfers between devices, body(): down.append(lax.ppermute(down[1], 'vocab', ahead))  4.61 us
  transfers between devices with their start and end apart: 17, of which 10 were waited for; matrix products, arithmetic and copies ran while one was open for 0% of the time, Pallas kernels for 30%

profile of v14, /device:TPU:0, one launch (start us, length us, event | category | flops | bytes accessed | tf_op | source)
XLA Modules:
  0.0 89.6 jit_solution(16065023430645733045)
XLA Ops:
  0.6 3.0 %collective-permute-start = (bf16[2,64,2304]{2,1,0:T(8,128)(2,1)}, bf16[2,64,2304]{2,1,0:T(8,128)(2,1)S(1)}, u32[]{:S(2)}, u32[]{:S(2)}) collective-permute-start(bf16[2,64,2304]{2,1,0:T(8,128)(2,1)} %down_ref.1), channel_id=1, source_target_pairs={{2,0},{4,2},{6,4},{7,6},{5,7},{3,5},{1,3},{0,1},{10,8},{12,10},{14... | collective-permute-start | bytes 1769480 | tf_op jit(solution)/shard_map/ppermute | solution.py:342
  3.6 0.2 collective-permute-start.2
  3.8 1.9 %collective-permute-start.5 = (bf16[64,288]{1,0:T(8,128)(2,1)}, bf16[64,288]{1,0:T(8,128)(2,1)S(1)}, u32[]{:S(2)}, u32[]{:S(2)}) collective-permute-start(bf16[64,288]{1,0:T(8,128)(2,1)} %bitcast.3), channel_id=1, source_target_pairs={{1,0},{0,1},{13,2},{12,3},{19,4},{18,5},{31,6},{30,7},{3,8},{2,9},... | collective-permute-start | bytes 110600 | tf_op jit(solution)/shard_map/ppermute | solution.py:340
  5.6 1.4 %collective-permute-start.4 = (bf16[64,288]{1,0:T(8,128)(2,1)}, bf16[64,288]{1,0:T(8,128)(2,1)S(1)}, u32[]{:S(2)}, u32[]{:S(2)}) collective-permute-start(bf16[64,288]{1,0:T(8,128)(2,1)} %bitcast.4), channel_id=1, source_target_pairs={{0,0},{1,1},{12,2},{13,3},{18,4},{19,5},{30,6},{31,7},{2,8},{3,9},... | collective-permute-start | bytes 110600 | tf_op jit(solution)/shard_map/ppermute | solution.py:340
  7.1 1.6 %collective-permute-start.3 = (bf16[64,1024]{1,0:T(8,128)(2,1)}, bf16[64,1024]{1,0:T(8,128)(2,1)S(1)}, u32[]{:S(2)}, u32[]{:S(2)}) collective-permute-start(bf16[64,1024]{1,0:T(8,128)(2,1)} %bitcast.2), channel_id=1, source_target_pairs={{0,0},{4,1},{8,2},{12,3},{16,4},{20,5},{24,6},{28,7},{2,8},{6,9},{... | collective-permute-start | bytes 393224 | tf_op jit(solution)/shard_map/ppermute | solution.py:332
  8.6 8.6 %collective-permute-done.up_ref = bf16[2,64,2304]{2,1,0:T(8,128)(2,1)S(1)} collective-permute-done((bf16[2,64,2304]{2,1,0:T(8,128)(2,1)}, bf16[2,64,2304]{2,1,0:T(8,128)(2,1)S(1)}, u32[]{:S(2)}, u32[]{:S(2)}) %collective-permute-start) | collective-permute-done | bytes 589856 | tf_op jit(solution)/shard_map/ppermute | solution.py:342
  17.2 2.2 %collective-permute-start.1 = (bf16[2,64,2304]{2,1,0:T(8,128)(2,1)S(1)}, bf16[2,64,2304]{2,1,0:T(8,128)(2,1)S(1)}, u32[]{:S(2)}, u32[]{:S(2)}) collective-permute-start(bf16[2,64,2304]{2,1,0:T(8,128)(2,1)S(1)} %collective-permute-done.up_ref), channel_id=1, source_target_pairs={{2,0},{4,2},{6,4},{7,6},{5,7},{3,5},{1,3},{0,1},{10,8},{12,10},{14... | collective-permute-start | bytes 1769480 | tf_op jit(solution)/shard_map/ppermute | solution.py:344
  19.4 0.0 copy-start
  19.4 1.1 %copy-done = bf16[2,64,2304]{2,1,0:T(8,128)(2,1)S(1)} copy-done((bf16[2,64,2304]{2,1,0:T(8,128)(2,1)S(1)}, bf16[2,64,2304]{2,1,0:T(8,128)(2,1)}, u32[]{:S(2)}) %copy-start) | copy-done | bytes 589848
  20.5 10.1 %base.2 = (f32[4096,256]{1,0:T(8,128)S(1)}, bf16[2304,256]{1,0:T(8,128)(2,1)S(1)}, bf16[4096,2304]{1,0:T(8,128)(2,1)S(1)}) custom-call(bf16[2,64,2304]{2,1,0:T(8,128)(2,1)S(1)} %collective-permute-done.up_ref, bf16[2,64,2304]{2,1,0:T(8,128)(2,1)S(1)} %copy-done, bf16[4096,2304]{1,0:T(8,128)(2,1)} %head_ref.1), custom_call_target="tpu_custom_call" | custom-call | flops 4831838208 | bytes 18874368 | tf_op jit(solution)/shard_map/base/pallas_call | solution.py:345
  30.6 0.0 collective-permute-done.5
  30.6 0.0 collective-permute-done.4
  30.6 0.0 collective-permute-done.3
  30.6 0.0 collective-permute-done.2.down_ref
  30.6 4.6 %collective-permute-start.7 = (bf16[2,64,2304]{2,1,0:T(8,128)(2,1)S(1)}, bf16[2,64,2304]{2,1,0:T(8,128)(2,1)S(1)}, u32[]{:S(2)}, u32[]{:S(2)}) collective-permute-start(bf16[2,64,2304]{2,1,0:T(8,128)(2,1)S(1)} %collective-permute-done.2.down_ref), channel_id=1, source_target_pairs={{0,2},{2,4},{4,6},{6,7},{7,5},{5,3},{3,1},{1,0},{8,10},{10,12},{12... | collective-permute-start | bytes 1769480 | tf_op jit(solution)/shard_map/ppermute | solution.py:356
  35.2 2.0 %collective-permute-done.1.up_ref = bf16[2,64,2304]{2,1,0:T(8,128)(2,1)S(1)} collective-permute-done((bf16[2,64,2304]{2,1,0:T(8,128)(2,1)S(1)}, bf16[2,64,2304]{2,1,0:T(8,128)(2,1)S(1)}, u32[]{:S(2)}, u32[]{:S(2)}) %collective-permute-start.1) | collective-permute-done | bytes 589856 | tf_op jit(solution)/shard_map/ppermute | solution.py:344
  37.3 0.0 collective-permute-start.6
  37.3 0.0 copy-start.1
  37.3 5.9 %base.3 = (f32[4096,256]{1,0:T(8,128)S(1)}, bf16[2304,256]{1,0:T(8,128)(2,1)S(1)}) custom-call(bf16[2,64,2304]{2,1,0:T(8,128)(2,1)S(1)} %collective-permute-done.1.up_ref, bf16[2,64,2304]{2,1,0:T(8,128)(2,1)S(1)} %collective-permute-done.2.down_ref, bf16[4096,2304]{1,0:T(8,128)(2,1)S(1)} %get-tuple-element.37.head_ref.refs_2_), custom_call_target="tpu_custom_call" | custom-call | flops 4831838208 | bytes 18874368 | tf_op jit(solution)/shard_map/base/pallas_call | solution.py:352
  43.2 1.0 %collective-permute-start.9 = (bf16[64,1792]{1,0:T(8,128)(2,1)S(1)}, bf16[64,1792]{1,0:T(8,128)(2,1)S(1)}, u32[]{:S(2)}, u32[]{:S(2)}) collective-permute-start(bf16[64,1792]{1,0:T(8,128)(2,1)S(1)} %fusion.4.refs_0_), channel_id=1, source_target_pairs={{0,16},{8,24},{16,0},{24,8},{1,17},{9,25},{17,1},{25,9},{2,18},{10... | collective-permute-start | bytes 688136 | tf_op jit(solution)/shard_map/ppermute | solution.py:325
  44.2 0.0 collective-permute-start.8
  44.2 5.1 %collective-permute-done.9.refs_2_ = bf16[64,1792]{1,0:T(8,128)(2,1)S(1)} collective-permute-done((bf16[64,1792]{1,0:T(8,128)(2,1)S(1)}, bf16[64,1792]{1,0:T(8,128)(2,1)S(1)}, u32[]{:S(2)}, u32[]{:S(2)}) %collective-permute-start.9) | collective-permute-done | bytes 229408 | tf_op jit(solution)/shard_map/ppermute | solution.py:325
  49.3 0.0 collective-permute-start.10
  49.3 0.0 collective-permute-done.8.refs_1_
  49.3 1.5 %collective-permute-done.10.refs_3_ = bf16[64,1792]{1,0:T(8,128)(2,1)S(1)} collective-permute-done((bf16[64,1792]{1,0:T(8,128)(2,1)S(1)}, bf16[64,1792]{1,0:T(8,128)(2,1)S(1)}, u32[]{:S(2)}, u32[]{:S(2)}) %collective-permute-start.10) | collective-permute-done | bytes 229408 | tf_op jit(solution)/shard_map/ppermute | solution.py:325
  50.8 0.0 copy-done.1
  50.8 0.8 assemble.1
  51.6 0.0 collective-permute-done.7.refs_1_
  51.6 4.7 %collective-permute-start.12 = (bf16[2,64,2304]{2,1,0:T(8,128)(2,1)S(1)}, bf16[2,64,2304]{2,1,0:T(8,128)(2,1)S(1)}, u32[]{:S(2)}, u32[]{:S(2)}) collective-permute-start(bf16[2,64,2304]{2,1,0:T(8,128)(2,1)S(1)} %collective-permute-done.7.refs_1_), channel_id=1, source_target_pairs={{0,2},{2,4},{4,6},{6,7},{7,5},{5,3},{3,1},{1,0},{8,10},{10,12},{12... | collective-permute-start | bytes 1769480 | tf_op jit(solution)/shard_map/ppermute | solution.py:377
  56.3 0.0 collective-permute-done.6.refs_0_
  56.3 0.3 collective-permute-start.11
  56.7 9.9 %chunk.2 = (f32[3,256]{1,0:T(4,128)S(1)}, f32[3,256]{1,0:T(4,128)S(1)}, f32[3,256]{1,0:T(4,128)S(1)}) custom-call(bf16[2,64,2304]{2,1,0:T(8,128)(2,1)S(1)} %collective-permute-done.6.refs_0_, bf16[2,64,2304]{2,1,0:T(8,128)(2,1)S(1)} %collective-permute-done.7.refs_1_, bf16[4096,2304]{1,0:T(8,128)(2,1)S(1)} %get-tuple-element.37.head_ref.refs_2_, ...), custom_call_target="tpu_custom_call" | custom-call | flops 5368709120 | bytes 19922944 | tf_op jit(solution)/shard_map/chunk/pallas_call | solution.py:373
  66.5 3.5 %collective-permute-done.12.refs_1_ = bf16[2,64,2304]{2,1,0:T(8,128)(2,1)S(1)} collective-permute-done((bf16[2,64,2304]{2,1,0:T(8,128)(2,1)S(1)}, bf16[2,64,2304]{2,1,0:T(8,128)(2,1)S(1)}, u32[]{:S(2)}, u32[]{:S(2)}) %collective-permute-start.12) | collective-permute-done | bytes 589856 | tf_op jit(solution)/shard_map/ppermute | solution.py:377
  70.0 1.4 %collective-permute-done.11.refs_0_ = bf16[2,64,2304]{2,1,0:T(8,128)(2,1)S(1)} collective-permute-done((bf16[2,64,2304]{2,1,0:T(8,128)(2,1)S(1)}, bf16[2,64,2304]{2,1,0:T(8,128)(2,1)S(1)}, u32[]{:S(2)}, u32[]{:S(2)}) %collective-permute-start.11) | collective-permute-done | bytes 589856 | tf_op jit(solution)/shard_map/ppermute | solution.py:376
  71.4 6.7 %chunk.3.refs_0_ = f32[3,8,128]{2,1,0:T(8,128)S(1)} custom-call(bf16[2,64,2304]{2,1,0:T(8,128)(2,1)S(1)} %collective-permute-done.11.refs_0_, bf16[2,64,2304]{2,1,0:T(8,128)(2,1)S(1)} %collective-permute-done.12.refs_1_, bf16[4096,2304]{1,0:T(8,128)(2,1)S(1)} %get-tuple-element.37.head_ref.refs_2_, bf16[4096,64]{1,0:T(8,128)(2,1)S(1)} %get-tuple-element.48.refs_3_, ...), custom_call_target="tpu_custom_call" | custom-call | flops 5368709120 | bytes 19922944 | tf_op jit(solution)/shard_map/chunk/pallas_call | solution.py:373
  78.2 1.2 %collective-permute-start.13 = (f32[3,8,128]{2,1,0:T(8,128)S(1)}, f32[3,8,128]{2,1,0:T(8,128)S(1)}, u32[]{:S(2)}, u32[]{:S(2)}) collective-permute-start(f32[3,8,128]{2,1,0:T(8,128)S(1)} %chunk.3.refs_0_), channel_id=1, source_target_pairs={{0,1},{1,0},{2,3},{3,2},{4,5},{5,4},{6,7},{7,6},{8,9},{9,8},{10,11... | collective-permute-start | bytes 36872 | tf_op jit(solution)/shard_map/ppermute | solution.py:325
  79.3 2.6 %collective-permute-done.13.refs_1_ = f32[3,8,128]{2,1,0:T(8,128)S(1)} collective-permute-done((f32[3,8,128]{2,1,0:T(8,128)S(1)}, f32[3,8,128]{2,1,0:T(8,128)S(1)}, u32[]{:S(2)}, u32[]{:S(2)}) %collective-permute-start.13) | collective-permute-done | bytes 12320 | tf_op jit(solution)/shard_map/ppermute | solution.py:325
  81.9 2.1 %collective-permute-start.16 = (f32[3,8,128]{2,1,0:T(8,128)S(1)}, f32[3,8,128]{2,1,0:T(8,128)S(1)}, u32[]{:S(2)}, u32[]{:S(2)}) collective-permute-start(f32[3,8,128]{2,1,0:T(8,128)S(1)} %combine.2.refs_0_), channel_id=1, source_target_pairs={{0,6},{1,7},{2,4},{3,5},{4,2},{5,3},{6,0},{7,1},{8,14},{9,15},{10,... | collective-permute-start | bytes 36872 | tf_op jit(solution)/shard_map/ppermute | solution.py:325
  84.0 1.2 %collective-permute-start.15 = (f32[3,8,128]{2,1,0:T(8,128)S(1)}, f32[3,8,128]{2,1,0:T(8,128)S(1)}, u32[]{:S(2)}, u32[]{:S(2)}) collective-permute-start(f32[3,8,128]{2,1,0:T(8,128)S(1)} %combine.2.refs_0_), channel_id=1, source_target_pairs={{0,4},{1,5},{2,6},{3,7},{4,0},{5,1},{6,2},{7,3},{8,12},{9,13},{10,... | collective-permute-start | bytes 36872 | tf_op jit(solution)/shard_map/ppermute | solution.py:325
  85.2 1.2 %collective-permute-start.14 = (f32[3,8,128]{2,1,0:T(8,128)S(1)}, f32[3,8,128]{2,1,0:T(8,128)S(1)}, u32[]{:S(2)}, u32[]{:S(2)}) collective-permute-start(f32[3,8,128]{2,1,0:T(8,128)S(1)} %combine.2.refs_0_), channel_id=1, source_target_pairs={{0,2},{1,3},{2,0},{3,1},{4,6},{5,7},{6,4},{7,5},{8,10},{9,11},{10,... | collective-permute-start | bytes 36872 | tf_op jit(solution)/shard_map/ppermute | solution.py:325
  86.4 1.1 %collective-permute-done.16.refs_3_ = f32[3,8,128]{2,1,0:T(8,128)S(1)} collective-permute-done((f32[3,8,128]{2,1,0:T(8,128)S(1)}, f32[3,8,128]{2,1,0:T(8,128)S(1)}, u32[]{:S(2)}, u32[]{:S(2)}) %collective-permute-start.16) | collective-permute-done | bytes 12320 | tf_op jit(solution)/shard_map/ppermute | solution.py:325
  87.5 1.2 %collective-permute-done.15.refs_2_ = f32[3,8,128]{2,1,0:T(8,128)S(1)} collective-permute-done((f32[3,8,128]{2,1,0:T(8,128)S(1)}, f32[3,8,128]{2,1,0:T(8,128)S(1)}, u32[]{:S(2)}, u32[]{:S(2)}) %collective-permute-start.15) | collective-permute-done | bytes 12320 | tf_op jit(solution)/shard_map/ppermute | solution.py:325
  88.7 0.2 collective-permute-done.14.refs_1_
  88.9 0.7 combine.3
  (2 shorter events, 0.0 us)
Async XLA Ops:
  0.6 16.6 %collective-permute-start = (bf16[2,64,2304]{2,1,0:T(8,128)(2,1)}, bf16[2,64,2304]{2,1,0:T(8,128)(2,1)S(1)}, u32[]{:S(2)}, u32[]{:S(2)}) collective-permute-start(bf16[2,64,2304]{2,1,0:T(8,128)(2,1)} %down_ref.1), channel_id=1, source_target_pairs={{2,0},{4,2},{6,4},{7,6},{5,7},{3,5},{1,3},{0,1},{10,8},{12,10},{14... | collective-permute-start | bytes 1769480 | tf_op jit(solution)/shard_map/ppermute | solution.py:342
  3.6 27.0 %collective-permute-start.2 = (bf16[2,64,2304]{2,1,0:T(8,128)(2,1)}, bf16[2,64,2304]{2,1,0:T(8,128)(2,1)S(1)}, u32[]{:S(2)}, u32[]{:S(2)}) collective-permute-start(bf16[2,64,2304]{2,1,0:T(8,128)(2,1)} %down_ref.1), channel_id=1, source_target_pairs={{0,2},{2,4},{4,6},{6,7},{7,5},{5,3},{3,1},{1,0},{8,10},{10,12},{12... | collective-permute-start | bytes 1769480 | tf_op jit(solution)/shard_map/ppermute | solution.py:343
  3.8 26.8 %collective-permute-start.5 = (bf16[64,288]{1,0:T(8,128)(2,1)}, bf16[64,288]{1,0:T(8,128)(2,1)S(1)}, u32[]{:S(2)}, u32[]{:S(2)}) collective-permute-start(bf16[64,288]{1,0:T(8,128)(2,1)} %bitcast.3), channel_id=1, source_target_pairs={{1,0},{0,1},{13,2},{12,3},{19,4},{18,5},{31,6},{30,7},{3,8},{2,9},... | collective-permute-start | bytes 110600 | tf_op jit(solution)/shard_map/ppermute | solution.py:340
  5.6 24.9 %collective-permute-start.4 = (bf16[64,288]{1,0:T(8,128)(2,1)}, bf16[64,288]{1,0:T(8,128)(2,1)S(1)}, u32[]{:S(2)}, u32[]{:S(2)}) collective-permute-start(bf16[64,288]{1,0:T(8,128)(2,1)} %bitcast.4), channel_id=1, source_target_pairs={{0,0},{1,1},{12,2},{13,3},{18,4},{19,5},{30,6},{31,7},{2,8},{3,9},... | collective-permute-start | bytes 110600 | tf_op jit(solution)/shard_map/ppermute | solution.py:340
  7.1 23.5 %collective-permute-start.3 = (bf16[64,1024]{1,0:T(8,128)(2,1)}, bf16[64,1024]{1,0:T(8,128)(2,1)S(1)}, u32[]{:S(2)}, u32[]{:S(2)}) collective-permute-start(bf16[64,1024]{1,0:T(8,128)(2,1)} %bitcast.2), channel_id=1, source_target_pairs={{0,0},{4,1},{8,2},{12,3},{16,4},{20,5},{24,6},{28,7},{2,8},{6,9},{... | collective-permute-start | bytes 393224 | tf_op jit(solution)/shard_map/ppermute | solution.py:332
  17.2 20.0 %collective-permute-start.1 = (bf16[2,64,2304]{2,1,0:T(8,128)(2,1)S(1)}, bf16[2,64,2304]{2,1,0:T(8,128)(2,1)S(1)}, u32[]{:S(2)}, u32[]{:S(2)}) collective-permute-start(bf16[2,64,2304]{2,1,0:T(8,128)(2,1)S(1)} %collective-permute-done.up_ref), channel_id=1, source_target_pairs={{2,0},{4,2},{6,4},{7,6},{5,7},{3,5},{1,3},{0,1},{10,8},{12,10},{14... | collective-permute-start | bytes 1769480 | tf_op jit(solution)/shard_map/ppermute | solution.py:344
  19.4 1.1 %copy-start = (bf16[2,64,2304]{2,1,0:T(8,128)(2,1)S(1)}, bf16[2,64,2304]{2,1,0:T(8,128)(2,1)}, u32[]{:S(2)}) copy-start(bf16[2,64,2304]{2,1,0:T(8,128)(2,1)} %down_ref.1) | copy-start | bytes 1769476
  30.6 21.0 %collective-permute-start.7 = (bf16[2,64,2304]{2,1,0:T(8,128)(2,1)S(1)}, bf16[2,64,2304]{2,1,0:T(8,128)(2,1)S(1)}, u32[]{:S(2)}, u32[]{:S(2)}) collective-permute-start(bf16[2,64,2304]{2,1,0:T(8,128)(2,1)S(1)} %collective-permute-done.2.down_ref), channel_id=1, source_target_pairs={{0,2},{2,4},{4,6},{6,7},{7,5},{5,3},{3,1},{1,0},{8,10},{10,12},{12... | collective-permute-start | bytes 1769480 | tf_op jit(solution)/shard_map/ppermute | solution.py:356
  37.3 19.1 %collective-permute-start.6 = (bf16[2,64,2304]{2,1,0:T(8,128)(2,1)S(1)}, bf16[2,64,2304]{2,1,0:T(8,128)(2,1)S(1)}, u32[]{:S(2)}, u32[]{:S(2)}) collective-permute-start(bf16[2,64,2304]{2,1,0:T(8,128)(2,1)S(1)} %collective-permute-done.1.up_ref), channel_id=1, source_target_pairs={{2,0},{4,2},{6,4},{7,6},{5,7},{3,5},{1,3},{0,1},{10,8},{12,10},{14... | collective-permute-start | bytes 1769480 | tf_op jit(solution)/shard_map/ppermute | solution.py:355
  37.3 13.5 %copy-start.1 = (s32[2,512]{1,0:T(2,128)S(1)}, s32[2,512]{1,0:T(2,128)}, u32[]{:S(2)}) copy-start(s32[2,512]{1,0:T(2,128)} %sampled_ref.1) | copy-start | bytes 12292
  43.2 6.1 %collective-permute-start.9 = (bf16[64,1792]{1,0:T(8,128)(2,1)S(1)}, bf16[64,1792]{1,0:T(8,128)(2,1)S(1)}, u32[]{:S(2)}, u32[]{:S(2)}) collective-permute-start(bf16[64,1792]{1,0:T(8,128)(2,1)S(1)} %fusion.4.refs_0_), channel_id=1, source_target_pairs={{0,16},{8,24},{16,0},{24,8},{1,17},{9,25},{17,1},{25,9},{2,18},{10... | collective-permute-start | bytes 688136 | tf_op jit(solution)/shard_map/ppermute | solution.py:325
  44.2 5.1 %collective-permute-start.8 = (bf16[64,1792]{1,0:T(8,128)(2,1)S(1)}, bf16[64,1792]{1,0:T(8,128)(2,1)S(1)}, u32[]{:S(2)}, u32[]{:S(2)}) collective-permute-start(bf16[64,1792]{1,0:T(8,128)(2,1)S(1)} %fusion.4.refs_0_), channel_id=1, source_target_pairs={{0,8},{8,0},{16,24},{24,16},{1,9},{9,1},{17,25},{25,17},{2,10},{10... | collective-permute-start | bytes 688136 | tf_op jit(solution)/shard_map/ppermute | solution.py:325
  49.3 1.5 %collective-permute-start.10 = (bf16[64,1792]{1,0:T(8,128)(2,1)S(1)}, bf16[64,1792]{1,0:T(8,128)(2,1)S(1)}, u32[]{:S(2)}, u32[]{:S(2)}) collective-permute-start(bf16[64,1792]{1,0:T(8,128)(2,1)S(1)} %collective-permute-done.9.refs_2_), channel_id=1, source_target_pairs={{0,8},{8,0},{16,24},{24,16},{1,9},{9,1},{17,25},{25,17},{2,10},{10... | collective-permute-start | bytes 688136 | tf_op jit(solution)/shard_map/ppermute | solution.py:325
  51.6 18.4 %collective-permute-start.12 = (bf16[2,64,2304]{2,1,0:T(8,128)(2,1)S(1)}, bf16[2,64,2304]{2,1,0:T(8,128)(2,1)S(1)}, u32[]{:S(2)}, u32[]{:S(2)}) collective-permute-start(bf16[2,64,2304]{2,1,0:T(8,128)(2,1)S(1)} %collective-permute-done.7.refs_1_), channel_id=1, source_target_pairs={{0,2},{2,4},{4,6},{6,7},{7,5},{5,3},{3,1},{1,0},{8,10},{10,12},{12... | collective-permute-start | bytes 1769480 | tf_op jit(solution)/shard_map/ppermute | solution.py:377
  56.3 15.1 %collective-permute-start.11 = (bf16[2,64,2304]{2,1,0:T(8,128)(2,1)S(1)}, bf16[2,64,2304]{2,1,0:T(8,128)(2,1)S(1)}, u32[]{:S(2)}, u32[]{:S(2)}) collective-permute-start(bf16[2,64,2304]{2,1,0:T(8,128)(2,1)S(1)} %collective-permute-done.6.refs_0_), channel_id=1, source_target_pairs={{2,0},{4,2},{6,4},{7,6},{5,7},{3,5},{1,3},{0,1},{10,8},{12,10},{14... | collective-permute-start | bytes 1769480 | tf_op jit(solution)/shard_map/ppermute | solution.py:376
  78.2 3.8 %collective-permute-start.13 = (f32[3,8,128]{2,1,0:T(8,128)S(1)}, f32[3,8,128]{2,1,0:T(8,128)S(1)}, u32[]{:S(2)}, u32[]{:S(2)}) collective-permute-start(f32[3,8,128]{2,1,0:T(8,128)S(1)} %chunk.3.refs_0_), channel_id=1, source_target_pairs={{0,1},{1,0},{2,3},{3,2},{4,5},{5,4},{6,7},{7,6},{8,9},{9,8},{10,11... | collective-permute-start | bytes 36872 | tf_op jit(solution)/shard_map/ppermute | solution.py:325
  81.9 5.6 %collective-permute-start.16 = (f32[3,8,128]{2,1,0:T(8,128)S(1)}, f32[3,8,128]{2,1,0:T(8,128)S(1)}, u32[]{:S(2)}, u32[]{:S(2)}) collective-permute-start(f32[3,8,128]{2,1,0:T(8,128)S(1)} %combine.2.refs_0_), channel_id=1, source_target_pairs={{0,6},{1,7},{2,4},{3,5},{4,2},{5,3},{6,0},{7,1},{8,14},{9,15},{10,... | collective-permute-start | bytes 36872 | tf_op jit(solution)/shard_map/ppermute | solution.py:325
  84.0 4.7 %collective-permute-start.15 = (f32[3,8,128]{2,1,0:T(8,128)S(1)}, f32[3,8,128]{2,1,0:T(8,128)S(1)}, u32[]{:S(2)}, u32[]{:S(2)}) collective-permute-start(f32[3,8,128]{2,1,0:T(8,128)S(1)} %combine.2.refs_0_), channel_id=1, source_target_pairs={{0,4},{1,5},{2,6},{3,7},{4,0},{5,1},{6,2},{7,3},{8,12},{9,13},{10,... | collective-permute-start | bytes 36872 | tf_op jit(solution)/shard_map/ppermute | solution.py:325
  85.2 3.7 %collective-permute-start.14 = (f32[3,8,128]{2,1,0:T(8,128)S(1)}, f32[3,8,128]{2,1,0:T(8,128)S(1)}, u32[]{:S(2)}, u32[]{:S(2)}) collective-permute-start(f32[3,8,128]{2,1,0:T(8,128)S(1)} %combine.2.refs_0_), channel_id=1, source_target_pairs={{0,2},{1,3},{2,0},{3,1},{4,6},{5,7},{6,4},{7,5},{8,10},{9,11},{10,... | collective-permute-start | bytes 36872 | tf_op jit(solution)/shard_map/ppermute | solution.py:325

commit v15 on v14

--- a/solution.py
+++ b/solution.py
@@ -347,19 +347,21 @@
     held = [base, base_rows]
     gap = ((0, 0), (0, padded(v_rows) - v_rows))
     pack = jnp.concatenate([block] + [jnp.pad(x, gap) for x in shards], axis=1)
+    packs = {0: pack}
+    near = [1 << k for k in reversed(range(n_group.bit_length() - 1))]
+    for bit in near:
+        packs[bit] = trade(pack, "group", n_group, bit)
     down[1], held[0] = lax.optimization_barrier((down[1], held[0]))
     up[2], held[0] = lax.optimization_barrier((up[2], held[0]))
     held += make_base(r, depth, entries, False)(up[2], down[1], head)
-    held[2], pack = lax.optimization_barrier((held[2], pack))
+    held[2], *crossed = lax.optimization_barrier((held[2], *[packs[bit] for bit in near]))
+    packs.update(zip(near, crossed))
 
     up.append(lax.ppermute(up[2], "vocab", behind))
     down.append(lax.ppermute(down[1], "vocab", ahead))
-    packs = {0: pack}
-    bit = n_group // 2
-    while bit:
-        for k in list(packs):
-            packs[k ^ bit] = trade(packs[k], "group", n_group, bit)
-        bit //= 2
+    for k in range(n_group):
+        if k not in packs:
+            packs[k] = trade(packs[k & (k - 1)], "group", n_group, k & -k)
     full_u, full_v, want = make_assemble(
         n_group, n_voc, u_rows, v_rows, rank, r, entries
     )(sampled, *[packs[k] for k in range(n_group)])

time: 89.9 us -> 86.4 us (0.961)
  waiting for transfers between devices: 27.2 us -> 23.4 us
    ppermute x7, waiting for transfers between devices: 11.7 us -> 6.09 us  [trade(): return lax.ppermute(x, axis, [(i, i ^ bit) for i in range(size)])]
    ppermute x1, waiting for transfers between devices: 0.01 us -> 5.25 us  [body(): down.append(lax.ppermute(down[1], 'vocab', ahead))]
    ppermute x1, starting transfers between devices: 4.7 us -> 0.01 us  [body(): down.append(lax.ppermute(down[-1], 'vocab', ahead))]
    ppermute x1, starting transfers between devices: 0.15 us -> 4.23 us  [body(): down = [hidden, lax.ppermute(hidden, 'vocab', ahead)]]
    ppermute x1, waiting for transfers between devices: 8.6 us -> 4.82 us  [body(): up = [hidden, lax.ppermute(hidden, 'vocab', behind)]]
    ppermute x1, waiting for transfers between devices: 0.01 us -> 2.08 us  [body(): up.append(lax.ppermute(up[2], 'vocab', behind))]
    ppermute x1, waiting for transfers between devices: 1.38 us -> 0.01 us  [body(): up.append(lax.ppermute(up[-1], 'vocab', behind))]
    ppermute x1, starting transfers between devices: 4.61 us -> 3.31 us  [body(): down.append(lax.ppermute(down[1], 'vocab', ahead))]
  transfers between devices with their start and end apart: 17 -> 17, of which waited for: 10 -> 9; matrix products, arithmetic and copies ran while one was open for 0% -> 0% of each run, Pallas kernels for 30% -> 31%
where the time goes in v15:
time: 86.4 us; the launch traced here: 86.1 us
  Pallas kernels  34.2 us (40%)
  starting transfers between devices  26.8 us (31%)
  waiting for transfers between devices  23.4 us (27%)
  local copies, waits for them, and re-layouts  1.07 us (1%)
    pallas_call x2, Pallas kernels, body(): out = chunk(up[hop], down[hop - 1], head, full_u, full_v, want, *extra)  16.6 us
    pallas_call x1, Pallas kernels, body(): make_base(r, depth, entries, True)(up[1], hidden, head)  10.1 us
    ppermute x7, starting transfers between devices, trade(): return lax.ppermute(x, axis, [(i, i ^ bit) for i in range(size)])  7.81 us
    ppermute x7, waiting for transfers between devices, trade(): return lax.ppermute(x, axis, [(i, i ^ bit) for i in range(size)])  6.09 us
    pallas_call x1, Pallas kernels, body(): held += make_base(r, depth, entries, False)(up[2], down[1], head)  5.92 us
    ppermute x1, waiting for transfers between devices, body(): down.append(lax.ppermute(down[1], 'vocab', ahead))  5.25 us
    ppermute x1, waiting for transfers between devices, body(): up = [hidden, lax.ppermute(hidden, 'vocab', behind)]  4.82 us
    ppermute x1, starting transfers between devices, body(): down = [hidden, lax.ppermute(hidden, 'vocab', ahead)]  4.23 us
  transfers between devices with their start and end apart: 17, of which 9 were waited for; matrix products, arithmetic and copies ran while one was open for 0% of the time, Pallas kernels for 31%

profile of v15, /device:TPU:0, one launch (start us, length us, event | category | flops | bytes accessed | tf_op | source)
XLA Modules:
  0.0 86.1 jit_solution(2955953548165939657)
XLA Ops:
  0.6 3.0 %collective-permute-start = (bf16[2,64,2304]{2,1,0:T(8,128)(2,1)}, bf16[2,64,2304]{2,1,0:T(8,128)(2,1)S(1)}, u32[]{:S(2)}, u32[]{:S(2)}) collective-permute-start(bf16[2,64,2304]{2,1,0:T(8,128)(2,1)} %down_ref.1), channel_id=1, source_target_pairs={{2,0},{4,2},{6,4},{7,6},{5,7},{3,5},{1,3},{0,1},{10,8},{12,10},{14... | collective-permute-start | bytes 1769480 | tf_op jit(solution)/shard_map/ppermute | solution.py:342
  3.6 1.6 %collective-permute-start.5 = (bf16[64,288]{1,0:T(8,128)(2,1)}, bf16[64,288]{1,0:T(8,128)(2,1)S(1)}, u32[]{:S(2)}, u32[]{:S(2)}) collective-permute-start(bf16[64,288]{1,0:T(8,128)(2,1)} %bitcast.3), channel_id=1, source_target_pairs={{1,0},{0,1},{13,2},{12,3},{19,4},{18,5},{31,6},{30,7},{3,8},{2,9},... | collective-permute-start | bytes 110600 | tf_op jit(solution)/shard_map/ppermute | solution.py:340
  5.2 1.4 %collective-permute-start.4 = (bf16[64,288]{1,0:T(8,128)(2,1)}, bf16[64,288]{1,0:T(8,128)(2,1)S(1)}, u32[]{:S(2)}, u32[]{:S(2)}) collective-permute-start(bf16[64,288]{1,0:T(8,128)(2,1)} %bitcast.4), channel_id=1, source_target_pairs={{0,0},{1,1},{12,2},{13,3},{18,4},{19,5},{30,6},{31,7},{2,8},{3,9},... | collective-permute-start | bytes 110600 | tf_op jit(solution)/shard_map/ppermute | solution.py:340
  6.6 4.2 %collective-permute-start.2 = (bf16[2,64,2304]{2,1,0:T(8,128)(2,1)}, bf16[2,64,2304]{2,1,0:T(8,128)(2,1)S(1)}, u32[]{:S(2)}, u32[]{:S(2)}) collective-permute-start(bf16[2,64,2304]{2,1,0:T(8,128)(2,1)} %down_ref.1), channel_id=1, source_target_pairs={{0,2},{2,4},{4,6},{6,7},{7,5},{5,3},{3,1},{1,0},{8,10},{10,12},{12... | collective-permute-start | bytes 1769480 | tf_op jit(solution)/shard_map/ppermute | solution.py:343
  10.9 1.6 %collective-permute-start.3 = (bf16[64,1024]{1,0:T(8,128)(2,1)}, bf16[64,1024]{1,0:T(8,128)(2,1)S(1)}, u32[]{:S(2)}, u32[]{:S(2)}) collective-permute-start(bf16[64,1024]{1,0:T(8,128)(2,1)} %bitcast.2), channel_id=1, source_target_pairs={{0,0},{4,1},{8,2},{12,3},{16,4},{20,5},{24,6},{28,7},{2,8},{6,9},{... | collective-permute-start | bytes 393224 | tf_op jit(solution)/shard_map/ppermute | solution.py:332
  12.4 4.8 %collective-permute-done.up_ref = bf16[2,64,2304]{2,1,0:T(8,128)(2,1)S(1)} collective-permute-done((bf16[2,64,2304]{2,1,0:T(8,128)(2,1)}, bf16[2,64,2304]{2,1,0:T(8,128)(2,1)S(1)}, u32[]{:S(2)}, u32[]{:S(2)}) %collective-permute-start) | collective-permute-done | bytes 589856 | tf_op jit(solution)/shard_map/ppermute | solution.py:342
  17.2 2.2 %collective-permute-start.1 = (bf16[2,64,2304]{2,1,0:T(8,128)(2,1)S(1)}, bf16[2,64,2304]{2,1,0:T(8,128)(2,1)S(1)}, u32[]{:S(2)}, u32[]{:S(2)}) collective-permute-start(bf16[2,64,2304]{2,1,0:T(8,128)(2,1)S(1)} %collective-permute-done.up_ref), channel_id=1, source_target_pairs={{2,0},{4,2},{6,4},{7,6},{5,7},{3,5},{1,3},{0,1},{10,8},{12,10},{14... | collective-permute-start | bytes 1769480 | tf_op jit(solution)/shard_map/ppermute | solution.py:344
  19.4 0.0 copy-start
  19.4 1.1 %copy-done = bf16[2,64,2304]{2,1,0:T(8,128)(2,1)S(1)} copy-done((bf16[2,64,2304]{2,1,0:T(8,128)(2,1)S(1)}, bf16[2,64,2304]{2,1,0:T(8,128)(2,1)}, u32[]{:S(2)}) %copy-start) | copy-done | bytes 589848
  20.5 10.1 %base.2 = (f32[4096,256]{1,0:T(8,128)S(1)}, bf16[2304,256]{1,0:T(8,128)(2,1)S(1)}, bf16[4096,2304]{1,0:T(8,128)(2,1)S(1)}) custom-call(bf16[2,64,2304]{2,1,0:T(8,128)(2,1)S(1)} %collective-permute-done.up_ref, bf16[2,64,2304]{2,1,0:T(8,128)(2,1)S(1)} %copy-done, bf16[4096,2304]{1,0:T(8,128)(2,1)} %head_ref.1), custom_call_target="tpu_custom_call" | custom-call | flops 4831838208 | bytes 18874368 | tf_op jit(solution)/shard_map/base/pallas_call | solution.py:345
  30.6 0.0 collective-permute-done.5
  30.6 0.0 collective-permute-done.4
  30.6 0.0 collective-permute-done.3
  30.6 0.1 collective-permute-start.8
  30.7 1.4 %collective-permute-start.7 = (bf16[64,1792]{1,0:T(8,128)(2,1)S(1)}, bf16[64,1792]{1,0:T(8,128)(2,1)S(1)}, u32[]{:S(2)}, u32[]{:S(2)}) collective-permute-start(bf16[64,1792]{1,0:T(8,128)(2,1)S(1)} %fusion.4.refs_0_), channel_id=1, source_target_pairs={{0,16},{8,24},{16,0},{24,8},{1,17},{9,25},{17,1},{25,9},{2,18},{10... | collective-permute-start | bytes 688136 | tf_op jit(solution)/shard_map/ppermute | solution.py:325
  32.1 0.0 collective-permute-done.2.down_ref
  32.1 3.3 %collective-permute-start.9 = (bf16[2,64,2304]{2,1,0:T(8,128)(2,1)S(1)}, bf16[2,64,2304]{2,1,0:T(8,128)(2,1)S(1)}, u32[]{:S(2)}, u32[]{:S(2)}) collective-permute-start(bf16[2,64,2304]{2,1,0:T(8,128)(2,1)S(1)} %collective-permute-done.2.down_ref), channel_id=1, source_target_pairs={{0,2},{2,4},{4,6},{6,7},{7,5},{5,3},{3,1},{1,0},{8,10},{10,12},{12... | collective-permute-start | bytes 1769480 | tf_op jit(solution)/shard_map/ppermute | solution.py:361
  35.4 1.8 %collective-permute-done.1.up_ref = bf16[2,64,2304]{2,1,0:T(8,128)(2,1)S(1)} collective-permute-done((bf16[2,64,2304]{2,1,0:T(8,128)(2,1)S(1)}, bf16[2,64,2304]{2,1,0:T(8,128)(2,1)S(1)}, u32[]{:S(2)}, u32[]{:S(2)}) %collective-permute-start.1) | collective-permute-done | bytes 589856 | tf_op jit(solution)/shard_map/ppermute | solution.py:344
  37.3 1.0 %collective-permute-start.6 = (bf16[2,64,2304]{2,1,0:T(8,128)(2,1)S(1)}, bf16[2,64,2304]{2,1,0:T(8,128)(2,1)S(1)}, u32[]{:S(2)}, u32[]{:S(2)}) collective-permute-start(bf16[2,64,2304]{2,1,0:T(8,128)(2,1)S(1)} %collective-permute-done.1.up_ref), channel_id=1, source_target_pairs={{2,0},{4,2},{6,4},{7,6},{5,7},{3,5},{1,3},{0,1},{10,8},{12,10},{14... | collective-permute-start | bytes 1769480 | tf_op jit(solution)/shard_map/ppermute | solution.py:360
  38.2 0.0 copy-start.1
  38.2 5.9 %base.3 = (f32[4096,256]{1,0:T(8,128)S(1)}, bf16[2304,256]{1,0:T(8,128)(2,1)S(1)}) custom-call(bf16[2,64,2304]{2,1,0:T(8,128)(2,1)S(1)} %collective-permute-done.1.up_ref, bf16[2,64,2304]{2,1,0:T(8,128)(2,1)S(1)} %collective-permute-done.2.down_ref, bf16[4096,2304]{1,0:T(8,128)(2,1)S(1)} %get-tuple-element.38.head_ref.refs_2_), custom_call_target="tpu_custom_call" | custom-call | flops 4831838208 | bytes 18874368 | tf_op jit(solution)/shard_map/base/pallas_call | solution.py:356
  44.2 0.0 collective-permute-done.8.refs_1_
  44.2 0.0 collective-permute-done.7.refs_2_
  44.2 0.1 collective-permute-start.10
  44.3 1.5 %collective-permute-done.10.refs_3_ = bf16[64,1792]{1,0:T(8,128)(2,1)S(1)} collective-permute-done((bf16[64,1792]{1,0:T(8,128)(2,1)S(1)}, bf16[64,1792]{1,0:T(8,128)(2,1)S(1)}, u32[]{:S(2)}, u32[]{:S(2)}) %collective-permute-start.10) | collective-permute-done | bytes 229408 | tf_op jit(solution)/shard_map/ppermute | solution.py:325
  45.7 0.0 copy-done.1
  45.7 0.8 assemble.1
  46.6 5.2 %collective-permute-done.9.refs_1_ = bf16[2,64,2304]{2,1,0:T(8,128)(2,1)S(1)} collective-permute-done((bf16[2,64,2304]{2,1,0:T(8,128)(2,1)S(1)}, bf16[2,64,2304]{2,1,0:T(8,128)(2,1)S(1)}, u32[]{:S(2)}, u32[]{:S(2)}) %collective-permute-start.9) | collective-permute-done | bytes 589856 | tf_op jit(solution)/shard_map/ppermute | solution.py:361
  51.8 0.0 collective-permute-start.12
  51.8 2.1 %collective-permute-done.6.refs_0_ = bf16[2,64,2304]{2,1,0:T(8,128)(2,1)S(1)} collective-permute-done((bf16[2,64,2304]{2,1,0:T(8,128)(2,1)S(1)}, bf16[2,64,2304]{2,1,0:T(8,128)(2,1)S(1)}, u32[]{:S(2)}, u32[]{:S(2)}) %collective-permute-start.6) | collective-permute-done | bytes 589856 | tf_op jit(solution)/shard_map/ppermute | solution.py:360
  53.9 0.7 collective-permute-start.11
  54.6 9.9 %chunk.2 = (f32[3,256]{1,0:T(4,128)S(1)}, f32[3,256]{1,0:T(4,128)S(1)}, f32[3,256]{1,0:T(4,128)S(1)}) custom-call(bf16[2,64,2304]{2,1,0:T(8,128)(2,1)S(1)} %collective-permute-done.6.refs_0_, bf16[2,64,2304]{2,1,0:T(8,128)(2,1)S(1)} %collective-permute-done.9.refs_1_, bf16[4096,2304]{1,0:T(8,128)(2,1)S(1)} %get-tuple-element.38.head_ref.refs_2_, ...), custom_call_target="tpu_custom_call" | custom-call | flops 5368709120 | bytes 19922944 | tf_op jit(solution)/shard_map/chunk/pallas_call | solution.py:375
  64.5 3.3 %collective-permute-done.12.refs_1_ = bf16[2,64,2304]{2,1,0:T(8,128)(2,1)S(1)} collective-permute-done((bf16[2,64,2304]{2,1,0:T(8,128)(2,1)S(1)}, bf16[2,64,2304]{2,1,0:T(8,128)(2,1)S(1)}, u32[]{:S(2)}, u32[]{:S(2)}) %collective-permute-start.12) | collective-permute-done | bytes 589856 | tf_op jit(solution)/shard_map/ppermute | solution.py:379
  67.8 0.0 collective-permute-done.11.refs_0_
  67.8 6.7 %chunk.3.refs_0_ = f32[3,8,128]{2,1,0:T(8,128)S(1)} custom-call(bf16[2,64,2304]{2,1,0:T(8,128)(2,1)S(1)} %collective-permute-done.11.refs_0_, bf16[2,64,2304]{2,1,0:T(8,128)(2,1)S(1)} %collective-permute-done.12.refs_1_, bf16[4096,2304]{1,0:T(8,128)(2,1)S(1)} %get-tuple-element.38.head_ref.refs_2_, bf16[4096,64]{1,0:T(8,128)(2,1)S(1)} %get-tuple-element.50.refs_3_, ...), custom_call_target="tpu_custom_call" | custom-call | flops 5368709120 | bytes 19922944 | tf_op jit(solution)/shard_map/chunk/pallas_call | solution.py:375
  74.5 1.8 %collective-permute-start.13 = (f32[3,8,128]{2,1,0:T(8,128)S(1)}, f32[3,8,128]{2,1,0:T(8,128)S(1)}, u32[]{:S(2)}, u32[]{:S(2)}) collective-permute-start(f32[3,8,128]{2,1,0:T(8,128)S(1)} %chunk.3.refs_0_), channel_id=1, source_target_pairs={{0,1},{1,0},{2,3},{3,2},{4,5},{5,4},{6,7},{7,6},{8,9},{9,8},{10,11... | collective-permute-start | bytes 36872 | tf_op jit(solution)/shard_map/ppermute | solution.py:325
  76.4 1.9 %collective-permute-done.13.refs_1_ = f32[3,8,128]{2,1,0:T(8,128)S(1)} collective-permute-done((f32[3,8,128]{2,1,0:T(8,128)S(1)}, f32[3,8,128]{2,1,0:T(8,128)S(1)}, u32[]{:S(2)}, u32[]{:S(2)}) %collective-permute-start.13) | collective-permute-done | bytes 12320 | tf_op jit(solution)/shard_map/ppermute | solution.py:325
  78.3 2.4 %collective-permute-start.16 = (f32[3,8,128]{2,1,0:T(8,128)S(1)}, f32[3,8,128]{2,1,0:T(8,128)S(1)}, u32[]{:S(2)}, u32[]{:S(2)}) collective-permute-start(f32[3,8,128]{2,1,0:T(8,128)S(1)} %combine.2.refs_0_), channel_id=1, source_target_pairs={{0,6},{1,7},{2,4},{3,5},{4,2},{5,3},{6,0},{7,1},{8,14},{9,15},{10,... | collective-permute-start | bytes 36872 | tf_op jit(solution)/shard_map/ppermute | solution.py:325
  80.7 0.6 collective-permute-start.15
  81.3 1.5 %collective-permute-start.14 = (f32[3,8,128]{2,1,0:T(8,128)S(1)}, f32[3,8,128]{2,1,0:T(8,128)S(1)}, u32[]{:S(2)}, u32[]{:S(2)}) collective-permute-start(f32[3,8,128]{2,1,0:T(8,128)S(1)} %combine.2.refs_0_), channel_id=1, source_target_pairs={{0,2},{1,3},{2,0},{3,1},{4,6},{5,7},{6,4},{7,5},{8,10},{9,11},{10,... | collective-permute-start | bytes 36872 | tf_op jit(solution)/shard_map/ppermute | solution.py:325
  82.8 1.1 %collective-permute-done.16.refs_3_ = f32[3,8,128]{2,1,0:T(8,128)S(1)} collective-permute-done((f32[3,8,128]{2,1,0:T(8,128)S(1)}, f32[3,8,128]{2,1,0:T(8,128)S(1)}, u32[]{:S(2)}, u32[]{:S(2)}) %collective-permute-start.16) | collective-permute-done | bytes 12320 | tf_op jit(solution)/shard_map/ppermute | solution.py:325
  83.9 1.6 %collective-permute-done.15.refs_2_ = f32[3,8,128]{2,1,0:T(8,128)S(1)} collective-permute-done((f32[3,8,128]{2,1,0:T(8,128)S(1)}, f32[3,8,128]{2,1,0:T(8,128)S(1)}, u32[]{:S(2)}, u32[]{:S(2)}) %collective-permute-start.15) | collective-permute-done | bytes 12320 | tf_op jit(solution)/shard_map/ppermute | solution.py:325
  85.4 0.0 collective-permute-done.14.refs_1_
  85.4 0.7 combine.3
  (2 shorter events, 0.0 us)
Async XLA Ops:
  0.6 16.6 %collective-permute-start = (bf16[2,64,2304]{2,1,0:T(8,128)(2,1)}, bf16[2,64,2304]{2,1,0:T(8,128)(2,1)S(1)}, u32[]{:S(2)}, u32[]{:S(2)}) collective-permute-start(bf16[2,64,2304]{2,1,0:T(8,128)(2,1)} %down_ref.1), channel_id=1, source_target_pairs={{2,0},{4,2},{6,4},{7,6},{5,7},{3,5},{1,3},{0,1},{10,8},{12,10},{14... | collective-permute-start | bytes 1769480 | tf_op jit(solution)/shard_map/ppermute | solution.py:342
  3.6 26.9 %collective-permute-start.5 = (bf16[64,288]{1,0:T(8,128)(2,1)}, bf16[64,288]{1,0:T(8,128)(2,1)S(1)}, u32[]{:S(2)}, u32[]{:S(2)}) collective-permute-start(bf16[64,288]{1,0:T(8,128)(2,1)} %bitcast.3), channel_id=1, source_target_pairs={{1,0},{0,1},{13,2},{12,3},{19,4},{18,5},{31,6},{30,7},{3,8},{2,9},... | collective-permute-start | bytes 110600 | tf_op jit(solution)/shard_map/ppermute | solution.py:340
  5.2 25.4 %collective-permute-start.4 = (bf16[64,288]{1,0:T(8,128)(2,1)}, bf16[64,288]{1,0:T(8,128)(2,1)S(1)}, u32[]{:S(2)}, u32[]{:S(2)}) collective-permute-start(bf16[64,288]{1,0:T(8,128)(2,1)} %bitcast.4), channel_id=1, source_target_pairs={{0,0},{1,1},{12,2},{13,3},{18,4},{19,5},{30,6},{31,7},{2,8},{3,9},... | collective-permute-start | bytes 110600 | tf_op jit(solution)/shard_map/ppermute | solution.py:340
  6.6 25.5 %collective-permute-start.2 = (bf16[2,64,2304]{2,1,0:T(8,128)(2,1)}, bf16[2,64,2304]{2,1,0:T(8,128)(2,1)S(1)}, u32[]{:S(2)}, u32[]{:S(2)}) collective-permute-start(bf16[2,64,2304]{2,1,0:T(8,128)(2,1)} %down_ref.1), channel_id=1, source_target_pairs={{0,2},{2,4},{4,6},{6,7},{7,5},{5,3},{3,1},{1,0},{8,10},{10,12},{12... | collective-permute-start | bytes 1769480 | tf_op jit(solution)/shard_map/ppermute | solution.py:343
  10.9 19.7 %collective-permute-start.3 = (bf16[64,1024]{1,0:T(8,128)(2,1)}, bf16[64,1024]{1,0:T(8,128)(2,1)S(1)}, u32[]{:S(2)}, u32[]{:S(2)}) collective-permute-start(bf16[64,1024]{1,0:T(8,128)(2,1)} %bitcast.2), channel_id=1, source_target_pairs={{0,0},{4,1},{8,2},{12,3},{16,4},{20,5},{24,6},{28,7},{2,8},{6,9},{... | collective-permute-start | bytes 393224 | tf_op jit(solution)/shard_map/ppermute | solution.py:332
  17.2 20.0 %collective-permute-start.1 = (bf16[2,64,2304]{2,1,0:T(8,128)(2,1)S(1)}, bf16[2,64,2304]{2,1,0:T(8,128)(2,1)S(1)}, u32[]{:S(2)}, u32[]{:S(2)}) collective-permute-start(bf16[2,64,2304]{2,1,0:T(8,128)(2,1)S(1)} %collective-permute-done.up_ref), channel_id=1, source_target_pairs={{2,0},{4,2},{6,4},{7,6},{5,7},{3,5},{1,3},{0,1},{10,8},{12,10},{14... | collective-permute-start | bytes 1769480 | tf_op jit(solution)/shard_map/ppermute | solution.py:344
  19.4 1.1 %copy-start = (bf16[2,64,2304]{2,1,0:T(8,128)(2,1)S(1)}, bf16[2,64,2304]{2,1,0:T(8,128)(2,1)}, u32[]{:S(2)}) copy-start(bf16[2,64,2304]{2,1,0:T(8,128)(2,1)} %down_ref.1) | copy-start | bytes 1769476
  30.6 13.5 %collective-permute-start.8 = (bf16[64,1792]{1,0:T(8,128)(2,1)S(1)}, bf16[64,1792]{1,0:T(8,128)(2,1)S(1)}, u32[]{:S(2)}, u32[]{:S(2)}) collective-permute-start(bf16[64,1792]{1,0:T(8,128)(2,1)S(1)} %fusion.4.refs_0_), channel_id=1, source_target_pairs={{0,8},{8,0},{16,24},{24,16},{1,9},{9,1},{17,25},{25,17},{2,10},{10... | collective-permute-start | bytes 688136 | tf_op jit(solution)/shard_map/ppermute | solution.py:325
  30.7 13.5 %collective-permute-start.7 = (bf16[64,1792]{1,0:T(8,128)(2,1)S(1)}, bf16[64,1792]{1,0:T(8,128)(2,1)S(1)}, u32[]{:S(2)}, u32[]{:S(2)}) collective-permute-start(bf16[64,1792]{1,0:T(8,128)(2,1)S(1)} %fusion.4.refs_0_), channel_id=1, source_target_pairs={{0,16},{8,24},{16,0},{24,8},{1,17},{9,25},{17,1},{25,9},{2,18},{10... | collective-permute-start | bytes 688136 | tf_op jit(solution)/shard_map/ppermute | solution.py:325
  32.1 19.7 %collective-permute-start.9 = (bf16[2,64,2304]{2,1,0:T(8,128)(2,1)S(1)}, bf16[2,64,2304]{2,1,0:T(8,128)(2,1)S(1)}, u32[]{:S(2)}, u32[]{:S(2)}) collective-permute-start(bf16[2,64,2304]{2,1,0:T(8,128)(2,1)S(1)} %collective-permute-done.2.down_ref), channel_id=1, source_target_pairs={{0,2},{2,4},{4,6},{6,7},{7,5},{5,3},{3,1},{1,0},{8,10},{10,12},{12... | collective-permute-start | bytes 1769480 | tf_op jit(solution)/shard_map/ppermute | solution.py:361
  37.3 16.7 %collective-permute-start.6 = (bf16[2,64,2304]{2,1,0:T(8,128)(2,1)S(1)}, bf16[2,64,2304]{2,1,0:T(8,128)(2,1)S(1)}, u32[]{:S(2)}, u32[]{:S(2)}) collective-permute-start(bf16[2,64,2304]{2,1,0:T(8,128)(2,1)S(1)} %collective-permute-done.1.up_ref), channel_id=1, source_target_pairs={{2,0},{4,2},{6,4},{7,6},{5,7},{3,5},{1,3},{0,1},{10,8},{12,10},{14... | collective-permute-start | bytes 1769480 | tf_op jit(solution)/shard_map/ppermute | solution.py:360
  38.2 7.5 %copy-start.1 = (s32[2,512]{1,0:T(2,128)S(1)}, s32[2,512]{1,0:T(2,128)}, u32[]{:S(2)}) copy-start(s32[2,512]{1,0:T(2,128)} %sampled_ref.1) | copy-start | bytes 12292
  44.2 1.6 %collective-permute-start.10 = (bf16[64,1792]{1,0:T(8,128)(2,1)S(1)}, bf16[64,1792]{1,0:T(8,128)(2,1)S(1)}, u32[]{:S(2)}, u32[]{:S(2)}) collective-permute-start(bf16[64,1792]{1,0:T(8,128)(2,1)S(1)} %collective-permute-done.7.refs_2_), channel_id=1, source_target_pairs={{0,8},{8,0},{16,24},{24,16},{1,9},{9,1},{17,25},{25,17},{2,10},{10... | collective-permute-start | bytes 688136 | tf_op jit(solution)/shard_map/ppermute | solution.py:325
  51.8 16.0 %collective-permute-start.12 = (bf16[2,64,2304]{2,1,0:T(8,128)(2,1)S(1)}, bf16[2,64,2304]{2,1,0:T(8,128)(2,1)S(1)}, u32[]{:S(2)}, u32[]{:S(2)}) collective-permute-start(bf16[2,64,2304]{2,1,0:T(8,128)(2,1)S(1)} %collective-permute-done.9.refs_1_), channel_id=1, source_target_pairs={{0,2},{2,4},{4,6},{6,7},{7,5},{5,3},{3,1},{1,0},{8,10},{10,12},{12... | collective-permute-start | bytes 1769480 | tf_op jit(solution)/shard_map/ppermute | solution.py:379
  53.9 13.9 %collective-permute-start.11 = (bf16[2,64,2304]{2,1,0:T(8,128)(2,1)S(1)}, bf16[2,64,2304]{2,1,0:T(8,128)(2,1)S(1)}, u32[]{:S(2)}, u32[]{:S(2)}) collective-permute-start(bf16[2,64,2304]{2,1,0:T(8,128)(2,1)S(1)} %collective-permute-done.6.refs_0_), channel_id=1, source_target_pairs={{2,0},{4,2},{6,4},{7,6},{5,7},{3,5},{1,3},{0,1},{10,8},{12,10},{14... | collective-permute-start | bytes 1769480 | tf_op jit(solution)/shard_map/ppermute | solution.py:378
  74.5 3.8 %collective-permute-start.13 = (f32[3,8,128]{2,1,0:T(8,128)S(1)}, f32[3,8,128]{2,1,0:T(8,128)S(1)}, u32[]{:S(2)}, u32[]{:S(2)}) collective-permute-start(f32[3,8,128]{2,1,0:T(8,128)S(1)} %chunk.3.refs_0_), channel_id=1, source_target_pairs={{0,1},{1,0},{2,3},{3,2},{4,5},{5,4},{6,7},{7,6},{8,9},{9,8},{10,11... | collective-permute-start | bytes 36872 | tf_op jit(solution)/shard_map/ppermute | solution.py:325
  78.3 5.6 %collective-permute-start.16 = (f32[3,8,128]{2,1,0:T(8,128)S(1)}, f32[3,8,128]{2,1,0:T(8,128)S(1)}, u32[]{:S(2)}, u32[]{:S(2)}) collective-permute-start(f32[3,8,128]{2,1,0:T(8,128)S(1)} %combine.2.refs_0_), channel_id=1, source_target_pairs={{0,6},{1,7},{2,4},{3,5},{4,2},{5,3},{6,0},{7,1},{8,14},{9,15},{10,... | collective-permute-start | bytes 36872 | tf_op jit(solution)/shard_map/ppermute | solution.py:325
  80.7 4.7 %collective-permute-start.15 = (f32[3,8,128]{2,1,0:T(8,128)S(1)}, f32[3,8,128]{2,1,0:T(8,128)S(1)}, u32[]{:S(2)}, u32[]{:S(2)}) collective-permute-start(f32[3,8,128]{2,1,0:T(8,128)S(1)} %combine.2.refs_0_), channel_id=1, source_target_pairs={{0,4},{1,5},{2,6},{3,7},{4,0},{5,1},{6,2},{7,3},{8,12},{9,13},{10,... | collective-permute-start | bytes 36872 | tf_op jit(solution)/shard_map/ppermute | solution.py:325
  81.3 4.1 %collective-permute-start.14 = (f32[3,8,128]{2,1,0:T(8,128)S(1)}, f32[3,8,128]{2,1,0:T(8,128)S(1)}, u32[]{:S(2)}, u32[]{:S(2)}) collective-permute-start(f32[3,8,128]{2,1,0:T(8,128)S(1)} %combine.2.refs_0_), channel_id=1, source_target_pairs={{0,2},{1,3},{2,0},{3,1},{4,6},{5,7},{6,4},{7,5},{8,10},{9,11},{10,... | collective-permute-start | bytes 36872 | tf_op jit(solution)/shard_map/ppermute | solution.py:325

commit v16 on v15

--- a/solution.py
+++ b/solution.py
@@ -146,72 +146,109 @@
     )
 
 
-def make_chunk(hop, r, depth, entries, rank, n_voc):
+def clear(top, total, pick):
+    top[...] = jnp.full(top.shape, -1e30, jnp.float32)
+    total[...] = jnp.zeros(total.shape, jnp.float32)
+    pick[...] = jnp.zeros(pick.shape, jnp.float32)
+
+
+def project(v_ref, source, into):
+    into[...] = jnp.dot(v_ref[...], source[...], preferred_element_type=jnp.float32).astype(
+        jnp.bfloat16
+    )
+
+
+def wanted(want_ref, hop, n_voc):
+    left, right = sources_of(hop, n_voc)
+    return jnp.concatenate([want_ref[left], want_ref[right]], axis=1)
+
+
+def reduce(x, want, top, total, pick):
+    size, n = x.shape
+    entry = lax.broadcasted_iota(jnp.int32, (size, n), 0)
+    hit = jnp.where(entry == want, x, 0.0)
+    x3 = x.reshape(size // 8, 8, n)
+    new = jnp.maximum(top[...], jnp.max(x3, axis=0))
+    total[...] = total[...] * jnp.exp(top[...] - new) + jnp.sum(jnp.exp(x3 - new[None]), axis=0)
+    pick[...] = pick[...] + jnp.sum(hit.reshape(size // 8, 8, n), axis=0)
+    top[...] = new
+
+
+def results(top, total, pick):
+    best = jnp.max(top[...], axis=0, keepdims=True)
+    sums = jnp.sum(total[...] * jnp.exp(top[...] - best), axis=0, keepdims=True)
+    return best, sums, jnp.sum(pick[...], axis=0, keepdims=True)
+
+
+def state_scratch(rank, n):
+    return [pltpu.VMEM((rank, n), jnp.bfloat16)] + [pltpu.VMEM((8, n), jnp.float32)] * 3
+
+
+def make_ends(r, depth, entries, rank, n_voc):
+    tile = tile_rows(entries)
+    n = 4 * r
+
+    def kernel(base_a, rows_a, base_b, rows_b, u_ref, v_ref, want_ref, out_a, out_b, *scratch):
+        bases = [
+            (base_a, wanted(want_ref, 1, n_voc), scratch[:4]),
+            (base_b, wanted(want_ref, 2, n_voc), scratch[4:]),
+        ]
+        for rows, (_, _, (proj, *state)) in zip((rows_a, rows_b), bases):
+            project(v_ref, rows, proj)
+            clear(*state)
+
+        @pl.loop(0, entries // tile)
+        def _(i):
+            span = pl.ds(pl.multiple_of(i * tile, tile), tile)
+            for base, want, (proj, *state) in bases:
+                x = base[span, :] + jnp.dot(
+                    u_ref[span, :], proj[...], preferred_element_type=jnp.float32
+                )
+                reduce(x, want - i * tile, *state)
+
+        for out, (_, _, (proj, *state)) in zip((out_a, out_b), bases):
+            for q, value in enumerate(results(*state)):
+                out[q : q + 1, :] = value
+
+    return pl.pallas_call(
+        kernel,
+        out_shape=(jax.ShapeDtypeStruct((3, n), jnp.float32),) * 2,
+        in_specs=[WHOLE] * 7,
+        out_specs=(WHOLE,) * 2,
+        scratch_shapes=state_scratch(rank, n) * 2,
+        compiler_params=pltpu.CompilerParams(vmem_limit_bytes=8 * MIB),
+        cost_estimate=pl.CostEstimate(
+            flops=4 * n * entries * 256,
+            bytes_accessed=8 * entries * n,
+            transcendentals=2 * n * entries,
+        ),
+        name="ends",
+    )
+
+
+def make_chunk(hop, pieces, r, depth, entries, rank, n_voc):
     tile = tile_rows(entries)
     sizes = [tile] * (entries // tile - 1) + [tile // 2] * 2
     n = 4 * r
-    carry, last = 2 * (hop == 3), hop == n_voc // 2
+    last = hop == n_voc // 2
     earlier = hop - 1 if last else 0
 
     def kernel(*refs):
-        piece, refs = refs[:2], refs[2:]
+        piece, refs = refs[:pieces], refs[pieces:]
         head_ref, u_ref, v_ref, want_ref, *refs = refs
-        bases, refs = refs[: 2 * carry], refs[2 * carry :]
         before, refs = refs[:earlier], refs[earlier:]
-        (out_ref, *base_outs), refs = refs[: 1 + carry], refs[1 + carry :]
-        rows, even, odd, *refs = refs
-        (proj, *state), *base_scratch = [refs[4 * k : 4 * k + 4] for k in range(1 + carry)]
-
-        def project(source, into):
-            into[...] = jnp.dot(
-                v_ref[...], source[...], preferred_element_type=jnp.float32
-            ).astype(jnp.bfloat16)
-
-        def clear(top, total, pick):
-            top[...] = jnp.full(top.shape, -1e30, jnp.float32)
-            total[...] = jnp.zeros(total.shape, jnp.float32)
-            pick[...] = jnp.zeros(pick.shape, jnp.float32)
-
-        def wanted(k):
-            left, right = sources_of(k, n_voc)
-            return jnp.concatenate([want_ref[left], want_ref[right]], axis=1)
+        out_ref, rows, even, odd, proj, *state = refs
 
         load_rows(rows, piece)
-        project(rows, proj)
+        project(v_ref, rows, proj)
         clear(*state)
-        want = wanted(hop)
-        base_wants = []
-        for k in range(carry):
-            project(bases[2 * k + 1], base_scratch[k][0])
-            clear(*base_scratch[k][1:])
-            base_wants.append(wanted(k + 1))
+        want = wanted(want_ref, hop, n_voc)
 
         def multiply(start, size, into):
             span = slice(start, start + size)
             into[:size, :] = jnp.dot(
                 head_ref[span, :], rows[...], preferred_element_type=jnp.float32
             ) + jnp.dot(u_ref[span, :], proj[...], preferred_element_type=jnp.float32)
-
-        def reduce(x, want, top, total, pick):
-            size = x.shape[0]
-            entry = lax.broadcasted_iota(jnp.int32, (size, n), 0)
-            hit = jnp.where(entry == want, x, 0.0)
-            x3 = x.reshape(size // 8, 8, n)
-            new = jnp.maximum(top[...], jnp.max(x3, axis=0))
-            total[...] = total[...] * jnp.exp(top[...] - new) + jnp.sum(
-                jnp.exp(x3 - new[None]), axis=0
-            )
-            pick[...] = pick[...] + jnp.sum(hit.reshape(size // 8, 8, n), axis=0)
-            top[...] = new
-
-        def finish_bases(start, size):
-            span = slice(start, start + size)
-            for k in range(carry):
-                base_proj, *base_state = base_scratch[k]
-                x = bases[2 * k][span, :] + jnp.dot(
-                    u_ref[span, :], base_proj[...], preferred_element_type=jnp.float32
-                )
-                reduce(x, base_wants[k] - start, *base_state)
 
         start = 0
         for i, size in enumerate(sizes):
@@ -219,18 +256,9 @@
             if i:
                 ahead = sizes[i - 1]
                 reduce((even, odd)[(i - 1) % 2][:ahead, :], want - (start - ahead), *state)
-            finish_bases(start, size)
             start += size
         reduce((even, odd)[(len(sizes) - 1) % 2][:size, :], want - (start - size), *state)
 
-        def results(top, total, pick):
-            best = jnp.max(top[...], axis=0, keepdims=True)
-            sums = jnp.sum(total[...] * jnp.exp(top[...] - best), axis=0, keepdims=True)
-            return best, sums, jnp.sum(pick[...], axis=0, keepdims=True)
-
-        for k in range(carry):
-            for q, value in enumerate(results(*base_scratch[k][1:])):
-                base_outs[k][q : q + 1, :] = value
         for q, value in enumerate(results(*state)):
             if not last:
                 out_ref[q : q + 1, :] = value
@@ -242,19 +270,17 @@
                 out_ref[q, pl.ds(left, 1), :] = lanes[:, : 2 * r]
                 out_ref[q, pl.ds(right, 1), :] = lanes[:, 2 * r :]
 
-    out_shape = jax.ShapeDtypeStruct((3, n_voc, 2 * r) if last else (3, n), jnp.float32)
-    small = [pltpu.VMEM((rank, n), jnp.bfloat16)] + [pltpu.VMEM((8, n), jnp.float32)] * 3
     return pl.pallas_call(
         kernel,
-        out_shape=(out_shape,) * (1 + carry) if carry else out_shape,
-        in_specs=[WHOLE] * (6 + 2 * carry + earlier),
-        out_specs=(WHOLE,) * (1 + carry) if carry else WHOLE,
+        out_shape=jax.ShapeDtypeStruct((3, n_voc, 2 * r) if last else (3, n), jnp.float32),
+        in_specs=[WHOLE] * (pieces + 4 + earlier),
+        out_specs=WHOLE,
         scratch_shapes=[
             pltpu.VMEM((depth, n), jnp.bfloat16),
             pltpu.VMEM((tile, n), jnp.float32),
             pltpu.VMEM((tile, n), jnp.float32),
         ]
-        + small * (1 + carry),
+        + state_scratch(rank, n),
         compiler_params=pltpu.CompilerParams(vmem_limit_bytes=8 * MIB),
         cost_estimate=pl.CostEstimate(
             flops=2 * n * entries * (depth + 256),
@@ -342,6 +368,7 @@
     up = [hidden, lax.ppermute(hidden, "vocab", behind)]
     down = [hidden, lax.ppermute(hidden, "vocab", ahead)]
     up.append(lax.ppermute(up[1], "vocab", behind))
+    down.append(lax.ppermute(down[1], "vocab", ahead))
     base, base_rows, head = make_base(r, depth, entries, True)(up[1], hidden, head)
     base, block, *shards = lax.optimization_barrier((base, block, *shards))
     held = [base, base_rows]
@@ -351,34 +378,40 @@
     near = [1 << k for k in reversed(range(n_group.bit_length() - 1))]
     for bit in near:
         packs[bit] = trade(pack, "group", n_group, bit)
-    down[1], held[0] = lax.optimization_barrier((down[1], held[0]))
+    down[2], held[0] = lax.optimization_barrier((down[2], held[0]))
     up[2], held[0] = lax.optimization_barrier((up[2], held[0]))
     held += make_base(r, depth, entries, False)(up[2], down[1], head)
     held[2], *crossed = lax.optimization_barrier((held[2], *[packs[bit] for bit in near]))
     packs.update(zip(near, crossed))
 
     up.append(lax.ppermute(up[2], "vocab", behind))
-    down.append(lax.ppermute(down[1], "vocab", ahead))
+    down.append(lax.ppermute(down[2], "vocab", ahead))
     for k in range(n_group):
         if k not in packs:
             packs[k] = trade(packs[k & (k - 1)], "group", n_group, k & -k)
     full_u, full_v, want = make_assemble(
         n_group, n_voc, u_rows, v_rows, rank, r, entries
     )(sampled, *[packs[k] for k in range(n_group)])
-    down[2], full_u = lax.optimization_barrier((down[2], full_u))
-    up[3], held[2], full_u = lax.optimization_barrier((up[3], held[2], full_u))
-
-    stats = []
-    for hop in range(3, half + 1):
-        extra = held if hop == 3 else stats if hop == half else []
-        chunk = make_chunk(hop, r, depth, entries, rank, n_voc)
-        out = chunk(up[hop], down[hop - 1], head, full_u, full_v, want, *extra)
-        stats += [out[1], out[2], out[0]] if hop == 3 else [out]
-        if hop < half:
-            up.append(lax.ppermute(up[-1], "vocab", behind))
-            down.append(lax.ppermute(down[-1], "vocab", ahead))
+    stats = list(make_ends(r, depth, entries, rank, n_voc)(*held, full_u, full_v, want))
+    down[3], stats[0] = lax.optimization_barrier((down[3], stats[0]))
+    up[3], stats[0] = lax.optimization_barrier((up[3], stats[0]))
+
+    for hop in range(3, half):
+        if hop + 1 < half:
+            up.append(lax.ppermute(up[hop], "vocab", behind))
+            down.append(lax.ppermute(down[hop], "vocab", ahead))
+        else:
+            opposite = [
+                lax.ppermute(up[hop][0], "vocab", behind),
+                lax.ppermute(down[hop][1], "vocab", ahead),
+            ]
+        chunk = make_chunk(hop, 2, r, depth, entries, rank, n_voc)
+        stats.append(chunk(up[hop], down[hop - 1], head, full_u, full_v, want))
+        if hop + 1 < half:
             down[-1], stats[-1] = lax.optimization_barrier((down[-1], stats[-1]))
             up[-1], stats[-1] = lax.optimization_barrier((up[-1], stats[-1]))
+    chunk = make_chunk(half, 3, r, depth, entries, rank, n_voc)
+    stats.append(chunk(*opposite, down[half - 1], head, full_u, full_v, want, *stats))
     part = stats[-1]
     low = 1
     while low < n_voc:

time: 86.4 us -> 85.6 us (level)
  waiting for transfers between devices: 23.4 us -> 20.2 us
  Pallas kernels: 34.2 us -> 35.6 us
  starting transfers between devices: 26.8 us -> 27.7 us
    ppermute x1, waiting for transfers between devices: 0.01 us -> 9.11 us  [body(): down = [hidden, lax.ppermute(hidden, 'vocab', ahead)]]
    ppermute x2 -> x3, starting transfers between devices: 0.74 us -> 6.35 us  [the longest x1 4.03 us: body(): down.append(lax.ppermute(down[2], 'vocab', ahead))]
    ppermute x1, waiting for transfers between devices: 5.25 us -> 0.01 us  [body(): down.append(lax.ppermute(down[1], 'vocab', ahead))]
    ppermute x1, waiting for transfers between devices: 4.82 us -> 0.01 us  [body(): up = [hidden, lax.ppermute(hidden, 'vocab', behind)]]
    ppermute x2 -> x3, waiting for transfers between devices: 3.26 us -> 0.01 us  [the longest x1 0.01 us: body(): down.append(lax.ppermute(down[2], 'vocab', ahead))]
    ppermute x7, starting transfers between devices: 7.81 us -> 11 us  [trade(): return lax.ppermute(x, axis, [(i, i ^ bit) for i in range(size)])]
    ppermute x1, starting transfers between devices: 2.99 us -> 0.01 us  [body(): up = [hidden, lax.ppermute(hidden, 'vocab', behind)]]
    ppermute x1, starting transfers between devices: 2.18 us -> 0.01 us  [body(): up.append(lax.ppermute(up[1], 'vocab', behind))]
  transfers between devices with their start and end apart: 17 -> 18, of which waited for: 9 -> 7; matrix products, arithmetic and copies ran while one was open for 0% -> 0% of each run, Pallas kernels for 31% -> 32%
where the time goes in v16:
time: 85.6 us; the launch traced here: 85.3 us
  Pallas kernels  35.6 us (42%)
  starting transfers between devices  27.7 us (32%)
  waiting for transfers between devices  20.2 us (24%)
  local copies, waits for them, and re-layouts  1.11 us (1%)
    ppermute x7, starting transfers between devices, trade(): return lax.ppermute(x, axis, [(i, i ^ bit) for i in range(size)])  11 us
    pallas_call x1, Pallas kernels, body(): make_base(r, depth, entries, True)(up[1], hidden, head)  10.1 us
    ppermute x1, waiting for transfers between devices, body(): down = [hidden, lax.ppermute(hidden, 'vocab', ahead)]  9.11 us
    ppermute x7, waiting for transfers between devices, trade(): return lax.ppermute(x, axis, [(i, i ^ bit) for i in range(size)])  7.83 us
    pallas_call x1, Pallas kernels, body(): chunk(*opposite, down[half - 1], head, full_u, full_v, want, *stats)  7.24 us
    pallas_call x1, Pallas kernels, body(): stats.append(chunk(up[hop], down[hop - 1], head, full_u, full_v, want))  6.73 us
    pallas_call x1, Pallas kernels, body(): held += make_base(r, depth, entries, False)(up[2], down[1], head)  5.9 us
    pallas_call x1, Pallas kernels, body(): make_ends(r, depth, entries, rank, n_voc)(*held, full_u, full_v, want)  4.06 us
  transfers between devices with their start and end apart: 18, of which 7 were waited for; matrix products, arithmetic and copies ran while one was open for 0% of the time, Pallas kernels for 32%

profile of v16, /device:TPU:0, one launch (start us, length us, event | category | flops | bytes accessed | tf_op | source)
XLA Modules:
  0.0 85.3 jit_solution(12559354860289390321)
XLA Ops:
  0.6 3.1 %collective-permute-start.2 = (bf16[2,64,2304]{2,1,0:T(8,128)(2,1)}, bf16[2,64,2304]{2,1,0:T(8,128)(2,1)S(1)}, u32[]{:S(2)}, u32[]{:S(2)}) collective-permute-start(bf16[2,64,2304]{2,1,0:T(8,128)(2,1)} %down_ref.1), channel_id=1, source_target_pairs={{0,2},{2,4},{4,6},{6,7},{7,5},{5,3},{3,1},{1,0},{8,10},{10,12},{12... | collective-permute-start | bytes 1769480 | tf_op jit(solution)/shard_map/ppermute | solution.py:369
  3.7 0.0 collective-permute-start
  3.7 1.4 %collective-permute-start.5 = (bf16[64,288]{1,0:T(8,128)(2,1)}, bf16[64,288]{1,0:T(8,128)(2,1)S(1)}, u32[]{:S(2)}, u32[]{:S(2)}) collective-permute-start(bf16[64,288]{1,0:T(8,128)(2,1)} %bitcast.7), channel_id=1, source_target_pairs={{0,0},{1,1},{12,2},{13,3},{18,4},{19,5},{30,6},{31,7},{2,8},{3,9},... | collective-permute-start | bytes 110600 | tf_op jit(solution)/shard_map/ppermute | solution.py:366
  5.2 1.9 %collective-permute-start.6 = (bf16[64,288]{1,0:T(8,128)(2,1)}, bf16[64,288]{1,0:T(8,128)(2,1)S(1)}, u32[]{:S(2)}, u32[]{:S(2)}) collective-permute-start(bf16[64,288]{1,0:T(8,128)(2,1)} %bitcast.8), channel_id=1, source_target_pairs={{1,0},{0,1},{13,2},{12,3},{19,4},{18,5},{31,6},{30,7},{3,8},{2,9},... | collective-permute-start | bytes 110600 | tf_op jit(solution)/shard_map/ppermute | solution.py:366
  7.1 1.6 %collective-permute-start.4 = (bf16[64,1024]{1,0:T(8,128)(2,1)}, bf16[64,1024]{1,0:T(8,128)(2,1)S(1)}, u32[]{:S(2)}, u32[]{:S(2)}) collective-permute-start(bf16[64,1024]{1,0:T(8,128)(2,1)} %bitcast.6), channel_id=1, source_target_pairs={{0,0},{4,1},{8,2},{12,3},{16,4},{20,5},{24,6},{28,7},{2,8},{6,9},{... | collective-permute-start | bytes 393224 | tf_op jit(solution)/shard_map/ppermute | solution.py:358
  8.6 9.1 %collective-permute-done.2.down_ref = bf16[2,64,2304]{2,1,0:T(8,128)(2,1)S(1)} collective-permute-done((bf16[2,64,2304]{2,1,0:T(8,128)(2,1)}, bf16[2,64,2304]{2,1,0:T(8,128)(2,1)S(1)}, u32[]{:S(2)}, u32[]{:S(2)}) %collective-permute-start.2) | collective-permute-done | bytes 589856 | tf_op jit(solution)/shard_map/ppermute | solution.py:369
  17.8 2.4 %collective-permute-start.3 = (bf16[2,64,2304]{2,1,0:T(8,128)(2,1)S(1)}, bf16[2,64,2304]{2,1,0:T(8,128)(2,1)S(1)}, u32[]{:S(2)}, u32[]{:S(2)}) collective-permute-start(bf16[2,64,2304]{2,1,0:T(8,128)(2,1)S(1)} %collective-permute-done.2.down_ref), channel_id=1, source_target_pairs={{0,2},{2,4},{4,6},{6,7},{7,5},{5,3},{3,1},{1,0},{8,10},{10,12},{12... | collective-permute-start | bytes 1769480 | tf_op jit(solution)/shard_map/ppermute | solution.py:371
  20.1 0.0 collective-permute-done.up_ref
  20.1 0.0 collective-permute-start.1
  20.1 0.0 copy-start
  20.1 1.1 %copy-done = bf16[2,64,2304]{2,1,0:T(8,128)(2,1)S(1)} copy-done((bf16[2,64,2304]{2,1,0:T(8,128)(2,1)S(1)}, bf16[2,64,2304]{2,1,0:T(8,128)(2,1)}, u32[]{:S(2)}) %copy-start) | copy-done | bytes 589848
  21.2 10.1 %base.2 = (f32[4096,256]{1,0:T(8,128)S(1)}, bf16[2304,256]{1,0:T(8,128)(2,1)S(1)}, bf16[4096,2304]{1,0:T(8,128)(2,1)S(1)}) custom-call(bf16[2,64,2304]{2,1,0:T(8,128)(2,1)S(1)} %collective-permute-done.up_ref, bf16[2,64,2304]{2,1,0:T(8,128)(2,1)S(1)} %copy-done, bf16[4096,2304]{1,0:T(8,128)(2,1)} %head_ref.1), custom_call_target="tpu_custom_call" | custom-call | flops 4831838208 | bytes 18874368 | tf_op jit(solution)/shard_map/base/pallas_call | solution.py:372
  31.3 0.0 collective-permute-done.5
  31.3 0.0 collective-permute-done.6
  31.3 0.0 collective-permute-done.4
  31.3 0.1 collective-permute-start.10
  31.4 5.3 %collective-permute-start.9 = (bf16[64,1792]{1,0:T(8,128)(2,1)S(1)}, bf16[64,1792]{1,0:T(8,128)(2,1)S(1)}, u32[]{:S(2)}, u32[]{:S(2)}) collective-permute-start(bf16[64,1792]{1,0:T(8,128)(2,1)S(1)} %fusion.4.refs_0_), channel_id=1, source_target_pairs={{0,16},{8,24},{16,0},{24,8},{1,17},{9,25},{17,1},{25,9},{2,18},{10... | collective-permute-start | bytes 688136 | tf_op jit(solution)/shard_map/ppermute | solution.py:351
  36.7 0.0 collective-permute-done.3.refs_1_
  36.7 2.0 %collective-permute-done.1.up_ref = bf16[2,64,2304]{2,1,0:T(8,128)(2,1)S(1)} collective-permute-done((bf16[2,64,2304]{2,1,0:T(8,128)(2,1)S(1)}, bf16[2,64,2304]{2,1,0:T(8,128)(2,1)S(1)}, u32[]{:S(2)}, u32[]{:S(2)}) %collective-permute-start.1) | collective-permute-done | bytes 589856 | tf_op jit(solution)/shard_map/ppermute | solution.py:370
  38.7 4.0 %collective-permute-start.8 = (bf16[2,64,2304]{2,1,0:T(8,128)(2,1)S(1)}, bf16[2,64,2304]{2,1,0:T(8,128)(2,1)S(1)}, u32[]{:S(2)}, u32[]{:S(2)}) collective-permute-start(bf16[2,64,2304]{2,1,0:T(8,128)(2,1)S(1)} %collective-permute-done.3.refs_1_), channel_id=1, source_target_pairs={{0,2},{2,4},{4,6},{6,7},{7,5},{5,3},{3,1},{1,0},{8,10},{10,12},{12... | collective-permute-start | bytes 1769480 | tf_op jit(solution)/shard_map/ppermute | solution.py:388
  42.8 0.0 collective-permute-start.7
  42.8 0.0 copy-start.1
  42.8 5.9 %base.3 = (f32[4096,256]{1,0:T(8,128)S(1)}, bf16[2304,256]{1,0:T(8,128)(2,1)S(1)}) custom-call(bf16[2,64,2304]{2,1,0:T(8,128)(2,1)S(1)} %collective-permute-done.1.up_ref, bf16[2,64,2304]{2,1,0:T(8,128)(2,1)S(1)} %collective-permute-done.2.down_ref, bf16[4096,2304]{1,0:T(8,128)(2,1)S(1)} %get-tuple-element.34.head_ref.refs_2_.refs_3_), custom_call_target="tpu_custom_call" | custom-call | flops 4831838208 | bytes 18874368 | tf_op jit(solution)/shard_map/base/pallas_call | solution.py:383
  48.7 0.0 collective-permute-done.10.refs_1_
  48.7 0.0 collective-permute-done.9.refs_2_
  48.7 0.1 collective-permute-start.11
  48.8 1.5 %collective-permute-done.11.refs_3_ = bf16[64,1792]{1,0:T(8,128)(2,1)S(1)} collective-permute-done((bf16[64,1792]{1,0:T(8,128)(2,1)S(1)}, bf16[64,1792]{1,0:T(8,128)(2,1)S(1)}, u32[]{:S(2)}, u32[]{:S(2)}) %collective-permute-start.11) | collective-permute-done | bytes 229408 | tf_op jit(solution)/shard_map/ppermute | solution.py:351
  50.2 0.0 copy-done.1
  50.2 0.8 assemble.1
  51.1 4.1 %ends.1 = (f32[3,256]{1,0:T(4,128)S(1)}, f32[3,256]{1,0:T(4,128)S(1)}) custom-call(f32[4096,256]{1,0:T(8,128)S(1)} %get-tuple-element.32.base_a, bf16[2304,256]{1,0:T(8,128)(2,1)S(1)} %get-tuple-element.33.rows_a, f32[4096,256]{1,0:T(8,128)S(1)} %get-tuple-element.39.base_b, bf16[2304,256]{1,0:T(8,128)(2,1)S(1)} %get-tuple-element.40.rows_b, ...), custom_call_target="tpu_custom_call" | custom-call | flops 1073741824 | bytes 8388608 | tf_op jit(solution)/shard_map/ends/pallas_call | solution.py:395
  55.2 0.0 collective-permute-done.8.refs_2_
  55.2 1.2 %collective-permute-done.7.refs_0_ = bf16[2,64,2304]{2,1,0:T(8,128)(2,1)S(1)} collective-permute-done((bf16[2,64,2304]{2,1,0:T(8,128)(2,1)S(1)}, bf16[2,64,2304]{2,1,0:T(8,128)(2,1)S(1)}, u32[]{:S(2)}, u32[]{:S(2)}) %collective-permute-start.7) | collective-permute-done | bytes 589856 | tf_op jit(solution)/shard_map/ppermute | solution.py:387
  56.4 0.3 collective-permute-start.12
  56.7 2.0 %collective-permute-start.13 = (bf16[64,2304]{1,0:T(8,128)(2,1)S(1)}, bf16[64,2304]{1,0:T(8,128)(2,1)S(1)}, u32[]{:S(2)}, u32[]{:S(2)}) collective-permute-start(bf16[64,2304]{1,0:T(8,128)(2,1)S(1)} %slice_bitcast_fusion), channel_id=1, source_target_pairs={{0,2},{2,4},{4,6},{6,7},{7,5},{5,3},{3,1},{1,0},{8,10},{10,12},{12... | collective-permute-start | bytes 884744 | tf_op jit(solution)/shard_map/ppermute | solution.py:406
  58.7 6.7 %chunk.2.refs_9_ = f32[3,256]{1,0:T(4,128)S(1)} custom-call(bf16[2,64,2304]{2,1,0:T(8,128)(2,1)S(1)} %collective-permute-done.7.refs_0_, bf16[2,64,2304]{2,1,0:T(8,128)(2,1)S(1)} %collective-permute-done.3.refs_1_, bf16[4096,2304]{1,0:T(8,128)(2,1)S(1)} %get-tuple-element.34.head_ref.refs_2_.refs_3_, ...), custom_call_target="tpu_custom_call" | custom-call | flops 5368709120 | bytes 19922944 | tf_op jit(solution)/shard_map/chunk/pallas_call | solution.py:409
  65.4 0.0 collective-permute-done.12.refs_0_
  65.5 0.0 collective-permute-done.13.refs_1_
  65.5 7.2 %chunk.3.refs_0_ = f32[3,8,128]{2,1,0:T(8,128)S(1)} custom-call(bf16[64,2304]{1,0:T(8,128)(2,1)S(1)} %collective-permute-done.12.refs_0_, bf16[64,2304]{1,0:T(8,128)(2,1)S(1)} %collective-permute-done.13.refs_1_, bf16[2,64,2304]{2,1,0:T(8,128)(2,1)S(1)} %collective-permute-done.8.refs_2_, bf16[4096,2304]{1,0:T(8,128)(2,1)S(1)} %get-tuple-element.34.head_ref.refs_2_.refs_3_, ...), custom_call_target="tpu_custom_call" | custom-call | flops 5368709120 | bytes 19922944 | tf_op jit(solution)/shard_map/chunk/pallas_call | solution.py:414
  72.7 1.1 %collective-permute-start.14 = (f32[3,8,128]{2,1,0:T(8,128)S(1)}, f32[3,8,128]{2,1,0:T(8,128)S(1)}, u32[]{:S(2)}, u32[]{:S(2)}) collective-permute-start(f32[3,8,128]{2,1,0:T(8,128)S(1)} %chunk.3.refs_0_), channel_id=1, source_target_pairs={{0,1},{1,0},{2,3},{3,2},{4,5},{5,4},{6,7},{7,6},{8,9},{9,8},{10,11... | collective-permute-start | bytes 36872 | tf_op jit(solution)/shard_map/ppermute | solution.py:351
  73.8 2.7 %collective-permute-done.14.refs_1_ = f32[3,8,128]{2,1,0:T(8,128)S(1)} collective-permute-done((f32[3,8,128]{2,1,0:T(8,128)S(1)}, f32[3,8,128]{2,1,0:T(8,128)S(1)}, u32[]{:S(2)}, u32[]{:S(2)}) %collective-permute-start.14) | collective-permute-done | bytes 12320 | tf_op jit(solution)/shard_map/ppermute | solution.py:351
  76.5 1.2 %collective-permute-start.15 = (f32[3,8,128]{2,1,0:T(8,128)S(1)}, f32[3,8,128]{2,1,0:T(8,128)S(1)}, u32[]{:S(2)}, u32[]{:S(2)}) collective-permute-start(f32[3,8,128]{2,1,0:T(8,128)S(1)} %combine.2.refs_0_), channel_id=1, source_target_pairs={{0,2},{1,3},{2,0},{3,1},{4,6},{5,7},{6,4},{7,5},{8,10},{9,11},{10,... | collective-permute-start | bytes 36872 | tf_op jit(solution)/shard_map/ppermute | solution.py:351
  77.7 1.5 %collective-permute-start.16 = (f32[3,8,128]{2,1,0:T(8,128)S(1)}, f32[3,8,128]{2,1,0:T(8,128)S(1)}, u32[]{:S(2)}, u32[]{:S(2)}) collective-permute-start(f32[3,8,128]{2,1,0:T(8,128)S(1)} %combine.2.refs_0_), channel_id=1, source_target_pairs={{0,4},{1,5},{2,6},{3,7},{4,0},{5,1},{6,2},{7,3},{8,12},{9,13},{10,... | collective-permute-start | bytes 36872 | tf_op jit(solution)/shard_map/ppermute | solution.py:351
  79.1 1.8 %collective-permute-start.17 = (f32[3,8,128]{2,1,0:T(8,128)S(1)}, f32[3,8,128]{2,1,0:T(8,128)S(1)}, u32[]{:S(2)}, u32[]{:S(2)}) collective-permute-start(f32[3,8,128]{2,1,0:T(8,128)S(1)} %combine.2.refs_0_), channel_id=1, source_target_pairs={{0,6},{1,7},{2,4},{3,5},{4,2},{5,3},{6,0},{7,1},{8,14},{9,15},{10,... | collective-permute-start | bytes 36872 | tf_op jit(solution)/shard_map/ppermute | solution.py:351
  80.9 0.0 collective-permute-done.15.refs_1_
  80.9 1.3 %collective-permute-done.16.refs_2_ = f32[3,8,128]{2,1,0:T(8,128)S(1)} collective-permute-done((f32[3,8,128]{2,1,0:T(8,128)S(1)}, f32[3,8,128]{2,1,0:T(8,128)S(1)}, u32[]{:S(2)}, u32[]{:S(2)}) %collective-permute-start.16) | collective-permute-done | bytes 12320 | tf_op jit(solution)/shard_map/ppermute | solution.py:351
  82.3 2.3 %collective-permute-done.17.refs_3_ = f32[3,8,128]{2,1,0:T(8,128)S(1)} collective-permute-done((f32[3,8,128]{2,1,0:T(8,128)S(1)}, f32[3,8,128]{2,1,0:T(8,128)S(1)}, u32[]{:S(2)}, u32[]{:S(2)}) %collective-permute-start.17) | collective-permute-done | bytes 12320 | tf_op jit(solution)/shard_map/ppermute | solution.py:351
  84.6 0.7 combine.3
  (4 shorter events, 0.1 us)
Async XLA Ops:
  0.6 17.1 %collective-permute-start.2 = (bf16[2,64,2304]{2,1,0:T(8,128)(2,1)}, bf16[2,64,2304]{2,1,0:T(8,128)(2,1)S(1)}, u32[]{:S(2)}, u32[]{:S(2)}) collective-permute-start(bf16[2,64,2304]{2,1,0:T(8,128)(2,1)} %down_ref.1), channel_id=1, source_target_pairs={{0,2},{2,4},{4,6},{6,7},{7,5},{5,3},{3,1},{1,0},{8,10},{10,12},{12... | collective-permute-start | bytes 1769480 | tf_op jit(solution)/shard_map/ppermute | solution.py:369
  3.7 16.4 %collective-permute-start = (bf16[2,64,2304]{2,1,0:T(8,128)(2,1)}, bf16[2,64,2304]{2,1,0:T(8,128)(2,1)S(1)}, u32[]{:S(2)}, u32[]{:S(2)}) collective-permute-start(bf16[2,64,2304]{2,1,0:T(8,128)(2,1)} %down_ref.1), channel_id=1, source_target_pairs={{2,0},{4,2},{6,4},{7,6},{5,7},{3,5},{1,3},{0,1},{10,8},{12,10},{14... | collective-permute-start | bytes 1769480 | tf_op jit(solution)/shard_map/ppermute | solution.py:368
  3.7 27.6 %collective-permute-start.5 = (bf16[64,288]{1,0:T(8,128)(2,1)}, bf16[64,288]{1,0:T(8,128)(2,1)S(1)}, u32[]{:S(2)}, u32[]{:S(2)}) collective-permute-start(bf16[64,288]{1,0:T(8,128)(2,1)} %bitcast.7), channel_id=1, source_target_pairs={{0,0},{1,1},{12,2},{13,3},{18,4},{19,5},{30,6},{31,7},{2,8},{3,9},... | collective-permute-start | bytes 110600 | tf_op jit(solution)/shard_map/ppermute | solution.py:366
  5.2 26.1 %collective-permute-start.6 = (bf16[64,288]{1,0:T(8,128)(2,1)}, bf16[64,288]{1,0:T(8,128)(2,1)S(1)}, u32[]{:S(2)}, u32[]{:S(2)}) collective-permute-start(bf16[64,288]{1,0:T(8,128)(2,1)} %bitcast.8), channel_id=1, source_target_pairs={{1,0},{0,1},{13,2},{12,3},{19,4},{18,5},{31,6},{30,7},{3,8},{2,9},... | collective-permute-start | bytes 110600 | tf_op jit(solution)/shard_map/ppermute | solution.py:366
  7.1 24.2 %collective-permute-start.4 = (bf16[64,1024]{1,0:T(8,128)(2,1)}, bf16[64,1024]{1,0:T(8,128)(2,1)S(1)}, u32[]{:S(2)}, u32[]{:S(2)}) collective-permute-start(bf16[64,1024]{1,0:T(8,128)(2,1)} %bitcast.6), channel_id=1, source_target_pairs={{0,0},{4,1},{8,2},{12,3},{16,4},{20,5},{24,6},{28,7},{2,8},{6,9},{... | collective-permute-start | bytes 393224 | tf_op jit(solution)/shard_map/ppermute | solution.py:358
  17.8 18.9 %collective-permute-start.3 = (bf16[2,64,2304]{2,1,0:T(8,128)(2,1)S(1)}, bf16[2,64,2304]{2,1,0:T(8,128)(2,1)S(1)}, u32[]{:S(2)}, u32[]{:S(2)}) collective-permute-start(bf16[2,64,2304]{2,1,0:T(8,128)(2,1)S(1)} %collective-permute-done.2.down_ref), channel_id=1, source_target_pairs={{0,2},{2,4},{4,6},{6,7},{7,5},{5,3},{3,1},{1,0},{8,10},{10,12},{12... | collective-permute-start | bytes 1769480 | tf_op jit(solution)/shard_map/ppermute | solution.py:371
  20.1 18.6 %collective-permute-start.1 = (bf16[2,64,2304]{2,1,0:T(8,128)(2,1)S(1)}, bf16[2,64,2304]{2,1,0:T(8,128)(2,1)S(1)}, u32[]{:S(2)}, u32[]{:S(2)}) collective-permute-start(bf16[2,64,2304]{2,1,0:T(8,128)(2,1)S(1)} %collective-permute-done.up_ref), channel_id=1, source_target_pairs={{2,0},{4,2},{6,4},{7,6},{5,7},{3,5},{1,3},{0,1},{10,8},{12,10},{14... | collective-permute-start | bytes 1769480 | tf_op jit(solution)/shard_map/ppermute | solution.py:370
  20.1 1.1 %copy-start = (bf16[2,64,2304]{2,1,0:T(8,128)(2,1)S(1)}, bf16[2,64,2304]{2,1,0:T(8,128)(2,1)}, u32[]{:S(2)}) copy-start(bf16[2,64,2304]{2,1,0:T(8,128)(2,1)} %down_ref.1) | copy-start | bytes 1769476
  31.3 17.3 %collective-permute-start.10 = (bf16[64,1792]{1,0:T(8,128)(2,1)S(1)}, bf16[64,1792]{1,0:T(8,128)(2,1)S(1)}, u32[]{:S(2)}, u32[]{:S(2)}) collective-permute-start(bf16[64,1792]{1,0:T(8,128)(2,1)S(1)} %fusion.4.refs_0_), channel_id=1, source_target_pairs={{0,8},{8,0},{16,24},{24,16},{1,9},{9,1},{17,25},{25,17},{2,10},{10... | collective-permute-start | bytes 688136 | tf_op jit(solution)/shard_map/ppermute | solution.py:351
  31.4 17.3 %collective-permute-start.9 = (bf16[64,1792]{1,0:T(8,128)(2,1)S(1)}, bf16[64,1792]{1,0:T(8,128)(2,1)S(1)}, u32[]{:S(2)}, u32[]{:S(2)}) collective-permute-start(bf16[64,1792]{1,0:T(8,128)(2,1)S(1)} %fusion.4.refs_0_), channel_id=1, source_target_pairs={{0,16},{8,24},{16,0},{24,8},{1,17},{9,25},{17,1},{25,9},{2,18},{10... | collective-permute-start | bytes 688136 | tf_op jit(solution)/shard_map/ppermute | solution.py:351
  38.7 16.4 %collective-permute-start.8 = (bf16[2,64,2304]{2,1,0:T(8,128)(2,1)S(1)}, bf16[2,64,2304]{2,1,0:T(8,128)(2,1)S(1)}, u32[]{:S(2)}, u32[]{:S(2)}) collective-permute-start(bf16[2,64,2304]{2,1,0:T(8,128)(2,1)S(1)} %collective-permute-done.3.refs_1_), channel_id=1, source_target_pairs={{0,2},{2,4},{4,6},{6,7},{7,5},{5,3},{3,1},{1,0},{8,10},{10,12},{12... | collective-permute-start | bytes 1769480 | tf_op jit(solution)/shard_map/ppermute | solution.py:388
  42.8 13.6 %collective-permute-start.7 = (bf16[2,64,2304]{2,1,0:T(8,128)(2,1)S(1)}, bf16[2,64,2304]{2,1,0:T(8,128)(2,1)S(1)}, u32[]{:S(2)}, u32[]{:S(2)}) collective-permute-start(bf16[2,64,2304]{2,1,0:T(8,128)(2,1)S(1)} %collective-permute-done.1.up_ref), channel_id=1, source_target_pairs={{2,0},{4,2},{6,4},{7,6},{5,7},{3,5},{1,3},{0,1},{10,8},{12,10},{14... | collective-permute-start | bytes 1769480 | tf_op jit(solution)/shard_map/ppermute | solution.py:387
  42.8 7.5 %copy-start.1 = (s32[2,512]{1,0:T(2,128)S(1)}, s32[2,512]{1,0:T(2,128)}, u32[]{:S(2)}) copy-start(s32[2,512]{1,0:T(2,128)} %sampled_ref.1) | copy-start | bytes 12292
  48.7 1.6 %collective-permute-start.11 = (bf16[64,1792]{1,0:T(8,128)(2,1)S(1)}, bf16[64,1792]{1,0:T(8,128)(2,1)S(1)}, u32[]{:S(2)}, u32[]{:S(2)}) collective-permute-start(bf16[64,1792]{1,0:T(8,128)(2,1)S(1)} %collective-permute-done.9.refs_2_), channel_id=1, source_target_pairs={{0,8},{8,0},{16,24},{24,16},{1,9},{9,1},{17,25},{25,17},{2,10},{10... | collective-permute-start | bytes 688136 | tf_op jit(solution)/shard_map/ppermute | solution.py:351
  56.4 9.1 %collective-permute-start.12 = (bf16[64,2304]{1,0:T(8,128)(2,1)S(1)}, bf16[64,2304]{1,0:T(8,128)(2,1)S(1)}, u32[]{:S(2)}, u32[]{:S(2)}) collective-permute-start(bf16[64,2304]{1,0:T(8,128)(2,1)S(1)} %slice_bitcast_fusion.1), channel_id=1, source_target_pairs={{2,0},{4,2},{6,4},{7,6},{5,7},{3,5},{1,3},{0,1},{10,8},{12,10},{14... | collective-permute-start | bytes 884744 | tf_op jit(solution)/shard_map/ppermute | solution.py:405
  56.7 8.7 %collective-permute-start.13 = (bf16[64,2304]{1,0:T(8,128)(2,1)S(1)}, bf16[64,2304]{1,0:T(8,128)(2,1)S(1)}, u32[]{:S(2)}, u32[]{:S(2)}) collective-permute-start(bf16[64,2304]{1,0:T(8,128)(2,1)S(1)} %slice_bitcast_fusion), channel_id=1, source_target_pairs={{0,2},{2,4},{4,6},{6,7},{7,5},{5,3},{3,1},{1,0},{8,10},{10,12},{12... | collective-permute-start | bytes 884744 | tf_op jit(solution)/shard_map/ppermute | solution.py:406
  72.7 3.8 %collective-permute-start.14 = (f32[3,8,128]{2,1,0:T(8,128)S(1)}, f32[3,8,128]{2,1,0:T(8,128)S(1)}, u32[]{:S(2)}, u32[]{:S(2)}) collective-permute-start(f32[3,8,128]{2,1,0:T(8,128)S(1)} %chunk.3.refs_0_), channel_id=1, source_target_pairs={{0,1},{1,0},{2,3},{3,2},{4,5},{5,4},{6,7},{7,6},{8,9},{9,8},{10,11... | collective-permute-start | bytes 36872 | tf_op jit(solution)/shard_map/ppermute | solution.py:351
  76.5 4.5 %collective-permute-start.15 = (f32[3,8,128]{2,1,0:T(8,128)S(1)}, f32[3,8,128]{2,1,0:T(8,128)S(1)}, u32[]{:S(2)}, u32[]{:S(2)}) collective-permute-start(f32[3,8,128]{2,1,0:T(8,128)S(1)} %combine.2.refs_0_), channel_id=1, source_target_pairs={{0,2},{1,3},{2,0},{3,1},{4,6},{5,7},{6,4},{7,5},{8,10},{9,11},{10,... | collective-permute-start | bytes 36872 | tf_op jit(solution)/shard_map/ppermute | solution.py:351
  77.7 4.6 %collective-permute-start.16 = (f32[3,8,128]{2,1,0:T(8,128)S(1)}, f32[3,8,128]{2,1,0:T(8,128)S(1)}, u32[]{:S(2)}, u32[]{:S(2)}) collective-permute-start(f32[3,8,128]{2,1,0:T(8,128)S(1)} %combine.2.refs_0_), channel_id=1, source_target_pairs={{0,4},{1,5},{2,6},{3,7},{4,0},{5,1},{6,2},{7,3},{8,12},{9,13},{10,... | collective-permute-start | bytes 36872 | tf_op jit(solution)/shard_map/ppermute | solution.py:351
  79.1 5.5 %collective-permute-start.17 = (f32[3,8,128]{2,1,0:T(8,128)S(1)}, f32[3,8,128]{2,1,0:T(8,128)S(1)}, u32[]{:S(2)}, u32[]{:S(2)}) collective-permute-start(f32[3,8,128]{2,1,0:T(8,128)S(1)} %combine.2.refs_0_), channel_id=1, source_target_pairs={{0,6},{1,7},{2,4},{3,5},{4,2},{5,3},{6,0},{7,1},{8,14},{9,15},{10,... | collective-permute-start | bytes 36872 | tf_op jit(solution)/shard_map/ppermute | solution.py:351

commit v17 on v16

--- a/solution.py
+++ b/solution.py
@@ -86,11 +86,8 @@
 
 
 def load_rows(rows, pieces):
-    at = 0
-    for ref in pieces:
-        block = ref[...].reshape(-1, ref.shape[-1])
-        rows[:, at : at + block.shape[0]] = block.T
-        at += block.shape[0]
+    blocks = [ref[...].reshape(-1, ref.shape[-1]) for ref in pieces]
+    rows[...] = jnp.concatenate(blocks, axis=0).T
 
 
 def make_base(r, depth, entries, load):

time: 85.6 us -> 85 us (level)
  no operation moved by 1% of the time
where the time goes in v17:
time: 85 us; the launch traced here: 84.7 us
  Pallas kernels  34.8 us (41%)
  starting transfers between devices  27.8 us (33%)
  waiting for transfers between devices  20.2 us (24%)
  local copies, waits for them, and re-layouts  1.11 us (1%)
    ppermute x7, starting transfers between devices, trade(): return lax.ppermute(x, axis, [(i, i ^ bit) for i in range(size)])  11.1 us
    pallas_call x1, Pallas kernels, body(): make_base(r, depth, entries, True)(up[1], hidden, head)  10.1 us
    ppermute x1, waiting for transfers between devices, body(): down = [hidden, lax.ppermute(hidden, 'vocab', ahead)]  9.11 us
    ppermute x7, waiting for transfers between devices, trade(): return lax.ppermute(x, axis, [(i, i ^ bit) for i in range(size)])  7.83 us
    pallas_call x1, Pallas kernels, body(): chunk(*opposite, down[half - 1], head, full_u, full_v, want, *stats)  6.6 us
    pallas_call x1, Pallas kernels, body(): stats.append(chunk(up[hop], down[hop - 1], head, full_u, full_v, want))  6.6 us
    pallas_call x1, Pallas kernels, body(): held += make_base(r, depth, entries, False)(up[2], down[1], head)  5.9 us
    pallas_call x1, Pallas kernels, body(): make_ends(r, depth, entries, rank, n_voc)(*held, full_u, full_v, want)  4.06 us
  transfers between devices with their start and end apart: 18, of which 7 were waited for; matrix products, arithmetic and copies ran while one was open for 0% of the time, Pallas kernels for 32%

profile of v17, /device:TPU:0, one launch (start us, length us, event | category | flops | bytes accessed | tf_op | source)
XLA Modules:
  0.0 84.7 jit_solution(5835298602768541668)
XLA Ops:
  0.6 3.1 %collective-permute-start.2 = (bf16[2,64,2304]{2,1,0:T(8,128)(2,1)}, bf16[2,64,2304]{2,1,0:T(8,128)(2,1)S(1)}, u32[]{:S(2)}, u32[]{:S(2)}) collective-permute-start(bf16[2,64,2304]{2,1,0:T(8,128)(2,1)} %down_ref.1), channel_id=1, source_target_pairs={{0,2},{2,4},{4,6},{6,7},{7,5},{5,3},{3,1},{1,0},{8,10},{10,12},{12... | collective-permute-start | bytes 1769480 | tf_op jit(solution)/shard_map/ppermute | solution.py:366
  3.7 0.0 collective-permute-start
  3.7 1.4 %collective-permute-start.5 = (bf16[64,288]{1,0:T(8,128)(2,1)}, bf16[64,288]{1,0:T(8,128)(2,1)S(1)}, u32[]{:S(2)}, u32[]{:S(2)}) collective-permute-start(bf16[64,288]{1,0:T(8,128)(2,1)} %bitcast.7), channel_id=1, source_target_pairs={{0,0},{1,1},{12,2},{13,3},{18,4},{19,5},{30,6},{31,7},{2,8},{3,9},... | collective-permute-start | bytes 110600 | tf_op jit(solution)/shard_map/ppermute | solution.py:363
  5.2 1.9 %collective-permute-start.6 = (bf16[64,288]{1,0:T(8,128)(2,1)}, bf16[64,288]{1,0:T(8,128)(2,1)S(1)}, u32[]{:S(2)}, u32[]{:S(2)}) collective-permute-start(bf16[64,288]{1,0:T(8,128)(2,1)} %bitcast.8), channel_id=1, source_target_pairs={{1,0},{0,1},{13,2},{12,3},{19,4},{18,5},{31,6},{30,7},{3,8},{2,9},... | collective-permute-start | bytes 110600 | tf_op jit(solution)/shard_map/ppermute | solution.py:363
  7.1 1.6 %collective-permute-start.4 = (bf16[64,1024]{1,0:T(8,128)(2,1)}, bf16[64,1024]{1,0:T(8,128)(2,1)S(1)}, u32[]{:S(2)}, u32[]{:S(2)}) collective-permute-start(bf16[64,1024]{1,0:T(8,128)(2,1)} %bitcast.6), channel_id=1, source_target_pairs={{0,0},{4,1},{8,2},{12,3},{16,4},{20,5},{24,6},{28,7},{2,8},{6,9},{... | collective-permute-start | bytes 393224 | tf_op jit(solution)/shard_map/ppermute | solution.py:355
  8.6 9.1 %collective-permute-done.2.down_ref = bf16[2,64,2304]{2,1,0:T(8,128)(2,1)S(1)} collective-permute-done((bf16[2,64,2304]{2,1,0:T(8,128)(2,1)}, bf16[2,64,2304]{2,1,0:T(8,128)(2,1)S(1)}, u32[]{:S(2)}, u32[]{:S(2)}) %collective-permute-start.2) | collective-permute-done | bytes 589856 | tf_op jit(solution)/shard_map/ppermute | solution.py:366
  17.8 2.4 %collective-permute-start.3 = (bf16[2,64,2304]{2,1,0:T(8,128)(2,1)S(1)}, bf16[2,64,2304]{2,1,0:T(8,128)(2,1)S(1)}, u32[]{:S(2)}, u32[]{:S(2)}) collective-permute-start(bf16[2,64,2304]{2,1,0:T(8,128)(2,1)S(1)} %collective-permute-done.2.down_ref), channel_id=1, source_target_pairs={{0,2},{2,4},{4,6},{6,7},{7,5},{5,3},{3,1},{1,0},{8,10},{10,12},{12... | collective-permute-start | bytes 1769480 | tf_op jit(solution)/shard_map/ppermute | solution.py:368
  20.1 0.0 collective-permute-done.up_ref
  20.1 0.0 collective-permute-start.1
  20.1 0.0 copy-start
  20.1 1.1 %copy-done = bf16[2,64,2304]{2,1,0:T(8,128)(2,1)S(1)} copy-done((bf16[2,64,2304]{2,1,0:T(8,128)(2,1)S(1)}, bf16[2,64,2304]{2,1,0:T(8,128)(2,1)}, u32[]{:S(2)}) %copy-start) | copy-done | bytes 589848
  21.2 10.1 %base.2 = (f32[4096,256]{1,0:T(8,128)S(1)}, bf16[2304,256]{1,0:T(8,128)(2,1)S(1)}, bf16[4096,2304]{1,0:T(8,128)(2,1)S(1)}) custom-call(bf16[2,64,2304]{2,1,0:T(8,128)(2,1)S(1)} %collective-permute-done.up_ref, bf16[2,64,2304]{2,1,0:T(8,128)(2,1)S(1)} %copy-done, bf16[4096,2304]{1,0:T(8,128)(2,1)} %head_ref.1), custom_call_target="tpu_custom_call" | custom-call | flops 4831838208 | bytes 18874368 | tf_op jit(solution)/shard_map/base/pallas_call | solution.py:369
  31.3 0.0 collective-permute-done.5
  31.3 0.0 collective-permute-done.6
  31.3 0.0 collective-permute-done.4
  31.3 0.1 collective-permute-start.10
  31.4 5.3 %collective-permute-start.9 = (bf16[64,1792]{1,0:T(8,128)(2,1)S(1)}, bf16[64,1792]{1,0:T(8,128)(2,1)S(1)}, u32[]{:S(2)}, u32[]{:S(2)}) collective-permute-start(bf16[64,1792]{1,0:T(8,128)(2,1)S(1)} %fusion.4.refs_0_), channel_id=1, source_target_pairs={{0,16},{8,24},{16,0},{24,8},{1,17},{9,25},{17,1},{25,9},{2,18},{10... | collective-permute-start | bytes 688136 | tf_op jit(solution)/shard_map/ppermute | solution.py:348
  36.7 0.0 collective-permute-done.3.refs_1_
  36.7 2.0 %collective-permute-done.1.up_ref = bf16[2,64,2304]{2,1,0:T(8,128)(2,1)S(1)} collective-permute-done((bf16[2,64,2304]{2,1,0:T(8,128)(2,1)S(1)}, bf16[2,64,2304]{2,1,0:T(8,128)(2,1)S(1)}, u32[]{:S(2)}, u32[]{:S(2)}) %collective-permute-start.1) | collective-permute-done | bytes 589856 | tf_op jit(solution)/shard_map/ppermute | solution.py:367
  38.7 4.0 %collective-permute-start.8 = (bf16[2,64,2304]{2,1,0:T(8,128)(2,1)S(1)}, bf16[2,64,2304]{2,1,0:T(8,128)(2,1)S(1)}, u32[]{:S(2)}, u32[]{:S(2)}) collective-permute-start(bf16[2,64,2304]{2,1,0:T(8,128)(2,1)S(1)} %collective-permute-done.3.refs_1_), channel_id=1, source_target_pairs={{0,2},{2,4},{4,6},{6,7},{7,5},{5,3},{3,1},{1,0},{8,10},{10,12},{12... | collective-permute-start | bytes 1769480 | tf_op jit(solution)/shard_map/ppermute | solution.py:385
  42.8 0.0 collective-permute-start.7
  42.8 0.0 copy-start.1
  42.8 5.9 %base.3 = (f32[4096,256]{1,0:T(8,128)S(1)}, bf16[2304,256]{1,0:T(8,128)(2,1)S(1)}) custom-call(bf16[2,64,2304]{2,1,0:T(8,128)(2,1)S(1)} %collective-permute-done.1.up_ref, bf16[2,64,2304]{2,1,0:T(8,128)(2,1)S(1)} %collective-permute-done.2.down_ref, bf16[4096,2304]{1,0:T(8,128)(2,1)S(1)} %get-tuple-element.34.head_ref.refs_2_.refs_3_), custom_call_target="tpu_custom_call" | custom-call | flops 4831838208 | bytes 18874368 | tf_op jit(solution)/shard_map/base/pallas_call | solution.py:380
  48.7 0.0 collective-permute-done.10.refs_1_
  48.7 0.0 collective-permute-done.9.refs_2_
  48.7 0.1 collective-permute-start.11
  48.8 1.5 %collective-permute-done.11.refs_3_ = bf16[64,1792]{1,0:T(8,128)(2,1)S(1)} collective-permute-done((bf16[64,1792]{1,0:T(8,128)(2,1)S(1)}, bf16[64,1792]{1,0:T(8,128)(2,1)S(1)}, u32[]{:S(2)}, u32[]{:S(2)}) %collective-permute-start.11) | collective-permute-done | bytes 229408 | tf_op jit(solution)/shard_map/ppermute | solution.py:348
  50.2 0.0 copy-done.1
  50.2 0.8 assemble.1
  51.1 4.1 %ends.1 = (f32[3,256]{1,0:T(4,128)S(1)}, f32[3,256]{1,0:T(4,128)S(1)}) custom-call(f32[4096,256]{1,0:T(8,128)S(1)} %get-tuple-element.32.base_a, bf16[2304,256]{1,0:T(8,128)(2,1)S(1)} %get-tuple-element.33.rows_a, f32[4096,256]{1,0:T(8,128)S(1)} %get-tuple-element.39.base_b, bf16[2304,256]{1,0:T(8,128)(2,1)S(1)} %get-tuple-element.40.rows_b, ...), custom_call_target="tpu_custom_call" | custom-call | flops 1073741824 | bytes 8388608 | tf_op jit(solution)/shard_map/ends/pallas_call | solution.py:392
  55.2 0.0 collective-permute-done.8.refs_2_
  55.2 1.2 %collective-permute-done.7.refs_0_ = bf16[2,64,2304]{2,1,0:T(8,128)(2,1)S(1)} collective-permute-done((bf16[2,64,2304]{2,1,0:T(8,128)(2,1)S(1)}, bf16[2,64,2304]{2,1,0:T(8,128)(2,1)S(1)}, u32[]{:S(2)}, u32[]{:S(2)}) %collective-permute-start.7) | collective-permute-done | bytes 589856 | tf_op jit(solution)/shard_map/ppermute | solution.py:384
  56.4 0.3 collective-permute-start.12
  56.7 2.0 %collective-permute-start.13 = (bf16[64,2304]{1,0:T(8,128)(2,1)S(1)}, bf16[64,2304]{1,0:T(8,128)(2,1)S(1)}, u32[]{:S(2)}, u32[]{:S(2)}) collective-permute-start(bf16[64,2304]{1,0:T(8,128)(2,1)S(1)} %slice_bitcast_fusion), channel_id=1, source_target_pairs={{0,2},{2,4},{4,6},{6,7},{7,5},{5,3},{3,1},{1,0},{8,10},{10,12},{12... | collective-permute-start | bytes 884744 | tf_op jit(solution)/shard_map/ppermute | solution.py:403
  58.7 6.6 %chunk.2.refs_9_ = f32[3,256]{1,0:T(4,128)S(1)} custom-call(bf16[2,64,2304]{2,1,0:T(8,128)(2,1)S(1)} %collective-permute-done.7.refs_0_, bf16[2,64,2304]{2,1,0:T(8,128)(2,1)S(1)} %collective-permute-done.3.refs_1_, bf16[4096,2304]{1,0:T(8,128)(2,1)S(1)} %get-tuple-element.34.head_ref.refs_2_.refs_3_, ...), custom_call_target="tpu_custom_call" | custom-call | flops 5368709120 | bytes 19922944 | tf_op jit(solution)/shard_map/chunk/pallas_call | solution.py:406
  65.3 0.0 collective-permute-done.12.refs_0_
  65.3 0.0 collective-permute-done.13.refs_1_
  65.3 6.6 %chunk.3.refs_0_ = f32[3,8,128]{2,1,0:T(8,128)S(1)} custom-call(bf16[64,2304]{1,0:T(8,128)(2,1)S(1)} %collective-permute-done.12.refs_0_, bf16[64,2304]{1,0:T(8,128)(2,1)S(1)} %collective-permute-done.13.refs_1_, bf16[2,64,2304]{2,1,0:T(8,128)(2,1)S(1)} %collective-permute-done.8.refs_2_, bf16[4096,2304]{1,0:T(8,128)(2,1)S(1)} %get-tuple-element.34.head_ref.refs_2_.refs_3_, ...), custom_call_target="tpu_custom_call" | custom-call | flops 5368709120 | bytes 19922944 | tf_op jit(solution)/shard_map/chunk/pallas_call | solution.py:411
  71.9 1.2 %collective-permute-start.14 = (f32[3,8,128]{2,1,0:T(8,128)S(1)}, f32[3,8,128]{2,1,0:T(8,128)S(1)}, u32[]{:S(2)}, u32[]{:S(2)}) collective-permute-start(f32[3,8,128]{2,1,0:T(8,128)S(1)} %chunk.3.refs_0_), channel_id=1, source_target_pairs={{0,1},{1,0},{2,3},{3,2},{4,5},{5,4},{6,7},{7,6},{8,9},{9,8},{10,11... | collective-permute-start | bytes 36872 | tf_op jit(solution)/shard_map/ppermute | solution.py:348
  73.2 2.5 %collective-permute-done.14.refs_1_ = f32[3,8,128]{2,1,0:T(8,128)S(1)} collective-permute-done((f32[3,8,128]{2,1,0:T(8,128)S(1)}, f32[3,8,128]{2,1,0:T(8,128)S(1)}, u32[]{:S(2)}, u32[]{:S(2)}) %collective-permute-start.14) | collective-permute-done | bytes 12320 | tf_op jit(solution)/shard_map/ppermute | solution.py:348
  75.7 1.3 %collective-permute-start.15 = (f32[3,8,128]{2,1,0:T(8,128)S(1)}, f32[3,8,128]{2,1,0:T(8,128)S(1)}, u32[]{:S(2)}, u32[]{:S(2)}) collective-permute-start(f32[3,8,128]{2,1,0:T(8,128)S(1)} %combine.2.refs_0_), channel_id=1, source_target_pairs={{0,2},{1,3},{2,0},{3,1},{4,6},{5,7},{6,4},{7,5},{8,10},{9,11},{10,... | collective-permute-start | bytes 36872 | tf_op jit(solution)/shard_map/ppermute | solution.py:348
  77.1 1.4 %collective-permute-start.16 = (f32[3,8,128]{2,1,0:T(8,128)S(1)}, f32[3,8,128]{2,1,0:T(8,128)S(1)}, u32[]{:S(2)}, u32[]{:S(2)}) collective-permute-start(f32[3,8,128]{2,1,0:T(8,128)S(1)} %combine.2.refs_0_), channel_id=1, source_target_pairs={{0,4},{1,5},{2,6},{3,7},{4,0},{5,1},{6,2},{7,3},{8,12},{9,13},{10,... | collective-permute-start | bytes 36872 | tf_op jit(solution)/shard_map/ppermute | solution.py:348
  78.5 1.7 %collective-permute-start.17 = (f32[3,8,128]{2,1,0:T(8,128)S(1)}, f32[3,8,128]{2,1,0:T(8,128)S(1)}, u32[]{:S(2)}, u32[]{:S(2)}) collective-permute-start(f32[3,8,128]{2,1,0:T(8,128)S(1)} %combine.2.refs_0_), channel_id=1, source_target_pairs={{0,6},{1,7},{2,4},{3,5},{4,2},{5,3},{6,0},{7,1},{8,14},{9,15},{10,... | collective-permute-start | bytes 36872 | tf_op jit(solution)/shard_map/ppermute | solution.py:348
  80.2 0.0 collective-permute-done.15.refs_1_
  80.2 1.5 %collective-permute-done.16.refs_2_ = f32[3,8,128]{2,1,0:T(8,128)S(1)} collective-permute-done((f32[3,8,128]{2,1,0:T(8,128)S(1)}, f32[3,8,128]{2,1,0:T(8,128)S(1)}, u32[]{:S(2)}, u32[]{:S(2)}) %collective-permute-start.16) | collective-permute-done | bytes 12320 | tf_op jit(solution)/shard_map/ppermute | solution.py:348
  81.6 2.3 %collective-permute-done.17.refs_3_ = f32[3,8,128]{2,1,0:T(8,128)S(1)} collective-permute-done((f32[3,8,128]{2,1,0:T(8,128)S(1)}, f32[3,8,128]{2,1,0:T(8,128)S(1)}, u32[]{:S(2)}, u32[]{:S(2)}) %collective-permute-start.17) | collective-permute-done | bytes 12320 | tf_op jit(solution)/shard_map/ppermute | solution.py:348
  84.0 0.7 combine.3
  (4 shorter events, 0.1 us)
Async XLA Ops:
  0.6 17.1 %collective-permute-start.2 = (bf16[2,64,2304]{2,1,0:T(8,128)(2,1)}, bf16[2,64,2304]{2,1,0:T(8,128)(2,1)S(1)}, u32[]{:S(2)}, u32[]{:S(2)}) collective-permute-start(bf16[2,64,2304]{2,1,0:T(8,128)(2,1)} %down_ref.1), channel_id=1, source_target_pairs={{0,2},{2,4},{4,6},{6,7},{7,5},{5,3},{3,1},{1,0},{8,10},{10,12},{12... | collective-permute-start | bytes 1769480 | tf_op jit(solution)/shard_map/ppermute | solution.py:366
  3.7 16.4 %collective-permute-start = (bf16[2,64,2304]{2,1,0:T(8,128)(2,1)}, bf16[2,64,2304]{2,1,0:T(8,128)(2,1)S(1)}, u32[]{:S(2)}, u32[]{:S(2)}) collective-permute-start(bf16[2,64,2304]{2,1,0:T(8,128)(2,1)} %down_ref.1), channel_id=1, source_target_pairs={{2,0},{4,2},{6,4},{7,6},{5,7},{3,5},{1,3},{0,1},{10,8},{12,10},{14... | collective-permute-start | bytes 1769480 | tf_op jit(solution)/shard_map/ppermute | solution.py:365
  3.7 27.6 %collective-permute-start.5 = (bf16[64,288]{1,0:T(8,128)(2,1)}, bf16[64,288]{1,0:T(8,128)(2,1)S(1)}, u32[]{:S(2)}, u32[]{:S(2)}) collective-permute-start(bf16[64,288]{1,0:T(8,128)(2,1)} %bitcast.7), channel_id=1, source_target_pairs={{0,0},{1,1},{12,2},{13,3},{18,4},{19,5},{30,6},{31,7},{2,8},{3,9},... | collective-permute-start | bytes 110600 | tf_op jit(solution)/shard_map/ppermute | solution.py:363
  5.2 26.1 %collective-permute-start.6 = (bf16[64,288]{1,0:T(8,128)(2,1)}, bf16[64,288]{1,0:T(8,128)(2,1)S(1)}, u32[]{:S(2)}, u32[]{:S(2)}) collective-permute-start(bf16[64,288]{1,0:T(8,128)(2,1)} %bitcast.8), channel_id=1, source_target_pairs={{1,0},{0,1},{13,2},{12,3},{19,4},{18,5},{31,6},{30,7},{3,8},{2,9},... | collective-permute-start | bytes 110600 | tf_op jit(solution)/shard_map/ppermute | solution.py:363
  7.1 24.2 %collective-permute-start.4 = (bf16[64,1024]{1,0:T(8,128)(2,1)}, bf16[64,1024]{1,0:T(8,128)(2,1)S(1)}, u32[]{:S(2)}, u32[]{:S(2)}) collective-permute-start(bf16[64,1024]{1,0:T(8,128)(2,1)} %bitcast.6), channel_id=1, source_target_pairs={{0,0},{4,1},{8,2},{12,3},{16,4},{20,5},{24,6},{28,7},{2,8},{6,9},{... | collective-permute-start | bytes 393224 | tf_op jit(solution)/shard_map/ppermute | solution.py:355
  17.8 18.9 %collective-permute-start.3 = (bf16[2,64,2304]{2,1,0:T(8,128)(2,1)S(1)}, bf16[2,64,2304]{2,1,0:T(8,128)(2,1)S(1)}, u32[]{:S(2)}, u32[]{:S(2)}) collective-permute-start(bf16[2,64,2304]{2,1,0:T(8,128)(2,1)S(1)} %collective-permute-done.2.down_ref), channel_id=1, source_target_pairs={{0,2},{2,4},{4,6},{6,7},{7,5},{5,3},{3,1},{1,0},{8,10},{10,12},{12... | collective-permute-start | bytes 1769480 | tf_op jit(solution)/shard_map/ppermute | solution.py:368
  20.1 18.6 %collective-permute-start.1 = (bf16[2,64,2304]{2,1,0:T(8,128)(2,1)S(1)}, bf16[2,64,2304]{2,1,0:T(8,128)(2,1)S(1)}, u32[]{:S(2)}, u32[]{:S(2)}) collective-permute-start(bf16[2,64,2304]{2,1,0:T(8,128)(2,1)S(1)} %collective-permute-done.up_ref), channel_id=1, source_target_pairs={{2,0},{4,2},{6,4},{7,6},{5,7},{3,5},{1,3},{0,1},{10,8},{12,10},{14... | collective-permute-start | bytes 1769480 | tf_op jit(solution)/shard_map/ppermute | solution.py:367
  20.1 1.1 %copy-start = (bf16[2,64,2304]{2,1,0:T(8,128)(2,1)S(1)}, bf16[2,64,2304]{2,1,0:T(8,128)(2,1)}, u32[]{:S(2)}) copy-start(bf16[2,64,2304]{2,1,0:T(8,128)(2,1)} %down_ref.1) | copy-start | bytes 1769476
  31.3 17.3 %collective-permute-start.10 = (bf16[64,1792]{1,0:T(8,128)(2,1)S(1)}, bf16[64,1792]{1,0:T(8,128)(2,1)S(1)}, u32[]{:S(2)}, u32[]{:S(2)}) collective-permute-start(bf16[64,1792]{1,0:T(8,128)(2,1)S(1)} %fusion.4.refs_0_), channel_id=1, source_target_pairs={{0,8},{8,0},{16,24},{24,16},{1,9},{9,1},{17,25},{25,17},{2,10},{10... | collective-permute-start | bytes 688136 | tf_op jit(solution)/shard_map/ppermute | solution.py:348
  31.4 17.3 %collective-permute-start.9 = (bf16[64,1792]{1,0:T(8,128)(2,1)S(1)}, bf16[64,1792]{1,0:T(8,128)(2,1)S(1)}, u32[]{:S(2)}, u32[]{:S(2)}) collective-permute-start(bf16[64,1792]{1,0:T(8,128)(2,1)S(1)} %fusion.4.refs_0_), channel_id=1, source_target_pairs={{0,16},{8,24},{16,0},{24,8},{1,17},{9,25},{17,1},{25,9},{2,18},{10... | collective-permute-start | bytes 688136 | tf_op jit(solution)/shard_map/ppermute | solution.py:348
  38.7 16.4 %collective-permute-start.8 = (bf16[2,64,2304]{2,1,0:T(8,128)(2,1)S(1)}, bf16[2,64,2304]{2,1,0:T(8,128)(2,1)S(1)}, u32[]{:S(2)}, u32[]{:S(2)}) collective-permute-start(bf16[2,64,2304]{2,1,0:T(8,128)(2,1)S(1)} %collective-permute-done.3.refs_1_), channel_id=1, source_target_pairs={{0,2},{2,4},{4,6},{6,7},{7,5},{5,3},{3,1},{1,0},{8,10},{10,12},{12... | collective-permute-start | bytes 1769480 | tf_op jit(solution)/shard_map/ppermute | solution.py:385
  42.8 13.6 %collective-permute-start.7 = (bf16[2,64,2304]{2,1,0:T(8,128)(2,1)S(1)}, bf16[2,64,2304]{2,1,0:T(8,128)(2,1)S(1)}, u32[]{:S(2)}, u32[]{:S(2)}) collective-permute-start(bf16[2,64,2304]{2,1,0:T(8,128)(2,1)S(1)} %collective-permute-done.1.up_ref), channel_id=1, source_target_pairs={{2,0},{4,2},{6,4},{7,6},{5,7},{3,5},{1,3},{0,1},{10,8},{12,10},{14... | collective-permute-start | bytes 1769480 | tf_op jit(solution)/shard_map/ppermute | solution.py:384
  42.8 7.5 %copy-start.1 = (s32[2,512]{1,0:T(2,128)S(1)}, s32[2,512]{1,0:T(2,128)}, u32[]{:S(2)}) copy-start(s32[2,512]{1,0:T(2,128)} %sampled_ref.1) | copy-start | bytes 12292
  48.7 1.6 %collective-permute-start.11 = (bf16[64,1792]{1,0:T(8,128)(2,1)S(1)}, bf16[64,1792]{1,0:T(8,128)(2,1)S(1)}, u32[]{:S(2)}, u32[]{:S(2)}) collective-permute-start(bf16[64,1792]{1,0:T(8,128)(2,1)S(1)} %collective-permute-done.9.refs_2_), channel_id=1, source_target_pairs={{0,8},{8,0},{16,24},{24,16},{1,9},{9,1},{17,25},{25,17},{2,10},{10... | collective-permute-start | bytes 688136 | tf_op jit(solution)/shard_map/ppermute | solution.py:348
  56.4 8.9 %collective-permute-start.12 = (bf16[64,2304]{1,0:T(8,128)(2,1)S(1)}, bf16[64,2304]{1,0:T(8,128)(2,1)S(1)}, u32[]{:S(2)}, u32[]{:S(2)}) collective-permute-start(bf16[64,2304]{1,0:T(8,128)(2,1)S(1)} %slice_bitcast_fusion.1), channel_id=1, source_target_pairs={{2,0},{4,2},{6,4},{7,6},{5,7},{3,5},{1,3},{0,1},{10,8},{12,10},{14... | collective-permute-start | bytes 884744 | tf_op jit(solution)/shard_map/ppermute | solution.py:402
  56.7 8.6 %collective-permute-start.13 = (bf16[64,2304]{1,0:T(8,128)(2,1)S(1)}, bf16[64,2304]{1,0:T(8,128)(2,1)S(1)}, u32[]{:S(2)}, u32[]{:S(2)}) collective-permute-start(bf16[64,2304]{1,0:T(8,128)(2,1)S(1)} %slice_bitcast_fusion), channel_id=1, source_target_pairs={{0,2},{2,4},{4,6},{6,7},{7,5},{5,3},{3,1},{1,0},{8,10},{10,12},{12... | collective-permute-start | bytes 884744 | tf_op jit(solution)/shard_map/ppermute | solution.py:403
  71.9 3.8 %collective-permute-start.14 = (f32[3,8,128]{2,1,0:T(8,128)S(1)}, f32[3,8,128]{2,1,0:T(8,128)S(1)}, u32[]{:S(2)}, u32[]{:S(2)}) collective-permute-start(f32[3,8,128]{2,1,0:T(8,128)S(1)} %chunk.3.refs_0_), channel_id=1, source_target_pairs={{0,1},{1,0},{2,3},{3,2},{4,5},{5,4},{6,7},{7,6},{8,9},{9,8},{10,11... | collective-permute-start | bytes 36872 | tf_op jit(solution)/shard_map/ppermute | solution.py:348
  75.7 4.5 %collective-permute-start.15 = (f32[3,8,128]{2,1,0:T(8,128)S(1)}, f32[3,8,128]{2,1,0:T(8,128)S(1)}, u32[]{:S(2)}, u32[]{:S(2)}) collective-permute-start(f32[3,8,128]{2,1,0:T(8,128)S(1)} %combine.2.refs_0_), channel_id=1, source_target_pairs={{0,2},{1,3},{2,0},{3,1},{4,6},{5,7},{6,4},{7,5},{8,10},{9,11},{10,... | collective-permute-start | bytes 36872 | tf_op jit(solution)/shard_map/ppermute | solution.py:348
  77.1 4.6 %collective-permute-start.16 = (f32[3,8,128]{2,1,0:T(8,128)S(1)}, f32[3,8,128]{2,1,0:T(8,128)S(1)}, u32[]{:S(2)}, u32[]{:S(2)}) collective-permute-start(f32[3,8,128]{2,1,0:T(8,128)S(1)} %combine.2.refs_0_), channel_id=1, source_target_pairs={{0,4},{1,5},{2,6},{3,7},{4,0},{5,1},{6,2},{7,3},{8,12},{9,13},{10,... | collective-permute-start | bytes 36872 | tf_op jit(solution)/shard_map/ppermute | solution.py:348
  78.5 5.5 %collective-permute-start.17 = (f32[3,8,128]{2,1,0:T(8,128)S(1)}, f32[3,8,128]{2,1,0:T(8,128)S(1)}, u32[]{:S(2)}, u32[]{:S(2)}) collective-permute-start(f32[3,8,128]{2,1,0:T(8,128)S(1)} %combine.2.refs_0_), channel_id=1, source_target_pairs={{0,6},{1,7},{2,4},{3,5},{4,2},{5,3},{6,0},{7,1},{8,14},{9,15},{10,... | collective-permute-start | bytes 36872 | tf_op jit(solution)/shard_map/ppermute | solution.py:348

commit v18 on v17

--- a/solution.py
+++ b/solution.py
@@ -81,7 +81,11 @@
 
 
 def sources_of(hop, n_voc):
-    position = ring_position(lax.axis_index("vocab"), n_voc)
+    voc = lax.axis_index("vocab")
+    if n_voc == 8:
+        steps = {1: (0, -2, 0, 0), 2: (2, 0, 0, 1), 3: (-2, 4, 1, 0), 4: (4, 2, 1, 1)}[hop]
+        return tuple(lax.rem(voc + steps[k] + n_voc, n_voc) ^ steps[2 + k] for k in range(2))
+    position = ring_position(voc, n_voc)
     return ring_device(position + hop, n_voc), ring_device(position - hop + 1, n_voc)
 
 
@@ -362,11 +366,25 @@
             moves.append((z * n_voc + plane * per + (v % per ^ t), g * n_voc + v))
         shards.append(lax.ppermute(factor_v.T, ("group", "vocab"), moves))
 
-    up = [hidden, lax.ppermute(hidden, "vocab", behind)]
-    down = [hidden, lax.ppermute(hidden, "vocab", ahead)]
-    up.append(lax.ppermute(up[1], "vocab", behind))
-    down.append(lax.ppermute(down[1], "vocab", ahead))
-    base, base_rows, head = make_base(r, depth, entries, True)(up[1], hidden, head)
+    square = n_voc == 8
+    if square:
+        def before(x):
+            return lax.ppermute(x, "vocab", [(v, (v + 2) % n_voc) for v in range(n_voc)])
+
+        def after(x):
+            return lax.ppermute(x, "vocab", [(v, (v - 2) % n_voc) for v in range(n_voc)])
+
+        a, b, c = before(hidden), after(hidden), trade(hidden, "vocab", n_voc, 1)
+        a, b, c = lax.optimization_barrier((a, b, c))
+        a2, b2, c2 = before(c), after(b), trade(b, "vocab", n_voc, 1)
+        first, second = (hidden, a), (b, c)
+    else:
+        up = [hidden, lax.ppermute(hidden, "vocab", behind)]
+        down = [hidden, lax.ppermute(hidden, "vocab", ahead)]
+        up.append(lax.ppermute(up[1], "vocab", behind))
+        down.append(lax.ppermute(down[1], "vocab", ahead))
+        first, second = (up[1], hidden), (up[2], down[1])
+    base, base_rows, head = make_base(r, depth, entries, True)(*first, head)
     base, block, *shards = lax.optimization_barrier((base, block, *shards))
     held = [base, base_rows]
     gap = ((0, 0), (0, padded(v_rows) - v_rows))
@@ -375,14 +393,21 @@
     near = [1 << k for k in reversed(range(n_group.bit_length() - 1))]
     for bit in near:
         packs[bit] = trade(pack, "group", n_group, bit)
-    down[2], held[0] = lax.optimization_barrier((down[2], held[0]))
-    up[2], held[0] = lax.optimization_barrier((up[2], held[0]))
-    held += make_base(r, depth, entries, False)(up[2], down[1], head)
+    if square:
+        b, c, a2, b2, c2, held[0] = lax.optimization_barrier((b, c, a2, b2, c2, held[0]))
+        second = b, c
+        opposite = [after(c2[0]), before(a2[1])]
+    else:
+        down[2], held[0] = lax.optimization_barrier((down[2], held[0]))
+        up[2], held[0] = lax.optimization_barrier((up[2], held[0]))
+        second = (up[2], down[1])
+    held += make_base(r, depth, entries, False)(*second, head)
     held[2], *crossed = lax.optimization_barrier((held[2], *[packs[bit] for bit in near]))
     packs.update(zip(near, crossed))
 
-    up.append(lax.ppermute(up[2], "vocab", behind))
-    down.append(lax.ppermute(down[2], "vocab", ahead))
+    if not square:
+        up.append(lax.ppermute(up[2], "vocab", behind))
+        down.append(lax.ppermute(down[2], "vocab", ahead))
     for k in range(n_group):
         if k not in packs:
             packs[k] = trade(packs[k & (k - 1)], "group", n_group, k & -k)
@@ -390,25 +415,30 @@
         n_group, n_voc, u_rows, v_rows, rank, r, entries
     )(sampled, *[packs[k] for k in range(n_group)])
     stats = list(make_ends(r, depth, entries, rank, n_voc)(*held, full_u, full_v, want))
-    down[3], stats[0] = lax.optimization_barrier((down[3], stats[0]))
-    up[3], stats[0] = lax.optimization_barrier((up[3], stats[0]))
-
-    for hop in range(3, half):
-        if hop + 1 < half:
-            up.append(lax.ppermute(up[hop], "vocab", behind))
-            down.append(lax.ppermute(down[hop], "vocab", ahead))
-        else:
-            opposite = [
-                lax.ppermute(up[hop][0], "vocab", behind),
-                lax.ppermute(down[hop][1], "vocab", ahead),
-            ]
-        chunk = make_chunk(hop, 2, r, depth, entries, rank, n_voc)
-        stats.append(chunk(up[hop], down[hop - 1], head, full_u, full_v, want))
-        if hop + 1 < half:
-            down[-1], stats[-1] = lax.optimization_barrier((down[-1], stats[-1]))
-            up[-1], stats[-1] = lax.optimization_barrier((up[-1], stats[-1]))
+    if square:
+        chunk = make_chunk(3, 2, r, depth, entries, rank, n_voc)
+        stats.append(chunk(a2, b2, head, full_u, full_v, want))
+        final = c2
+    else:
+        down[3], stats[0] = lax.optimization_barrier((down[3], stats[0]))
+        up[3], stats[0] = lax.optimization_barrier((up[3], stats[0]))
+        for hop in range(3, half):
+            if hop + 1 < half:
+                up.append(lax.ppermute(up[hop], "vocab", behind))
+                down.append(lax.ppermute(down[hop], "vocab", ahead))
+            else:
+                opposite = [
+                    lax.ppermute(up[hop][0], "vocab", behind),
+                    lax.ppermute(down[hop][1], "vocab", ahead),
+                ]
+            chunk = make_chunk(hop, 2, r, depth, entries, rank, n_voc)
+            stats.append(chunk(up[hop], down[hop - 1], head, full_u, full_v, want))
+            if hop + 1 < half:
+                down[-1], stats[-1] = lax.optimization_barrier((down[-1], stats[-1]))
+                up[-1], stats[-1] = lax.optimization_barrier((up[-1], stats[-1]))
+        final = down[half - 1]
     chunk = make_chunk(half, 3, r, depth, entries, rank, n_voc)
-    stats.append(chunk(*opposite, down[half - 1], head, full_u, full_v, want, *stats))
+    stats.append(chunk(*opposite, final, head, full_u, full_v, want, *stats))
     part = stats[-1]
     low = 1
     while low < n_voc:

time: 85 us -> 109 us (1.28)
  waiting for transfers between devices: 20.2 us -> 39.8 us
  starting transfers between devices: 27.8 us -> 31.8 us
    ppermute x8 -> x6, waiting for transfers between devices: 12.3 us -> 32 us  [the longest x3 21.1 us: after(): lax.ppermute(x, 'vocab', [(v, (v - 2) % n_voc) for v in range(n_voc)])]
    ppermute x7 -> x9, starting transfers between devices: 11.1 us -> 15 us  [trade(): return lax.ppermute(x, axis, [(i, i ^ bit) for i in range(size)])]
    ppermute x8 -> x6, starting transfers between devices: 11.8 us -> 13.4 us  [the longest x3 7.5 us: before(): lax.ppermute(x, 'vocab', [(v, (v + 2) % n_voc) for v in range(n_voc)])]
    ppermute x2, starting transfers between devices: 3.38 us -> 1.82 us  [body(): shards.append(lax.ppermute(factor_v.T, ('group', 'vocab'), moves))]
    ppermute x7 -> x9, waiting for transfers between devices: 7.83 us -> 7.78 us  [trade(): return lax.ppermute(x, axis, [(i, i ^ bit) for i in range(size)])]
  transfers between devices with their start and end apart: 18 -> 18, of which waited for: 7 -> 7; matrix products, arithmetic and copies ran while one was open for 0% -> 0% of each run, Pallas kernels for 32% -> 26%
where the time goes in v18:
time: 109 us; the launch traced here: 108 us
  waiting for transfers between devices  39.8 us (37%)
  Pallas kernels  35 us (32%)
  starting transfers between devices  31.8 us (29%)
  local copies, waits for them, and re-layouts  1.11 us (1%)
    ppermute x3, waiting for transfers between devices, after(): lax.ppermute(x, 'vocab', [(v, (v - 2) % n_voc) for v in range(n_voc)])  21.1 us
    ppermute x9, starting transfers between devices, trade(): return lax.ppermute(x, axis, [(i, i ^ bit) for i in range(size)])  15 us
    ppermute x3, waiting for transfers between devices, before(): lax.ppermute(x, 'vocab', [(v, (v + 2) % n_voc) for v in range(n_voc)])  10.9 us
    pallas_call x1, Pallas kernels, body(): base, base_rows, head = make_base(r, depth, entries, True)(*first, head)  10.1 us
    ppermute x9, waiting for transfers between devices, trade(): return lax.ppermute(x, axis, [(i, i ^ bit) for i in range(size)])  7.78 us
    ppermute x3, starting transfers between devices, before(): lax.ppermute(x, 'vocab', [(v, (v + 2) % n_voc) for v in range(n_voc)])  7.5 us
    pallas_call x1, Pallas kernels, body(): stats.append(chunk(a2, b2, head, full_u, full_v, want))  6.62 us
    pallas_call x1, Pallas kernels, body(): stats.append(chunk(*opposite, final, head, full_u, full_v, want, *stats))  6.62 us
  transfers between devices with their start and end apart: 18, of which 7 were waited for; matrix products, arithmetic and copies ran while one was open for 0% of the time, Pallas kernels for 26%

profile of v18, /device:TPU:0, one launch (start us, length us, event | category | flops | bytes accessed | tf_op | source)
XLA Modules:
  0.0 108.5 jit_solution(15143880598099110609)
XLA Ops:
  0.6 3.1 %collective-permute-start = (bf16[2,64,2304]{2,1,0:T(8,128)(2,1)}, bf16[2,64,2304]{2,1,0:T(8,128)(2,1)S(1)}, u32[]{:S(2)}, u32[]{:S(2)}) collective-permute-start(bf16[2,64,2304]{2,1,0:T(8,128)(2,1)} %up_ref.1), channel_id=1, source_target_pairs={{0,2},{1,3},{2,4},{3,5},{4,6},{5,7},{6,0},{7,1},{8,10},{9,11},{10,... | collective-permute-start | bytes 1769480 | tf_op jit(solution)/shard_map/ppermute | solution.py:372
  3.7 2.1 %collective-permute-start.1 = (bf16[2,64,2304]{2,1,0:T(8,128)(2,1)}, bf16[2,64,2304]{2,1,0:T(8,128)(2,1)S(1)}, u32[]{:S(2)}, u32[]{:S(2)}) collective-permute-start(bf16[2,64,2304]{2,1,0:T(8,128)(2,1)} %up_ref.1), channel_id=1, source_target_pairs={{0,6},{1,7},{2,0},{3,1},{4,2},{5,3},{6,4},{7,5},{8,14},{9,15},{10,... | collective-permute-start | bytes 1769480 | tf_op jit(solution)/shard_map/ppermute | solution.py:375
  5.8 1.6 %collective-permute-start.2 = (bf16[2,64,2304]{2,1,0:T(8,128)(2,1)}, bf16[2,64,2304]{2,1,0:T(8,128)(2,1)S(1)}, u32[]{:S(2)}, u32[]{:S(2)}) collective-permute-start(bf16[2,64,2304]{2,1,0:T(8,128)(2,1)} %up_ref.1), channel_id=1, source_target_pairs={{0,1},{1,0},{2,3},{3,2},{4,5},{5,4},{6,7},{7,6},{8,9},{9,8},{10,11... | collective-permute-start | bytes 1769480 | tf_op jit(solution)/shard_map/ppermute | solution.py:352
  7.4 1.4 %collective-permute-start.7 = (bf16[64,288]{1,0:T(8,128)(2,1)}, bf16[64,288]{1,0:T(8,128)(2,1)S(1)}, u32[]{:S(2)}, u32[]{:S(2)}) collective-permute-start(bf16[64,288]{1,0:T(8,128)(2,1)} %bitcast.7), channel_id=1, source_target_pairs={{0,0},{1,1},{12,2},{13,3},{18,4},{19,5},{30,6},{31,7},{2,8},{3,9},... | collective-permute-start | bytes 110600 | tf_op jit(solution)/shard_map/ppermute | solution.py:367
  8.9 0.4 collective-permute-start.8
  9.3 10.9 %collective-permute-done.down_ref = bf16[2,64,2304]{2,1,0:T(8,128)(2,1)S(1)} collective-permute-done((bf16[2,64,2304]{2,1,0:T(8,128)(2,1)}, bf16[2,64,2304]{2,1,0:T(8,128)(2,1)S(1)}, u32[]{:S(2)}, u32[]{:S(2)}) %collective-permute-start) | collective-permute-done | bytes 589856 | tf_op jit(solution)/shard_map/ppermute | solution.py:372
  20.1 1.6 %collective-permute-start.6 = (bf16[64,1024]{1,0:T(8,128)(2,1)}, bf16[64,1024]{1,0:T(8,128)(2,1)S(1)}, u32[]{:S(2)}, u32[]{:S(2)}) collective-permute-start(bf16[64,1024]{1,0:T(8,128)(2,1)} %bitcast.6), channel_id=1, source_target_pairs={{0,0},{4,1},{8,2},{12,3},{16,4},{20,5},{24,6},{28,7},{2,8},{6,9},{... | collective-permute-start | bytes 393224 | tf_op jit(solution)/shard_map/ppermute | solution.py:359
  21.7 9.7 %collective-permute-done.1.up_ref = bf16[2,64,2304]{2,1,0:T(8,128)(2,1)S(1)} collective-permute-done((bf16[2,64,2304]{2,1,0:T(8,128)(2,1)}, bf16[2,64,2304]{2,1,0:T(8,128)(2,1)S(1)}, u32[]{:S(2)}, u32[]{:S(2)}) %collective-permute-start.1) | collective-permute-done | bytes 589856 | tf_op jit(solution)/shard_map/ppermute | solution.py:375
  31.3 0.0 collective-permute-done.2.down_ref
  31.3 3.3 %collective-permute-start.4 = (bf16[2,64,2304]{2,1,0:T(8,128)(2,1)S(1)}, bf16[2,64,2304]{2,1,0:T(8,128)(2,1)S(1)}, u32[]{:S(2)}, u32[]{:S(2)}) collective-permute-start(bf16[2,64,2304]{2,1,0:T(8,128)(2,1)S(1)} %collective-permute-done.1.up_ref), channel_id=1, source_target_pairs={{0,6},{1,7},{2,0},{3,1},{4,2},{5,3},{6,4},{7,5},{8,14},{9,15},{10,... | collective-permute-start | bytes 1769480 | tf_op jit(solution)/shard_map/ppermute | solution.py:375
  34.7 1.5 %collective-permute-start.5 = (bf16[2,64,2304]{2,1,0:T(8,128)(2,1)S(1)}, bf16[2,64,2304]{2,1,0:T(8,128)(2,1)S(1)}, u32[]{:S(2)}, u32[]{:S(2)}) collective-permute-start(bf16[2,64,2304]{2,1,0:T(8,128)(2,1)S(1)} %collective-permute-done.1.up_ref), channel_id=1, source_target_pairs={{0,1},{1,0},{2,3},{3,2},{4,5},{5,4},{6,7},{7,6},{8,9},{9,8},{10,11... | collective-permute-start | bytes 1769480 | tf_op jit(solution)/shard_map/ppermute | solution.py:352
  36.2 0.0 collective-permute-done.7
  36.2 0.8 collective-permute-start.3
  36.9 0.0 copy-start
  36.9 1.1 copy-done
  38.0 10.1 %base.2 = (f32[4096,256]{1,0:T(8,128)S(1)}, bf16[2304,256]{1,0:T(8,128)(2,1)S(1)}, bf16[4096,2304]{1,0:T(8,128)(2,1)S(1)}) custom-call(bf16[2,64,2304]{2,1,0:T(8,128)(2,1)S(1)} %copy-done, bf16[2,64,2304]{2,1,0:T(8,128)(2,1)S(1)} %collective-permute-done.down_ref, bf16[4096,2304]{1,0:T(8,128)(2,1)} %head_ref.1), custom_call_target="tpu_custom_call" | custom-call | flops 4831838208 | bytes 18874368 | tf_op jit(solution)/shard_map/base/pallas_call | solution.py:387
  48.1 0.0 collective-permute-done.8
  48.1 0.0 collective-permute-done.6
  48.1 6.0 %collective-permute-start.11 = (bf16[64,1792]{1,0:T(8,128)(2,1)S(1)}, bf16[64,1792]{1,0:T(8,128)(2,1)S(1)}, u32[]{:S(2)}, u32[]{:S(2)}) collective-permute-start(bf16[64,1792]{1,0:T(8,128)(2,1)S(1)} %fusion.4.refs_0_), channel_id=1, source_target_pairs={{0,16},{8,24},{16,0},{24,8},{1,17},{9,25},{17,1},{25,9},{2,18},{10... | collective-permute-start | bytes 688136 | tf_op jit(solution)/shard_map/ppermute | solution.py:352
  54.1 0.1 collective-permute-start.12
  54.3 9.7 %collective-permute-done.4.refs_1_ = bf16[2,64,2304]{2,1,0:T(8,128)(2,1)S(1)} collective-permute-done((bf16[2,64,2304]{2,1,0:T(8,128)(2,1)S(1)}, bf16[2,64,2304]{2,1,0:T(8,128)(2,1)S(1)}, u32[]{:S(2)}, u32[]{:S(2)}) %collective-permute-start.4) | collective-permute-done | bytes 589856 | tf_op jit(solution)/shard_map/ppermute | solution.py:375
  64.0 0.0 collective-permute-done.5.refs_2_
  64.0 0.0 collective-permute-done.3.refs_0_
  64.0 0.0 copy-start.1
  64.0 5.9 %base.3 = (f32[4096,256]{1,0:T(8,128)S(1)}, bf16[2304,256]{1,0:T(8,128)(2,1)S(1)}) custom-call(bf16[2,64,2304]{2,1,0:T(8,128)(2,1)S(1)} %collective-permute-done.1.up_ref, bf16[2,64,2304]{2,1,0:T(8,128)(2,1)S(1)} %collective-permute-done.2.down_ref, bf16[4096,2304]{1,0:T(8,128)(2,1)S(1)} %get-tuple-element.35.head_ref.refs_2_.refs_3_), custom_call_target="tpu_custom_call" | custom-call | flops 4831838208 | bytes 18874368 | tf_op jit(solution)/shard_map/base/pallas_call | solution.py:404
  69.9 0.0 collective-permute-done.11.refs_2_
  70.0 0.0 collective-permute-done.12.refs_1_
  70.0 0.1 collective-permute-start.13
  70.1 3.6 %collective-permute-start.10 = (bf16[64,2304]{1,0:T(8,128)(2,1)S(1)}, bf16[64,2304]{1,0:T(8,128)(2,1)S(1)}, u32[]{:S(2)}, u32[]{:S(2)}) collective-permute-start(bf16[64,2304]{1,0:T(8,128)(2,1)S(1)} %slice_bitcast_fusion), channel_id=1, source_target_pairs={{0,2},{1,3},{2,4},{3,5},{4,6},{5,7},{6,0},{7,1},{8,10},{9,11},{10,... | collective-permute-start | bytes 884744 | tf_op jit(solution)/shard_map/ppermute | solution.py:372
  73.7 0.5 collective-permute-start.9
  74.2 0.0 collective-permute-done.13.refs_3_
  74.2 0.0 copy-done.1
  74.2 0.8 assemble.1
  75.1 6.6 %chunk.2.refs_9_ = f32[3,256]{1,0:T(4,128)S(1)} custom-call(bf16[2,64,2304]{2,1,0:T(8,128)(2,1)S(1)} %collective-permute-done.3.refs_0_, bf16[2,64,2304]{2,1,0:T(8,128)(2,1)S(1)} %collective-permute-done.4.refs_1_, bf16[4096,2304]{1,0:T(8,128)(2,1)S(1)} %get-tuple-element.35.head_ref.refs_2_.refs_3_, ...), custom_call_target="tpu_custom_call" | custom-call | flops 5368709120 | bytes 19922944 | tf_op jit(solution)/shard_map/chunk/pallas_call | solution.py:420
  81.7 4.2 %ends.1 = (f32[3,256]{1,0:T(4,128)S(1)}, f32[3,256]{1,0:T(4,128)S(1)}) custom-call(f32[4096,256]{1,0:T(8,128)S(1)} %get-tuple-element.47.base_a, bf16[2304,256]{1,0:T(8,128)(2,1)S(1)} %get-tuple-element.48.rows_a, f32[4096,256]{1,0:T(8,128)S(1)} %get-tuple-element.49.base_b, bf16[2304,256]{1,0:T(8,128)(2,1)S(1)} %get-tuple-element.50.rows_b, ...), custom_call_target="tpu_custom_call" | custom-call | flops 1073741824 | bytes 8388608 | tf_op jit(solution)/shard_map/ends/pallas_call | solution.py:417
  85.9 0.0 collective-permute-done.10.refs_1_
  85.9 1.7 %collective-permute-done.9.refs_0_ = bf16[64,2304]{1,0:T(8,128)(2,1)S(1)} collective-permute-done((bf16[64,2304]{1,0:T(8,128)(2,1)S(1)}, bf16[64,2304]{1,0:T(8,128)(2,1)S(1)}, u32[]{:S(2)}, u32[]{:S(2)}) %collective-permute-start.9) | collective-permute-done | bytes 294944 | tf_op jit(solution)/shard_map/ppermute | solution.py:375
  87.7 6.6 %chunk.3.refs_0_ = f32[3,8,128]{2,1,0:T(8,128)S(1)} custom-call(bf16[64,2304]{1,0:T(8,128)(2,1)S(1)} %collective-permute-done.9.refs_0_, bf16[64,2304]{1,0:T(8,128)(2,1)S(1)} %collective-permute-done.10.refs_1_, bf16[2,64,2304]{2,1,0:T(8,128)(2,1)S(1)} %collective-permute-done.5.refs_2_, bf16[4096,2304]{1,0:T(8,128)(2,1)S(1)} %get-tuple-element.35.head_ref.refs_2_.refs_3_, ...), custom_call_target="tpu_custom_call" | custom-call | flops 5368709120 | bytes 19922944 | tf_op jit(solution)/shard_map/chunk/pallas_call | solution.py:441
  94.3 1.2 %collective-permute-start.14 = (f32[3,8,128]{2,1,0:T(8,128)S(1)}, f32[3,8,128]{2,1,0:T(8,128)S(1)}, u32[]{:S(2)}, u32[]{:S(2)}) collective-permute-start(f32[3,8,128]{2,1,0:T(8,128)S(1)} %chunk.3.refs_0_), channel_id=1, source_target_pairs={{0,1},{1,0},{2,3},{3,2},{4,5},{5,4},{6,7},{7,6},{8,9},{9,8},{10,11... | collective-permute-start | bytes 36872 | tf_op jit(solution)/shard_map/ppermute | solution.py:352
  95.5 2.5 %collective-permute-done.14.refs_1_ = f32[3,8,128]{2,1,0:T(8,128)S(1)} collective-permute-done((f32[3,8,128]{2,1,0:T(8,128)S(1)}, f32[3,8,128]{2,1,0:T(8,128)S(1)}, u32[]{:S(2)}, u32[]{:S(2)}) %collective-permute-start.14) | collective-permute-done | bytes 12320 | tf_op jit(solution)/shard_map/ppermute | solution.py:352
  98.1 0.6 collective-permute-start.15
  98.7 3.6 %collective-permute-start.16 = (f32[3,8,128]{2,1,0:T(8,128)S(1)}, f32[3,8,128]{2,1,0:T(8,128)S(1)}, u32[]{:S(2)}, u32[]{:S(2)}) collective-permute-start(f32[3,8,128]{2,1,0:T(8,128)S(1)} %combine.2.refs_0_), channel_id=1, source_target_pairs={{0,4},{1,5},{2,6},{3,7},{4,0},{5,1},{6,2},{7,3},{8,12},{9,13},{10,... | collective-permute-start | bytes 36872 | tf_op jit(solution)/shard_map/ppermute | solution.py:352
  102.3 0.3 collective-permute-start.17
  102.5 0.0 collective-permute-done.15.refs_1_
  102.5 1.4 %collective-permute-done.16.refs_2_ = f32[3,8,128]{2,1,0:T(8,128)S(1)} collective-permute-done((f32[3,8,128]{2,1,0:T(8,128)S(1)}, f32[3,8,128]{2,1,0:T(8,128)S(1)}, u32[]{:S(2)}, u32[]{:S(2)}) %collective-permute-start.16) | collective-permute-done | bytes 12320 | tf_op jit(solution)/shard_map/ppermute | solution.py:352
  103.9 3.8 %collective-permute-done.17.refs_3_ = f32[3,8,128]{2,1,0:T(8,128)S(1)} collective-permute-done((f32[3,8,128]{2,1,0:T(8,128)S(1)}, f32[3,8,128]{2,1,0:T(8,128)S(1)}, u32[]{:S(2)}, u32[]{:S(2)}) %collective-permute-start.17) | collective-permute-done | bytes 12320 | tf_op jit(solution)/shard_map/ppermute | solution.py:352
  107.8 0.7 combine.3
  (4 shorter events, 0.1 us)
Async XLA Ops:
  0.6 19.5 %collective-permute-start = (bf16[2,64,2304]{2,1,0:T(8,128)(2,1)}, bf16[2,64,2304]{2,1,0:T(8,128)(2,1)S(1)}, u32[]{:S(2)}, u32[]{:S(2)}) collective-permute-start(bf16[2,64,2304]{2,1,0:T(8,128)(2,1)} %up_ref.1), channel_id=1, source_target_pairs={{0,2},{1,3},{2,4},{3,5},{4,6},{5,7},{6,0},{7,1},{8,10},{9,11},{10,... | collective-permute-start | bytes 1769480 | tf_op jit(solution)/shard_map/ppermute | solution.py:372
  3.7 27.6 %collective-permute-start.1 = (bf16[2,64,2304]{2,1,0:T(8,128)(2,1)}, bf16[2,64,2304]{2,1,0:T(8,128)(2,1)S(1)}, u32[]{:S(2)}, u32[]{:S(2)}) collective-permute-start(bf16[2,64,2304]{2,1,0:T(8,128)(2,1)} %up_ref.1), channel_id=1, source_target_pairs={{0,6},{1,7},{2,0},{3,1},{4,2},{5,3},{6,4},{7,5},{8,14},{9,15},{10,... | collective-permute-start | bytes 1769480 | tf_op jit(solution)/shard_map/ppermute | solution.py:375
  5.8 25.6 %collective-permute-start.2 = (bf16[2,64,2304]{2,1,0:T(8,128)(2,1)}, bf16[2,64,2304]{2,1,0:T(8,128)(2,1)S(1)}, u32[]{:S(2)}, u32[]{:S(2)}) collective-permute-start(bf16[2,64,2304]{2,1,0:T(8,128)(2,1)} %up_ref.1), channel_id=1, source_target_pairs={{0,1},{1,0},{2,3},{3,2},{4,5},{5,4},{6,7},{7,6},{8,9},{9,8},{10,11... | collective-permute-start | bytes 1769480 | tf_op jit(solution)/shard_map/ppermute | solution.py:352
  7.4 28.7 %collective-permute-start.7 = (bf16[64,288]{1,0:T(8,128)(2,1)}, bf16[64,288]{1,0:T(8,128)(2,1)S(1)}, u32[]{:S(2)}, u32[]{:S(2)}) collective-permute-start(bf16[64,288]{1,0:T(8,128)(2,1)} %bitcast.7), channel_id=1, source_target_pairs={{0,0},{1,1},{12,2},{13,3},{18,4},{19,5},{30,6},{31,7},{2,8},{3,9},... | collective-permute-start | bytes 110600 | tf_op jit(solution)/shard_map/ppermute | solution.py:367
  8.9 39.2 %collective-permute-start.8 = (bf16[64,288]{1,0:T(8,128)(2,1)}, bf16[64,288]{1,0:T(8,128)(2,1)S(1)}, u32[]{:S(2)}, u32[]{:S(2)}) collective-permute-start(bf16[64,288]{1,0:T(8,128)(2,1)} %bitcast.8), channel_id=1, source_target_pairs={{1,0},{0,1},{13,2},{12,3},{19,4},{18,5},{31,6},{30,7},{3,8},{2,9},... | collective-permute-start | bytes 110600 | tf_op jit(solution)/shard_map/ppermute | solution.py:367
  20.1 27.9 %collective-permute-start.6 = (bf16[64,1024]{1,0:T(8,128)(2,1)}, bf16[64,1024]{1,0:T(8,128)(2,1)S(1)}, u32[]{:S(2)}, u32[]{:S(2)}) collective-permute-start(bf16[64,1024]{1,0:T(8,128)(2,1)} %bitcast.6), channel_id=1, source_target_pairs={{0,0},{4,1},{8,2},{12,3},{16,4},{20,5},{24,6},{28,7},{2,8},{6,9},{... | collective-permute-start | bytes 393224 | tf_op jit(solution)/shard_map/ppermute | solution.py:359
  31.3 32.6 %collective-permute-start.4 = (bf16[2,64,2304]{2,1,0:T(8,128)(2,1)S(1)}, bf16[2,64,2304]{2,1,0:T(8,128)(2,1)S(1)}, u32[]{:S(2)}, u32[]{:S(2)}) collective-permute-start(bf16[2,64,2304]{2,1,0:T(8,128)(2,1)S(1)} %collective-permute-done.1.up_ref), channel_id=1, source_target_pairs={{0,6},{1,7},{2,0},{3,1},{4,2},{5,3},{6,4},{7,5},{8,14},{9,15},{10,... | collective-permute-start | bytes 1769480 | tf_op jit(solution)/shard_map/ppermute | solution.py:375
  34.7 29.3 %collective-permute-start.5 = (bf16[2,64,2304]{2,1,0:T(8,128)(2,1)S(1)}, bf16[2,64,2304]{2,1,0:T(8,128)(2,1)S(1)}, u32[]{:S(2)}, u32[]{:S(2)}) collective-permute-start(bf16[2,64,2304]{2,1,0:T(8,128)(2,1)S(1)} %collective-permute-done.1.up_ref), channel_id=1, source_target_pairs={{0,1},{1,0},{2,3},{3,2},{4,5},{5,4},{6,7},{7,6},{8,9},{9,8},{10,11... | collective-permute-start | bytes 1769480 | tf_op jit(solution)/shard_map/ppermute | solution.py:352
  36.2 27.8 %collective-permute-start.3 = (bf16[2,64,2304]{2,1,0:T(8,128)(2,1)S(1)}, bf16[2,64,2304]{2,1,0:T(8,128)(2,1)S(1)}, u32[]{:S(2)}, u32[]{:S(2)}) collective-permute-start(bf16[2,64,2304]{2,1,0:T(8,128)(2,1)S(1)} %collective-permute-done.2.down_ref), channel_id=1, source_target_pairs={{0,2},{1,3},{2,4},{3,5},{4,6},{5,7},{6,0},{7,1},{8,10},{9,11},{10,... | collective-permute-start | bytes 1769480 | tf_op jit(solution)/shard_map/ppermute | solution.py:372
  36.9 1.1 copy-start
  48.1 21.8 %collective-permute-start.11 = (bf16[64,1792]{1,0:T(8,128)(2,1)S(1)}, bf16[64,1792]{1,0:T(8,128)(2,1)S(1)}, u32[]{:S(2)}, u32[]{:S(2)}) collective-permute-start(bf16[64,1792]{1,0:T(8,128)(2,1)S(1)} %fusion.4.refs_0_), channel_id=1, source_target_pairs={{0,16},{8,24},{16,0},{24,8},{1,17},{9,25},{17,1},{25,9},{2,18},{10... | collective-permute-start | bytes 688136 | tf_op jit(solution)/shard_map/ppermute | solution.py:352
  54.1 15.8 %collective-permute-start.12 = (bf16[64,1792]{1,0:T(8,128)(2,1)S(1)}, bf16[64,1792]{1,0:T(8,128)(2,1)S(1)}, u32[]{:S(2)}, u32[]{:S(2)}) collective-permute-start(bf16[64,1792]{1,0:T(8,128)(2,1)S(1)} %fusion.4.refs_0_), channel_id=1, source_target_pairs={{0,8},{8,0},{16,24},{24,16},{1,9},{9,1},{17,25},{25,17},{2,10},{10... | collective-permute-start | bytes 688136 | tf_op jit(solution)/shard_map/ppermute | solution.py:352
  64.0 10.2 %copy-start.1 = (s32[2,512]{1,0:T(2,128)S(1)}, s32[2,512]{1,0:T(2,128)}, u32[]{:S(2)}) copy-start(s32[2,512]{1,0:T(2,128)} %sampled_ref.1) | copy-start | bytes 12292
  70.0 4.2 %collective-permute-start.13 = (bf16[64,1792]{1,0:T(8,128)(2,1)S(1)}, bf16[64,1792]{1,0:T(8,128)(2,1)S(1)}, u32[]{:S(2)}, u32[]{:S(2)}) collective-permute-start(bf16[64,1792]{1,0:T(8,128)(2,1)S(1)} %collective-permute-done.11.refs_2_), channel_id=1, source_target_pairs={{0,8},{8,0},{16,24},{24,16},{1,9},{9,1},{17,25},{25,17},{2,10},{10... | collective-permute-start | bytes 688136 | tf_op jit(solution)/shard_map/ppermute | solution.py:352
  70.1 15.9 %collective-permute-start.10 = (bf16[64,2304]{1,0:T(8,128)(2,1)S(1)}, bf16[64,2304]{1,0:T(8,128)(2,1)S(1)}, u32[]{:S(2)}, u32[]{:S(2)}) collective-permute-start(bf16[64,2304]{1,0:T(8,128)(2,1)S(1)} %slice_bitcast_fusion), channel_id=1, source_target_pairs={{0,2},{1,3},{2,4},{3,5},{4,6},{5,7},{6,0},{7,1},{8,10},{9,11},{10,... | collective-permute-start | bytes 884744 | tf_op jit(solution)/shard_map/ppermute | solution.py:372
  73.7 13.9 %collective-permute-start.9 = (bf16[64,2304]{1,0:T(8,128)(2,1)S(1)}, bf16[64,2304]{1,0:T(8,128)(2,1)S(1)}, u32[]{:S(2)}, u32[]{:S(2)}) collective-permute-start(bf16[64,2304]{1,0:T(8,128)(2,1)S(1)} %slice_bitcast_fusion.1), channel_id=1, source_target_pairs={{0,6},{1,7},{2,0},{3,1},{4,2},{5,3},{6,4},{7,5},{8,14},{9,15},{10,... | collective-permute-start | bytes 884744 | tf_op jit(solution)/shard_map/ppermute | solution.py:375
  94.3 3.8 %collective-permute-start.14 = (f32[3,8,128]{2,1,0:T(8,128)S(1)}, f32[3,8,128]{2,1,0:T(8,128)S(1)}, u32[]{:S(2)}, u32[]{:S(2)}) collective-permute-start(f32[3,8,128]{2,1,0:T(8,128)S(1)} %chunk.3.refs_0_), channel_id=1, source_target_pairs={{0,1},{1,0},{2,3},{3,2},{4,5},{5,4},{6,7},{7,6},{8,9},{9,8},{10,11... | collective-permute-start | bytes 36872 | tf_op jit(solution)/shard_map/ppermute | solution.py:352
  98.1 4.5 %collective-permute-start.15 = (f32[3,8,128]{2,1,0:T(8,128)S(1)}, f32[3,8,128]{2,1,0:T(8,128)S(1)}, u32[]{:S(2)}, u32[]{:S(2)}) collective-permute-start(f32[3,8,128]{2,1,0:T(8,128)S(1)} %combine.2.refs_0_), channel_id=1, source_target_pairs={{0,2},{1,3},{2,0},{3,1},{4,6},{5,7},{6,4},{7,5},{8,10},{9,11},{10,... | collective-permute-start | bytes 36872 | tf_op jit(solution)/shard_map/ppermute | solution.py:352
  98.7 5.3 %collective-permute-start.16 = (f32[3,8,128]{2,1,0:T(8,128)S(1)}, f32[3,8,128]{2,1,0:T(8,128)S(1)}, u32[]{:S(2)}, u32[]{:S(2)}) collective-permute-start(f32[3,8,128]{2,1,0:T(8,128)S(1)} %combine.2.refs_0_), channel_id=1, source_target_pairs={{0,4},{1,5},{2,6},{3,7},{4,0},{5,1},{6,2},{7,3},{8,12},{9,13},{10,... | collective-permute-start | bytes 36872 | tf_op jit(solution)/shard_map/ppermute | solution.py:352
  102.3 5.5 %collective-permute-start.17 = (f32[3,8,128]{2,1,0:T(8,128)S(1)}, f32[3,8,128]{2,1,0:T(8,128)S(1)}, u32[]{:S(2)}, u32[]{:S(2)}) collective-permute-start(f32[3,8,128]{2,1,0:T(8,128)S(1)} %combine.2.refs_0_), channel_id=1, source_target_pairs={{0,6},{1,7},{2,4},{3,5},{4,2},{5,3},{6,0},{7,1},{8,14},{9,15},{10,... | collective-permute-start | bytes 36872 | tf_op jit(solution)/shard_map/ppermute | solution.py:352

commit v19 on v17

--- a/solution.py
+++ b/solution.py
@@ -225,7 +225,7 @@
 
 def make_chunk(hop, pieces, r, depth, entries, rank, n_voc):
     tile = tile_rows(entries)
-    sizes = [tile] * (entries // tile - 1) + [tile // 2] * 2
+    sizes = [tile] * (entries // tile - 1) + [tile // 2, tile // 4, tile // 4]
     n = 4 * r
     last = hop == n_voc // 2
     earlier = hop - 1 if last else 0

time: 85 us -> 85 us (level)
  no operation moved by 1% of the time
where the time goes in v19:
time: 85 us; the launch traced here: 84.7 us
  Pallas kernels  34.8 us (41%)
  starting transfers between devices  27.8 us (33%)
  waiting for transfers between devices  20.2 us (24%)
  local copies, waits for them, and re-layouts  1.11 us (1%)
    ppermute x7, starting transfers between devices, trade(): return lax.ppermute(x, axis, [(i, i ^ bit) for i in range(size)])  11.1 us
    pallas_call x1, Pallas kernels, body(): make_base(r, depth, entries, True)(up[1], hidden, head)  10.1 us
    ppermute x1, waiting for transfers between devices, body(): down = [hidden, lax.ppermute(hidden, 'vocab', ahead)]  9.11 us
    ppermute x7, waiting for transfers between devices, trade(): return lax.ppermute(x, axis, [(i, i ^ bit) for i in range(size)])  7.83 us
    pallas_call x1, Pallas kernels, body(): chunk(*opposite, down[half - 1], head, full_u, full_v, want, *stats)  6.61 us
    pallas_call x1, Pallas kernels, body(): stats.append(chunk(up[hop], down[hop - 1], head, full_u, full_v, want))  6.6 us
    pallas_call x1, Pallas kernels, body(): held += make_base(r, depth, entries, False)(up[2], down[1], head)  5.9 us
    pallas_call x1, Pallas kernels, body(): make_ends(r, depth, entries, rank, n_voc)(*held, full_u, full_v, want)  4.06 us
  transfers between devices with their start and end apart: 18, of which 7 were waited for; matrix products, arithmetic and copies ran while one was open for 0% of the time, Pallas kernels for 32%

profile of v19, /device:TPU:0, one launch (start us, length us, event | category | flops | bytes accessed | tf_op | source)
XLA Modules:
  0.0 84.7 jit_solution(6143890618554916083)
XLA Ops:
  0.6 3.1 %collective-permute-start.2 = (bf16[2,64,2304]{2,1,0:T(8,128)(2,1)}, bf16[2,64,2304]{2,1,0:T(8,128)(2,1)S(1)}, u32[]{:S(2)}, u32[]{:S(2)}) collective-permute-start(bf16[2,64,2304]{2,1,0:T(8,128)(2,1)} %down_ref.1), channel_id=1, source_target_pairs={{0,2},{2,4},{4,6},{6,7},{7,5},{5,3},{3,1},{1,0},{8,10},{10,12},{12... | collective-permute-start | bytes 1769480 | tf_op jit(solution)/shard_map/ppermute | solution.py:366
  3.7 0.0 collective-permute-start
  3.7 1.4 %collective-permute-start.5 = (bf16[64,288]{1,0:T(8,128)(2,1)}, bf16[64,288]{1,0:T(8,128)(2,1)S(1)}, u32[]{:S(2)}, u32[]{:S(2)}) collective-permute-start(bf16[64,288]{1,0:T(8,128)(2,1)} %bitcast.7), channel_id=1, source_target_pairs={{0,0},{1,1},{12,2},{13,3},{18,4},{19,5},{30,6},{31,7},{2,8},{3,9},... | collective-permute-start | bytes 110600 | tf_op jit(solution)/shard_map/ppermute | solution.py:363
  5.2 1.9 %collective-permute-start.6 = (bf16[64,288]{1,0:T(8,128)(2,1)}, bf16[64,288]{1,0:T(8,128)(2,1)S(1)}, u32[]{:S(2)}, u32[]{:S(2)}) collective-permute-start(bf16[64,288]{1,0:T(8,128)(2,1)} %bitcast.8), channel_id=1, source_target_pairs={{1,0},{0,1},{13,2},{12,3},{19,4},{18,5},{31,6},{30,7},{3,8},{2,9},... | collective-permute-start | bytes 110600 | tf_op jit(solution)/shard_map/ppermute | solution.py:363
  7.1 1.6 %collective-permute-start.4 = (bf16[64,1024]{1,0:T(8,128)(2,1)}, bf16[64,1024]{1,0:T(8,128)(2,1)S(1)}, u32[]{:S(2)}, u32[]{:S(2)}) collective-permute-start(bf16[64,1024]{1,0:T(8,128)(2,1)} %bitcast.6), channel_id=1, source_target_pairs={{0,0},{4,1},{8,2},{12,3},{16,4},{20,5},{24,6},{28,7},{2,8},{6,9},{... | collective-permute-start | bytes 393224 | tf_op jit(solution)/shard_map/ppermute | solution.py:355
  8.6 9.1 %collective-permute-done.2.down_ref = bf16[2,64,2304]{2,1,0:T(8,128)(2,1)S(1)} collective-permute-done((bf16[2,64,2304]{2,1,0:T(8,128)(2,1)}, bf16[2,64,2304]{2,1,0:T(8,128)(2,1)S(1)}, u32[]{:S(2)}, u32[]{:S(2)}) %collective-permute-start.2) | collective-permute-done | bytes 589856 | tf_op jit(solution)/shard_map/ppermute | solution.py:366
  17.8 2.4 %collective-permute-start.3 = (bf16[2,64,2304]{2,1,0:T(8,128)(2,1)S(1)}, bf16[2,64,2304]{2,1,0:T(8,128)(2,1)S(1)}, u32[]{:S(2)}, u32[]{:S(2)}) collective-permute-start(bf16[2,64,2304]{2,1,0:T(8,128)(2,1)S(1)} %collective-permute-done.2.down_ref), channel_id=1, source_target_pairs={{0,2},{2,4},{4,6},{6,7},{7,5},{5,3},{3,1},{1,0},{8,10},{10,12},{12... | collective-permute-start | bytes 1769480 | tf_op jit(solution)/shard_map/ppermute | solution.py:368
  20.1 0.0 collective-permute-done.up_ref
  20.1 0.0 collective-permute-start.1
  20.1 0.0 copy-start
  20.1 1.1 %copy-done = bf16[2,64,2304]{2,1,0:T(8,128)(2,1)S(1)} copy-done((bf16[2,64,2304]{2,1,0:T(8,128)(2,1)S(1)}, bf16[2,64,2304]{2,1,0:T(8,128)(2,1)}, u32[]{:S(2)}) %copy-start) | copy-done | bytes 589848
  21.2 10.1 %base.2 = (f32[4096,256]{1,0:T(8,128)S(1)}, bf16[2304,256]{1,0:T(8,128)(2,1)S(1)}, bf16[4096,2304]{1,0:T(8,128)(2,1)S(1)}) custom-call(bf16[2,64,2304]{2,1,0:T(8,128)(2,1)S(1)} %collective-permute-done.up_ref, bf16[2,64,2304]{2,1,0:T(8,128)(2,1)S(1)} %copy-done, bf16[4096,2304]{1,0:T(8,128)(2,1)} %head_ref.1), custom_call_target="tpu_custom_call" | custom-call | flops 4831838208 | bytes 18874368 | tf_op jit(solution)/shard_map/base/pallas_call | solution.py:369
  31.3 0.0 collective-permute-done.5
  31.3 0.0 collective-permute-done.6
  31.3 0.0 collective-permute-done.4
  31.3 0.1 collective-permute-start.10
  31.4 5.3 %collective-permute-start.9 = (bf16[64,1792]{1,0:T(8,128)(2,1)S(1)}, bf16[64,1792]{1,0:T(8,128)(2,1)S(1)}, u32[]{:S(2)}, u32[]{:S(2)}) collective-permute-start(bf16[64,1792]{1,0:T(8,128)(2,1)S(1)} %fusion.4.refs_0_), channel_id=1, source_target_pairs={{0,16},{8,24},{16,0},{24,8},{1,17},{9,25},{17,1},{25,9},{2,18},{10... | collective-permute-start | bytes 688136 | tf_op jit(solution)/shard_map/ppermute | solution.py:348
  36.7 0.0 collective-permute-done.3.refs_1_
  36.7 2.0 %collective-permute-done.1.up_ref = bf16[2,64,2304]{2,1,0:T(8,128)(2,1)S(1)} collective-permute-done((bf16[2,64,2304]{2,1,0:T(8,128)(2,1)S(1)}, bf16[2,64,2304]{2,1,0:T(8,128)(2,1)S(1)}, u32[]{:S(2)}, u32[]{:S(2)}) %collective-permute-start.1) | collective-permute-done | bytes 589856 | tf_op jit(solution)/shard_map/ppermute | solution.py:367
  38.7 4.0 %collective-permute-start.8 = (bf16[2,64,2304]{2,1,0:T(8,128)(2,1)S(1)}, bf16[2,64,2304]{2,1,0:T(8,128)(2,1)S(1)}, u32[]{:S(2)}, u32[]{:S(2)}) collective-permute-start(bf16[2,64,2304]{2,1,0:T(8,128)(2,1)S(1)} %collective-permute-done.3.refs_1_), channel_id=1, source_target_pairs={{0,2},{2,4},{4,6},{6,7},{7,5},{5,3},{3,1},{1,0},{8,10},{10,12},{12... | collective-permute-start | bytes 1769480 | tf_op jit(solution)/shard_map/ppermute | solution.py:385
  42.8 0.0 collective-permute-start.7
  42.8 0.0 copy-start.1
  42.8 5.9 %base.3 = (f32[4096,256]{1,0:T(8,128)S(1)}, bf16[2304,256]{1,0:T(8,128)(2,1)S(1)}) custom-call(bf16[2,64,2304]{2,1,0:T(8,128)(2,1)S(1)} %collective-permute-done.1.up_ref, bf16[2,64,2304]{2,1,0:T(8,128)(2,1)S(1)} %collective-permute-done.2.down_ref, bf16[4096,2304]{1,0:T(8,128)(2,1)S(1)} %get-tuple-element.34.head_ref.refs_2_.refs_3_), custom_call_target="tpu_custom_call" | custom-call | flops 4831838208 | bytes 18874368 | tf_op jit(solution)/shard_map/base/pallas_call | solution.py:380
  48.7 0.0 collective-permute-done.10.refs_1_
  48.7 0.0 collective-permute-done.9.refs_2_
  48.7 0.1 collective-permute-start.11
  48.8 1.5 %collective-permute-done.11.refs_3_ = bf16[64,1792]{1,0:T(8,128)(2,1)S(1)} collective-permute-done((bf16[64,1792]{1,0:T(8,128)(2,1)S(1)}, bf16[64,1792]{1,0:T(8,128)(2,1)S(1)}, u32[]{:S(2)}, u32[]{:S(2)}) %collective-permute-start.11) | collective-permute-done | bytes 229408 | tf_op jit(solution)/shard_map/ppermute | solution.py:348
  50.2 0.0 copy-done.1
  50.2 0.8 assemble.1
  51.1 4.1 %ends.1 = (f32[3,256]{1,0:T(4,128)S(1)}, f32[3,256]{1,0:T(4,128)S(1)}) custom-call(f32[4096,256]{1,0:T(8,128)S(1)} %get-tuple-element.32.base_a, bf16[2304,256]{1,0:T(8,128)(2,1)S(1)} %get-tuple-element.33.rows_a, f32[4096,256]{1,0:T(8,128)S(1)} %get-tuple-element.39.base_b, bf16[2304,256]{1,0:T(8,128)(2,1)S(1)} %get-tuple-element.40.rows_b, ...), custom_call_target="tpu_custom_call" | custom-call | flops 1073741824 | bytes 8388608 | tf_op jit(solution)/shard_map/ends/pallas_call | solution.py:392
  55.2 0.0 collective-permute-done.8.refs_2_
  55.2 1.2 %collective-permute-done.7.refs_0_ = bf16[2,64,2304]{2,1,0:T(8,128)(2,1)S(1)} collective-permute-done((bf16[2,64,2304]{2,1,0:T(8,128)(2,1)S(1)}, bf16[2,64,2304]{2,1,0:T(8,128)(2,1)S(1)}, u32[]{:S(2)}, u32[]{:S(2)}) %collective-permute-start.7) | collective-permute-done | bytes 589856 | tf_op jit(solution)/shard_map/ppermute | solution.py:384
  56.4 0.3 collective-permute-start.12
  56.7 2.0 %collective-permute-start.13 = (bf16[64,2304]{1,0:T(8,128)(2,1)S(1)}, bf16[64,2304]{1,0:T(8,128)(2,1)S(1)}, u32[]{:S(2)}, u32[]{:S(2)}) collective-permute-start(bf16[64,2304]{1,0:T(8,128)(2,1)S(1)} %slice_bitcast_fusion), channel_id=1, source_target_pairs={{0,2},{2,4},{4,6},{6,7},{7,5},{5,3},{3,1},{1,0},{8,10},{10,12},{12... | collective-permute-start | bytes 884744 | tf_op jit(solution)/shard_map/ppermute | solution.py:403
  58.7 6.6 %chunk.2.refs_9_ = f32[3,256]{1,0:T(4,128)S(1)} custom-call(bf16[2,64,2304]{2,1,0:T(8,128)(2,1)S(1)} %collective-permute-done.7.refs_0_, bf16[2,64,2304]{2,1,0:T(8,128)(2,1)S(1)} %collective-permute-done.3.refs_1_, bf16[4096,2304]{1,0:T(8,128)(2,1)S(1)} %get-tuple-element.34.head_ref.refs_2_.refs_3_, ...), custom_call_target="tpu_custom_call" | custom-call | flops 5368709120 | bytes 19922944 | tf_op jit(solution)/shard_map/chunk/pallas_call | solution.py:406
  65.3 0.0 collective-permute-done.12.refs_0_
  65.3 0.0 collective-permute-done.13.refs_1_
  65.3 6.6 %chunk.3.refs_0_ = f32[3,8,128]{2,1,0:T(8,128)S(1)} custom-call(bf16[64,2304]{1,0:T(8,128)(2,1)S(1)} %collective-permute-done.12.refs_0_, bf16[64,2304]{1,0:T(8,128)(2,1)S(1)} %collective-permute-done.13.refs_1_, bf16[2,64,2304]{2,1,0:T(8,128)(2,1)S(1)} %collective-permute-done.8.refs_2_, bf16[4096,2304]{1,0:T(8,128)(2,1)S(1)} %get-tuple-element.34.head_ref.refs_2_.refs_3_, ...), custom_call_target="tpu_custom_call" | custom-call | flops 5368709120 | bytes 19922944 | tf_op jit(solution)/shard_map/chunk/pallas_call | solution.py:411
  71.9 1.2 %collective-permute-start.14 = (f32[3,8,128]{2,1,0:T(8,128)S(1)}, f32[3,8,128]{2,1,0:T(8,128)S(1)}, u32[]{:S(2)}, u32[]{:S(2)}) collective-permute-start(f32[3,8,128]{2,1,0:T(8,128)S(1)} %chunk.3.refs_0_), channel_id=1, source_target_pairs={{0,1},{1,0},{2,3},{3,2},{4,5},{5,4},{6,7},{7,6},{8,9},{9,8},{10,11... | collective-permute-start | bytes 36872 | tf_op jit(solution)/shard_map/ppermute | solution.py:348
  73.2 2.5 %collective-permute-done.14.refs_1_ = f32[3,8,128]{2,1,0:T(8,128)S(1)} collective-permute-done((f32[3,8,128]{2,1,0:T(8,128)S(1)}, f32[3,8,128]{2,1,0:T(8,128)S(1)}, u32[]{:S(2)}, u32[]{:S(2)}) %collective-permute-start.14) | collective-permute-done | bytes 12320 | tf_op jit(solution)/shard_map/ppermute | solution.py:348
  75.7 1.3 %collective-permute-start.15 = (f32[3,8,128]{2,1,0:T(8,128)S(1)}, f32[3,8,128]{2,1,0:T(8,128)S(1)}, u32[]{:S(2)}, u32[]{:S(2)}) collective-permute-start(f32[3,8,128]{2,1,0:T(8,128)S(1)} %combine.2.refs_0_), channel_id=1, source_target_pairs={{0,2},{1,3},{2,0},{3,1},{4,6},{5,7},{6,4},{7,5},{8,10},{9,11},{10,... | collective-permute-start | bytes 36872 | tf_op jit(solution)/shard_map/ppermute | solution.py:348
  77.1 1.4 %collective-permute-start.16 = (f32[3,8,128]{2,1,0:T(8,128)S(1)}, f32[3,8,128]{2,1,0:T(8,128)S(1)}, u32[]{:S(2)}, u32[]{:S(2)}) collective-permute-start(f32[3,8,128]{2,1,0:T(8,128)S(1)} %combine.2.refs_0_), channel_id=1, source_target_pairs={{0,4},{1,5},{2,6},{3,7},{4,0},{5,1},{6,2},{7,3},{8,12},{9,13},{10,... | collective-permute-start | bytes 36872 | tf_op jit(solution)/shard_map/ppermute | solution.py:348
  78.5 1.7 %collective-permute-start.17 = (f32[3,8,128]{2,1,0:T(8,128)S(1)}, f32[3,8,128]{2,1,0:T(8,128)S(1)}, u32[]{:S(2)}, u32[]{:S(2)}) collective-permute-start(f32[3,8,128]{2,1,0:T(8,128)S(1)} %combine.2.refs_0_), channel_id=1, source_target_pairs={{0,6},{1,7},{2,4},{3,5},{4,2},{5,3},{6,0},{7,1},{8,14},{9,15},{10,... | collective-permute-start | bytes 36872 | tf_op jit(solution)/shard_map/ppermute | solution.py:348
  80.2 0.0 collective-permute-done.15.refs_1_
  80.2 1.5 %collective-permute-done.16.refs_2_ = f32[3,8,128]{2,1,0:T(8,128)S(1)} collective-permute-done((f32[3,8,128]{2,1,0:T(8,128)S(1)}, f32[3,8,128]{2,1,0:T(8,128)S(1)}, u32[]{:S(2)}, u32[]{:S(2)}) %collective-permute-start.16) | collective-permute-done | bytes 12320 | tf_op jit(solution)/shard_map/ppermute | solution.py:348
  81.7 2.3 %collective-permute-done.17.refs_3_ = f32[3,8,128]{2,1,0:T(8,128)S(1)} collective-permute-done((f32[3,8,128]{2,1,0:T(8,128)S(1)}, f32[3,8,128]{2,1,0:T(8,128)S(1)}, u32[]{:S(2)}, u32[]{:S(2)}) %collective-permute-start.17) | collective-permute-done | bytes 12320 | tf_op jit(solution)/shard_map/ppermute | solution.py:348
  84.0 0.7 combine.3
  (4 shorter events, 0.1 us)
Async XLA Ops:
  0.6 17.1 %collective-permute-start.2 = (bf16[2,64,2304]{2,1,0:T(8,128)(2,1)}, bf16[2,64,2304]{2,1,0:T(8,128)(2,1)S(1)}, u32[]{:S(2)}, u32[]{:S(2)}) collective-permute-start(bf16[2,64,2304]{2,1,0:T(8,128)(2,1)} %down_ref.1), channel_id=1, source_target_pairs={{0,2},{2,4},{4,6},{6,7},{7,5},{5,3},{3,1},{1,0},{8,10},{10,12},{12... | collective-permute-start | bytes 1769480 | tf_op jit(solution)/shard_map/ppermute | solution.py:366
  3.7 16.4 %collective-permute-start = (bf16[2,64,2304]{2,1,0:T(8,128)(2,1)}, bf16[2,64,2304]{2,1,0:T(8,128)(2,1)S(1)}, u32[]{:S(2)}, u32[]{:S(2)}) collective-permute-start(bf16[2,64,2304]{2,1,0:T(8,128)(2,1)} %down_ref.1), channel_id=1, source_target_pairs={{2,0},{4,2},{6,4},{7,6},{5,7},{3,5},{1,3},{0,1},{10,8},{12,10},{14... | collective-permute-start | bytes 1769480 | tf_op jit(solution)/shard_map/ppermute | solution.py:365
  3.7 27.6 %collective-permute-start.5 = (bf16[64,288]{1,0:T(8,128)(2,1)}, bf16[64,288]{1,0:T(8,128)(2,1)S(1)}, u32[]{:S(2)}, u32[]{:S(2)}) collective-permute-start(bf16[64,288]{1,0:T(8,128)(2,1)} %bitcast.7), channel_id=1, source_target_pairs={{0,0},{1,1},{12,2},{13,3},{18,4},{19,5},{30,6},{31,7},{2,8},{3,9},... | collective-permute-start | bytes 110600 | tf_op jit(solution)/shard_map/ppermute | solution.py:363
  5.2 26.1 %collective-permute-start.6 = (bf16[64,288]{1,0:T(8,128)(2,1)}, bf16[64,288]{1,0:T(8,128)(2,1)S(1)}, u32[]{:S(2)}, u32[]{:S(2)}) collective-permute-start(bf16[64,288]{1,0:T(8,128)(2,1)} %bitcast.8), channel_id=1, source_target_pairs={{1,0},{0,1},{13,2},{12,3},{19,4},{18,5},{31,6},{30,7},{3,8},{2,9},... | collective-permute-start | bytes 110600 | tf_op jit(solution)/shard_map/ppermute | solution.py:363
  7.1 24.2 %collective-permute-start.4 = (bf16[64,1024]{1,0:T(8,128)(2,1)}, bf16[64,1024]{1,0:T(8,128)(2,1)S(1)}, u32[]{:S(2)}, u32[]{:S(2)}) collective-permute-start(bf16[64,1024]{1,0:T(8,128)(2,1)} %bitcast.6), channel_id=1, source_target_pairs={{0,0},{4,1},{8,2},{12,3},{16,4},{20,5},{24,6},{28,7},{2,8},{6,9},{... | collective-permute-start | bytes 393224 | tf_op jit(solution)/shard_map/ppermute | solution.py:355
  17.8 18.9 %collective-permute-start.3 = (bf16[2,64,2304]{2,1,0:T(8,128)(2,1)S(1)}, bf16[2,64,2304]{2,1,0:T(8,128)(2,1)S(1)}, u32[]{:S(2)}, u32[]{:S(2)}) collective-permute-start(bf16[2,64,2304]{2,1,0:T(8,128)(2,1)S(1)} %collective-permute-done.2.down_ref), channel_id=1, source_target_pairs={{0,2},{2,4},{4,6},{6,7},{7,5},{5,3},{3,1},{1,0},{8,10},{10,12},{12... | collective-permute-start | bytes 1769480 | tf_op jit(solution)/shard_map/ppermute | solution.py:368
  20.1 18.6 %collective-permute-start.1 = (bf16[2,64,2304]{2,1,0:T(8,128)(2,1)S(1)}, bf16[2,64,2304]{2,1,0:T(8,128)(2,1)S(1)}, u32[]{:S(2)}, u32[]{:S(2)}) collective-permute-start(bf16[2,64,2304]{2,1,0:T(8,128)(2,1)S(1)} %collective-permute-done.up_ref), channel_id=1, source_target_pairs={{2,0},{4,2},{6,4},{7,6},{5,7},{3,5},{1,3},{0,1},{10,8},{12,10},{14... | collective-permute-start | bytes 1769480 | tf_op jit(solution)/shard_map/ppermute | solution.py:367
  20.1 1.1 %copy-start = (bf16[2,64,2304]{2,1,0:T(8,128)(2,1)S(1)}, bf16[2,64,2304]{2,1,0:T(8,128)(2,1)}, u32[]{:S(2)}) copy-start(bf16[2,64,2304]{2,1,0:T(8,128)(2,1)} %down_ref.1) | copy-start | bytes 1769476
  31.3 17.3 %collective-permute-start.10 = (bf16[64,1792]{1,0:T(8,128)(2,1)S(1)}, bf16[64,1792]{1,0:T(8,128)(2,1)S(1)}, u32[]{:S(2)}, u32[]{:S(2)}) collective-permute-start(bf16[64,1792]{1,0:T(8,128)(2,1)S(1)} %fusion.4.refs_0_), channel_id=1, source_target_pairs={{0,8},{8,0},{16,24},{24,16},{1,9},{9,1},{17,25},{25,17},{2,10},{10... | collective-permute-start | bytes 688136 | tf_op jit(solution)/shard_map/ppermute | solution.py:348
  31.4 17.3 %collective-permute-start.9 = (bf16[64,1792]{1,0:T(8,128)(2,1)S(1)}, bf16[64,1792]{1,0:T(8,128)(2,1)S(1)}, u32[]{:S(2)}, u32[]{:S(2)}) collective-permute-start(bf16[64,1792]{1,0:T(8,128)(2,1)S(1)} %fusion.4.refs_0_), channel_id=1, source_target_pairs={{0,16},{8,24},{16,0},{24,8},{1,17},{9,25},{17,1},{25,9},{2,18},{10... | collective-permute-start | bytes 688136 | tf_op jit(solution)/shard_map/ppermute | solution.py:348
  38.7 16.4 %collective-permute-start.8 = (bf16[2,64,2304]{2,1,0:T(8,128)(2,1)S(1)}, bf16[2,64,2304]{2,1,0:T(8,128)(2,1)S(1)}, u32[]{:S(2)}, u32[]{:S(2)}) collective-permute-start(bf16[2,64,2304]{2,1,0:T(8,128)(2,1)S(1)} %collective-permute-done.3.refs_1_), channel_id=1, source_target_pairs={{0,2},{2,4},{4,6},{6,7},{7,5},{5,3},{3,1},{1,0},{8,10},{10,12},{12... | collective-permute-start | bytes 1769480 | tf_op jit(solution)/shard_map/ppermute | solution.py:385
  42.8 13.6 %collective-permute-start.7 = (bf16[2,64,2304]{2,1,0:T(8,128)(2,1)S(1)}, bf16[2,64,2304]{2,1,0:T(8,128)(2,1)S(1)}, u32[]{:S(2)}, u32[]{:S(2)}) collective-permute-start(bf16[2,64,2304]{2,1,0:T(8,128)(2,1)S(1)} %collective-permute-done.1.up_ref), channel_id=1, source_target_pairs={{2,0},{4,2},{6,4},{7,6},{5,7},{3,5},{1,3},{0,1},{10,8},{12,10},{14... | collective-permute-start | bytes 1769480 | tf_op jit(solution)/shard_map/ppermute | solution.py:384
  42.8 7.5 %copy-start.1 = (s32[2,512]{1,0:T(2,128)S(1)}, s32[2,512]{1,0:T(2,128)}, u32[]{:S(2)}) copy-start(s32[2,512]{1,0:T(2,128)} %sampled_ref.1) | copy-start | bytes 12292
  48.7 1.6 %collective-permute-start.11 = (bf16[64,1792]{1,0:T(8,128)(2,1)S(1)}, bf16[64,1792]{1,0:T(8,128)(2,1)S(1)}, u32[]{:S(2)}, u32[]{:S(2)}) collective-permute-start(bf16[64,1792]{1,0:T(8,128)(2,1)S(1)} %collective-permute-done.9.refs_2_), channel_id=1, source_target_pairs={{0,8},{8,0},{16,24},{24,16},{1,9},{9,1},{17,25},{25,17},{2,10},{10... | collective-permute-start | bytes 688136 | tf_op jit(solution)/shard_map/ppermute | solution.py:348
  56.4 8.9 %collective-permute-start.12 = (bf16[64,2304]{1,0:T(8,128)(2,1)S(1)}, bf16[64,2304]{1,0:T(8,128)(2,1)S(1)}, u32[]{:S(2)}, u32[]{:S(2)}) collective-permute-start(bf16[64,2304]{1,0:T(8,128)(2,1)S(1)} %slice_bitcast_fusion.1), channel_id=1, source_target_pairs={{2,0},{4,2},{6,4},{7,6},{5,7},{3,5},{1,3},{0,1},{10,8},{12,10},{14... | collective-permute-start | bytes 884744 | tf_op jit(solution)/shard_map/ppermute | solution.py:402
  56.7 8.6 %collective-permute-start.13 = (bf16[64,2304]{1,0:T(8,128)(2,1)S(1)}, bf16[64,2304]{1,0:T(8,128)(2,1)S(1)}, u32[]{:S(2)}, u32[]{:S(2)}) collective-permute-start(bf16[64,2304]{1,0:T(8,128)(2,1)S(1)} %slice_bitcast_fusion), channel_id=1, source_target_pairs={{0,2},{2,4},{4,6},{6,7},{7,5},{5,3},{3,1},{1,0},{8,10},{10,12},{12... | collective-permute-start | bytes 884744 | tf_op jit(solution)/shard_map/ppermute | solution.py:403
  71.9 3.8 %collective-permute-start.14 = (f32[3,8,128]{2,1,0:T(8,128)S(1)}, f32[3,8,128]{2,1,0:T(8,128)S(1)}, u32[]{:S(2)}, u32[]{:S(2)}) collective-permute-start(f32[3,8,128]{2,1,0:T(8,128)S(1)} %chunk.3.refs_0_), channel_id=1, source_target_pairs={{0,1},{1,0},{2,3},{3,2},{4,5},{5,4},{6,7},{7,6},{8,9},{9,8},{10,11... | collective-permute-start | bytes 36872 | tf_op jit(solution)/shard_map/ppermute | solution.py:348
  75.7 4.5 %collective-permute-start.15 = (f32[3,8,128]{2,1,0:T(8,128)S(1)}, f32[3,8,128]{2,1,0:T(8,128)S(1)}, u32[]{:S(2)}, u32[]{:S(2)}) collective-permute-start(f32[3,8,128]{2,1,0:T(8,128)S(1)} %combine.2.refs_0_), channel_id=1, source_target_pairs={{0,2},{1,3},{2,0},{3,1},{4,6},{5,7},{6,4},{7,5},{8,10},{9,11},{10,... | collective-permute-start | bytes 36872 | tf_op jit(solution)/shard_map/ppermute | solution.py:348
  77.1 4.6 %collective-permute-start.16 = (f32[3,8,128]{2,1,0:T(8,128)S(1)}, f32[3,8,128]{2,1,0:T(8,128)S(1)}, u32[]{:S(2)}, u32[]{:S(2)}) collective-permute-start(f32[3,8,128]{2,1,0:T(8,128)S(1)} %combine.2.refs_0_), channel_id=1, source_target_pairs={{0,4},{1,5},{2,6},{3,7},{4,0},{5,1},{6,2},{7,3},{8,12},{9,13},{10,... | collective-permute-start | bytes 36872 | tf_op jit(solution)/shard_map/ppermute | solution.py:348
  78.5 5.5 %collective-permute-start.17 = (f32[3,8,128]{2,1,0:T(8,128)S(1)}, f32[3,8,128]{2,1,0:T(8,128)S(1)}, u32[]{:S(2)}, u32[]{:S(2)}) collective-permute-start(f32[3,8,128]{2,1,0:T(8,128)S(1)} %combine.2.refs_0_), channel_id=1, source_target_pairs={{0,6},{1,7},{2,4},{3,5},{4,2},{5,3},{6,0},{7,1},{8,14},{9,15},{10,... | collective-permute-start | bytes 36872 | tf_op jit(solution)/shard_map/ppermute | solution.py:348

commit v20 on v17

--- a/solution.py
+++ b/solution.py
@@ -226,6 +226,8 @@
 def make_chunk(hop, pieces, r, depth, entries, rank, n_voc):
     tile = tile_rows(entries)
     sizes = [tile] * (entries // tile - 1) + [tile // 2] * 2
+    if len(sizes) > 3:
+        sizes[:2] = [2 * tile]
     n = 4 * r
     last = hop == n_voc // 2
     earlier = hop - 1 if last else 0
@@ -274,11 +276,11 @@
         out_specs=WHOLE,
         scratch_shapes=[
             pltpu.VMEM((depth, n), jnp.bfloat16),
-            pltpu.VMEM((tile, n), jnp.float32),
-            pltpu.VMEM((tile, n), jnp.float32),
+            pltpu.VMEM((max(sizes[::2]), n), jnp.float32),
+            pltpu.VMEM((max(sizes[1::2]), n), jnp.float32),
         ]
         + state_scratch(rank, n),
-        compiler_params=pltpu.CompilerParams(vmem_limit_bytes=8 * MIB),
+        compiler_params=pltpu.CompilerParams(vmem_limit_bytes=12 * MIB),
         cost_estimate=pl.CostEstimate(
             flops=2 * n * entries * (depth + 256),
             bytes_accessed=2 * entries * (depth + LANES),

time: 85 us -> 85.7 us (level)
  Pallas kernels: 34.8 us -> 36 us
  transfers between devices with their start and end apart: 18 -> 18, of which waited for: 7 -> 7; matrix products, arithmetic and copies ran while one was open for 0% -> 0% of each run, Pallas kernels for 32% -> 33%
where the time goes in v20:
time: 85.7 us; the launch traced here: 85.4 us
  Pallas kernels  36 us (42%)
  starting transfers between devices  27.6 us (32%)
  waiting for transfers between devices  20 us (23%)
  local copies, waits for them, and re-layouts  1.11 us (1%)
    ppermute x7, starting transfers between devices, trade(): return lax.ppermute(x, axis, [(i, i ^ bit) for i in range(size)])  10.8 us
    pallas_call x1, Pallas kernels, body(): make_base(r, depth, entries, True)(up[1], hidden, head)  10.1 us
    ppermute x1, waiting for transfers between devices, body(): down = [hidden, lax.ppermute(hidden, 'vocab', ahead)]  9.11 us
    ppermute x7, waiting for transfers between devices, trade(): return lax.ppermute(x, axis, [(i, i ^ bit) for i in range(size)])  7.84 us
    pallas_call x1, Pallas kernels, body(): chunk(*opposite, down[half - 1], head, full_u, full_v, want, *stats)  7.09 us
    pallas_call x1, Pallas kernels, body(): stats.append(chunk(up[hop], down[hop - 1], head, full_u, full_v, want))  7.07 us
    pallas_call x1, Pallas kernels, body(): held += make_base(r, depth, entries, False)(up[2], down[1], head)  5.93 us
    pallas_call x1, Pallas kernels, body(): make_ends(r, depth, entries, rank, n_voc)(*held, full_u, full_v, want)  4.23 us
  transfers between devices with their start and end apart: 18, of which 7 were waited for; matrix products, arithmetic and copies ran while one was open for 0% of the time, Pallas kernels for 33%

profile of v20, /device:TPU:0, one launch (start us, length us, event | category | flops | bytes accessed | tf_op | source)
XLA Modules:
  0.0 85.4 jit_solution(11331026680564823513)
XLA Ops:
  0.6 3.1 %collective-permute-start.2 = (bf16[2,64,2304]{2,1,0:T(8,128)(2,1)}, bf16[2,64,2304]{2,1,0:T(8,128)(2,1)S(1)}, u32[]{:S(2)}, u32[]{:S(2)}) collective-permute-start(bf16[2,64,2304]{2,1,0:T(8,128)(2,1)} %down_ref.1), channel_id=1, source_target_pairs={{0,2},{2,4},{4,6},{6,7},{7,5},{5,3},{3,1},{1,0},{8,10},{10,12},{12... | collective-permute-start | bytes 1769480 | tf_op jit(solution)/shard_map/ppermute | solution.py:368
  3.7 0.0 collective-permute-start
  3.7 1.4 %collective-permute-start.5 = (bf16[64,288]{1,0:T(8,128)(2,1)}, bf16[64,288]{1,0:T(8,128)(2,1)S(1)}, u32[]{:S(2)}, u32[]{:S(2)}) collective-permute-start(bf16[64,288]{1,0:T(8,128)(2,1)} %bitcast.7), channel_id=1, source_target_pairs={{0,0},{1,1},{12,2},{13,3},{18,4},{19,5},{30,6},{31,7},{2,8},{3,9},... | collective-permute-start | bytes 110600 | tf_op jit(solution)/shard_map/ppermute | solution.py:365
  5.2 1.9 %collective-permute-start.6 = (bf16[64,288]{1,0:T(8,128)(2,1)}, bf16[64,288]{1,0:T(8,128)(2,1)S(1)}, u32[]{:S(2)}, u32[]{:S(2)}) collective-permute-start(bf16[64,288]{1,0:T(8,128)(2,1)} %bitcast.8), channel_id=1, source_target_pairs={{1,0},{0,1},{13,2},{12,3},{19,4},{18,5},{31,6},{30,7},{3,8},{2,9},... | collective-permute-start | bytes 110600 | tf_op jit(solution)/shard_map/ppermute | solution.py:365
  7.1 1.6 %collective-permute-start.4 = (bf16[64,1024]{1,0:T(8,128)(2,1)}, bf16[64,1024]{1,0:T(8,128)(2,1)S(1)}, u32[]{:S(2)}, u32[]{:S(2)}) collective-permute-start(bf16[64,1024]{1,0:T(8,128)(2,1)} %bitcast.6), channel_id=1, source_target_pairs={{0,0},{4,1},{8,2},{12,3},{16,4},{20,5},{24,6},{28,7},{2,8},{6,9},{... | collective-permute-start | bytes 393224 | tf_op jit(solution)/shard_map/ppermute | solution.py:357
  8.6 9.1 %collective-permute-done.2.down_ref = bf16[2,64,2304]{2,1,0:T(8,128)(2,1)S(1)} collective-permute-done((bf16[2,64,2304]{2,1,0:T(8,128)(2,1)}, bf16[2,64,2304]{2,1,0:T(8,128)(2,1)S(1)}, u32[]{:S(2)}, u32[]{:S(2)}) %collective-permute-start.2) | collective-permute-done | bytes 589856 | tf_op jit(solution)/shard_map/ppermute | solution.py:368
  17.8 2.4 %collective-permute-start.3 = (bf16[2,64,2304]{2,1,0:T(8,128)(2,1)S(1)}, bf16[2,64,2304]{2,1,0:T(8,128)(2,1)S(1)}, u32[]{:S(2)}, u32[]{:S(2)}) collective-permute-start(bf16[2,64,2304]{2,1,0:T(8,128)(2,1)S(1)} %collective-permute-done.2.down_ref), channel_id=1, source_target_pairs={{0,2},{2,4},{4,6},{6,7},{7,5},{5,3},{3,1},{1,0},{8,10},{10,12},{12... | collective-permute-start | bytes 1769480 | tf_op jit(solution)/shard_map/ppermute | solution.py:370
  20.1 0.0 collective-permute-done.up_ref
  20.1 0.0 collective-permute-start.1
  20.1 0.0 copy-start
  20.1 1.1 %copy-done = bf16[2,64,2304]{2,1,0:T(8,128)(2,1)S(1)} copy-done((bf16[2,64,2304]{2,1,0:T(8,128)(2,1)S(1)}, bf16[2,64,2304]{2,1,0:T(8,128)(2,1)}, u32[]{:S(2)}) %copy-start) | copy-done | bytes 589848
  21.2 10.1 %base.2 = (f32[4096,256]{1,0:T(8,128)S(1)}, bf16[2304,256]{1,0:T(8,128)(2,1)S(1)}, bf16[4096,2304]{1,0:T(8,128)(2,1)S(1)}) custom-call(bf16[2,64,2304]{2,1,0:T(8,128)(2,1)S(1)} %collective-permute-done.up_ref, bf16[2,64,2304]{2,1,0:T(8,128)(2,1)S(1)} %copy-done, bf16[4096,2304]{1,0:T(8,128)(2,1)} %head_ref.1), custom_call_target="tpu_custom_call" | custom-call | flops 4831838208 | bytes 18874368 | tf_op jit(solution)/shard_map/base/pallas_call | solution.py:371
  31.3 0.0 collective-permute-done.5
  31.3 0.0 collective-permute-done.6
  31.3 0.0 collective-permute-done.4
  31.4 0.1 collective-permute-start.10
  31.4 5.3 %collective-permute-start.9 = (bf16[64,1792]{1,0:T(8,128)(2,1)S(1)}, bf16[64,1792]{1,0:T(8,128)(2,1)S(1)}, u32[]{:S(2)}, u32[]{:S(2)}) collective-permute-start(bf16[64,1792]{1,0:T(8,128)(2,1)S(1)} %fusion.4.refs_0_), channel_id=1, source_target_pairs={{0,16},{8,24},{16,0},{24,8},{1,17},{9,25},{17,1},{25,9},{2,18},{10... | collective-permute-start | bytes 688136 | tf_op jit(solution)/shard_map/ppermute | solution.py:350
  36.7 0.0 collective-permute-done.3.refs_1_
  36.7 2.0 %collective-permute-done.1.up_ref = bf16[2,64,2304]{2,1,0:T(8,128)(2,1)S(1)} collective-permute-done((bf16[2,64,2304]{2,1,0:T(8,128)(2,1)S(1)}, bf16[2,64,2304]{2,1,0:T(8,128)(2,1)S(1)}, u32[]{:S(2)}, u32[]{:S(2)}) %collective-permute-start.1) | collective-permute-done | bytes 589856 | tf_op jit(solution)/shard_map/ppermute | solution.py:369
  38.7 4.0 %collective-permute-start.8 = (bf16[2,64,2304]{2,1,0:T(8,128)(2,1)S(1)}, bf16[2,64,2304]{2,1,0:T(8,128)(2,1)S(1)}, u32[]{:S(2)}, u32[]{:S(2)}) collective-permute-start(bf16[2,64,2304]{2,1,0:T(8,128)(2,1)S(1)} %collective-permute-done.3.refs_1_), channel_id=1, source_target_pairs={{0,2},{2,4},{4,6},{6,7},{7,5},{5,3},{3,1},{1,0},{8,10},{10,12},{12... | collective-permute-start | bytes 1769480 | tf_op jit(solution)/shard_map/ppermute | solution.py:387
  42.8 0.0 collective-permute-start.7
  42.8 0.0 copy-start.1
  42.8 5.9 %base.3 = (f32[4096,256]{1,0:T(8,128)S(1)}, bf16[2304,256]{1,0:T(8,128)(2,1)S(1)}) custom-call(bf16[2,64,2304]{2,1,0:T(8,128)(2,1)S(1)} %collective-permute-done.1.up_ref, bf16[2,64,2304]{2,1,0:T(8,128)(2,1)S(1)} %collective-permute-done.2.down_ref, bf16[4096,2304]{1,0:T(8,128)(2,1)S(1)} %get-tuple-element.34.head_ref.refs_2_.refs_3_), custom_call_target="tpu_custom_call" | custom-call | flops 4831838208 | bytes 18874368 | tf_op jit(solution)/shard_map/base/pallas_call | solution.py:382
  48.7 0.0 collective-permute-done.10.refs_1_
  48.7 0.0 collective-permute-done.9.refs_2_
  48.7 0.1 collective-permute-start.11
  48.8 1.5 %collective-permute-done.11.refs_3_ = bf16[64,1792]{1,0:T(8,128)(2,1)S(1)} collective-permute-done((bf16[64,1792]{1,0:T(8,128)(2,1)S(1)}, bf16[64,1792]{1,0:T(8,128)(2,1)S(1)}, u32[]{:S(2)}, u32[]{:S(2)}) %collective-permute-start.11) | collective-permute-done | bytes 229408 | tf_op jit(solution)/shard_map/ppermute | solution.py:350
  50.3 0.0 copy-done.1
  50.3 0.8 assemble.1
  51.1 4.2 %ends.1 = (f32[3,256]{1,0:T(4,128)S(1)}, f32[3,256]{1,0:T(4,128)S(1)}) custom-call(f32[4096,256]{1,0:T(8,128)S(1)} %get-tuple-element.32.base_a, bf16[2304,256]{1,0:T(8,128)(2,1)S(1)} %get-tuple-element.33.rows_a, f32[4096,256]{1,0:T(8,128)S(1)} %get-tuple-element.39.base_b, bf16[2304,256]{1,0:T(8,128)(2,1)S(1)} %get-tuple-element.40.rows_b, ...), custom_call_target="tpu_custom_call" | custom-call | flops 1073741824 | bytes 8388608 | tf_op jit(solution)/shard_map/ends/pallas_call | solution.py:394
  55.4 0.0 collective-permute-done.8.refs_2_
  55.4 1.0 %collective-permute-done.7.refs_0_ = bf16[2,64,2304]{2,1,0:T(8,128)(2,1)S(1)} collective-permute-done((bf16[2,64,2304]{2,1,0:T(8,128)(2,1)S(1)}, bf16[2,64,2304]{2,1,0:T(8,128)(2,1)S(1)}, u32[]{:S(2)}, u32[]{:S(2)}) %collective-permute-start.7) | collective-permute-done | bytes 589856 | tf_op jit(solution)/shard_map/ppermute | solution.py:386
  56.4 0.3 collective-permute-start.12
  56.7 2.0 %collective-permute-start.13 = (bf16[64,2304]{1,0:T(8,128)(2,1)S(1)}, bf16[64,2304]{1,0:T(8,128)(2,1)S(1)}, u32[]{:S(2)}, u32[]{:S(2)}) collective-permute-start(bf16[64,2304]{1,0:T(8,128)(2,1)S(1)} %slice_bitcast_fusion), channel_id=1, source_target_pairs={{0,2},{2,4},{4,6},{6,7},{7,5},{5,3},{3,1},{1,0},{8,10},{10,12},{12... | collective-permute-start | bytes 884744 | tf_op jit(solution)/shard_map/ppermute | solution.py:405
  58.7 7.1 %chunk.2.refs_9_ = f32[3,256]{1,0:T(4,128)S(1)} custom-call(bf16[2,64,2304]{2,1,0:T(8,128)(2,1)S(1)} %collective-permute-done.7.refs_0_, bf16[2,64,2304]{2,1,0:T(8,128)(2,1)S(1)} %collective-permute-done.3.refs_1_, bf16[4096,2304]{1,0:T(8,128)(2,1)S(1)} %get-tuple-element.34.head_ref.refs_2_.refs_3_, ...), custom_call_target="tpu_custom_call" | custom-call | flops 5368709120 | bytes 19922944 | tf_op jit(solution)/shard_map/chunk/pallas_call | solution.py:408
  65.8 0.0 collective-permute-done.12.refs_0_
  65.8 0.0 collective-permute-done.13.refs_1_
  65.8 7.1 %chunk.3.refs_0_ = f32[3,8,128]{2,1,0:T(8,128)S(1)} custom-call(bf16[64,2304]{1,0:T(8,128)(2,1)S(1)} %collective-permute-done.12.refs_0_, bf16[64,2304]{1,0:T(8,128)(2,1)S(1)} %collective-permute-done.13.refs_1_, bf16[2,64,2304]{2,1,0:T(8,128)(2,1)S(1)} %collective-permute-done.8.refs_2_, bf16[4096,2304]{1,0:T(8,128)(2,1)S(1)} %get-tuple-element.34.head_ref.refs_2_.refs_3_, ...), custom_call_target="tpu_custom_call" | custom-call | flops 5368709120 | bytes 19922944 | tf_op jit(solution)/shard_map/chunk/pallas_call | solution.py:413
  72.9 1.0 %collective-permute-start.14 = (f32[3,8,128]{2,1,0:T(8,128)S(1)}, f32[3,8,128]{2,1,0:T(8,128)S(1)}, u32[]{:S(2)}, u32[]{:S(2)}) collective-permute-start(f32[3,8,128]{2,1,0:T(8,128)S(1)} %chunk.3.refs_0_), channel_id=1, source_target_pairs={{0,1},{1,0},{2,3},{3,2},{4,5},{5,4},{6,7},{7,6},{8,9},{9,8},{10,11... | collective-permute-start | bytes 36872 | tf_op jit(solution)/shard_map/ppermute | solution.py:350
  73.9 2.8 %collective-permute-done.14.refs_1_ = f32[3,8,128]{2,1,0:T(8,128)S(1)} collective-permute-done((f32[3,8,128]{2,1,0:T(8,128)S(1)}, f32[3,8,128]{2,1,0:T(8,128)S(1)}, u32[]{:S(2)}, u32[]{:S(2)}) %collective-permute-start.14) | collective-permute-done | bytes 12320 | tf_op jit(solution)/shard_map/ppermute | solution.py:350
  76.7 1.1 %collective-permute-start.15 = (f32[3,8,128]{2,1,0:T(8,128)S(1)}, f32[3,8,128]{2,1,0:T(8,128)S(1)}, u32[]{:S(2)}, u32[]{:S(2)}) collective-permute-start(f32[3,8,128]{2,1,0:T(8,128)S(1)} %combine.2.refs_0_), channel_id=1, source_target_pairs={{0,2},{1,3},{2,0},{3,1},{4,6},{5,7},{6,4},{7,5},{8,10},{9,11},{10,... | collective-permute-start | bytes 36872 | tf_op jit(solution)/shard_map/ppermute | solution.py:350
  77.8 1.4 %collective-permute-start.16 = (f32[3,8,128]{2,1,0:T(8,128)S(1)}, f32[3,8,128]{2,1,0:T(8,128)S(1)}, u32[]{:S(2)}, u32[]{:S(2)}) collective-permute-start(f32[3,8,128]{2,1,0:T(8,128)S(1)} %combine.2.refs_0_), channel_id=1, source_target_pairs={{0,4},{1,5},{2,6},{3,7},{4,0},{5,1},{6,2},{7,3},{8,12},{9,13},{10,... | collective-permute-start | bytes 36872 | tf_op jit(solution)/shard_map/ppermute | solution.py:350
  79.2 1.9 %collective-permute-start.17 = (f32[3,8,128]{2,1,0:T(8,128)S(1)}, f32[3,8,128]{2,1,0:T(8,128)S(1)}, u32[]{:S(2)}, u32[]{:S(2)}) collective-permute-start(f32[3,8,128]{2,1,0:T(8,128)S(1)} %combine.2.refs_0_), channel_id=1, source_target_pairs={{0,6},{1,7},{2,4},{3,5},{4,2},{5,3},{6,0},{7,1},{8,14},{9,15},{10,... | collective-permute-start | bytes 36872 | tf_op jit(solution)/shard_map/ppermute | solution.py:350
  81.1 0.0 collective-permute-done.15.refs_1_
  81.1 1.3 %collective-permute-done.16.refs_2_ = f32[3,8,128]{2,1,0:T(8,128)S(1)} collective-permute-done((f32[3,8,128]{2,1,0:T(8,128)S(1)}, f32[3,8,128]{2,1,0:T(8,128)S(1)}, u32[]{:S(2)}, u32[]{:S(2)}) %collective-permute-start.16) | collective-permute-done | bytes 12320 | tf_op jit(solution)/shard_map/ppermute | solution.py:350
  82.4 2.3 %collective-permute-done.17.refs_3_ = f32[3,8,128]{2,1,0:T(8,128)S(1)} collective-permute-done((f32[3,8,128]{2,1,0:T(8,128)S(1)}, f32[3,8,128]{2,1,0:T(8,128)S(1)}, u32[]{:S(2)}, u32[]{:S(2)}) %collective-permute-start.17) | collective-permute-done | bytes 12320 | tf_op jit(solution)/shard_map/ppermute | solution.py:350
  84.7 0.7 combine.3
  (4 shorter events, 0.1 us)
Async XLA Ops:
  0.6 17.1 %collective-permute-start.2 = (bf16[2,64,2304]{2,1,0:T(8,128)(2,1)}, bf16[2,64,2304]{2,1,0:T(8,128)(2,1)S(1)}, u32[]{:S(2)}, u32[]{:S(2)}) collective-permute-start(bf16[2,64,2304]{2,1,0:T(8,128)(2,1)} %down_ref.1), channel_id=1, source_target_pairs={{0,2},{2,4},{4,6},{6,7},{7,5},{5,3},{3,1},{1,0},{8,10},{10,12},{12... | collective-permute-start | bytes 1769480 | tf_op jit(solution)/shard_map/ppermute | solution.py:368
  3.7 16.4 %collective-permute-start = (bf16[2,64,2304]{2,1,0:T(8,128)(2,1)}, bf16[2,64,2304]{2,1,0:T(8,128)(2,1)S(1)}, u32[]{:S(2)}, u32[]{:S(2)}) collective-permute-start(bf16[2,64,2304]{2,1,0:T(8,128)(2,1)} %down_ref.1), channel_id=1, source_target_pairs={{2,0},{4,2},{6,4},{7,6},{5,7},{3,5},{1,3},{0,1},{10,8},{12,10},{14... | collective-permute-start | bytes 1769480 | tf_op jit(solution)/shard_map/ppermute | solution.py:367
  3.7 27.6 %collective-permute-start.5 = (bf16[64,288]{1,0:T(8,128)(2,1)}, bf16[64,288]{1,0:T(8,128)(2,1)S(1)}, u32[]{:S(2)}, u32[]{:S(2)}) collective-permute-start(bf16[64,288]{1,0:T(8,128)(2,1)} %bitcast.7), channel_id=1, source_target_pairs={{0,0},{1,1},{12,2},{13,3},{18,4},{19,5},{30,6},{31,7},{2,8},{3,9},... | collective-permute-start | bytes 110600 | tf_op jit(solution)/shard_map/ppermute | solution.py:365
  5.2 26.2 %collective-permute-start.6 = (bf16[64,288]{1,0:T(8,128)(2,1)}, bf16[64,288]{1,0:T(8,128)(2,1)S(1)}, u32[]{:S(2)}, u32[]{:S(2)}) collective-permute-start(bf16[64,288]{1,0:T(8,128)(2,1)} %bitcast.8), channel_id=1, source_target_pairs={{1,0},{0,1},{13,2},{12,3},{19,4},{18,5},{31,6},{30,7},{3,8},{2,9},... | collective-permute-start | bytes 110600 | tf_op jit(solution)/shard_map/ppermute | solution.py:365
  7.1 24.2 %collective-permute-start.4 = (bf16[64,1024]{1,0:T(8,128)(2,1)}, bf16[64,1024]{1,0:T(8,128)(2,1)S(1)}, u32[]{:S(2)}, u32[]{:S(2)}) collective-permute-start(bf16[64,1024]{1,0:T(8,128)(2,1)} %bitcast.6), channel_id=1, source_target_pairs={{0,0},{4,1},{8,2},{12,3},{16,4},{20,5},{24,6},{28,7},{2,8},{6,9},{... | collective-permute-start | bytes 393224 | tf_op jit(solution)/shard_map/ppermute | solution.py:357
  17.8 19.0 %collective-permute-start.3 = (bf16[2,64,2304]{2,1,0:T(8,128)(2,1)S(1)}, bf16[2,64,2304]{2,1,0:T(8,128)(2,1)S(1)}, u32[]{:S(2)}, u32[]{:S(2)}) collective-permute-start(bf16[2,64,2304]{2,1,0:T(8,128)(2,1)S(1)} %collective-permute-done.2.down_ref), channel_id=1, source_target_pairs={{0,2},{2,4},{4,6},{6,7},{7,5},{5,3},{3,1},{1,0},{8,10},{10,12},{12... | collective-permute-start | bytes 1769480 | tf_op jit(solution)/shard_map/ppermute | solution.py:370
  20.1 18.6 %collective-permute-start.1 = (bf16[2,64,2304]{2,1,0:T(8,128)(2,1)S(1)}, bf16[2,64,2304]{2,1,0:T(8,128)(2,1)S(1)}, u32[]{:S(2)}, u32[]{:S(2)}) collective-permute-start(bf16[2,64,2304]{2,1,0:T(8,128)(2,1)S(1)} %collective-permute-done.up_ref), channel_id=1, source_target_pairs={{2,0},{4,2},{6,4},{7,6},{5,7},{3,5},{1,3},{0,1},{10,8},{12,10},{14... | collective-permute-start | bytes 1769480 | tf_op jit(solution)/shard_map/ppermute | solution.py:369
  20.1 1.1 %copy-start = (bf16[2,64,2304]{2,1,0:T(8,128)(2,1)S(1)}, bf16[2,64,2304]{2,1,0:T(8,128)(2,1)}, u32[]{:S(2)}) copy-start(bf16[2,64,2304]{2,1,0:T(8,128)(2,1)} %down_ref.1) | copy-start | bytes 1769476
  31.4 17.3 %collective-permute-start.10 = (bf16[64,1792]{1,0:T(8,128)(2,1)S(1)}, bf16[64,1792]{1,0:T(8,128)(2,1)S(1)}, u32[]{:S(2)}, u32[]{:S(2)}) collective-permute-start(bf16[64,1792]{1,0:T(8,128)(2,1)S(1)} %fusion.4.refs_0_), channel_id=1, source_target_pairs={{0,8},{8,0},{16,24},{24,16},{1,9},{9,1},{17,25},{25,17},{2,10},{10... | collective-permute-start | bytes 688136 | tf_op jit(solution)/shard_map/ppermute | solution.py:350
  31.4 17.3 %collective-permute-start.9 = (bf16[64,1792]{1,0:T(8,128)(2,1)S(1)}, bf16[64,1792]{1,0:T(8,128)(2,1)S(1)}, u32[]{:S(2)}, u32[]{:S(2)}) collective-permute-start(bf16[64,1792]{1,0:T(8,128)(2,1)S(1)} %fusion.4.refs_0_), channel_id=1, source_target_pairs={{0,16},{8,24},{16,0},{24,8},{1,17},{9,25},{17,1},{25,9},{2,18},{10... | collective-permute-start | bytes 688136 | tf_op jit(solution)/shard_map/ppermute | solution.py:350
  38.7 16.6 %collective-permute-start.8 = (bf16[2,64,2304]{2,1,0:T(8,128)(2,1)S(1)}, bf16[2,64,2304]{2,1,0:T(8,128)(2,1)S(1)}, u32[]{:S(2)}, u32[]{:S(2)}) collective-permute-start(bf16[2,64,2304]{2,1,0:T(8,128)(2,1)S(1)} %collective-permute-done.3.refs_1_), channel_id=1, source_target_pairs={{0,2},{2,4},{4,6},{6,7},{7,5},{5,3},{3,1},{1,0},{8,10},{10,12},{12... | collective-permute-start | bytes 1769480 | tf_op jit(solution)/shard_map/ppermute | solution.py:387
  42.8 13.6 %collective-permute-start.7 = (bf16[2,64,2304]{2,1,0:T(8,128)(2,1)S(1)}, bf16[2,64,2304]{2,1,0:T(8,128)(2,1)S(1)}, u32[]{:S(2)}, u32[]{:S(2)}) collective-permute-start(bf16[2,64,2304]{2,1,0:T(8,128)(2,1)S(1)} %collective-permute-done.1.up_ref), channel_id=1, source_target_pairs={{2,0},{4,2},{6,4},{7,6},{5,7},{3,5},{1,3},{0,1},{10,8},{12,10},{14... | collective-permute-start | bytes 1769480 | tf_op jit(solution)/shard_map/ppermute | solution.py:386
  42.8 7.5 %copy-start.1 = (s32[2,512]{1,0:T(2,128)S(1)}, s32[2,512]{1,0:T(2,128)}, u32[]{:S(2)}) copy-start(s32[2,512]{1,0:T(2,128)} %sampled_ref.1) | copy-start | bytes 12292
  48.7 1.6 %collective-permute-start.11 = (bf16[64,1792]{1,0:T(8,128)(2,1)S(1)}, bf16[64,1792]{1,0:T(8,128)(2,1)S(1)}, u32[]{:S(2)}, u32[]{:S(2)}) collective-permute-start(bf16[64,1792]{1,0:T(8,128)(2,1)S(1)} %collective-permute-done.9.refs_2_), channel_id=1, source_target_pairs={{0,8},{8,0},{16,24},{24,16},{1,9},{9,1},{17,25},{25,17},{2,10},{10... | collective-permute-start | bytes 688136 | tf_op jit(solution)/shard_map/ppermute | solution.py:350
  56.4 9.4 %collective-permute-start.12 = (bf16[64,2304]{1,0:T(8,128)(2,1)S(1)}, bf16[64,2304]{1,0:T(8,128)(2,1)S(1)}, u32[]{:S(2)}, u32[]{:S(2)}) collective-permute-start(bf16[64,2304]{1,0:T(8,128)(2,1)S(1)} %slice_bitcast_fusion.1), channel_id=1, source_target_pairs={{2,0},{4,2},{6,4},{7,6},{5,7},{3,5},{1,3},{0,1},{10,8},{12,10},{14... | collective-permute-start | bytes 884744 | tf_op jit(solution)/shard_map/ppermute | solution.py:404
  56.7 9.1 %collective-permute-start.13 = (bf16[64,2304]{1,0:T(8,128)(2,1)S(1)}, bf16[64,2304]{1,0:T(8,128)(2,1)S(1)}, u32[]{:S(2)}, u32[]{:S(2)}) collective-permute-start(bf16[64,2304]{1,0:T(8,128)(2,1)S(1)} %slice_bitcast_fusion), channel_id=1, source_target_pairs={{0,2},{2,4},{4,6},{6,7},{7,5},{5,3},{3,1},{1,0},{8,10},{10,12},{12... | collective-permute-start | bytes 884744 | tf_op jit(solution)/shard_map/ppermute | solution.py:405
  72.9 3.8 %collective-permute-start.14 = (f32[3,8,128]{2,1,0:T(8,128)S(1)}, f32[3,8,128]{2,1,0:T(8,128)S(1)}, u32[]{:S(2)}, u32[]{:S(2)}) collective-permute-start(f32[3,8,128]{2,1,0:T(8,128)S(1)} %chunk.3.refs_0_), channel_id=1, source_target_pairs={{0,1},{1,0},{2,3},{3,2},{4,5},{5,4},{6,7},{7,6},{8,9},{9,8},{10,11... | collective-permute-start | bytes 36872 | tf_op jit(solution)/shard_map/ppermute | solution.py:350
  76.7 4.5 %collective-permute-start.15 = (f32[3,8,128]{2,1,0:T(8,128)S(1)}, f32[3,8,128]{2,1,0:T(8,128)S(1)}, u32[]{:S(2)}, u32[]{:S(2)}) collective-permute-start(f32[3,8,128]{2,1,0:T(8,128)S(1)} %combine.2.refs_0_), channel_id=1, source_target_pairs={{0,2},{1,3},{2,0},{3,1},{4,6},{5,7},{6,4},{7,5},{8,10},{9,11},{10,... | collective-permute-start | bytes 36872 | tf_op jit(solution)/shard_map/ppermute | solution.py:350
  77.8 4.6 %collective-permute-start.16 = (f32[3,8,128]{2,1,0:T(8,128)S(1)}, f32[3,8,128]{2,1,0:T(8,128)S(1)}, u32[]{:S(2)}, u32[]{:S(2)}) collective-permute-start(f32[3,8,128]{2,1,0:T(8,128)S(1)} %combine.2.refs_0_), channel_id=1, source_target_pairs={{0,4},{1,5},{2,6},{3,7},{4,0},{5,1},{6,2},{7,3},{8,12},{9,13},{10,... | collective-permute-start | bytes 36872 | tf_op jit(solution)/shard_map/ppermute | solution.py:350
  79.2 5.5 %collective-permute-start.17 = (f32[3,8,128]{2,1,0:T(8,128)S(1)}, f32[3,8,128]{2,1,0:T(8,128)S(1)}, u32[]{:S(2)}, u32[]{:S(2)}) collective-permute-start(f32[3,8,128]{2,1,0:T(8,128)S(1)} %combine.2.refs_0_), channel_id=1, source_target_pairs={{0,6},{1,7},{2,4},{3,5},{4,2},{5,3},{6,0},{7,1},{8,14},{9,15},{10,... | collective-permute-start | bytes 36872 | tf_op jit(solution)/shard_map/ppermute | solution.py:350
